TPU v7x, 32 devices: a whole 2x2x4 slice. The times are simulated.
32 devices in a mesh: seq: 8 (over z, core), head: 4 (over y, x).
Axes of the slice: x: 2, y: 2, z: 4, core: 2. Of those that a mesh axis runs over, the one named last changes fastest.
Arguments:
- tokens: bfloat16 [6144, 2048], P('seq'), may hold values from -6 to 6
- lengths: int32 [4], replicated, may hold values from 96 to 5760, as said below
- norm1_gain: float32 [2048], replicated, may hold values from 0.5 to 1.5
- w_query: bfloat16 [2048, 2048], P(None, 'head'), may hold values from -0.125 to 0.125
- key_matrix: bfloat16 [2048, 1024], P(None, 'head'), may hold values from -0.125 to 0.125
- value_matrix: bfloat16 [2048, 1024], P(None, 'head'), may hold values from -0.125 to 0.125
- query_gain: float32 [128], replicated, may hold values from 1 to 2
- key_gain: float32 [128], replicated, may hold values from 0.5 to 1.5
- w_output: bfloat16 [2048, 2048], P('head'), may hold values from -0.5 to 0.5
- norm2_gain: float32 [2048], replicated, may hold values from 0.5 to 1.5
- w_gate: bfloat16 [2048, 6144], P(None, 'head'), may hold values from -0.125 to 0.125
- w_up: bfloat16 [2048, 6144], P(None, 'head'), may hold values from -0.125 to 0.125
- w_down: bfloat16 [6144, 2048], P('head'), may hold values from -0.15625 to 0.15625
- cotangent: bfloat16 [6144, 2048], P('seq'), may hold values from -6 to 6
Outputs:
- mixed: bfloat16 [6144, 2048], P('seq')
- grad_tokens: float32 [6144, 2048], P('seq')
- grad_norm1: float32 [2048], replicated
- grad_query: float32 [2048, 2048], P('seq', 'head')
- grad_key: float32 [2048, 1024], P('seq', 'head')
- grad_value: float32 [2048, 1024], P('seq', 'head')
- grad_qgain: float32 [128], replicated
- grad_kgain: float32 [128], replicated
- grad_output: float32 [2048, 2048], P('head', 'seq')
- grad_norm2: float32 [2048], replicated
- grad_gate: float32 [2048, 6144], P('seq', 'head')
- grad_up: float32 [2048, 6144], P('seq', 'head')
- grad_down: float32 [6144, 2048], P('head', 'seq')
Inputs may be any that keep to these rules, and one draw needn't show every extreme that they name: 4 lengths in packing order summing to 6144. One of them, at a place drawn from the seed, holds exactly 5760 tokens; the others together hold 384, each 96 to 192, and one of them exactly 96.
All inputs are finite; a program needn't handle non-finite values.
Results may differ from a plain program's by a relative error of at most 0.025.
Values may be sent and summed in bfloat16 or wider, within the bound.
No kernel may reach another device: no remote copies, remote signals or barrier semaphores. Data moves between devices by JAX's collectives and lax.ppermute only.
A program may use at most 192 MiB of HBM per device.

v0:
```python
import math

import jax
import jax.numpy as jnp
from jax import lax
from jax.sharding import PartitionSpec as P

HEAD_WIDTH = 128


EPSILON = 1e-06
ROPE_BASE = 1000000.0
NEGATIVE = -1e30


def locate(index, lengths):
    ends = jnp.cumsum(lengths)
    starts = ends - lengths
    segment = jnp.sum((index[:, None] >= ends[None, :]).astype(jnp.int32), axis=1)
    chosen = segment[:, None] == jnp.arange(lengths.shape[0], dtype=jnp.int32)[None, :]
    begin = jnp.sum(jnp.where(chosen, starts[None, :], 0), axis=1)
    return (segment, index - begin)


def rotary(position, head_size):
    half_size = head_size // 2
    freq_table = jnp.exp(
        jnp.arange(half_size, dtype=jnp.float32) * (-2.0 * math.log(ROPE_BASE) / head_size)
    )
    angle = position.astype(jnp.float32)[:, None] * freq_table[None, :]
    cosine = jnp.concatenate([jnp.cos(angle), jnp.cos(angle)], axis=1)
    sine_table = jnp.concatenate([jnp.sin(angle), jnp.sin(angle)], axis=1)
    return (cosine, sine_table)


def rotate(values, cosine, sine_table):
    half_size = values.shape[-1] // 2
    turned = jnp.concatenate([-values[..., half_size:], values[..., :half_size]], axis=-1)
    return values * cosine[:, None, :] + turned * sine_table[:, None, :]


def rms_scale(values, gain):
    inverse = lax.rsqrt(jnp.mean(values * values, axis=-1, keepdims=True) + EPSILON)
    return values * inverse * gain


def prepare(query_in, key_in, query_gain, key_gain, cosine, sine_table):
    row_count = query_in.shape[0]
    head_size = query_gain.shape[0]
    query_heads = query_in.reshape(row_count, -1, head_size)
    key_head_rows = key_in.reshape(row_count, -1, head_size)
    query_rot = rotate(rms_scale(query_heads, query_gain), cosine, sine_table)
    key_rot = rotate(rms_scale(key_head_rows, key_gain), cosine, sine_table)
    return (query_rot.reshape(row_count, -1), key_rot.reshape(row_count, -1))


def allowed_pairs(query_index, query_segment, key_start, key_rows, lengths):
    key_index = key_start + jnp.arange(key_rows, dtype=jnp.int32)
    key_segment, unused_position = locate(key_index, lengths)
    return (key_index[None, :] <= query_index[:, None]) & (
        key_segment[None, :] == query_segment[:, None]
    )


def attend(q_low, k_low, v_low, query_index, query_segment, lengths):
    row_count = q_low.shape[0]
    kv_heads = k_low.shape[1] // HEAD_WIDTH
    query_group_width = q_low.shape[1] // k_low.shape[1]
    query_four = q_low.reshape(row_count, kv_heads, query_group_width, HEAD_WIDTH)
    score_scale = 1.0 / math.sqrt(HEAD_WIDTH)
    last_query = query_index[row_count - 1]

    def one_block(carried, key_block, value_block, key_start):

        def one_work(running):
            running_max, running_sum, accumulated = running
            block_rows = key_block.shape[0]
            allowed = allowed_pairs(query_index, query_segment, key_start, block_rows, lengths)
            score = (
                jnp.einsum(
                    "qkgd,rkd->kgqr",
                    query_four,
                    key_block.reshape(block_rows, kv_heads, HEAD_WIDTH),
                    preferred_element_type=jnp.float32,
                )
                * score_scale
            )
            score = jnp.where(allowed, score, NEGATIVE)
            new_max = jnp.maximum(running_max, jnp.max(score, axis=-1))
            weights = jnp.where(allowed, jnp.exp(score - new_max[..., None]), 0.0)
            factor = jnp.exp(running_max - new_max)
            running_sum = running_sum * factor + jnp.sum(weights, axis=-1)
            update = jnp.einsum(
                "kgqr,rkd->qkgd",
                weights.astype(jnp.bfloat16),
                value_block.reshape(block_rows, kv_heads, HEAD_WIDTH),
                preferred_element_type=jnp.float32,
            )
            accumulated = accumulated * jnp.transpose(factor, (2, 0, 1))[..., None] + update
            return (new_max, running_sum, accumulated)

        def keep_state(running):
            return running

        return lax.cond(key_start <= last_query, one_work, keep_state, carried)

    initial = (
        jnp.full((kv_heads, query_group_width, row_count), NEGATIVE, jnp.float32),
        jnp.zeros((kv_heads, query_group_width, row_count), jnp.float32),
        jnp.zeros((row_count, kv_heads, query_group_width, HEAD_WIDTH), jnp.float32),
    )
    carried = initial
    key_piece = lax.all_gather(k_low, "seq", axis=0, tiled=True)
    value_piece = lax.all_gather(v_low, "seq", axis=0, tiled=True)
    piece_rows = key_piece.shape[0]
    block_count = piece_rows // row_count
    key_blocks = key_piece.reshape(block_count, row_count, -1)
    value_blocks = value_piece.reshape(block_count, row_count, -1)
    block_starts = row_count * jnp.arange(block_count, dtype=jnp.int32)

    def fold_scan_step(running, block_items):
        return (one_block(running, block_items[0], block_items[1], block_items[2]), None)

    carried, unused_out = lax.scan(
        fold_scan_step, carried, (key_blocks, value_blocks, block_starts)
    )
    final_max, final_sum, accumulated = carried
    outcome = accumulated / jnp.transpose(final_sum, (2, 0, 1))[..., None]
    logsum = final_max + jnp.log(final_sum)
    return (outcome.reshape(row_count, -1), logsum)


def attend_back(
    q_low, key_all, value_all, grad_low, outcome, logsum, query_index, query_segment, lengths
):
    row_count = q_low.shape[0]
    kv_heads = key_all.shape[1] // HEAD_WIDTH
    query_group_width = q_low.shape[1] // key_all.shape[1]
    query_four = q_low.reshape(row_count, kv_heads, query_group_width, HEAD_WIDTH)
    grad_four = grad_low.reshape(row_count, kv_heads, query_group_width, HEAD_WIDTH)
    score_scale = 1.0 / math.sqrt(HEAD_WIDTH)
    last_query = query_index[row_count - 1]
    delta = jnp.transpose(
        jnp.sum(
            grad_four.astype(jnp.float32)
            * outcome.reshape(row_count, kv_heads, query_group_width, HEAD_WIDTH),
            axis=-1,
        ),
        (1, 2, 0),
    )
    block_count = key_all.shape[0] // row_count
    key_blocks = key_all.reshape(block_count, row_count, kv_heads, HEAD_WIDTH)
    value_blocks = value_all.reshape(block_count, row_count, kv_heads, HEAD_WIDTH)
    block_starts = row_count * jnp.arange(block_count, dtype=jnp.int32)

    def attend_scan_step(query_grad, block_items):
        key_block, value_block, key_start = block_items

        def attend_work(grad_in):
            allowed = allowed_pairs(query_index, query_segment, key_start, row_count, lengths)
            score = (
                jnp.einsum(
                    "qkgd,rkd->kgqr", query_four, key_block, preferred_element_type=jnp.float32
                )
                * score_scale
            )
            weights = jnp.exp(jnp.where(allowed, score - logsum[..., None], NEGATIVE))
            value_grad = jnp.einsum(
                "kgqr,qkgd->rkd",
                weights.astype(jnp.bfloat16),
                grad_four,
                preferred_element_type=jnp.float32,
            )
            prob_grad = jnp.einsum(
                "qkgd,rkd->kgqr", grad_four, value_block, preferred_element_type=jnp.float32
            )
            score_grad = (weights * (prob_grad - delta[..., None])).astype(jnp.bfloat16)
            grad_out = grad_in + score_scale * jnp.einsum(
                "kgqr,rkd->qkgd", score_grad, key_block, preferred_element_type=jnp.float32
            )
            key_grad = score_scale * jnp.einsum(
                "kgqr,qkgd->rkd", score_grad, query_four, preferred_element_type=jnp.float32
            )
            return (grad_out, key_grad.reshape(row_count, -1), value_grad.reshape(row_count, -1))

        def skipped(grad_in):
            empty = jnp.zeros((row_count, kv_heads * HEAD_WIDTH), jnp.float32)
            return (grad_in, empty, empty)

        grad_out, key_grad, value_grad = lax.cond(
            key_start <= last_query, attend_work, skipped, query_grad
        )
        return (grad_out, (key_grad, value_grad))

    initial = jnp.zeros((row_count, kv_heads, query_group_width, HEAD_WIDTH), jnp.float32)
    query_grad, block_grads = lax.scan(
        attend_scan_step, initial, (key_blocks, value_blocks, block_starts)
    )
    key_grads = block_grads[0].reshape(-1, kv_heads * HEAD_WIDTH)
    value_grads = block_grads[1].reshape(-1, kv_heads * HEAD_WIDTH)
    return (query_grad.reshape(row_count, -1), key_grads, value_grads)


def forward_pass(tokens, weights, frame, finish):
    (
        norm1_gain,
        w_query,
        key_matrix,
        value_matrix,
        query_gain,
        key_gain,
        w_output,
        norm2_gain,
        w_gate,
        w_up,
        w_down,
    ) = weights
    query_index, query_segment, lengths, cosine, sine_table = frame
    token_float = tokens.astype(jnp.float32)
    first_in = rms_scale(token_float, norm1_gain).astype(jnp.bfloat16)
    query_raw = jnp.dot(first_in, w_query, preferred_element_type=jnp.float32)
    key_raw = jnp.dot(first_in, key_matrix, preferred_element_type=jnp.float32)
    value_raw = jnp.dot(first_in, value_matrix, preferred_element_type=jnp.float32)
    query_rot, key_rot = prepare(query_raw, key_raw, query_gain, key_gain, cosine, sine_table)
    q_low = query_rot.astype(jnp.bfloat16)
    k_low = key_rot.astype(jnp.bfloat16)
    v_low = value_raw.astype(jnp.bfloat16)
    outcome, logsum = attend(q_low, k_low, v_low, query_index, query_segment, lengths)
    o_low = outcome.astype(jnp.bfloat16)
    attn_partial = jnp.dot(o_low, w_output, preferred_element_type=jnp.float32)
    hidden = token_float + lax.psum(attn_partial.astype(jnp.bfloat16), "head").astype(jnp.float32)
    second_in = rms_scale(hidden, norm2_gain).astype(jnp.bfloat16)
    gate_raw = jnp.dot(second_in, w_gate, preferred_element_type=jnp.float32)
    up_raw = jnp.dot(second_in, w_up, preferred_element_type=jnp.float32)
    mixed_low = (jax.nn.silu(gate_raw) * up_raw).astype(jnp.bfloat16)
    saved = (
        first_in,
        query_raw,
        key_raw,
        q_low,
        k_low,
        v_low,
        outcome,
        logsum,
        o_low,
        hidden,
        second_in,
        gate_raw,
        up_raw,
        mixed_low,
    )
    if not finish:
        return (None, saved)
    down_partial = jnp.dot(mixed_low, w_down, preferred_element_type=jnp.float32)
    mixed = (
        hidden + lax.psum(down_partial.astype(jnp.bfloat16), "head").astype(jnp.float32)
    ).astype(jnp.bfloat16)
    return (mixed, saved)


def body(
    tokens,
    lengths,
    norm1_gain,
    w_query,
    key_matrix,
    value_matrix,
    query_gain,
    key_gain,
    w_output,
    norm2_gain,
    w_gate,
    w_up,
    w_down,
    cotangent,
):
    row_count = tokens.shape[0]
    query_index = lax.axis_index("seq") * row_count + jnp.arange(row_count, dtype=jnp.int32)
    query_segment, position = locate(query_index, lengths)
    cosine, sine_table = rotary(position, HEAD_WIDTH)
    frame = (query_index, query_segment, lengths, cosine, sine_table)
    weights = (
        norm1_gain,
        w_query,
        key_matrix,
        value_matrix,
        query_gain,
        key_gain,
        w_output,
        norm2_gain,
        w_gate,
        w_up,
        w_down,
    )
    result, saved = forward_pass(tokens, weights, frame, True)
    barrier_out = lax.optimization_barrier((tokens, weights, result))
    unused_result, restored = forward_pass(barrier_out[0], barrier_out[1], frame, False)
    (
        first_in,
        query_raw,
        key_raw,
        q_low,
        k_low,
        v_low,
        outcome,
        logsum,
        o_low,
        hidden,
        second_in,
        gate_raw,
        up_raw,
        mixed_low,
    ) = restored
    token_float = tokens.astype(jnp.float32)
    upstream = cotangent.astype(jnp.float32)
    grad_down = jnp.dot(mixed_low.T, cotangent, preferred_element_type=jnp.float32)
    mixed_grad = jnp.dot(cotangent, w_down.T, preferred_element_type=jnp.float32)
    unused_swiglu, swiglu_back = jax.vjp(
        lambda gate_in, up_in: jax.nn.silu(gate_in) * up_in, gate_raw, up_raw
    )
    gate_grad, up_grad = swiglu_back(mixed_grad)
    gate_low = gate_grad.astype(jnp.bfloat16)
    up_low = up_grad.astype(jnp.bfloat16)
    grad_gate = jnp.dot(second_in.T, gate_low, preferred_element_type=jnp.float32)
    grad_up = jnp.dot(second_in.T, up_low, preferred_element_type=jnp.float32)
    second_grad = jnp.dot(gate_low, w_gate.T, preferred_element_type=jnp.float32) + jnp.dot(
        up_low, w_up.T, preferred_element_type=jnp.float32
    )
    grad_gate, grad_up, grad_down = (
        lax.psum_scatter(
            grad_gate.astype(jnp.bfloat16), "seq", scatter_dimension=0, tiled=True
        ).astype(jnp.float32),
        lax.psum_scatter(
            grad_up.astype(jnp.bfloat16), "seq", scatter_dimension=0, tiled=True
        ).astype(jnp.float32),
        lax.psum_scatter(
            grad_down.astype(jnp.bfloat16), "seq", scatter_dimension=1, tiled=True
        ).astype(jnp.float32),
    )
    unused_norm2, norm2_back = jax.vjp(rms_scale, hidden, norm2_gain)
    hidden_part, grad_norm2 = norm2_back(second_grad)
    hidden_grad = upstream + lax.psum(hidden_part.astype(jnp.bfloat16), "head").astype(jnp.float32)
    branch_low = hidden_grad.astype(jnp.bfloat16)
    grad_output = jnp.dot(o_low.T, branch_low, preferred_element_type=jnp.float32)
    outcome_grad = jnp.dot(branch_low, w_output.T, preferred_element_type=jnp.float32).astype(
        jnp.bfloat16
    )
    key_all, value_all = (
        lax.all_gather(k_low, "seq", axis=0, tiled=True),
        lax.all_gather(v_low, "seq", axis=0, tiled=True),
    )
    rot_query_grad, key_grad_all, value_grad_all = attend_back(
        q_low,
        key_all,
        value_all,
        outcome_grad,
        outcome,
        logsum,
        query_index,
        query_segment,
        lengths,
    )
    rot_key_grad, value_grad = (
        lax.psum_scatter(
            key_grad_all.astype(jnp.bfloat16), "seq", scatter_dimension=0, tiled=True
        ).astype(jnp.float32),
        lax.psum_scatter(
            value_grad_all.astype(jnp.bfloat16), "seq", scatter_dimension=0, tiled=True
        ).astype(jnp.float32),
    )
    unused_prep, prep_back = jax.vjp(
        lambda query_in, key_in, qgain_in, kgain_in: prepare(
            query_in, key_in, qgain_in, kgain_in, cosine, sine_table
        ),
        query_raw,
        key_raw,
        query_gain,
        key_gain,
    )
    query_grad, key_grad, grad_qgain, grad_kgain = prep_back((rot_query_grad, rot_key_grad))
    query_reduced = query_grad.astype(jnp.bfloat16)
    key_reduced = key_grad.astype(jnp.bfloat16)
    value_reduced = value_grad.astype(jnp.bfloat16)
    grad_query = jnp.dot(first_in.T, query_reduced, preferred_element_type=jnp.float32)
    grad_key = jnp.dot(first_in.T, key_reduced, preferred_element_type=jnp.float32)
    grad_value = jnp.dot(first_in.T, value_reduced, preferred_element_type=jnp.float32)
    first_grad = (
        jnp.dot(query_reduced, w_query.T, preferred_element_type=jnp.float32)
        + jnp.dot(key_reduced, key_matrix.T, preferred_element_type=jnp.float32)
        + jnp.dot(value_reduced, value_matrix.T, preferred_element_type=jnp.float32)
    )
    unused_norm1, norm1_back = jax.vjp(rms_scale, token_float, norm1_gain)
    token_part, grad_norm1 = norm1_back(first_grad)
    grad_tokens = hidden_grad + lax.psum(token_part.astype(jnp.bfloat16), "head").astype(
        jnp.float32
    )
    grad_query, grad_key, grad_value, grad_output = (
        lax.psum_scatter(
            grad_query.astype(jnp.bfloat16), "seq", scatter_dimension=0, tiled=True
        ).astype(jnp.float32),
        lax.psum_scatter(
            grad_key.astype(jnp.bfloat16), "seq", scatter_dimension=0, tiled=True
        ).astype(jnp.float32),
        lax.psum_scatter(
            grad_value.astype(jnp.bfloat16), "seq", scatter_dimension=0, tiled=True
        ).astype(jnp.float32),
        lax.psum_scatter(
            grad_output.astype(jnp.bfloat16), "seq", scatter_dimension=1, tiled=True
        ).astype(jnp.float32),
    )
    grad_norm1, grad_qgain, grad_kgain, grad_norm2 = lax.psum(
        (grad_norm1, grad_qgain, grad_kgain, grad_norm2), ("seq", "head")
    )
    return (
        result,
        grad_tokens,
        grad_norm1,
        grad_query,
        grad_key,
        grad_value,
        grad_qgain,
        grad_kgain,
        grad_output,
        grad_norm2,
        grad_gate,
        grad_up,
        grad_down,
    )


def solution(mesh):
    in_specs = (
        P("seq", None),
        P(),
        P(),
        P(None, "head"),
        P(None, "head"),
        P(None, "head"),
        P(),
        P(),
        P("head", None),
        P(),
        P(None, "head"),
        P(None, "head"),
        P("head", None),
        P("seq", None),
    )
    out_specs = (
        P("seq", None),
        P("seq", None),
        P(),
        P("seq", "head"),
        P("seq", "head"),
        P("seq", "head"),
        P(),
        P(),
        P("head", "seq"),
        P(),
        P("seq", "head"),
        P("seq", "head"),
        P("head", "seq"),
    )
    return jax.shard_map(body, mesh=mesh, in_specs=in_specs, out_specs=out_specs, check_vma=False)
```

profile of v0, /device:TPU:0, one launch (start us, length us, event | category | flops | bytes accessed | tf_op | source)
XLA Modules:
  0.0 1614.7 jit_solution(17710229401439462399)
XLA Ops:
  29.9 28.4 %all-gather.5.cloned.1.call-done = bf16[6144,256]{0,1:T(8,128)(2,1)} async-done(((bf16[768,256]{0,1:T(8,128)(2,1)}), bf16[6144,256]{0,1:T(8,128)(2,1)}) %all-gather.5.cloned.1.call-update) | async-done | bytes 3145744 | tf_op jit(solution)/shard_map/all_gather | solution.py:113
  62.1 35.6 %all-gather.7.cloned.1.call-done = bf16[6144,256]{1,0:T(8,128)(2,1)} async-done(((bf16[768,256]{1,0:T(8,128)(2,1)}), bf16[6144,256]{1,0:T(8,128)(2,1)}) %all-gather.7.cloned.1.call-update) | async-done | bytes 3145744 | tf_op jit(solution)/shard_map/all_gather | solution.py:114
  103.8 27.0 %while.48 = (s32[]{:T(128)}, f32[2,2,768]{2,1,0:T(2,128)S(1)}, f32[2,2,768]{2,1,0:T(2,128)S(1)}, f32[768,2,2,128]{3,0,2,1:T(8,128)}, s32[8]{0:T(128)S(1)}, /*ind...) while((s32[]{:T(128)}, f32[2,2,768]{2,1,0:T(2,128)S(1)}, ...), condition=%wide.region_13.14_spmd.clone, body=%wide.region_6.13_spmd.clone.sunk | while | flops 1241205504 | bytes 49772968 | solution.py:124
  138.9 164.5 %all-reduce.11.cloned.1.call-done = bf16[768,2048]{1,0:T(8,128)(2,1)} async-done(((bf16[768,2048]{1,0:T(8,128)(2,1)}), bf16[768,2048]{1,0:T(8,128)(2,1)}) %all-reduce.11.cloned.1.call-update) | async-done | bytes 3145744 | tf_op jit(solution)/shard_map/psum | solution.py:231
  318.2 18.7 %convolution_convert_fusion.5 = bf16[768,2048]{1,0:T(8,128)(2,1)} fusion(bf16[1536,2048]{1,0:T(8,128)(2,1)} %param.38, f32[768,1536]{1,0:T(8,128)} %fusion.91, bf16[2048,1536]{1,0:T(8,128)(2,1)} %param.37, bf16[768,2048]{1,0:T(8,128)(2,1)} %all-reduce.11.cloned.1.call-done, bf16[768,2048]{1,0:T(8,128)(2,1)} %param.26, f32[2048]{0:T(1024)S(1)} %copy-done.49, ...), kind=kOutput, calls=%fused_computation.120 | convolution fusion | flops 9681764352 | bytes 26749952 | tf_op jit(solution)/shard_map/dot_general | solution.py:254
  337.0 87.3 %all-reduce.13.cloned.1.call-done = bf16[768,2048]{1,0:T(8,128)(2,1)} async-done(((bf16[768,2048]{1,0:T(8,128)(2,1)}), bf16[768,2048]{1,0:T(8,128)(2,1)}) %all-reduce.13.cloned.1.call-update) | async-done | bytes 3145744 | tf_op jit(solution)/shard_map/psum | solution.py:256
  448.8 25.0 %all-gather.11.cloned.1.call-done = bf16[6144,256]{1,0:T(8,128)(2,1)} async-done(((bf16[768,256]{1,0:T(8,128)(2,1)}), bf16[6144,256]{1,0:T(8,128)(2,1)}) %all-gather.11.cloned.1.call-update) | async-done | bytes 3145744 | tf_op jit(solution)/shard_map/all_gather | solution.py:114
  478.6 34.4 %all-gather.9.cloned.1.call-done = bf16[6144,256]{0,1:T(8,128)(2,1)} async-done(((bf16[768,256]{0,1:T(8,128)(2,1)}), bf16[6144,256]{0,1:T(8,128)(2,1)}) %all-gather.9.cloned.1.call-update) | async-done | bytes 3145744 | tf_op jit(solution)/shard_map/all_gather | solution.py:113
  518.0 28.0 %while.49 = (s32[]{:T(128)}, f32[2,2,768]{2,1,0:T(2,128)S(1)}, f32[2,2,768]{2,1,0:T(2,128)S(1)}, f32[768,2,2,128]{3,0,2,1:T(8,128)}, s32[8]{0:T(128)S(1)}, /*ind...) while((s32[]{:T(128)}, f32[2,2,768]{2,1,0:T(2,128)S(1)}, ...), condition=%wide.region_27.28_spmd.clone, body=%wide.region_20.0_spmd.clone.sunk | while | flops 1241205504 | bytes 49772968 | solution.py:124
  519.9 12.2 conditional.10
  555.4 171.1 %all-reduce.15.cloned.1.call-done = bf16[768,2048]{1,0:T(8,128)(2,1)} async-done(((bf16[768,2048]{1,0:T(8,128)(2,1)}), bf16[768,2048]{1,0:T(8,128)(2,1)}) %all-reduce.15.cloned.1.call-update) | async-done | bytes 3145744 | tf_op jit(solution)/shard_map/psum | solution.py:231
  805.5 69.5 %all-reduce.17.cloned.1.call-done = bf16[768,2048]{1,0:T(8,128)(2,1)} async-done(((bf16[768,2048]{1,0:T(8,128)(2,1)}), bf16[768,2048]{1,0:T(8,128)(2,1)}) %all-reduce.17.cloned.1.call-update) | async-done | bytes 3145744 | tf_op jit(solution)/shard_map/psum | solution.py:342
  882.3 77.6 %while.50 = (s32[]{:T(128)}, f32[768,2,2,128]{3,0,2,1:T(8,128)}, bf16[8,768,256]{2,1,0:T(8,128)(2,1)}, bf16[8,768,256]{2,1,0:T(8,128)(2,1)}, s32[8]{0:T(128)S(1)...) while((s32[]{:T(128)}, f32[768,2,2,128]{3,0,2,1:T(8,128)}, ...), condition=%wide.region_38.39_spmd.clone, body=%wide.region_33.38_spmd.clone.sunk | while | flops 3046450944 | bytes 71438784 | solution.py:196
  884.3 17.3 %conditional.11 = (f32[768,2,2,128]{3,0,2,1:T(8,128)}, bf16[1,768,256]{1,2,0:T(8,128)(2,1)S(1)}, bf16[1,768,256]{1,2,0:T(8,128)(2,1)}) conditional(s32[]{:T(128)} %convert_element_type.478, f32[768,2,2,128]{3,0,2,1:T(8,128)} %get-tuple-element.1280, (s32[]{:T(128)}, s32[]{:T(128)}, s32[4]{0:T(128)S(1)}, s32[768]{0:T(1024)S(1)}, ...), branch_computations={%region_34.34_spmd, %region_35.37_spmd} | conditional | flops 3046450944 | bytes 68289192 | solution.py:190
  979.2 136.1 %reduce-scatter.12.cloned.1.call-done = bf16[768,256]{1,0:T(8,128)(2,1)} async-done(((bf16[6144,256]{1,0:T(8,128)(2,1)}), bf16[768,256]{1,0:T(8,128)(2,1)}) %reduce-scatter.12.cloned.1.call-update) | async-done | bytes 393232 | tf_op jit(solution)/shard_map/reduce_scatter | solution.py:367
  1119.7 37.8 %reduce-scatter.10.cloned.1.call-done = bf16[768,256]{1,0:T(8,128)(2,1)} async-done(((bf16[6144,256]{1,0:T(8,128)(2,1)}), bf16[768,256]{1,0:T(8,128)(2,1)}) %reduce-scatter.10.cloned.1.call-update) | async-done | bytes 393232 | tf_op jit(solution)/shard_map/reduce_scatter | solution.py:364
  1165.5 11.5 convolution_convert_fusion
  1210.2 21.1 %reduce-scatter.14.cloned.1.call-done = bf16[256,512]{1,0:T(8,128)(2,1)} async-done(((bf16[2048,512]{1,0:T(8,128)(2,1)}), bf16[256,512]{1,0:T(8,128)(2,1)}) %reduce-scatter.14.cloned.1.call-update) | async-done | bytes 262160 | tf_op jit(solution)/shard_map/reduce_scatter | solution.py:398
  1233.2 38.8 %all-reduce.4 = (f32[2048]{0:T(1024)}, f32[128]{0:T(128)}, f32[128]{0:T(128)}, f32[2048]{0:T(1024)}) all-reduce(f32[2048]{0:T(1024)S(1)} %get-tuple-element.768, f32[128]{0:T(128)S(1)} %get-tuple-element.770, f32[128]{0:T(128)S(1)} %get-tuple-element.772, f32[2048]{0:T(1024)S(1)} %copy-done.58), channel_id=1, replica_groups=mesh['seq'=8,'head'=4] {'seq','head'}, use_global_device_ids=true, to_apply=%region_46.47 | all-reduce | flops 4352 | bytes 34816 | tf_op jit(solution)/shard_map/psum | solution.py:411
  1273.6 25.5 %reduce-scatter.16.cloned.1.call-done = bf16[256,256]{1,0:T(8,128)(2,1)} async-done(((bf16[2048,256]{1,0:T(8,128)(2,1)}), bf16[256,256]{1,0:T(8,128)(2,1)}) %reduce-scatter.16.cloned.1.call-update) | async-done | bytes 131088 | tf_op jit(solution)/shard_map/reduce_scatter | solution.py:401
  1300.7 68.6 %reduce-scatter.26.cloned.1.call-done = bf16[1536,256]{1,0:T(8,128)(2,1)} async-done(((bf16[1536,2048]{1,0:T(8,128)(2,1)}), bf16[1536,256]{1,0:T(8,128)(2,1)}) %reduce-scatter.26.cloned.1.call-update) | async-done | bytes 786448 | tf_op jit(solution)/shard_map/reduce_scatter | solution.py:336
  1371.7 68.0 %reduce-scatter.24.cloned.1.call-done = bf16[256,1536]{1,0:T(8,128)(2,1)} async-done(((bf16[2048,1536]{1,0:T(8,128)(2,1)}), bf16[256,1536]{1,0:T(8,128)(2,1)}) %reduce-scatter.24.cloned.1.call-update) | async-done | bytes 786448 | tf_op jit(solution)/shard_map/reduce_scatter | solution.py:333
  1442.1 68.5 %reduce-scatter.22.cloned.1.call-done = bf16[256,1536]{1,0:T(8,128)(2,1)} async-done(((bf16[2048,1536]{1,0:T(8,128)(2,1)}), bf16[256,1536]{1,0:T(8,128)(2,1)}) %reduce-scatter.22.cloned.1.call-update) | async-done | bytes 786448 | tf_op jit(solution)/shard_map/reduce_scatter | solution.py:330
  1513.1 86.1 %all-reduce.19.cloned.1.call-done = bf16[768,2048]{1,0:T(8,128)(2,1)} async-done(((bf16[768,2048]{1,0:T(8,128)(2,1)}), bf16[768,2048]{1,0:T(8,128)(2,1)}) %all-reduce.19.cloned.1.call-update) | async-done | bytes 3145744 | tf_op jit(solution)/shard_map/psum | solution.py:394
  (427 shorter events, 386.6 us)
Async XLA Ops:
  7.2 128.1 %copy-start = (bf16[512,2048]{1,0:T(8,128)(2,1)S(1)}, bf16[512,2048]{1,0:T(8,128)(2,1)}, u32[]{:S(2)}) copy-start(bf16[512,2048]{1,0:T(8,128)(2,1)} %param.34) | copy-start | bytes 6291460
  7.2 51.1 %all-gather.5.cloned.1.call-start = ((), (), s32[]{:S(2)}) async-start(), calls=%async_computation.9 | async-start | bytes 3538944 | tf_op jit(solution)/shard_map/all_gather | solution.py:113
  16.1 430.7 %copy-start.15 = (f32[768,128]{0,1:T(8,128)}, f32[768,128]{0,1:T(8,128)S(1)}, u32[]{:S(2)}) copy-start(f32[768,128]{0,1:T(8,128)S(1)} %get-tuple-element.906) | copy-start | bytes 1179652
  17.2 80.5 %all-gather.7.cloned.1.call-start = ((), (), s32[]{:S(2)}) async-start(), calls=%async_computation.10 | async-start | bytes 3538944 | tf_op jit(solution)/shard_map/all_gather | solution.py:114
  21.2 282.2 %all-reduce.11.cloned.1.call-start = ((), (), s32[]{:S(2)}) async-start(), calls=%async_computation.11 | async-start | bytes 6291456 | tf_op jit(solution)/shard_map/psum | solution.py:231
  138.8 168.6 %copy-start.49 = (f32[2048]{0:T(1024)S(1)}, f32[2048]{0:T(1024)}, u32[]{:S(2)}) copy-start(f32[2048]{0:T(1024)} %param.35) | copy-start | bytes 24580
  138.8 285.5 %all-reduce.13.cloned.1.call-start = ((), (), s32[]{:S(2)}) async-start(), calls=%async_computation.12 | async-start | bytes 6291456 | tf_op jit(solution)/shard_map/psum | solution.py:256
  337.0 136.8 %all-gather.11.cloned.1.call-start = ((), (), s32[]{:S(2)}) async-start(), calls=%async_computation.14 | async-start | bytes 3538944 | tf_op jit(solution)/shard_map/all_gather | solution.py:114
  435.3 77.7 %all-gather.9.cloned.1.call-start = ((), (), s32[]{:S(2)}) async-start(), calls=%async_computation.13 | async-start | bytes 3538944 | tf_op jit(solution)/shard_map/all_gather | solution.py:113
  441.2 285.3 %all-reduce.15.cloned.1.call-start = ((), (), s32[]{:S(2)}) async-start(), calls=%async_computation.15 | async-start | bytes 6291456 | tf_op jit(solution)/shard_map/psum | solution.py:231
  554.9 320.1 %all-reduce.17.cloned.1.call-start = ((), (), s32[]{:S(2)}) async-start(), calls=%async_computation.16 | async-start | bytes 6291456 | tf_op jit(solution)/shard_map/psum | solution.py:342
  787.7 327.7 %reduce-scatter.12.cloned.1.call-start = ((), (), s32[]{:S(2)}) async-start(), calls=%async_computation.18 | async-start | bytes 3538944 | tf_op jit(solution)/shard_map/reduce_scatter | solution.py:367
  960.0 197.5 %reduce-scatter.10.cloned.1.call-start = ((), (), s32[]{:S(2)}) async-start(), calls=%async_computation.17 | async-start | bytes 3538944 | tf_op jit(solution)/shard_map/reduce_scatter | solution.py:364
  960.6 247.8 %reduce-scatter.20.cloned.1.call-start = ((), (), s32[]{:S(2)}) async-start(), calls=%async_computation.23 | async-start | bytes 2359296 | tf_op jit(solution)/shard_map/reduce_scatter | solution.py:407
  967.2 264.2 %reduce-scatter.14.cloned.1.call-start = ((), (), s32[]{:S(2)}) async-start(), calls=%async_computation.20 | async-start | bytes 2359296 | tf_op jit(solution)/shard_map/reduce_scatter | solution.py:398
  979.1 292.8 %reduce-scatter.18.cloned.1.call-start = ((), (), s32[]{:S(2)}) async-start(), calls=%async_computation.22 | async-start | bytes 1179648 | tf_op jit(solution)/shard_map/reduce_scatter | solution.py:404
  1119.6 41.4 %copy-start.14 = (f32[768,256]{0,1:T(8,128)S(1)}, f32[768,256]{0,1:T(8,128)}, u32[]{:S(2)}) copy-start(f32[768,256]{0,1:T(8,128)} %copy-done.13) | copy-start | bytes 2359300
  1119.6 41.4 %copy-start.42 = (f32[768,2]{0,1:T(2,128)S(1)}, f32[768,2]{0,1:T(2,128)}, u32[]{:S(2)}) copy-start(f32[768,2]{0,1:T(2,128)} %copy-done.41) | copy-start | bytes 18436
  1119.6 41.4 %copy-start.57 = (f32[128]{0:T(128)S(1)}, f32[128]{0:T(128)}, u32[]{:S(2)}) copy-start(f32[128]{0:T(128)} %param.33) | copy-start | bytes 1540
  1119.6 179.5 %reduce-scatter.16.cloned.1.call-start = ((), (), s32[]{:S(2)}) async-start(), calls=%async_computation.21 | async-start | bytes 1179648 | tf_op jit(solution)/shard_map/reduce_scatter | solution.py:401
  1165.4 203.9 %reduce-scatter.26.cloned.1.call-start = ((), (), s32[]{:S(2)}) async-start(), calls=%async_computation.26 | async-start | bytes 7077888 | tf_op jit(solution)/shard_map/reduce_scatter | solution.py:336
  1177.0 262.7 %reduce-scatter.24.cloned.1.call-start = ((), (), s32[]{:S(2)}) async-start(), calls=%async_computation.25 | async-start | bytes 7077888 | tf_op jit(solution)/shard_map/reduce_scatter | solution.py:333
  1186.7 323.9 %reduce-scatter.22.cloned.1.call-start = ((), (), s32[]{:S(2)}) async-start(), calls=%async_computation.24 | async-start | bytes 7077888 | tf_op jit(solution)/shard_map/reduce_scatter | solution.py:330
  1196.0 403.2 %all-reduce.19.cloned.1.call-start = ((), (), s32[]{:S(2)}) async-start(), calls=%async_computation.19 | async-start | bytes 6291456 | tf_op jit(solution)/shard_map/psum | solution.py:394
  (60 other events, 270.9 us)
Sparse Core Ops, SparseCore 0:
  17.3 40.9 all-gather.4
  60.5 37.1 all-gather.6
  139.0 164.3 all-reduce.10
  337.1 87.1 all-reduce.12
  435.4 38.2 all-gather.10
  475.8 37.1 all-gather.8
  555.1 171.3 all-reduce.14
  787.8 87.1 all-reduce.16
  960.1 155.1 reduce-scatter.11
  1118.1 39.3 reduce-scatter.9
  1159.8 34.8 reduce-scatter.19
  1196.8 34.4 reduce-scatter.13
  1234.2 31.5 reduce-scatter.17
  1268.5 30.5 reduce-scatter.15
  1301.3 67.9 reduce-scatter.25
  1371.5 68.1 reduce-scatter.23
  1442.4 68.1 reduce-scatter.21
  1513.6 85.5 all-reduce.18
where the time goes:
time: 1630 us; the launch traced here: 1610 us
  waiting for transfers between devices  1130 us (69%)
  matrix products  197 us (12%)
  local copies, waits for them, and re-layouts  126 us (8%)
  other arithmetic  74.9 us (5%)
  blocking collectives  38.8 us (2%)
  loops' own time  33.4 us (2%)
    psum x2, waiting for transfers between devices, forward_pass(): lax.psum(attn_partial.astype(jnp.bfloat16), 'head').astype(jnp.float32)  336 us
    reduce_scatter x1, waiting for transfers between devices, body(): lax.psum_scatter(value_grad_all.astype(jnp.bfloat16), 'seq', scatter_dime...  136 us
    psum x1, waiting for transfers between devices, forward_pass(): lax.psum(down_partial.astype(jnp.bfloat16), 'head').astype(jnp.float32)  87.3 us
    psum x1, waiting for transfers between devices, body(): lax.psum(token_part.astype(jnp.bfloat16), 'head').astype(jnp.float32)  86.1 us
    psum x1, waiting for transfers between devices, body(): lax.psum(hidden_part.astype(jnp.bfloat16), 'head').astype(jnp.float32)  69.5 us
    reduce_scatter x1, waiting for transfers between devices, body(): lax.psum_scatter(grad_down.astype(jnp.bfloat16), 'seq', scatter_dimension...  68.6 us
    reduce_scatter x1, waiting for transfers between devices, body(): lax.psum_scatter(grad_gate.astype(jnp.bfloat16), 'seq', scatter_dimension...  68.5 us
    reduce_scatter x1, waiting for transfers between devices, body(): lax.psum_scatter(grad_up.astype(jnp.bfloat16), 'seq', scatter_dimension=0...  68 us
  transfers between devices with their start and end apart: 18, of which 16 were waited for; matrix products, arithmetic and copies ran while one was open for 8% of the time, Pallas kernels for 0%

commit v1 on v0

v1 whole, which is shorter than its diff:
```python
import functools
import math

import jax
import jax.numpy as jnp
from jax import lax
from jax.experimental import pallas as pl
from jax.experimental.pallas import tpu as pltpu
from jax.sharding import PartitionSpec as P

HEAD_WIDTH = 128
EPSILON = 1e-06
ROPE_BASE = 1000000.0
LOG2E = math.log2(math.e)
SCORE_SCALE = 1.0 / math.sqrt(HEAD_WIDTH)
SCORE_SCALE_2 = LOG2E / math.sqrt(HEAD_WIDTH)
KEY_CHUNK = 256
MIB = 2**20

f32 = jnp.float32
bf16 = jnp.bfloat16
NT = (((1,), (1,)), ((), ()))
TN = (((0,), (0,)), ((), ()))


def dot(left, right):
    return jnp.dot(left, right, preferred_element_type=f32)


def dot_nt(left, right):
    return lax.dot_general(left, right, NT, preferred_element_type=f32)


def dot_tn(left, right):
    return lax.dot_general(left, right, TN, preferred_element_type=f32)


def locate(index, lengths):
    ends = jnp.cumsum(lengths)
    starts = ends - lengths
    segment = jnp.sum((index[:, None] >= ends[None, :]).astype(jnp.int32), axis=1)
    chosen = segment[:, None] == jnp.arange(lengths.shape[0], dtype=jnp.int32)[None, :]
    return jnp.sum(jnp.where(chosen, starts[None, :], 0), axis=1)


def rotary(position):
    half = HEAD_WIDTH // 2
    freq = jnp.exp(jnp.arange(half, dtype=f32) * (-2.0 * math.log(ROPE_BASE) / HEAD_WIDTH))
    angle = position.astype(f32)[:, None] * freq[None, :]
    cosine = jnp.cos(angle)
    sine = jnp.sin(angle)
    return (
        jnp.concatenate([cosine, cosine], axis=1),
        jnp.concatenate([-sine, sine], axis=1),
    )


def head_prep_kernel(raw_ref, gain_ref, cos_ref, sin_ref, out_ref):
    raw = raw_ref[...]
    inverse = lax.rsqrt(jnp.mean(raw * raw, axis=-1, keepdims=True) + EPSILON)
    scaled = raw * inverse * gain_ref[...]
    turned = pltpu.roll(scaled, HEAD_WIDTH // 2, 1)
    out_ref[...] = (scaled * cos_ref[...] + turned * sin_ref[...]).astype(bf16)


def head_prep(raw, gain, cosine, sine):
    rows, width = raw.shape
    block = pl.BlockSpec((rows, HEAD_WIDTH), lambda j: (0, j))
    table = pl.BlockSpec((rows, HEAD_WIDTH), lambda j: (0, 0))
    return pl.pallas_call(
        head_prep_kernel,
        grid=(width // HEAD_WIDTH,),
        in_specs=[block, pl.BlockSpec((1, HEAD_WIDTH), lambda j: (0, 0)), table, table],
        out_specs=block,
        out_shape=jax.ShapeDtypeStruct((rows, width), bf16),
        name="head_prep",
    )(raw, gain[None, :], cosine, sine)


def head_back_kernel(raw_ref, grad_ref, gain_ref, cos_ref, sin_ref, out_ref, gain_grad_ref):
    @pl.when(pl.program_id(0) == 0)
    def _():
        gain_grad_ref[...] = jnp.zeros_like(gain_grad_ref)

    raw = raw_ref[...]
    inverse = lax.rsqrt(jnp.mean(raw * raw, axis=-1, keepdims=True) + EPSILON)
    hat = raw * inverse
    grad = grad_ref[...] * SCORE_SCALE
    back = grad * cos_ref[...] - pltpu.roll(grad, HEAD_WIDTH // 2, 1) * sin_ref[...]
    gain_grad_ref[...] += jnp.sum(back * hat, axis=0, keepdims=True)
    back = back * gain_ref[...]
    out_ref[...] = (inverse * (back - hat * jnp.mean(back * hat, axis=-1, keepdims=True))).astype(
        bf16
    )


def head_back(raw, grad, gain, cosine, sine):
    rows, width = raw.shape
    block = pl.BlockSpec((rows, HEAD_WIDTH), lambda j: (0, j))
    table = pl.BlockSpec((rows, HEAD_WIDTH), lambda j: (0, 0))
    one = pl.BlockSpec((1, HEAD_WIDTH), lambda j: (0, 0))
    return pl.pallas_call(
        head_back_kernel,
        grid=(width // HEAD_WIDTH,),
        in_specs=[block, block, one, table, table],
        out_specs=[block, one],
        out_shape=[
            jax.ShapeDtypeStruct((rows, width), bf16),
            jax.ShapeDtypeStruct((1, HEAD_WIDTH), f32),
        ],
        name="head_back",
    )(raw, grad, gain[None, :], cosine, sine)


def block_cases(meta, key_start, key_rows, rows):
    whole = (key_start + key_rows - 1 <= meta[0]) & (key_start >= meta[2]) & (key_start >= 0)
    none = (
        (key_start > meta[0] + rows - 1) | (key_start + key_rows - 1 < meta[1]) | (key_start < 0)
    )
    return whole, jnp.logical_not(whole | none)


def attend_kernel(
    meta,
    q_ref,
    ka_ref,
    va_ref,
    kb_ref,
    vb_ref,
    begin_ref,
    acc_in,
    sum_in,
    acc_ref,
    sum_ref,
    *,
    first,
):
    rows = q_ref.shape[0]
    if first:
        acc_ref[...] = jnp.zeros_like(acc_ref)
        sum_ref[...] = jnp.zeros_like(sum_ref)
    else:
        acc_ref[...] = acc_in[...]
        sum_ref[...] = sum_in[...]
    ones = jnp.ones((KEY_CHUNK, HEAD_WIDTH), bf16)
    for k_ref, v_ref, key_start in ((ka_ref, va_ref, meta[3]), (kb_ref, vb_ref, meta[4])):
        key_rows = k_ref.shape[0]
        whole, part = block_cases(meta, key_start, key_rows, rows)

        def work(keys, queries, mask):
            score = dot_nt(q_ref[queries, :], k_ref[keys, :])
            weight = jnp.exp2(score * SCORE_SCALE_2)
            if mask is not None:
                weight = jnp.where(mask, weight, 0.0)
            out = dot(weight.astype(bf16), jnp.concatenate([v_ref[keys, :], ones], axis=1))
            acc_ref[queries, :] += out[:, :HEAD_WIDTH]
            sum_ref[queries, :] += out[:, HEAD_WIDTH:]

        @pl.when(whole)
        def _():
            for c in range(key_rows // KEY_CHUNK):
                work(slice(c * KEY_CHUNK, (c + 1) * KEY_CHUNK), slice(0, rows), None)

        @pl.when(part)
        def _():
            for c in range(key_rows // KEY_CHUNK):
                for r in range(rows // KEY_CHUNK):
                    key0 = key_start + c * KEY_CHUNK
                    row0 = meta[0] + r * KEY_CHUNK

                    @pl.when(key0 <= row0 + KEY_CHUNK - 1)
                    def _():
                        queries = slice(r * KEY_CHUNK, (r + 1) * KEY_CHUNK)
                        shape = (KEY_CHUNK, KEY_CHUNK)
                        query_index = row0 + lax.broadcasted_iota(jnp.int32, shape, 0)
                        key_index = key0 + lax.broadcasted_iota(jnp.int32, shape, 1)
                        mask = (key_index <= query_index) & (
                            key_index >= begin_ref[queries, :][:, :1]
                        )
                        work(slice(c * KEY_CHUNK, (c + 1) * KEY_CHUNK), queries, mask)


def attend_stage(q, kv_a, kv_b, begin, meta, acc, total):
    rows, width = q.shape
    key_rows = kv_a.shape[0]
    q_heads = width // HEAD_WIDTH
    kv_heads = kv_a.shape[1] // (2 * HEAD_WIDTH)
    group = q_heads // kv_heads
    first = acc is None
    if first:
        acc = total = jnp.zeros((8, HEAD_WIDTH), f32)
    per_q = pl.BlockSpec((rows, HEAD_WIDTH), lambda j, m: (0, j))
    per_k = pl.BlockSpec((key_rows, HEAD_WIDTH), lambda j, m: (0, j // group))
    per_v = pl.BlockSpec((key_rows, HEAD_WIDTH), lambda j, m: (0, kv_heads + j // group))
    carried = pl.BlockSpec((8, HEAD_WIDTH), lambda j, m: (0, 0)) if first else per_q
    return pl.pallas_call(
        functools.partial(attend_kernel, first=first),
        grid_spec=pltpu.PrefetchScalarGridSpec(
            num_scalar_prefetch=1,
            grid=(q_heads,),
            in_specs=[
                per_q,
                per_k,
                per_v,
                per_k,
                per_v,
                pl.BlockSpec(begin.shape, lambda j, m: (0, 0)),
                carried,
                carried,
            ],
            out_specs=[per_q, per_q],
        ),
        out_shape=[jax.ShapeDtypeStruct(q.shape, f32)] * 2,
        compiler_params=pltpu.CompilerParams(vmem_limit_bytes=40 * MIB),
        cost_estimate=pl.CostEstimate(
            flops=8 * rows * key_rows * width,
            bytes_accessed=10 * MIB,
            transcendentals=2 * rows * key_rows * q_heads,
        ),
        name="attend_stage",
    )(meta, q, kv_a, kv_a, kv_b, kv_b, begin, acc, total)


def attend_back_kernel(
    meta,
    q_ref,
    do_ref,
    ka_ref,
    va_ref,
    kb_ref,
    vb_ref,
    begin_ref,
    lse_ref,
    delta_ref,
    dq_in,
    dq_ref,
    dka_ref,
    dva_ref,
    dkb_ref,
    dvb_ref,
    *,
    first,
    group,
):
    rows = q_ref.shape[0]
    if first:
        dq_ref[...] = jnp.zeros_like(dq_ref)
    else:
        dq_ref[...] = dq_in[...]

    @pl.when(lax.rem(pl.program_id(0), group) == 0)
    def _():
        for ref in (dka_ref, dva_ref, dkb_ref, dvb_ref):
            ref[...] = jnp.zeros_like(ref)

    for k_ref, v_ref, dk_ref, dv_ref, key_start in (
        (ka_ref, va_ref, dka_ref, dva_ref, meta[3]),
        (kb_ref, vb_ref, dkb_ref, dvb_ref, meta[4]),
    ):
        key_rows = k_ref.shape[0]
        whole, part = block_cases(meta, key_start, key_rows, rows)

        def work(keys, queries, mask):
            k = k_ref[keys, :]
            q = q_ref[queries, :]
            do = do_ref[queries, :]
            score = dot_nt(k, q)
            weight = jnp.exp2(score * SCORE_SCALE_2 - lse_ref[0, :, queries])
            if mask is not None:
                weight = jnp.where(mask, weight, 0.0)
            d_weight = dot_nt(v_ref[keys, :], do)
            d_score = (weight * (d_weight - delta_ref[0, :, queries])).astype(bf16)
            dv_ref[keys, :] += dot(weight.astype(bf16), do)
            dk_ref[keys, :] += dot(d_score, q)
            dq_ref[queries, :] += dot_tn(k, d_score).T

        @pl.when(whole)
        def _():
            for c in range(key_rows // KEY_CHUNK):
                work(slice(c * KEY_CHUNK, (c + 1) * KEY_CHUNK), slice(0, rows), None)

        @pl.when(part)
        def _():
            for c in range(key_rows // KEY_CHUNK):
                for r in range(rows // KEY_CHUNK):
                    key0 = key_start + c * KEY_CHUNK
                    row0 = meta[0] + r * KEY_CHUNK

                    @pl.when(key0 <= row0 + KEY_CHUNK - 1)
                    def _():
                        queries = slice(r * KEY_CHUNK, (r + 1) * KEY_CHUNK)
                        shape = (KEY_CHUNK, KEY_CHUNK)
                        key_index = key0 + lax.broadcasted_iota(jnp.int32, shape, 0)
                        query_index = row0 + lax.broadcasted_iota(jnp.int32, shape, 1)
                        mask = (key_index <= query_index) & (key_index >= begin_ref[:, queries])
                        work(slice(c * KEY_CHUNK, (c + 1) * KEY_CHUNK), queries, mask)


def attend_back_stage(q, do, kv_a, kv_b, begin, lse, delta, meta, dq):
    rows, width = q.shape
    key_rows = kv_a.shape[0]
    q_heads = width // HEAD_WIDTH
    kv_heads = kv_a.shape[1] // (2 * HEAD_WIDTH)
    group = q_heads // kv_heads
    first = dq is None
    if first:
        dq = jnp.zeros((8, HEAD_WIDTH), f32)
    per_q = pl.BlockSpec((rows, HEAD_WIDTH), lambda j, m: (0, j))
    per_k = pl.BlockSpec((key_rows, HEAD_WIDTH), lambda j, m: (0, j // group))
    per_v = pl.BlockSpec((key_rows, HEAD_WIDTH), lambda j, m: (0, kv_heads + j // group))
    per_row = pl.BlockSpec((1, 1, rows), lambda j, m: (j, 0, 0))
    carried = pl.BlockSpec((8, HEAD_WIDTH), lambda j, m: (0, 0)) if first else per_q
    grad_shape = jax.ShapeDtypeStruct((key_rows, kv_heads * HEAD_WIDTH), f32)
    return pl.pallas_call(
        functools.partial(attend_back_kernel, first=first, group=group),
        grid_spec=pltpu.PrefetchScalarGridSpec(
            num_scalar_prefetch=1,
            grid=(q_heads,),
            in_specs=[
                per_q,
                per_q,
                per_k,
                per_v,
                per_k,
                per_v,
                pl.BlockSpec(begin.shape, lambda j, m: (0, 0)),
                per_row,
                per_row,
                carried,
            ],
            out_specs=[per_q, per_k, per_k, per_k, per_k],
        ),
        out_shape=[jax.ShapeDtypeStruct(q.shape, f32)] + [grad_shape] * 4,
        compiler_params=pltpu.CompilerParams(vmem_limit_bytes=40 * MIB),
        cost_estimate=pl.CostEstimate(
            flops=20 * rows * key_rows * width,
            bytes_accessed=16 * MIB,
            transcendentals=2 * rows * key_rows * q_heads,
        ),
        name="attend_back_stage",
    )(meta, q, do, kv_a, kv_a, kv_b, kv_b, begin, lse, delta, dq)


def pick(array, index):
    return lax.dynamic_index_in_dim(array, index, 0, keepdims=False)


def solution(mesh):
    n_seq = mesh.shape["seq"]
    n_head = mesh.shape["head"]
    n_chip = n_seq // 2

    def swap_core(value):
        return lax.ppermute(value, "seq", [(i, i ^ 1) for i in range(n_seq)])

    def to_next(value):
        return lax.ppermute(value, "seq", [(i, i + 2) for i in range(n_seq - 2)])

    def to_previous(value):
        return lax.ppermute(value, "seq", [(i + 2, i) for i in range(n_seq - 2)])

    def across(value, bits):
        return lax.ppermute(value, "head", [(i, i ^ bits) for i in range(n_head)])

    def gather_head(value):
        me = lax.axis_index("head")
        if n_head != 4:
            every = lax.all_gather(value, "head", axis=0)
            return [(every[i], i) for i in range(n_head)]
        half = value.shape[0] // 2
        by_x = across(value, 1)
        by_y = across(value, 2)
        low = across(by_x[:half], 2)
        high = across(by_y[half:], 1)
        far = jnp.concatenate([low, high], axis=0)
        return [(value, me), (by_x, me ^ 1), (by_y, me ^ 2), (far, me ^ 3)]

    def scatter_head(value):
        rows, width = value.shape
        if n_head != 4:
            return lax.psum_scatter(value, "head", scatter_dimension=0, tiled=True).astype(f32)
        me = lax.axis_index("head")
        x, y = me & 1, me >> 1
        part = value.reshape(2, 2, 2, rows // 8, width)
        first, second = part[:, :, 0], part[:, :, 1]
        first_x = jnp.swapaxes(first, 0, 1)
        got_first = across(pick(first_x, 1 - x), 1)
        got_second = across(pick(second, 1 - y), 2)
        sum_first = pick(first_x, x).astype(f32) + got_first.astype(f32)
        sum_second = pick(second, y).astype(f32) + got_second.astype(f32)
        last_first = across(pick(sum_first, 1 - y).astype(bf16), 2)
        last_second = across(pick(sum_second, 1 - x).astype(bf16), 1)
        return jnp.concatenate(
            [
                pick(sum_first, y) + last_first.astype(f32),
                pick(sum_second, x) + last_second.astype(f32),
            ],
            axis=0,
        )

    def in_order(pieces):
        rows = pieces[0][0].shape[0]
        out = jnp.zeros((rows * len(pieces),) + pieces[0][0].shape[1:], pieces[0][0].dtype)
        for piece, owner in pieces:
            out = lax.dynamic_update_slice_in_dim(out, piece, owner * rows, 0)
        return out

    def exchange_head(value):
        me = lax.axis_index("head")
        if n_head != 4:
            got = lax.all_to_all(value, "head", 0, 0)
            return got.reshape(-1, value.shape[-1])
        pieces = [(pick(value, me), me)]
        for bits in (3, 1, 2):
            pieces.append((across(pick(value, me ^ bits), bits), me ^ bits))
        return in_order(pieces)

    def body(
        tokens,
        lengths,
        norm1_gain,
        w_query,
        key_matrix,
        value_matrix,
        query_gain,
        key_gain,
        w_output,
        norm2_gain,
        w_gate,
        w_up,
        w_down,
        cotangent,
    ):
        rows = tokens.shape[0]
        share = rows // n_head
        seq_index = lax.axis_index("seq")
        head_index = lax.axis_index("head")
        chip, core = seq_index // 2, seq_index % 2

        half_rows = w_output.shape[0] // 2
        w_half = lax.dynamic_slice_in_dim(w_output, core * half_rows, half_rows, 0)
        w_mine = lax.all_gather(w_half, "head", axis=0)

        index = seq_index * rows + jnp.arange(rows, dtype=jnp.int32)
        begin = locate(index, lengths)
        cosine, sine = rotary(index - begin)
        begin_column = jnp.broadcast_to(begin[:, None], (rows, HEAD_WIDTH))
        begin_row = begin[None, :]

        xf = tokens.astype(f32)
        inverse1 = lax.rsqrt(jnp.mean(xf * xf, axis=-1, keepdims=True) + EPSILON)
        first_in = (xf * inverse1 * norm1_gain).astype(bf16)
        key_raw = dot(first_in, key_matrix)
        v_low = dot(first_in, value_matrix).astype(bf16)
        k_low = head_prep(key_raw, key_gain, cosine, sine)
        current = jnp.concatenate([k_low, v_low], axis=1)
        query_raw = dot(first_in, w_query)
        q_low = head_prep(query_raw, query_gain, cosine, sine)

        stages = []
        acc = total = None
        for stage in range(n_chip):
            sibling = swap_core(current)
            following = to_next(current) if stage + 1 < n_chip else None
            source = chip - stage
            meta = jnp.stack(
                [
                    seq_index * rows,
                    begin[0],
                    begin[rows - 1],
                    (2 * source + core) * rows,
                    (2 * source + 1 - core) * rows,
                ]
            ).astype(jnp.int32)
            stages.append((current, sibling, meta))
            acc, total = attend_stage(q_low, current, sibling, begin_column, meta, acc, total)
            current = following
        outcome = acc / total
        o_low = outcome.astype(bf16)
        q_heads = o_low.shape[1] // HEAD_WIDTH
        lse = jnp.log2(total[:, ::HEAD_WIDTH]).T[:, None, :]

        w_other = swap_core(w_mine)
        w_full = jnp.where(
            core == 0,
            jnp.concatenate([w_mine, w_other], axis=1),
            jnp.concatenate([w_other, w_mine], axis=1),
        )
        hidden = xf
        for piece, owner in gather_head(o_low):
            hidden = hidden + dot(piece, pick(w_full, owner))

        inverse2 = lax.rsqrt(jnp.mean(hidden * hidden, axis=-1, keepdims=True) + EPSILON)
        second_in = (hidden * inverse2 * norm2_gain).astype(bf16)
        gate_raw = dot(second_in, w_gate)
        up_raw = dot(second_in, w_up)
        d_mixed = dot_nt(cotangent, w_down)
        sigmoid = jax.nn.sigmoid(gate_raw)
        silu = gate_raw * sigmoid
        mixed_low = (silu * up_raw).astype(bf16)
        gate_low = (d_mixed * up_raw * (sigmoid * (1.0 + gate_raw * (1.0 - sigmoid)))).astype(bf16)
        up_low = (d_mixed * silu).astype(bf16)
        second_part = (dot_nt(gate_low, w_gate) + dot_nt(up_low, w_up)).astype(bf16)

        def scatter_seq(value, dimension):
            return lax.psum_scatter(
                value.astype(bf16), "seq", scatter_dimension=dimension, tiled=True
            ).astype(f32)

        grad_down = scatter_seq(dot_tn(mixed_low, cotangent), 1)
        grad_gate = scatter_seq(dot_tn(second_in, gate_low), 0)
        grad_up = scatter_seq(dot_tn(second_in, up_low), 0)

        second_grad = scatter_head(second_part)
        my_hidden = lax.dynamic_slice_in_dim(hidden, head_index * share, share, 0)
        my_inverse = lax.rsqrt(jnp.mean(my_hidden * my_hidden, axis=-1, keepdims=True) + EPSILON)
        my_hat = my_hidden * my_inverse
        grad_norm2 = jnp.sum(second_grad * my_hat, axis=0)
        scaled = second_grad * norm2_gain
        my_dy = lax.dynamic_slice_in_dim(cotangent, head_index * share, share, 0).astype(f32)
        hidden_grad = my_dy + my_inverse * (
            scaled - my_hat * jnp.mean(scaled * my_hat, axis=-1, keepdims=True)
        )
        my_branch = hidden_grad.astype(bf16)
        do_rows = dot_nt(my_branch, w_full.reshape(-1, w_full.shape[-1])).astype(bf16)
        do_pieces = jnp.stack(jnp.split(do_rows, n_head, axis=1))
        do_low = exchange_head(do_pieces)

        branch, down_part, do_low = lax.optimization_barrier(
            (my_branch, dot(mixed_low, w_down).astype(bf16), do_low)
        )
        branch = lax.all_gather(branch, "head", axis=0, tiled=True)
        mixed = (hidden + lax.psum(down_part, "head").astype(f32)).astype(bf16)
        grad_output = scatter_seq(dot_tn(o_low, branch), 1)

        product = do_low.astype(f32) * outcome
        delta = jnp.stack(
            [
                jnp.sum(product[:, j * HEAD_WIDTH : (j + 1) * HEAD_WIDTH], axis=-1)
                for j in range(q_heads)
            ]
        )[:, None, :]

        dq = None
        arrived = None
        for stage in reversed(range(n_chip)):
            kv_a, kv_b, meta = stages[stage]
            dq, dk_a, dv_a, dk_b, dv_b = attend_back_stage(
                q_low, do_low, kv_a, kv_b, begin_row, lse, delta, meta, dq
            )
            theirs = swap_core(jnp.concatenate([dk_b, dv_b], axis=1).astype(bf16))
            mine = jnp.concatenate([dk_a, dv_a], axis=1) + theirs.astype(f32)
            if arrived is not None:
                mine = mine + arrived.astype(f32)
            if stage > 0:
                arrived = to_previous(mine.astype(bf16))
        key_width = key_raw.shape[1]
        query_grad, grad_qgain = head_back(query_raw, dq, query_gain, cosine, sine)
        key_grad, grad_kgain = head_back(key_raw, mine[:, :key_width], key_gain, cosine, sine)
        value_grad = mine[:, key_width:].astype(bf16)

        first_part = (
            dot_nt(query_grad, w_query)
            + dot_nt(key_grad, key_matrix)
            + dot_nt(value_grad, value_matrix)
        ).astype(bf16)
        grad_query = scatter_seq(dot_tn(first_in, query_grad), 0)
        grad_key = scatter_seq(dot_tn(first_in, key_grad), 0)
        grad_value = scatter_seq(dot_tn(first_in, value_grad), 0)

        first_grad = scatter_head(first_part)
        my_x = lax.dynamic_slice_in_dim(tokens, head_index * share, share, 0).astype(f32)
        my_inverse1 = lax.rsqrt(jnp.mean(my_x * my_x, axis=-1, keepdims=True) + EPSILON)
        my_hat1 = my_x * my_inverse1
        grad_norm1 = jnp.sum(first_grad * my_hat1, axis=0)
        scaled1 = first_grad * norm1_gain
        my_tokens_grad = hidden_grad + my_inverse1 * (
            scaled1 - my_hat1 * jnp.mean(scaled1 * my_hat1, axis=-1, keepdims=True)
        )
        grad_tokens = in_order(gather_head(my_tokens_grad.astype(bf16))).astype(f32)

        grad_norm1, grad_qgain, grad_kgain, grad_norm2 = lax.psum(
            (grad_norm1, grad_qgain[0], grad_kgain[0], grad_norm2), ("seq", "head")
        )
        return (
            mixed,
            grad_tokens,
            grad_norm1,
            grad_query,
            grad_key,
            grad_value,
            grad_qgain,
            grad_kgain,
            grad_output,
            grad_norm2,
            grad_gate,
            grad_up,
            grad_down,
        )

    in_specs = (
        P("seq", None),
        P(),
        P(),
        P(None, "head"),
        P(None, "head"),
        P(None, "head"),
        P(),
        P(),
        P("head", None),
        P(),
        P(None, "head"),
        P(None, "head"),
        P("head", None),
        P("seq", None),
    )
    out_specs = (
        P("seq", None),
        P("seq", None),
        P(),
        P("seq", "head"),
        P("seq", "head"),
        P("seq", "head"),
        P(),
        P(),
        P("head", "seq"),
        P(),
        P("seq", "head"),
        P("seq", "head"),
        P("head", "seq"),
    )
    return jax.shard_map(body, mesh=mesh, in_specs=in_specs, out_specs=out_specs, check_vma=False)
```

time: 1630 us -> 955 us (0.59)
  waiting for transfers between devices: 1130 us -> 499 us
  local copies, waits for them, and re-layouts: 126 us -> 47.3 us
  starting transfers between devices: 1.56 us -> 72.2 us
  Pallas kernels: 0 us -> 67.2 us
  matrix products: 197 us -> 145 us
  loops' own time: 33.4 us -> 0 us
    psum x5 -> x1, waiting for transfers between devices: 578 us -> 0.01 us  [body(): mixed = (hidden + lax.psum(down_part, 'head').astype(f32)).astype(bf16)]
    ppermute x0 -> x34, waiting for transfers between devices: none -> 305 us  [the longest x3 235 us: to_previous(): return lax.ppermute(value, 'seq', [(i + 2, i) for i in range(n_seq - 2)])]
    reduce_scatter x9 -> x7, waiting for transfers between devices: 426 us -> 155 us  [scatter_seq(): lax.psum_scatter(value.astype(bf16), 'seq', scatter_dimension=dimension,...]
    all_gather x4 -> x2, waiting for transfers between devices: 123 us -> 38.6 us  [the longest x1 38.5 us: body(): w_mine = lax.all_gather(w_half, 'head', axis=0)]
    ppermute x0 -> x34, starting transfers between devices: none -> 71.8 us  [the longest x9 27.6 us: swap_core(): return lax.ppermute(value, 'seq', [(i, i ^ 1) for i in range(n_seq)])]
    pallas_call x0 -> x12, Pallas kernels: none -> 67.2 us  [the longest x4 29.3 us: attend_back_stage(): pl.pallas_call(functools.partial(attend_back_kernel, first=first, group=g...]
    dot_general x35 -> x24, matrix products: 197 us -> 145 us  [the longest x10 63.2 us: dot(): return jnp.dot(left, right, preferred_element_type=f32)]
    dynamic_update_slice x24 -> x6, local copies, waits for them, and re-layouts: 39 us -> 5.06 us  [in_order(): out = lax.dynamic_update_slice_in_dim(out, piece, owner * rows, 0)]
  transfers between devices with their start and end apart: 18 -> 44, of which waited for: 16 -> 20; matrix products, arithmetic and copies ran while one was open for 8% -> 18% of each run, Pallas kernels for 0% -> 7%
where the time goes in v1:
time: 955 us; the launch traced here: 947 us
  waiting for transfers between devices  499 us (52%)
  matrix products  145 us (15%)
  starting transfers between devices  72.2 us (8%)
  Pallas kernels  67.2 us (7%)
  other arithmetic  60.4 us (6%)
  local copies, waits for them, and re-layouts  47.3 us (5%)
  blocking collectives  40.6 us (4%)
  between operations  15.7 us (2%)
    ppermute x3, waiting for transfers between devices, to_previous(): return lax.ppermute(value, 'seq', [(i + 2, i) for i in range(n_seq - 2)])  235 us
    reduce_scatter x7, waiting for transfers between devices, scatter_seq(): lax.psum_scatter(value.astype(bf16), 'seq', scatter_dimension=dimension,...  155 us
    dot_general x10, matrix products, dot(): return jnp.dot(left, right, preferred_element_type=f32)  63.2 us
    dot_general x7, matrix products, dot_tn(): return lax.dot_general(left, right, TN, preferred_element_type=f32)  46.9 us
    ppermute x19, waiting for transfers between devices, across(): return lax.ppermute(value, 'head', [(i, i ^ bits) for i in range(n_head)])  46.8 us
    psum x1, blocking collectives, body(): lax.psum((grad_norm1, grad_qgain[0], grad_kgain[0], grad_norm2), ('seq',...  40.6 us
    all_gather x1, waiting for transfers between devices, body(): w_mine = lax.all_gather(w_half, 'head', axis=0)  38.5 us
    dot_general x7, matrix products, dot_nt(): return lax.dot_general(left, right, NT, preferred_element_type=f32)  34.6 us
  transfers between devices with their start and end apart: 44, of which 20 were waited for; matrix products, arithmetic and copies ran while one was open for 18% of the time, Pallas kernels for 7%

profile of v1, /device:TPU:0, one launch (start us, length us, event | category | flops | bytes accessed | tf_op | source)
XLA Modules:
  0.0 947.3 jit_solution(18063641715432996597)
XLA Ops:
  27.3 38.5 %all-gather.6.cloned.1.call-done = bf16[1024,2048]{1,0:T(8,128)(2,1)} async-done(((bf16[256,2048]{1,0:T(8,128)(2,1)}), bf16[1024,2048]{1,0:T(8,128)(2,1)}) %all-gather.6.cloned.1.call-update) | async-done | bytes 4194320 | tf_op jit(solution)/shard_map/all_gather | solution.py:442
  70.2 16.9 %collective-permute-done.1.ka_ref.va_ref = bf16[768,512]{1,0:T(8,128)(2,1)} collective-permute-done((bf16[768,512]{1,0:T(8,128)(2,1)}, bf16[768,512]{1,0:T(8,128)(2,1)}, u32[]{:S(2)}, u32[]{:S(2)}) %collective-permute-start.1) | collective-permute-done | bytes 786464 | tf_op jit(solution)/shard_map/ppermute | solution.py:357
  115.8 11.0 %attend_stage.4 = (f32[768,512]{1,0:T(8,128)S(1)}, f32[768,512]{1,0:T(8,128)S(1)}) custom-call(s32[5]{0:T(128)S(1)} %stack.84.meta, bf16[768,512]{1,0:T(8,128)(2,1)S(1)} %copy-done.24, bf16[768,512]{1,0:T(8,128)(2,1)S(1)} %pad_maximum_fusion.2.ka_ref.va_ref, bf16[768,512]{1,0:T(8,128)(2,1)S(1)} %pad_maximum_fusion.2.ka_ref.va_ref, ...), custom_call_target="tpu_custom_call" | custom-call | flops 2415919104 | bytes 10485760 | tf_op jit(solution)/shard_map/attend_stage/pallas_call | solution.py:196
  141.9 9.9 %fusion.64 = f32[768,1536]{1,0:T(8,128)} fusion(bf16[768,2048]{1,0:T(8,128)(2,1)S(1)} %copy-done.61, bf16[1536,2048]{1,0:T(8,128)(2,1)} %param.26), kind=kOutput, calls=%fused_computation.154 | convolution fusion | flops 4831838208 | bytes 14155776 | tf_op jit(solution)/shard_map/dot_general | solution.py:31
  175.2 8.2 multiply_reduce_fusion
  186.6 10.9 %fusion.65 = f32[768,1536]{1,0:T(8,128)} fusion(bf16[768,2048]{1,0:T(8,128)(2,1)S(1)} %multiply_convert_fusion, bf16[2048,1536]{1,0:T(8,128)(2,1)} %param.24), kind=kOutput, calls=%fused_computation.155 | convolution fusion | flops 4831838208 | bytes 14155776 | tf_op jit(solution)/shard_map/dot_general | solution.py:27
  197.6 10.7 %multiply_convert_fusion.1 = (bf16[768,1536]{1,0:T(8,128)(2,1)}, bf16[768,1536]{1,0:T(8,128)(2,1)S(1)}, bf16[768,1536]{1,0:T(8,128)(2,1)S(1)}) fusion(f32[768,1536]{1,0:T(8,128)} %fusion.65, f32[768,1536]{1,0:T(8,128)} %fusion.64, bf16[768,2048]{1,0:T(8,128)(2,1)S(1)} %multiply_convert_fusion, bf16[2048,1536]{1,0:T(8,128)(2,1)S(1)} %bitcast.160), kind=kOutput, calls=%fused_computation.18 | convolution fusion | flops 4849532928 | bytes 25952256 | tf_op jit(solution)/shard_map/dot_general | solution.py:27
  215.4 7.2 add_convert_fusion.2
  230.3 7.1 collective-permute-done.12
  265.5 9.3 convolution_convert_fusion.3
  298.8 8.9 collective-permute-start.22
  322.0 16.5 %attend_back_stage.7 = (f32[768,512]{1,0:T(8,128)S(1)}, f32[768,256]{1,0:T(8,128)S(1)}, f32[768,256]{1,0:T(8,128)S(1)}, f32[768,256]{1,0:T(8,128)S(1)}, f32[768,256]{1,0:T(8,128)S(1)}) custom-call(s32[5]{0:T(128)S(1)} %stack.84.meta, bf16[768,512]{1,0:T(8,128)(2,1)S(1)} %copy-done.27, bf16[768,512]{1,0:T(8,128)(2,1)S(1)} %constant_dynamic-update-slice_fusion.3.do_ref, ...), custom_call_target="tpu_custom_call" | custom-call | flops 6039797760 | bytes 16777216 | tf_op jit(solution)/shard_map/attend_back_stage/pallas_call | solution.py:314
  355.4 17.8 %collective-permute-start.21 = (bf16[768,512]{1,0:T(8,128)(2,1)S(1)}, bf16[768,512]{1,0:T(8,128)(2,1)S(1)}, u32[]{:S(2)}, u32[]{:S(2)}) collective-permute-start(bf16[768,512]{1,0:T(8,128)(2,1)S(1)} %pad_maximum_fusion.6), channel_id=1, source_target_pairs={{0,4},{4,0},{8,12},{12,8},{16,20},{20,16},{24,28},{28,24},{1,5},{5... | collective-permute-start | bytes 2359304 | tf_op jit(solution)/shard_map/ppermute | solution.py:354
  376.5 47.2 %collective-permute-done.23 = bf16[768,512]{1,0:T(8,128)(2,1)S(1)} collective-permute-done((bf16[768,512]{1,0:T(8,128)(2,1)S(1)}, bf16[768,512]{1,0:T(8,128)(2,1)S(1)}, u32[]{:S(2)}, u32[]{:S(2)}) %collective-permute-start.23) | collective-permute-done | bytes 786464 | tf_op jit(solution)/shard_map/ppermute | solution.py:360
  425.7 38.8 %collective-permute-done.24 = bf16[768,512]{1,0:T(8,128)(2,1)S(1)} collective-permute-done((bf16[768,512]{1,0:T(8,128)(2,1)S(1)}, bf16[768,512]{1,0:T(8,128)(2,1)S(1)}, u32[]{:S(2)}, u32[]{:S(2)}) %collective-permute-start.24) | collective-permute-done | bytes 786464 | tf_op jit(solution)/shard_map/ppermute | solution.py:360
  466.1 149.4 %collective-permute-done.25 = bf16[768,512]{1,0:T(8,128)(2,1)S(1)} collective-permute-done((bf16[768,512]{1,0:T(8,128)(2,1)S(1)}, bf16[768,512]{1,0:T(8,128)(2,1)S(1)}, u32[]{:S(2)}, u32[]{:S(2)}) %collective-permute-start.25) | collective-permute-done | bytes 786464 | tf_op jit(solution)/shard_map/ppermute | solution.py:360
  634.9 9.2 convolution_convert_fusion.2
  644.2 9.3 convolution_convert_fusion.1
  653.5 9.4 convolution_convert_fusion
  672.4 14.3 %collective-permute-done.26 = bf16[2,96,2048]{2,1,0:T(8,128)(2,1)S(1)} collective-permute-done((bf16[2,96,2048]{2,1,0:T(8,128)(2,1)S(1)}, bf16[2,96,2048]{2,1,0:T(8,128)(2,1)S(1)}, u32[]{:S(2)}, u32[]{:S(2)}) %collective-permute-start.26) | collective-permute-done | bytes 786464 | tf_op jit(solution)/shard_map/ppermute | solution.py:363
  713.0 40.6 %all-reduce = (f32[2048]{0:T(1024)}, f32[128]{0:T(128)}, f32[128]{0:T(128)}, f32[2048]{0:T(1024)}) all-reduce(f32[2048]{0:T(1024)S(1)} %get-tuple-element.85, f32[128]{0:T(128)S(1)} %bitcast.154, f32[128]{0:T(128)S(1)} %bitcast.155, f32[2048]{0:T(1024)S(1)} %get-tuple-element.83), channel_id=1, replica_groups=mesh['seq'=8,'head'=4] {'seq','head'}, use_global_device_ids=true, to_apply=%region_15.16 | all-reduce | flops 4352 | bytes 34816 | tf_op jit(solution)/shard_map/psum | solution.py:582
  777.6 19.4 %reduce-scatter.16.cloned.1.call-done = bf16[256,1536]{1,0:T(8,128)(2,1)} async-done(((bf16[2048,1536]{1,0:T(8,128)(2,1)}), bf16[256,1536]{1,0:T(8,128)(2,1)}) %reduce-scatter.16.cloned.1.call-update) | async-done | bytes 786448 | tf_op jit(solution)/shard_map/reduce_scatter | solution.py:506
  799.6 67.9 %reduce-scatter.18.cloned.1.call-done = bf16[256,1536]{1,0:T(8,128)(2,1)} async-done(((bf16[2048,1536]{1,0:T(8,128)(2,1)}), bf16[256,1536]{1,0:T(8,128)(2,1)}) %reduce-scatter.18.cloned.1.call-update) | async-done | bytes 786448 | tf_op jit(solution)/shard_map/reduce_scatter | solution.py:506
  869.9 68.0 %reduce-scatter.20.cloned.1.call-done = bf16[1536,256]{1,0:T(8,128)(2,1)} async-done(((bf16[1536,2048]{1,0:T(8,128)(2,1)}), bf16[1536,256]{1,0:T(8,128)(2,1)}) %reduce-scatter.20.cloned.1.call-update) | async-done | bytes 786448 | tf_op jit(solution)/shard_map/reduce_scatter | solution.py:506
  (373 shorter events, 285.3 us)
Async XLA Ops:
  7.2 58.7 %all-gather.6.cloned.1.call-start = ((), (), s32[]{:S(2)}) async-start(), calls=%async_computation.16 | async-start | bytes 5242880 | tf_op jit(solution)/shard_map/all_gather | solution.py:442
  9.7 620.0 %all-gather.4.cloned.1.call-start = ((), (), s32[]{:S(2)}) async-start(), calls=%async_computation.11 | async-start | bytes 3932160 | tf_op jit(solution)/shard_map/all_gather | solution.py:532
  21.3 44.6 %collective-permute-start = (bf16[768,512]{1,0:T(8,128)(2,1)S(1)}, bf16[768,512]{1,0:T(8,128)(2,1)}, u32[]{:S(2)}, u32[]{:S(2)}) collective-permute-start(bf16[768,512]{1,0:T(8,128)(2,1)S(1)} %pad_maximum_fusion.2.ka_ref.va_ref), channel_id=1, source_target_pairs={{0,8},{4,12},{8,16},{12,20},{16,24},{20,28},{1,9},{5,13},{9,17},{1... | collective-permute-start | bytes 2359304 | tf_op jit(solution)/shard_map/ppermute | solution.py:357
  65.9 88.2 %collective-permute-start.7 = (bf16[4,256,2048]{2,1,0:T(8,128)(2,1)}, bf16[4,256,2048]{2,1,0:T(8,128)(2,1)}, u32[]{:S(2)}, u32[]{:S(2)}) collective-permute-start(bf16[4,256,2048]{2,1,0:T(8,128)(2,1)} %bitcast.147), channel_id=1, source_target_pairs={{0,4},{4,0},{8,12},{12,8},{16,20},{20,16},{24,28},{28,24},{1,5},{5... | collective-permute-start | bytes 12582920 | tf_op jit(solution)/shard_map/ppermute | solution.py:354
  92.3 34.5 %collective-permute-start.5 = (bf16[768,512]{1,0:T(8,128)(2,1)}, bf16[768,512]{1,0:T(8,128)(2,1)}, u32[]{:S(2)}, u32[]{:S(2)}) collective-permute-start(bf16[768,512]{1,0:T(8,128)(2,1)} %collective-permute-done.ka_ref.va_ref), channel_id=1, source_target_pairs={{0,4},{4,0},{8,12},{12,8},{16,20},{20,16},{24,28},{28,24},{1,5},{5... | collective-permute-start | bytes 2359304 | tf_op jit(solution)/shard_map/ppermute | solution.py:354
  92.9 37.8 %collective-permute-start.4 = (bf16[768,512]{1,0:T(8,128)(2,1)}, bf16[768,512]{1,0:T(8,128)(2,1)}, u32[]{:S(2)}, u32[]{:S(2)}) collective-permute-start(bf16[768,512]{1,0:T(8,128)(2,1)} %collective-permute-done.1.ka_ref.va_ref), channel_id=1, source_target_pairs={{0,4},{4,0},{8,12},{12,8},{16,20},{20,16},{24,28},{28,24},{1,5},{5... | collective-permute-start | bytes 2359304 | tf_op jit(solution)/shard_map/ppermute | solution.py:354
  108.4 26.2 %collective-permute-start.3 = (bf16[768,512]{1,0:T(8,128)(2,1)}, bf16[768,512]{1,0:T(8,128)(2,1)}, u32[]{:S(2)}, u32[]{:S(2)}) collective-permute-start(bf16[768,512]{1,0:T(8,128)(2,1)} %collective-permute-done.2.ka_ref.va_ref), channel_id=1, source_target_pairs={{0,4},{4,0},{8,12},{12,8},{16,20},{20,16},{24,28},{28,24},{1,5},{5... | collective-permute-start | bytes 2359304 | tf_op jit(solution)/shard_map/ppermute | solution.py:354
  151.9 23.2 %collective-permute-start.10 = (bf16[384,512]{1,0:T(8,128)(2,1)S(1)}, bf16[384,512]{1,0:T(8,128)(2,1)S(1)}, u32[]{:S(2)}, u32[]{:S(2)}) collective-permute-start(bf16[384,512]{1,0:T(8,128)(2,1)S(1)} %slice.75), channel_id=1, source_target_pairs={{0,2},{1,3},{2,0},{3,1},{4,6},{5,7},{6,4},{7,5},{8,10},{9,11},{10,... | collective-permute-start | bytes 1179656 | tf_op jit(solution)/shard_map/ppermute | solution.py:363
  283.2 421.3 %all-reduce.3.cloned.1.call-start = ((), (), s32[]{:S(2)}) async-start(), calls=%async_computation.7 | async-start | bytes 6291456 | tf_op jit(solution)/shard_map/psum | solution.py:533
  290.6 420.6 %reduce-scatter.8.cloned.1.call-start = ((), (), s32[]{:S(2)}) async-start(), calls=%async_computation.8 | async-start | bytes 2359296 | tf_op jit(solution)/shard_map/reduce_scatter | solution.py:506
  298.8 74.4 %collective-permute-start.22 = (bf16[768,512]{1,0:T(8,128)(2,1)}, bf16[768,512]{1,0:T(8,128)(2,1)}, u32[]{:S(2)}, u32[]{:S(2)}) collective-permute-start(bf16[768,512]{1,0:T(8,128)(2,1)} %pad_maximum_fusion.7), channel_id=1, source_target_pairs={{0,4},{4,0},{8,12},{12,8},{16,20},{20,16},{24,28},{28,24},{1,5},{5... | collective-permute-start | bytes 2359304 | tf_op jit(solution)/shard_map/ppermute | solution.py:354
  353.9 409.0 %reduce-scatter.10.cloned.1.call-start = ((), (), s32[]{:S(2)}) async-start(), calls=%async_computation.9 | async-start | bytes 1179648 | tf_op jit(solution)/shard_map/reduce_scatter | solution.py:506
  374.7 49.0 %collective-permute-start.23 = (bf16[768,512]{1,0:T(8,128)(2,1)S(1)}, bf16[768,512]{1,0:T(8,128)(2,1)S(1)}, u32[]{:S(2)}, u32[]{:S(2)}) collective-permute-start(bf16[768,512]{1,0:T(8,128)(2,1)S(1)} %fusion.36), channel_id=1, source_target_pairs={{8,0},{12,4},{16,8},{20,12},{24,16},{28,20},{9,1},{13,5},{17,9},{2... | collective-permute-start | bytes 2359304 | tf_op jit(solution)/shard_map/ppermute | solution.py:360
  376.2 49.5 %collective-permute-start.20 = (bf16[768,512]{1,0:T(8,128)(2,1)S(1)}, bf16[768,512]{1,0:T(8,128)(2,1)S(1)}, u32[]{:S(2)}, u32[]{:S(2)}) collective-permute-start(bf16[768,512]{1,0:T(8,128)(2,1)S(1)} %pad_maximum_fusion.5), channel_id=1, source_target_pairs={{0,4},{4,0},{8,12},{12,8},{16,20},{20,16},{24,28},{28,24},{1,5},{5... | collective-permute-start | bytes 2359304 | tf_op jit(solution)/shard_map/ppermute | solution.py:354
  424.0 40.5 %collective-permute-start.24 = (bf16[768,512]{1,0:T(8,128)(2,1)S(1)}, bf16[768,512]{1,0:T(8,128)(2,1)S(1)}, u32[]{:S(2)}, u32[]{:S(2)}) collective-permute-start(bf16[768,512]{1,0:T(8,128)(2,1)S(1)} %fusion.35), channel_id=1, source_target_pairs={{8,0},{12,4},{16,8},{20,12},{24,16},{28,20},{9,1},{13,5},{17,9},{2... | collective-permute-start | bytes 2359304 | tf_op jit(solution)/shard_map/ppermute | solution.py:360
  425.6 40.5 %collective-permute-start.19 = (bf16[768,512]{1,0:T(8,128)(2,1)S(1)}, bf16[768,512]{1,0:T(8,128)(2,1)S(1)}, u32[]{:S(2)}, u32[]{:S(2)}) collective-permute-start(bf16[768,512]{1,0:T(8,128)(2,1)S(1)} %pad_maximum_fusion.4), channel_id=1, source_target_pairs={{0,4},{4,0},{8,12},{12,8},{16,20},{20,16},{24,28},{28,24},{1,5},{5... | collective-permute-start | bytes 2359304 | tf_op jit(solution)/shard_map/ppermute | solution.py:354
  464.8 150.7 %collective-permute-start.25 = (bf16[768,512]{1,0:T(8,128)(2,1)S(1)}, bf16[768,512]{1,0:T(8,128)(2,1)S(1)}, u32[]{:S(2)}, u32[]{:S(2)}) collective-permute-start(bf16[768,512]{1,0:T(8,128)(2,1)S(1)} %fusion.33), channel_id=1, source_target_pairs={{8,0},{12,4},{16,8},{20,12},{24,16},{28,20},{9,1},{13,5},{17,9},{2... | collective-permute-start | bytes 2359304 | tf_op jit(solution)/shard_map/ppermute | solution.py:360
  625.2 139.3 %reduce-scatter.12.cloned.1.call-start = ((), (), s32[]{:S(2)}) async-start(), calls=%async_computation.10 | async-start | bytes 1179648 | tf_op jit(solution)/shard_map/reduce_scatter | solution.py:506
  629.7 146.1 %reduce-scatter.14.cloned.1.call-start = ((), (), s32[]{:S(2)}) async-start(), calls=%async_computation.12 | async-start | bytes 2359296 | tf_op jit(solution)/shard_map/reduce_scatter | solution.py:506
  634.9 162.2 %reduce-scatter.16.cloned.1.call-start = ((), (), s32[]{:S(2)}) async-start(), calls=%async_computation.13 | async-start | bytes 7077888 | tf_op jit(solution)/shard_map/reduce_scatter | solution.py:506
  644.1 223.3 %reduce-scatter.18.cloned.1.call-start = ((), (), s32[]{:S(2)}) async-start(), calls=%async_computation.14 | async-start | bytes 7077888 | tf_op jit(solution)/shard_map/reduce_scatter | solution.py:506
  653.4 284.4 %reduce-scatter.20.cloned.1.call-start = ((), (), s32[]{:S(2)}) async-start(), calls=%async_computation.15 | async-start | bytes 7077888 | tf_op jit(solution)/shard_map/reduce_scatter | solution.py:506
  702.5 51.0 %collective-permute-start.30 = (bf16[192,2048]{1,0:T(8,128)(2,1)}, bf16[192,2048]{1,0:T(8,128)(2,1)S(1)}, u32[]{:S(2)}, u32[]{:S(2)}) collective-permute-start(bf16[192,2048]{1,0:T(8,128)(2,1)} %get-tuple-element.96), channel_id=1, source_target_pairs={{0,1},{1,0},{2,3},{3,2},{4,5},{5,4},{6,7},{7,6},{8,9},{9,8},{10,11... | collective-permute-start | bytes 2359304 | tf_op jit(solution)/shard_map/ppermute | solution.py:363
  704.0 52.4 %collective-permute-start.31 = (bf16[192,2048]{1,0:T(8,128)(2,1)}, bf16[192,2048]{1,0:T(8,128)(2,1)}, u32[]{:S(2)}, u32[]{:S(2)}) collective-permute-start(bf16[192,2048]{1,0:T(8,128)(2,1)} %get-tuple-element.96), channel_id=1, source_target_pairs={{0,2},{1,3},{2,0},{3,1},{4,6},{5,7},{6,4},{7,5},{8,10},{9,11},{10,... | collective-permute-start | bytes 2359304 | tf_op jit(solution)/shard_map/ppermute | solution.py:363
  (96 other events, 1583.5 us)
Sparse Core Ops, SparseCore 0:
  10.5 55.3 all-gather.5
  283.3 117.4 all-gather.3
  404.5 87.2 all-reduce.2
  494.0 86.8 reduce-scatter.7
  625.3 31.0 reduce-scatter.9
  658.6 30.5 reduce-scatter.11
  691.6 34.1 reduce-scatter.13
  728.2 68.8 reduce-scatter.15
  799.5 67.8 reduce-scatter.17
  869.7 68.1 reduce-scatter.19

commit v2 on v1

v2 whole, which is shorter than its diff:
```python
import functools
import math

import jax
import jax.numpy as jnp
from jax import lax
from jax.experimental import pallas as pl
from jax.experimental.pallas import tpu as pltpu
from jax.sharding import PartitionSpec as P

HEAD_WIDTH = 128
EPSILON = 1e-06
ROPE_BASE = 1000000.0
LOG2E = math.log2(math.e)
SCORE_SCALE = 1.0 / math.sqrt(HEAD_WIDTH)
SCORE_SCALE_2 = LOG2E / math.sqrt(HEAD_WIDTH)
KEY_CHUNK = 256
FAR = 512.0
LOG_LANE = 64
MIB = 2**20
SMALL = pl.CostEstimate(flops=1, bytes_accessed=1, transcendentals=0)

f32 = jnp.float32
bf16 = jnp.bfloat16
NT = (((1,), (1,)), ((), ()))
TN = (((0,), (0,)), ((), ()))


def dot(left, right):
    return jnp.dot(left, right, preferred_element_type=f32)


def dot_nt(left, right):
    return lax.dot_general(left, right, NT, preferred_element_type=f32)


def dot_tn(left, right):
    return lax.dot_general(left, right, TN, preferred_element_type=f32)


def locate(index, lengths):
    ends = jnp.cumsum(lengths)
    starts = ends - lengths
    segment = jnp.sum((index[:, None] >= ends[None, :]).astype(jnp.int32), axis=1)
    chosen = segment[:, None] == jnp.arange(lengths.shape[0], dtype=jnp.int32)[None, :]
    return jnp.sum(jnp.where(chosen, starts[None, :], 0), axis=1)


def rotary(position):
    half = HEAD_WIDTH // 2
    freq = jnp.exp(jnp.arange(half, dtype=f32) * (-2.0 * math.log(ROPE_BASE) / HEAD_WIDTH))
    angle = position.astype(f32)[:, None] * freq[None, :]
    cosine = jnp.cos(angle)
    sine = jnp.sin(angle)
    return (
        jnp.concatenate([cosine, cosine], axis=1),
        jnp.concatenate([-sine, sine], axis=1),
    )


def lane_index(rows):
    return lax.broadcasted_iota(jnp.int32, (rows, HEAD_WIDTH), 1)


def row_index(rows):
    return lax.broadcasted_iota(jnp.int32, (rows, HEAD_WIDTH), 0)


def in_segment(index, bounds_ref):
    return (index >= bounds_ref[0:1, :]) & (index < bounds_ref[1:2, :])


def split_parts(value):
    high = value.astype(bf16)
    rest = value - high.astype(f32)
    middle = rest.astype(bf16)
    return high, middle, (rest - middle.astype(f32)).astype(bf16)


def normed(raw, gain, cosine, sine):
    inverse = lax.rsqrt(jnp.mean(raw * raw, axis=-1, keepdims=True) + EPSILON)
    scaled = raw * inverse * gain
    return scaled * cosine + pltpu.roll(scaled, HEAD_WIDTH // 2, 1) * sine


def key_prep_kernel(raw_ref, value_ref, gain_ref, cos_ref, sin_ref, out_ref):
    key = normed(raw_ref[...], gain_ref[...], cos_ref[...], sin_ref[...])
    out_ref[:, :HEAD_WIDTH] = key.astype(bf16)
    out_ref[:, HEAD_WIDTH:] = value_ref[...].astype(bf16)


def key_prep(raw, value, gain, cosine, sine):
    rows, width = raw.shape
    block = pl.BlockSpec((rows, HEAD_WIDTH), lambda j: (0, j))
    table = pl.BlockSpec((rows, HEAD_WIDTH), lambda j: (0, 0))
    return pl.pallas_call(
        key_prep_kernel,
        grid=(width // HEAD_WIDTH,),
        in_specs=[block, block, pl.BlockSpec((1, HEAD_WIDTH), lambda j: (0, 0)), table, table],
        out_specs=pl.BlockSpec((rows, 2 * HEAD_WIDTH), lambda j: (0, j)),
        out_shape=jax.ShapeDtypeStruct((rows, 2 * width), bf16),
        name="key_prep",
    )(raw, value, gain[None, :], cosine, sine)


def query_prep_kernel(meta, raw_ref, gain_ref, cos_ref, sin_ref, bounds_ref, out_ref):
    rows = raw_ref.shape[0]
    query = normed(raw_ref[...], gain_ref[...], cos_ref[...], sin_ref[...])
    out_ref[:, :HEAD_WIDTH] = (query * SCORE_SCALE_2).astype(bf16)
    inside = in_segment(meta[0] + row_index(rows), bounds_ref)
    free = inside | (lane_index(rows) >= LOG_LANE)
    out_ref[:, HEAD_WIDTH:] = jnp.where(free, 0.0, -FAR).astype(bf16)


def query_prep(meta, raw, gain, cosine, sine, bounds):
    rows, width = raw.shape
    table = pl.BlockSpec((rows, HEAD_WIDTH), lambda j, m: (0, 0))
    return pl.pallas_call(
        query_prep_kernel,
        grid_spec=pltpu.PrefetchScalarGridSpec(
            num_scalar_prefetch=1,
            grid=(width // HEAD_WIDTH,),
            in_specs=[
                pl.BlockSpec((rows, HEAD_WIDTH), lambda j, m: (0, j)),
                pl.BlockSpec((1, HEAD_WIDTH), lambda j, m: (0, 0)),
                table,
                table,
                pl.BlockSpec((8, HEAD_WIDTH), lambda j, m: (0, 0)),
            ],
            out_specs=pl.BlockSpec((rows, 2 * HEAD_WIDTH), lambda j, m: (0, j)),
        ),
        out_shape=jax.ShapeDtypeStruct((rows, 2 * width), bf16),
        name="query_prep",
    )(meta, raw, gain[None, :], cosine, sine, bounds)


def head_back_kernel(raw_ref, grad_ref, gain_ref, cos_ref, sin_ref, out_ref, gain_grad_ref, *, scale):
    @pl.when(pl.program_id(0) == 0)
    def _():
        gain_grad_ref[...] = jnp.zeros_like(gain_grad_ref)

    raw = raw_ref[...]
    inverse = lax.rsqrt(jnp.mean(raw * raw, axis=-1, keepdims=True) + EPSILON)
    hat = raw * inverse
    grad = grad_ref[...] * scale
    back = grad * cos_ref[...] - pltpu.roll(grad, HEAD_WIDTH // 2, 1) * sin_ref[...]
    gain_grad_ref[...] += jnp.sum(back * hat, axis=0, keepdims=True)
    back = back * gain_ref[...]
    out_ref[...] = (inverse * (back - hat * jnp.mean(back * hat, axis=-1, keepdims=True))).astype(
        bf16
    )


def head_back(raw, grad, gain, cosine, sine, scale, stride):
    rows, width = raw.shape
    block = pl.BlockSpec((rows, HEAD_WIDTH), lambda j: (0, j))
    spaced = pl.BlockSpec((rows, HEAD_WIDTH), lambda j: (0, j * stride))
    table = pl.BlockSpec((rows, HEAD_WIDTH), lambda j: (0, 0))
    one = pl.BlockSpec((1, HEAD_WIDTH), lambda j: (0, 0))
    return pl.pallas_call(
        functools.partial(head_back_kernel, scale=scale),
        grid=(width // HEAD_WIDTH,),
        in_specs=[block, spaced, one, table, table],
        out_specs=[block, one],
        out_shape=[
            jax.ShapeDtypeStruct((rows, width), bf16),
            jax.ShapeDtypeStruct((1, HEAD_WIDTH), f32),
        ],
        name="head_back",
    )(raw, grad, gain[None, :], cosine, sine)


def key_lanes(meta, key_start, rows, bounds_ref):
    inside = in_segment(key_start + row_index(rows), bounds_ref)
    lanes = lane_index(rows)
    log_lanes = (lanes >= LOG_LANE) & (lanes < LOG_LANE + 3)
    return jnp.where(inside | log_lanes, 1.0, 0.0).astype(bf16)


def block_used(meta, key_start, key_rows, rows):
    return (
        (key_start >= 0) & (key_start <= meta[0] + rows - 1) & (key_start + key_rows - 1 >= meta[1])
    )


def lower_mask(transposed):
    shape = (KEY_CHUNK, KEY_CHUNK)
    first = lax.broadcasted_iota(jnp.int32, shape, 0)
    second = lax.broadcasted_iota(jnp.int32, shape, 1)
    return first <= second if transposed else second <= first


def chunk(i, n=1):
    return slice(i * KEY_CHUNK, (i + n) * KEY_CHUNK)


def attend_kernel(
    meta, q_ref, kva_ref, kvb_ref, bounds_ref, acc_in, sum_in, acc_ref, sum_ref, *, first
):
    rows = q_ref.shape[0]
    key_rows = kva_ref.shape[0]
    if first:
        acc_ref[...] = jnp.zeros_like(acc_ref)
        sum_ref[...] = jnp.zeros_like(sum_ref)
    else:
        acc_ref[...] = acc_in[...]
        sum_ref[...] = sum_in[...]
    ones = jnp.ones((KEY_CHUNK, HEAD_WIDTH), bf16)

    def work(kv_ref, lanes, keys, queries, mask):
        key = jnp.concatenate([kv_ref[keys, :HEAD_WIDTH], lanes[keys, :]], axis=1)
        weight = jnp.exp2(dot_nt(q_ref[queries, :], key))
        if mask:
            weight = jnp.where(lower_mask(False), weight, 0.0)
        value = jnp.concatenate([kv_ref[keys, HEAD_WIDTH:], ones], axis=1)
        out = dot(weight.astype(bf16), value)
        acc_ref[queries, :] += out[:, :HEAD_WIDTH]
        sum_ref[queries, :] += out[:, HEAD_WIDTH:]

    for place, kv_ref in enumerate((kva_ref, kvb_ref)):
        key_start = meta[2 + place]
        diagonal = first and place == 0

        @pl.when(block_used(meta, key_start, key_rows, rows))
        def _():
            lanes = key_lanes(meta, key_start, key_rows, bounds_ref)
            for c in range(key_rows // KEY_CHUNK):
                if diagonal:
                    work(kv_ref, lanes, chunk(c), chunk(c), True)
                    if c + 1 < rows // KEY_CHUNK:
                        work(kv_ref, lanes, chunk(c), slice((c + 1) * KEY_CHUNK, rows), False)
                else:
                    work(kv_ref, lanes, chunk(c), slice(0, rows), False)


def attend_stage(q, kv_a, kv_b, bounds, meta, acc, total):
    rows = q.shape[0]
    key_rows = kv_a.shape[0]
    q_heads = q.shape[1] // (2 * HEAD_WIDTH)
    group = q.shape[1] // kv_a.shape[1]
    width = q_heads * HEAD_WIDTH
    first = acc is None
    if first:
        acc = total = jnp.zeros((8, HEAD_WIDTH), f32)
    wide = 2 * HEAD_WIDTH
    per_q = pl.BlockSpec((rows, wide), lambda j, m: (0, j))
    per_kv = pl.BlockSpec((key_rows, wide), lambda j, m: (0, j // group))
    per_out = pl.BlockSpec((rows, HEAD_WIDTH), lambda j, m: (0, j))
    carried = pl.BlockSpec((8, HEAD_WIDTH), lambda j, m: (0, 0)) if first else per_out
    return pl.pallas_call(
        functools.partial(attend_kernel, first=first),
        grid_spec=pltpu.PrefetchScalarGridSpec(
            num_scalar_prefetch=1,
            grid=(q_heads,),
            in_specs=[
                per_q,
                per_kv,
                per_kv,
                pl.BlockSpec((8, HEAD_WIDTH), lambda j, m: (0, 0)),
                carried,
                carried,
            ],
            out_specs=[per_out, per_out],
        ),
        out_shape=[jax.ShapeDtypeStruct((rows, width), f32)] * 2,
        input_output_aliases={} if first else {5: 0, 6: 1},
        compiler_params=pltpu.CompilerParams(vmem_limit_bytes=40 * MIB),
        cost_estimate=SMALL,
        name="attend_stage",
    )(meta, q, kv_a, kv_b, bounds, acc, total)


def finish_kernel(q_ref, acc_ref, sum_ref, o_ref, q_out_ref):
    total = sum_ref[...]
    o_ref[...] = (acc_ref[...] / total).astype(bf16)
    rows = total.shape[0]
    lanes = lane_index(rows)
    extra = q_ref[:, HEAD_WIDTH:].astype(f32)
    for i, part in enumerate(split_parts(jnp.log2(total))):
        extra = jnp.where(lanes == LOG_LANE + i, -part.astype(f32), extra)
    q_out_ref[:, :HEAD_WIDTH] = q_ref[:, :HEAD_WIDTH]
    q_out_ref[:, HEAD_WIDTH:] = extra.astype(bf16)


def finish(q, acc, total):
    rows, width = acc.shape
    narrow = pl.BlockSpec((rows, HEAD_WIDTH), lambda j: (0, j))
    wide = pl.BlockSpec((rows, 2 * HEAD_WIDTH), lambda j: (0, j))
    return pl.pallas_call(
        finish_kernel,
        grid=(width // HEAD_WIDTH,),
        in_specs=[wide, narrow, narrow],
        out_specs=[narrow, wide],
        out_shape=[
            jax.ShapeDtypeStruct((rows, width), bf16),
            jax.ShapeDtypeStruct((rows, 2 * width), bf16),
        ],
        name="finish",
    )(q, acc, total)


def delta_kernel(do_ref, acc_ref, sum_ref, out_ref):
    do = do_ref[...]
    outcome = acc_ref[...] / sum_ref[...]
    delta = jnp.sum(do.astype(f32) * outcome, axis=-1, keepdims=True)
    rows = do.shape[0]
    lanes = lane_index(rows)
    extra = jnp.zeros((rows, HEAD_WIDTH), f32)
    for i, part in enumerate(split_parts(delta)):
        extra = jnp.where(lanes == i, -part.astype(f32), extra)
    out_ref[:, :HEAD_WIDTH] = do
    out_ref[:, HEAD_WIDTH:] = extra.astype(bf16)


def with_delta(do, acc, total):
    rows, width = acc.shape
    narrow = pl.BlockSpec((rows, HEAD_WIDTH), lambda j: (0, j))
    return pl.pallas_call(
        delta_kernel,
        grid=(width // HEAD_WIDTH,),
        in_specs=[narrow, narrow, narrow],
        out_specs=pl.BlockSpec((rows, 2 * HEAD_WIDTH), lambda j: (0, j)),
        out_shape=jax.ShapeDtypeStruct((rows, 2 * width), bf16),
        name="with_delta",
    )(do, acc, total)


def attend_back_kernel(
    meta,
    q_ref,
    do_ref,
    kv_ref,
    bounds_ref,
    dq_in,
    dq_ref,
    dkv_ref,
    dq_turned,
    dkv_sum,
    *,
    first,
    group,
    diagonal,
    place,
):
    rows = q_ref.shape[0]
    key_rows = kv_ref.shape[0]
    key_start = meta[2 + place]
    step = lax.rem(pl.program_id(0), group)

    @pl.when(step == 0)
    def _():
        dkv_sum[...] = jnp.zeros_like(dkv_sum)

    def work(lanes, ones, keys, queries, mask):
        key = kv_ref[keys, :HEAD_WIDTH]
        q = q_ref[queries, :]
        do = do_ref[queries, :]
        weight = jnp.exp2(dot_nt(jnp.concatenate([key, lanes[keys, :]], axis=1), q))
        if mask:
            weight = jnp.where(lower_mask(True), weight, 0.0)
        value = jnp.concatenate([kv_ref[keys, HEAD_WIDTH:], ones], axis=1)
        d_score = (weight * dot_nt(value, do)).astype(bf16)
        dkv_sum[keys, HEAD_WIDTH:] += dot(weight.astype(bf16), do[:, :HEAD_WIDTH])
        dkv_sum[keys, :HEAD_WIDTH] += dot(d_score, q[:, :HEAD_WIDTH])
        dq_turned[:, queries] += dot_tn(key, d_score)

    used = block_used(meta, key_start, key_rows, rows)

    @pl.when(used)
    def _():
        dq_turned[...] = jnp.zeros_like(dq_turned)
        lanes = key_lanes(meta, key_start, key_rows, bounds_ref)
        ones = jnp.where(lane_index(KEY_CHUNK) < 3, 1.0, 0.0).astype(bf16)
        for c in range(key_rows // KEY_CHUNK):
            if diagonal:
                work(lanes, ones, chunk(c), chunk(c), True)
                if c + 1 < rows // KEY_CHUNK:
                    work(lanes, ones, chunk(c), slice((c + 1) * KEY_CHUNK, rows), False)
            else:
                work(lanes, ones, chunk(c), slice(0, rows), False)
        turned = dq_turned[...].T
        dq_ref[...] = turned if first else dq_in[...] + turned

    @pl.when(jnp.logical_not(used))
    def _():
        dq_ref[...] = jnp.zeros_like(dq_ref) if first else dq_in[...]

    @pl.when(step == group - 1)
    def _():
        dkv_ref[...] = dkv_sum[...].astype(dkv_ref.dtype)


def attend_back(q, do, kv, bounds, meta, dq, place, diagonal, kind):
    rows = q.shape[0]
    key_rows = kv.shape[0]
    q_heads = q.shape[1] // (2 * HEAD_WIDTH)
    group = q.shape[1] // kv.shape[1]
    width = q_heads * HEAD_WIDTH
    first = dq is None
    if first:
        dq = jnp.zeros((8, HEAD_WIDTH), f32)
    wide = 2 * HEAD_WIDTH
    per_q = pl.BlockSpec((rows, wide), lambda j, m: (0, j))
    per_kv = pl.BlockSpec((key_rows, wide), lambda j, m: (0, j // group))
    per_out = pl.BlockSpec((rows, HEAD_WIDTH), lambda j, m: (0, j))
    carried = pl.BlockSpec((8, HEAD_WIDTH), lambda j, m: (0, 0)) if first else per_out
    return pl.pallas_call(
        functools.partial(
            attend_back_kernel, first=first, group=group, diagonal=diagonal, place=place
        ),
        grid_spec=pltpu.PrefetchScalarGridSpec(
            num_scalar_prefetch=1,
            grid=(q_heads,),
            in_specs=[
                per_q,
                per_q,
                per_kv,
                pl.BlockSpec((8, HEAD_WIDTH), lambda j, m: (0, 0)),
                carried,
            ],
            out_specs=[per_out, per_kv],
            scratch_shapes=[
                pltpu.VMEM((HEAD_WIDTH, rows), f32),
                pltpu.VMEM((key_rows, wide), f32),
            ],
        ),
        out_shape=[
            jax.ShapeDtypeStruct((rows, width), f32),
            jax.ShapeDtypeStruct(kv.shape, kind),
        ],
        input_output_aliases={} if first else {5: 0},
        compiler_params=pltpu.CompilerParams(vmem_limit_bytes=40 * MIB),
        cost_estimate=SMALL,
        name="attend_back",
    )(meta, q, do, kv, bounds, dq)


def after(values):
    return lax.optimization_barrier(values)


def pick(array, index):
    return lax.dynamic_index_in_dim(array, index, 0, keepdims=False)


def solution(mesh):
    n_seq = mesh.shape["seq"]
    n_head = mesh.shape["head"]
    n_chip = n_seq // 2

    def swap_core(value):
        return lax.ppermute(value, "seq", [(i, i ^ 1) for i in range(n_seq)])

    def to_next(value):
        return lax.ppermute(value, "seq", [(i, i + 2) for i in range(n_seq - 2)])

    def to_previous(value):
        return lax.ppermute(value, "seq", [(i + 2, i) for i in range(n_seq - 2)])

    def across(value, bits):
        return lax.ppermute(value, "head", [(i, i ^ bits) for i in range(n_head)])

    def gather_head(value):
        me = lax.axis_index("head")
        if n_head != 4:
            every = lax.all_gather(value, "head", axis=0)
            return [(every[i], i) for i in range(n_head)]
        half = value.shape[0] // 2
        by_x = across(value, 1)
        by_y = across(value, 2)
        low = across(by_x[:half], 2)
        high = across(by_y[half:], 1)
        far = jnp.concatenate([low, high], axis=0)
        return [(value, me), (by_x, me ^ 1), (by_y, me ^ 2), (far, me ^ 3)]

    def scatter_head(value, *beside):
        rows, width = value.shape
        if n_head != 4:
            total = lax.psum_scatter(value, "head", scatter_dimension=0, tiled=True).astype(f32)
            return total, [work() for work in beside]
        me = lax.axis_index("head")
        x, y = me & 1, me >> 1
        part = value.reshape(2, 2, 2, rows // 8, width)
        first, second = part[:, :, 0], part[:, :, 1]
        first_x = jnp.swapaxes(first, 0, 1)
        got_first = across(pick(first_x, 1 - x), 1)
        got_second = across(pick(second, 1 - y), 2)
        made = []
        if beside:
            got_first, got_second, made_first = after((got_first, got_second, beside[0]()))
            made.append(made_first)
        sum_first = pick(first_x, x).astype(f32) + got_first.astype(f32)
        sum_second = pick(second, y).astype(f32) + got_second.astype(f32)
        last_first = across(pick(sum_first, 1 - y).astype(bf16), 2)
        last_second = across(pick(sum_second, 1 - x).astype(bf16), 1)
        if beside:
            last_first, last_second, made_second = after((last_first, last_second, beside[1]()))
            made.append(made_second)
        total = jnp.concatenate(
            [
                pick(sum_first, y) + last_first.astype(f32),
                pick(sum_second, x) + last_second.astype(f32),
            ],
            axis=0,
        )
        return total, made

    def in_order(pieces):
        rows = pieces[0][0].shape[0]
        out = jnp.zeros((rows * len(pieces),) + pieces[0][0].shape[1:], pieces[0][0].dtype)
        for piece, owner in pieces:
            out = lax.dynamic_update_slice_in_dim(out, piece, owner * rows, 0)
        return out

    def exchange_head(value):
        me = lax.axis_index("head")
        if n_head != 4:
            got = lax.all_to_all(value, "head", 0, 0)
            return got.reshape(-1, value.shape[-1])
        pieces = [(pick(value, me), me)]
        for bits in (3, 1, 2):
            pieces.append((across(pick(value, me ^ bits), bits), me ^ bits))
        return in_order(pieces)

    def body(
        tokens,
        lengths,
        norm1_gain,
        w_query,
        key_matrix,
        value_matrix,
        query_gain,
        key_gain,
        w_output,
        norm2_gain,
        w_gate,
        w_up,
        w_down,
        cotangent,
    ):
        rows = tokens.shape[0]
        share = rows // n_head
        seq_index = lax.axis_index("seq")
        head_index = lax.axis_index("head")
        chip, core = seq_index // 2, seq_index % 2

        half_rows = w_output.shape[0] // 2
        w_half = lax.dynamic_slice_in_dim(w_output, core * half_rows, half_rows, 0)
        w_mine = lax.all_gather(w_half, "head", axis=0)

        index = seq_index * rows + jnp.arange(rows, dtype=jnp.int32)
        begin = locate(index, lengths)
        cosine, sine = rotary(index - begin)
        ends = jnp.cumsum(lengths)
        n_lengths = lengths.shape[0]
        bounds = jnp.zeros((8, HEAD_WIDTH), jnp.int32).at[0].set(2**30)
        bounds = bounds.at[0, :n_lengths].set(ends - lengths).at[1, :n_lengths].set(ends)

        def stage_meta(stage):
            source = 2 * (chip - stage)
            return jnp.stack(
                [seq_index * rows, begin[0], (source + core) * rows, (source + 1 - core) * rows]
            ).astype(jnp.int32)

        metas = [stage_meta(stage) for stage in range(n_chip)]

        xf = tokens.astype(f32)
        inverse1 = lax.rsqrt(jnp.mean(xf * xf, axis=-1, keepdims=True) + EPSILON)
        first_in = (xf * inverse1 * norm1_gain).astype(bf16)
        key_raw = dot(first_in, key_matrix)
        value_raw = dot(first_in, value_matrix)
        current = key_prep(key_raw, value_raw, key_gain, cosine, sine)
        sibling = swap_core(current)
        following = to_next(current)
        query_raw = dot(first_in, w_query)
        q_wide = query_prep(metas[0], query_raw, query_gain, cosine, sine, bounds)
        d_mixed = dot_nt(cotangent, w_down)
        following, q_wide, d_mixed = after((following, q_wide, d_mixed))

        blocks = []
        acc = total = None
        for stage in range(n_chip):
            blocks.append((current, sibling))
            if stage + 1 < n_chip:
                current = following
                sibling = swap_core(current)
                following = to_next(current) if stage + 2 < n_chip else None
            acc, total = attend_stage(q_wide, *blocks[stage], bounds, metas[stage], acc, total)
            if following is not None:
                following, acc, total = after((following, acc, total))
            if stage == 1:
                w_mine, acc = after((w_mine, acc))
                w_other = swap_core(w_mine)
                w_full = jnp.where(
                    core == 0,
                    jnp.concatenate([w_mine, w_other], axis=1),
                    jnp.concatenate([w_other, w_mine], axis=1),
                )
            if stage == n_chip - 2:
                w_full, acc = after((w_full, acc))
        o_low, q_back = finish(q_wide, acc, total)

        hidden = xf
        for piece, owner in gather_head(o_low):
            hidden = hidden + dot(piece, pick(w_full, owner))

        inverse2 = lax.rsqrt(jnp.mean(hidden * hidden, axis=-1, keepdims=True) + EPSILON)
        second_in = (hidden * inverse2 * norm2_gain).astype(bf16)
        gate_raw = dot(second_in, w_gate)
        up_raw = dot(second_in, w_up)
        sigmoid = jax.nn.sigmoid(gate_raw)
        silu = gate_raw * sigmoid
        mixed_low = (silu * up_raw).astype(bf16)
        gate_low = (d_mixed * up_raw * (sigmoid * (1.0 + gate_raw * (1.0 - sigmoid)))).astype(bf16)
        up_low = (d_mixed * silu).astype(bf16)

        def scatter_seq(value, dimension):
            return lax.psum_scatter(value, "seq", scatter_dimension=dimension, tiled=True)

        down_sum = dot_tn(mixed_low, cotangent).astype(bf16)
        down_sum, gate_low, up_low = after((down_sum, gate_low, up_low))
        grad_down = scatter_seq(down_sum, 1)
        second_part = (dot_nt(gate_low, w_gate) + dot_nt(up_low, w_up)).astype(bf16)

        second_grad, (gate_sum, up_sum) = scatter_head(
            second_part,
            lambda: dot_tn(second_in, gate_low).astype(bf16),
            lambda: dot_tn(second_in, up_low).astype(bf16),
        )
        gate_up_sum = jnp.concatenate([gate_sum, up_sum], axis=1)
        my_hidden = lax.dynamic_slice_in_dim(hidden, head_index * share, share, 0)
        my_inverse = lax.rsqrt(jnp.mean(my_hidden * my_hidden, axis=-1, keepdims=True) + EPSILON)
        my_hat = my_hidden * my_inverse
        grad_norm2 = jnp.sum(second_grad * my_hat, axis=0)
        scaled = second_grad * norm2_gain
        my_dy = lax.dynamic_slice_in_dim(cotangent, head_index * share, share, 0).astype(f32)
        hidden_grad = my_dy + my_inverse * (
            scaled - my_hat * jnp.mean(scaled * my_hat, axis=-1, keepdims=True)
        )
        my_branch = hidden_grad.astype(bf16)
        do_rows = dot_nt(my_branch, w_full.reshape(-1, w_full.shape[-1])).astype(bf16)
        do_pieces = jnp.stack(jnp.split(do_rows, n_head, axis=1))
        do_low = exchange_head(do_pieces)

        do_wide = with_delta(do_low, acc, total)
        grad_down, gate_up_sum, do_wide = after((grad_down, gate_up_sum, do_wide))
        grad_gate_up = scatter_seq(gate_up_sum, 0)

        mixed_late, my_branch, do_wide = after((mixed_low, my_branch, do_wide))
        mixed_sum, unused = scatter_head(dot(mixed_late, w_down).astype(bf16))
        mixed = in_order(gather_head((my_hidden + mixed_sum).astype(bf16)))
        branch = in_order(gather_head(my_branch))

        dq = None
        arrived = None
        for stage in reversed(range(n_chip)):
            kv_a, kv_b = blocks[stage]
            meta = metas[stage]
            dq, dkv_b = attend_back(q_back, do_wide, kv_b, bounds, meta, dq, 1, False, bf16)
            theirs = swap_core(dkv_b)
            dq, dkv_a = attend_back(q_back, do_wide, kv_a, bounds, meta, dq, 0, stage == 0, f32)
            dkv = dkv_a + theirs.astype(f32)
            if arrived is not None:
                dkv = dkv + arrived.astype(f32)
            if stage > 0:
                sent, dq = after((dkv.astype(bf16), dq))
                arrived = to_previous(sent)
        query_grad, grad_qgain = head_back(
            query_raw, dq, query_gain, cosine, sine, SCORE_SCALE, 1
        )
        key_grad, grad_kgain = head_back(
            key_raw, dkv, key_gain, cosine, sine, 1.0 / LOG2E, 2
        )
        value_grad = jnp.concatenate(
            [
                dkv[:, (2 * j + 1) * HEAD_WIDTH : (2 * j + 2) * HEAD_WIDTH]
                for j in range(dkv.shape[1] // (2 * HEAD_WIDTH))
            ],
            axis=1,
        ).astype(bf16)

        first_part = (
            dot_nt(query_grad, w_query)
            + dot_nt(key_grad, key_matrix)
            + dot_nt(value_grad, value_matrix)
        ).astype(bf16)
        first_grad, (attn_sum, output_sum) = scatter_head(
            first_part,
            lambda: jnp.concatenate(
                [
                    dot_tn(first_in, query_grad).astype(bf16),
                    dot_tn(first_in, key_grad).astype(bf16),
                    dot_tn(first_in, value_grad).astype(bf16),
                ],
                axis=1,
            ),
            lambda: dot_tn(o_low, branch).astype(bf16),
        )
        grad_gate_up, attn_sum, output_sum = after((grad_gate_up, attn_sum, output_sum))
        grad_attn = scatter_seq(attn_sum, 0)
        grad_output = scatter_seq(output_sum, 1)
        widths = (query_grad.shape[1], query_grad.shape[1] + key_grad.shape[1])
        grad_query, grad_key, grad_value = jnp.split(grad_attn, widths, axis=1)

        my_x = lax.dynamic_slice_in_dim(tokens, head_index * share, share, 0).astype(f32)
        my_inverse1 = lax.rsqrt(jnp.mean(my_x * my_x, axis=-1, keepdims=True) + EPSILON)
        my_hat1 = my_x * my_inverse1
        grad_norm1 = jnp.sum(first_grad * my_hat1, axis=0)
        scaled1 = first_grad * norm1_gain
        my_tokens_grad = hidden_grad + my_inverse1 * (
            scaled1 - my_hat1 * jnp.mean(scaled1 * my_hat1, axis=-1, keepdims=True)
        )
        grad_tokens = in_order(gather_head(my_tokens_grad.astype(bf16))).astype(f32)

        gains = jnp.concatenate([grad_norm1, grad_norm2, grad_qgain[0], grad_kgain[0]])
        gains = gains.reshape(-1, HEAD_WIDTH)
        for axis, size in (("head", n_head), ("seq", n_seq)):
            bit = 1
            while bit < size:
                gains = gains + lax.ppermute(gains, axis, [(i, i ^ bit) for i in range(size)])
                bit *= 2
        gains = gains.reshape(-1)
        width = tokens.shape[1]
        grad_norm1, grad_norm2 = gains[:width], gains[width : 2 * width]
        grad_qgain = gains[2 * width : 2 * width + HEAD_WIDTH]
        grad_kgain = gains[2 * width + HEAD_WIDTH :]
        return (
            mixed,
            grad_tokens,
            grad_norm1,
            grad_query.astype(f32),
            grad_key.astype(f32),
            grad_value.astype(f32),
            grad_qgain,
            grad_kgain,
            grad_output.astype(f32),
            grad_norm2,
            grad_gate_up[:, : w_gate.shape[1]].astype(f32),
            grad_gate_up[:, w_gate.shape[1] :].astype(f32),
            grad_down.astype(f32),
        )

    in_specs = (
        P("seq", None),
        P(),
        P(),
        P(None, "head"),
        P(None, "head"),
        P(None, "head"),
        P(),
        P(),
        P("head", None),
        P(),
        P(None, "head"),
        P(None, "head"),
        P("head", None),
        P("seq", None),
    )
    out_specs = (
        P("seq", None),
        P("seq", None),
        P(),
        P("seq", "head"),
        P("seq", "head"),
        P("seq", "head"),
        P(),
        P(),
        P("head", "seq"),
        P(),
        P("seq", "head"),
        P("seq", "head"),
        P("head", "seq"),
    )
    return jax.shard_map(body, mesh=mesh, in_specs=in_specs, out_specs=out_specs, check_vma=False)
```

time: 955 us -> 655 us (0.69)
  waiting for transfers between devices: 499 us -> 258 us
  blocking collectives: 40.6 us -> 0 us
  matrix products: 145 us -> 125 us
    reduce_scatter x7 -> x4, waiting for transfers between devices: 155 us -> 8.26 us  [scatter_seq(): lax.psum_scatter(value, 'seq', scatter_dimension=dimension, tiled=True)]
    ppermute x3, waiting for transfers between devices: 235 us -> 105 us  [to_previous(): return lax.ppermute(value, 'seq', [(i + 2, i) for i in range(n_seq - 2)])]
    ppermute x19 -> x31, waiting for transfers between devices: 46.8 us -> 101 us  [across(): return lax.ppermute(value, 'head', [(i, i ^ bits) for i in range(n_head)])]
    psum x1 -> x0, blocking collectives: 40.6 us -> none  [body(): lax.psum((grad_norm1, grad_qgain[0], grad_kgain[0], grad_norm2), ('seq',...]
    all_gather x1, waiting for transfers between devices: 38.5 us -> 0.01 us  [body(): w_mine = lax.all_gather(w_half, 'head', axis=0)]
    ppermute x9, starting transfers between devices: 27.6 us -> 7.85 us  [swap_core(): return lax.ppermute(value, 'seq', [(i, i ^ 1) for i in range(n_seq)])]
    dot_general x7, matrix products: 46.9 us -> 30.4 us  [dot_tn(): return lax.dot_general(left, right, TN, preferred_element_type=f32)]
    ppermute x19 -> x31, starting transfers between devices: 24.5 us -> 40.6 us  [across(): return lax.ppermute(value, 'head', [(i, i ^ bits) for i in range(n_head)])]
  transfers between devices with their start and end apart: 44 -> 56, of which waited for: 20 -> 28; matrix products, arithmetic and copies ran while one was open for 18% -> 25% of each run, Pallas kernels for 7% -> 9%
where the time goes in v2:
time: 655 us; the launch traced here: 646 us
  waiting for transfers between devices  258 us (39%)
  matrix products  125 us (19%)
  starting transfers between devices  70.1 us (11%)
  Pallas kernels  67.9 us (10%)
  other arithmetic  57.7 us (9%)
  local copies, waits for them, and re-layouts  51 us (8%)
  between operations  16 us (2%)
    ppermute x3, waiting for transfers between devices, to_previous(): return lax.ppermute(value, 'seq', [(i + 2, i) for i in range(n_seq - 2)])  105 us
    ppermute x31, waiting for transfers between devices, across(): return lax.ppermute(value, 'head', [(i, i ^ bits) for i in range(n_head)])  101 us
    dot_general x10, matrix products, dot(): return jnp.dot(left, right, preferred_element_type=f32)  57 us
    ppermute x31, starting transfers between devices, across(): return lax.ppermute(value, 'head', [(i, i ^ bits) for i in range(n_head)])  40.6 us
    dot_general x7, matrix products, dot_nt(): return lax.dot_general(left, right, NT, preferred_element_type=f32)  37.9 us
    unnamed x190, local copies, waits for them, and re-layouts  30.5 us
    dot_general x7, matrix products, dot_tn(): return lax.dot_general(left, right, TN, preferred_element_type=f32)  30.4 us
    pallas_call x8, Pallas kernels, attend_back(): pl.pallas_call(functools.partial(attend_back_kernel, first=first, group=g...  27.2 us
  transfers between devices with their start and end apart: 56, of which 28 were waited for; matrix products, arithmetic and copies ran while one was open for 25% of the time, Pallas kernels for 9%

profile of v2, /device:TPU:0, one launch (start us, length us, event | category | flops | bytes accessed | tf_op | source)
XLA Modules:
  0.0 646.4 jit_solution(11635453044058675382)
XLA Ops:
  26.7 9.6 %fusion.68 = f32[768,1536]{1,0:T(8,128)} fusion(bf16[768,2048]{1,0:T(8,128)(2,1)} %param.33, bf16[1536,2048]{1,0:T(8,128)(2,1)} %param.32), kind=kOutput, calls=%fused_computation.176 | convolution fusion | flops 4831838208 | bytes 14155776 | tf_op jit(solution)/shard_map/dot_general | solution.py:34
  58.9 9.9 %collective-permute-done.1.kva_ref.kv_ref = bf16[768,512]{1,0:T(8,128)(2,1)S(1)} collective-permute-done((bf16[768,512]{1,0:T(8,128)(2,1)}, bf16[768,512]{1,0:T(8,128)(2,1)S(1)}, u32[]{:S(2)}, u32[]{:S(2)}) %collective-permute-start.1) | collective-permute-done | bytes 786464 | tf_op jit(solution)/shard_map/ppermute | solution.py:455
  78.7 11.0 %collective-permute-done.3.kva_ref.kv_ref = bf16[768,512]{1,0:T(8,128)(2,1)S(1)} collective-permute-done((bf16[768,512]{1,0:T(8,128)(2,1)S(1)}, bf16[768,512]{1,0:T(8,128)(2,1)S(1)}, u32[]{:S(2)}, u32[]{:S(2)}) %collective-permute-start.3) | collective-permute-done | bytes 786464 | tf_op jit(solution)/shard_map/ppermute | solution.py:455
  91.1 9.2 %collective-permute-done.7.kvb_ref.kv_ref = bf16[768,512]{1,0:T(8,128)(2,1)} collective-permute-done((bf16[768,512]{1,0:T(8,128)(2,1)}, bf16[768,512]{1,0:T(8,128)(2,1)}, u32[]{:S(2)}, u32[]{:S(2)}) %collective-permute-start.7) | collective-permute-done | bytes 786464 | tf_op jit(solution)/shard_map/ppermute | solution.py:452
  109.4 9.7 %maximum_select_fusion = bf16[4,512,2048]{2,1,0:T(8,128)(2,1)} fusion(bf16[4,256,2048]{2,1,0:T(8,128)(2,1)} %collective-permute-done.6, bf16[4,256,2048]{2,1,0:T(8,128)(2,1)S(1)} %bitcast.198, pred[]{:T(512)S(6)} %eq.21), kind=kLoop, calls=%fused_computation.4 | loop fusion | flops 37748736 | bytes 16777216 | tf_op jit(solution)/shard_map/jit(_where)/select_n | solution.py:594
  138.0 10.5 %collective-permute-done.8 = bf16[768,512]{1,0:T(8,128)(2,1)} collective-permute-done((bf16[768,512]{1,0:T(8,128)(2,1)}, bf16[768,512]{1,0:T(8,128)(2,1)}, u32[]{:S(2)}, u32[]{:S(2)}) %collective-permute-start.8) | collective-permute-done | bytes 786464 | tf_op jit(solution)/shard_map/ppermute | solution.py:461
  165.8 8.2 %multiply_reduce_fusion = (f32[768]{0:T(1024)S(1)}, f32[768,2048]{1,0:T(8,128)S(1)}) fusion(bf16[4,512,2048]{2,1,0:T(8,128)(2,1)S(1)} %bitcast.188, s32[]{:T(128)S(6)} %select_n.114, bf16[384,512]{1,0:T(8,128)(2,1)S(1)} %collective-permute-done.11, bf16[384,512]{1,0:T(8,128)(2,1)S(1)} %collective-permute-done.10, f32[768,2048]{1,0:T(8,128)} %fusion.11, ...), kind=kOutput, calls=%fused_computation.17 | convolution fusion | flops 1623194880 | bytes 31198212 | tf_op jit(solution)/shard_map/dot_general | solution.py:30
  177.3 8.6 %fusion.69 = f32[768,1536]{1,0:T(8,128)S(1)} fusion(bf16[768,2048]{1,0:T(8,128)(2,1)S(1)} %multiply_convert_fusion, bf16[2048,1536]{1,0:T(8,128)(2,1)} %param.30), kind=kOutput, calls=%fused_computation.177 | convolution fusion | flops 4831838208 | bytes 14155776 | tf_op jit(solution)/shard_map/dot_general | solution.py:30
  197.5 7.0 %convolution_convert_fusion.2 = bf16[1536,2048]{1,0:T(8,128)(2,1)} fusion(bf16[768,1536]{1,0:T(8,128)(2,1)S(1)} %get-tuple-element.154, bf16[768,2048]{1,0:T(8,128)(2,1)S(1)} %copy-done.71), kind=kOutput, calls=%fused_computation.7 | convolution fusion | flops 4834983936 | bytes 11796480 | tf_op jit(solution)/shard_map/dot_general | solution.py:38
  204.6 8.1 %fusion.71 = f32[768,2048]{1,0:T(8,128)S(1)} fusion(bf16[768,1536]{1,0:T(8,128)(2,1)} %get-tuple-element.144, bf16[2048,1536]{1,0:T(8,128)(2,1)} %param.30), kind=kOutput, calls=%fused_computation.179 | convolution fusion | flops 4831838208 | bytes 14942208 | tf_op jit(solution)/shard_map/dot_general | solution.py:34
  212.7 8.2 %add_convert_fusion.1 = bf16[768,2048]{1,0:T(8,128)(2,1)S(1)} fusion(f32[768,2048]{1,0:T(8,128)S(1)} %fusion.71, bf16[768,1536]{1,0:T(8,128)(2,1)S(1)} %copy-done.58, bf16[2048,1536]{1,0:T(8,128)(2,1)} %param.31), kind=kOutput, calls=%fused_computation.15 | convolution fusion | flops 4834983936 | bytes 18087936 | tf_op jit(solution)/shard_map/dot_general | solution.py:34
  229.1 10.6 %collective-permute-done.13 = bf16[2,96,2048]{2,1,0:T(8,128)(2,1)S(1)} collective-permute-done((bf16[2,96,2048]{2,1,0:T(8,128)(2,1)S(1)}, bf16[2,96,2048]{2,1,0:T(8,128)(2,1)S(1)}, u32[]{:S(2)}, u32[]{:S(2)}) %collective-permute-start.13) | collective-permute-done | bytes 786464 | tf_op jit(solution)/shard_map/ppermute | solution.py:461
  242.9 8.7 %convolution_convert_fusion = bf16[2048,1536]{1,0:T(8,128)(2,1)S(1)} fusion(bf16[768,2048]{1,0:T(8,128)(2,1)} %copy-done.50, bf16[768,1536]{1,0:T(8,128)(2,1)} %get-tuple-element.145), kind=kOutput, calls=%fused_computation.5 | convolution fusion | flops 4834983936 | bytes 11796480 | tf_op jit(solution)/shard_map/dot_general | solution.py:38
  280.5 8.3 %reduce-scatter.5.cloned.1.call-done = bf16[1536,256]{1,0:T(8,128)(2,1)} async-done(((bf16[1536,2048]{1,0:T(8,128)(2,1)}), bf16[1536,256]{1,0:T(8,128)(2,1)}) %reduce-scatter.5.cloned.1.call-update) | async-done | bytes 786448 | tf_op jit(solution)/shard_map/reduce_scatter | solution.py:618
  307.5 41.4 %collective-permute-done.29 = bf16[768,512]{1,0:T(8,128)(2,1)S(1)} collective-permute-done((bf16[768,512]{1,0:T(8,128)(2,1)S(1)}, bf16[768,512]{1,0:T(8,128)(2,1)S(1)}, u32[]{:S(2)}, u32[]{:S(2)}) %collective-permute-start.29) | collective-permute-done | bytes 786464 | tf_op jit(solution)/shard_map/ppermute | solution.py:458
  356.1 8.6 %collective-permute-done.40 = bf16[96,2048]{1,0:T(8,128)(2,1)S(1)} collective-permute-done((bf16[96,2048]{1,0:T(8,128)(2,1)S(1)}, bf16[96,2048]{1,0:T(8,128)(2,1)S(1)}, u32[]{:S(2)}, u32[]{:S(2)}) %collective-permute-start.40) | collective-permute-done | bytes 393248 | tf_op jit(solution)/shard_map/ppermute | solution.py:461
  371.0 34.5 %collective-permute-done.31 = bf16[768,512]{1,0:T(8,128)(2,1)S(1)} collective-permute-done((bf16[768,512]{1,0:T(8,128)(2,1)S(1)}, bf16[768,512]{1,0:T(8,128)(2,1)S(1)}, u32[]{:S(2)}, u32[]{:S(2)}) %collective-permute-start.31) | collective-permute-done | bytes 786464 | tf_op jit(solution)/shard_map/ppermute | solution.py:458
  410.7 8.3 %attend_back.15 = (f32[768,512]{1,0:T(8,128)S(1)}, f32[768,512]{1,0:T(8,128)S(1)}) custom-call(s32[4]{0:T(128)S(1)} %copy-done.29, bf16[768,1024]{1,0:T(8,128)(2,1)S(1)} %copy-done.3, bf16[768,1024]{1,0:T(8,128)(2,1)S(1)} %copy-done.2, bf16[768,512]{1,0:T(8,128)(2,1)S(1)} %copy-done.14, s32[8,128]{1,0:T(8,128)S(1)} %copy-done.28, ...), custom_call_target="tpu_custom_call", output_to_operand_aliasing={{0}: (5, {})} | custom-call | flops 1 | bytes 1 | tf_op jit(solution)/shard_map/attend_back/pallas_call | solution.py:407
  443.5 29.0 %collective-permute-done.33 = bf16[768,512]{1,0:T(8,128)(2,1)} collective-permute-done((bf16[768,512]{1,0:T(8,128)(2,1)}, bf16[768,512]{1,0:T(8,128)(2,1)}, u32[]{:S(2)}, u32[]{:S(2)}) %collective-permute-start.33) | collective-permute-done | bytes 786464 | tf_op jit(solution)/shard_map/ppermute | solution.py:458
  492.8 10.2 %collective-permute-done.35 = bf16[2,96,2048]{2,1,0:T(8,128)(2,1)} collective-permute-done((bf16[2,96,2048]{2,1,0:T(8,128)(2,1)S(1)}, bf16[2,96,2048]{2,1,0:T(8,128)(2,1)}, u32[]{:S(2)}, u32[]{:S(2)}) %collective-permute-start.35) | collective-permute-done | bytes 786464 | tf_op jit(solution)/shard_map/ppermute | solution.py:461
  521.6 7.9 %convolution_convert_fusion.3 = bf16[768,2048]{1,0:T(8,128)(2,1)S(1)} fusion(bf16[768,1536]{1,0:T(8,128)(2,1)} %copy-done.57, bf16[1536,2048]{1,0:T(8,128)(2,1)} %param.32), kind=kOutput, calls=%fused_computation.24 | convolution fusion | flops 4833411072 | bytes 11796480 | tf_op jit(solution)/shard_map/dot_general | solution.py:30
  532.8 16.0 %collective-permute-done.19 = bf16[2,96,2048]{2,1,0:T(8,128)(2,1)} collective-permute-done((bf16[2,96,2048]{2,1,0:T(8,128)(2,1)}, bf16[2,96,2048]{2,1,0:T(8,128)(2,1)}, u32[]{:S(2)}, u32[]{:S(2)}) %collective-permute-start.19) | collective-permute-done | bytes 786464 | tf_op jit(solution)/shard_map/ppermute | solution.py:461
  566.3 12.6 %collective-permute-done.23 = bf16[192,2048]{1,0:T(8,128)(2,1)S(1)} collective-permute-done((bf16[192,2048]{1,0:T(8,128)(2,1)S(1)}, bf16[192,2048]{1,0:T(8,128)(2,1)S(1)}, u32[]{:S(2)}, u32[]{:S(2)}) %collective-permute-start.23) | collective-permute-done | bytes 786464 | tf_op jit(solution)/shard_map/ppermute | solution.py:461
  618.5 7.4 %collective-permute-done.44 = bf16[96,2048]{1,0:T(8,128)(2,1)S(1)} collective-permute-done((bf16[96,2048]{1,0:T(8,128)(2,1)S(1)}, bf16[96,2048]{1,0:T(8,128)(2,1)S(1)}, u32[]{:S(2)}, u32[]{:S(2)}) %collective-permute-start.44) | collective-permute-done | bytes 393248 | tf_op jit(solution)/shard_map/ppermute | solution.py:461
  (441 shorter events, 326.7 us)
Async XLA Ops:
  7.2 83.4 %all-gather.3.cloned.1.call-start = ((), (), s32[]{:S(2)}) async-start(), calls=%async_computation.8 | async-start | bytes 5242880 | tf_op jit(solution)/shard_map/all_gather | solution.py:549
  9.7 279.0 %reduce-scatter.5.cloned.1.call-start = ((), (), s32[]{:S(2)}) async-start(), calls=%async_computation.4 | async-start | bytes 7077888 | tf_op jit(solution)/shard_map/reduce_scatter | solution.py:618
  20.1 28.3 %collective-permute-start = (bf16[768,512]{1,0:T(8,128)(2,1)}, bf16[768,512]{1,0:T(8,128)(2,1)}, u32[]{:S(2)}, u32[]{:S(2)}) collective-permute-start(bf16[768,512]{1,0:T(8,128)(2,1)} %key_prep.1.kva_ref.kv_ref), channel_id=1, source_target_pairs={{0,8},{4,12},{8,16},{12,20},{16,24},{20,28},{1,9},{5,13},{9,17},{1... | collective-permute-start | bytes 2359304 | tf_op jit(solution)/shard_map/ppermute | solution.py:455
  26.2 25.4 %collective-permute-start.2 = (bf16[768,512]{1,0:T(8,128)(2,1)}, bf16[768,512]{1,0:T(8,128)(2,1)}, u32[]{:S(2)}, u32[]{:S(2)}) collective-permute-start(bf16[768,512]{1,0:T(8,128)(2,1)} %key_prep.1.kva_ref.kv_ref), channel_id=1, source_target_pairs={{0,4},{4,0},{8,12},{12,8},{16,20},{20,16},{24,28},{28,24},{1,5},{5... | collective-permute-start | bytes 2359304 | tf_op jit(solution)/shard_map/ppermute | solution.py:452
  48.4 20.4 %collective-permute-start.1 = (bf16[768,512]{1,0:T(8,128)(2,1)}, bf16[768,512]{1,0:T(8,128)(2,1)S(1)}, u32[]{:S(2)}, u32[]{:S(2)}) collective-permute-start(bf16[768,512]{1,0:T(8,128)(2,1)} %collective-permute-done.kva_ref.kv_ref), channel_id=1, source_target_pairs={{0,8},{4,12},{8,16},{12,20},{16,24},{20,28},{1,9},{5,13},{9,17},{1... | collective-permute-start | bytes 2359304 | tf_op jit(solution)/shard_map/ppermute | solution.py:455
  51.3 21.8 %collective-permute-start.4 = (bf16[768,512]{1,0:T(8,128)(2,1)}, bf16[768,512]{1,0:T(8,128)(2,1)S(1)}, u32[]{:S(2)}, u32[]{:S(2)}) collective-permute-start(bf16[768,512]{1,0:T(8,128)(2,1)} %collective-permute-done.kva_ref.kv_ref), channel_id=1, source_target_pairs={{0,4},{4,0},{8,12},{12,8},{16,20},{20,16},{24,28},{28,24},{1,5},{5... | collective-permute-start | bytes 2359304 | tf_op jit(solution)/shard_map/ppermute | solution.py:452
  68.8 20.9 %collective-permute-start.3 = (bf16[768,512]{1,0:T(8,128)(2,1)S(1)}, bf16[768,512]{1,0:T(8,128)(2,1)S(1)}, u32[]{:S(2)}, u32[]{:S(2)}) collective-permute-start(bf16[768,512]{1,0:T(8,128)(2,1)S(1)} %collective-permute-done.1.kva_ref.kv_ref), channel_id=1, source_target_pairs={{0,8},{4,12},{8,16},{12,20},{16,24},{20,28},{1,9},{5,13},{9,17},{1... | collective-permute-start | bytes 2359304 | tf_op jit(solution)/shard_map/ppermute | solution.py:455
  91.1 27.9 %collective-permute-start.5 = (bf16[768,512]{1,0:T(8,128)(2,1)}, bf16[768,512]{1,0:T(8,128)(2,1)S(1)}, u32[]{:S(2)}, u32[]{:S(2)}) collective-permute-start(bf16[768,512]{1,0:T(8,128)(2,1)} %copy-done.20), channel_id=1, source_target_pairs={{0,4},{4,0},{8,12},{12,8},{16,20},{20,16},{24,28},{28,24},{1,5},{5... | collective-permute-start | bytes 2359304 | tf_op jit(solution)/shard_map/ppermute | solution.py:452
  128.6 20.0 %collective-permute-start.8 = (bf16[768,512]{1,0:T(8,128)(2,1)}, bf16[768,512]{1,0:T(8,128)(2,1)}, u32[]{:S(2)}, u32[]{:S(2)}) collective-permute-start(bf16[768,512]{1,0:T(8,128)(2,1)} %get-tuple-element.141), channel_id=1, source_target_pairs={{0,1},{1,0},{2,3},{3,2},{4,5},{5,4},{6,7},{7,6},{8,9},{9,8},{10,11... | collective-permute-start | bytes 2359304 | tf_op jit(solution)/shard_map/ppermute | solution.py:461
  130.1 21.0 %collective-permute-start.9 = (bf16[768,512]{1,0:T(8,128)(2,1)}, bf16[768,512]{1,0:T(8,128)(2,1)}, u32[]{:S(2)}, u32[]{:S(2)}) collective-permute-start(bf16[768,512]{1,0:T(8,128)(2,1)} %get-tuple-element.141), channel_id=1, source_target_pairs={{0,2},{1,3},{2,0},{3,1},{4,6},{5,7},{6,4},{7,5},{8,10},{9,11},{10,... | collective-permute-start | bytes 2359304 | tf_op jit(solution)/shard_map/ppermute | solution.py:461
  204.5 317.0 %reduce-scatter.7.cloned.1.call-start = ((), (), s32[]{:S(2)}) async-start(), calls=%async_computation.5 | async-start | bytes 14155776 | tf_op jit(solution)/shard_map/reduce_scatter | solution.py:618
  288.7 344.2 %reduce-scatter.11.cloned.1.call-start = ((), (), s32[]{:S(2)}) async-start(), calls=%async_computation.7 | async-start | bytes 2359296 | tf_op jit(solution)/shard_map/reduce_scatter | solution.py:618
  300.9 48.0 %collective-permute-start.29 = (bf16[768,512]{1,0:T(8,128)(2,1)S(1)}, bf16[768,512]{1,0:T(8,128)(2,1)S(1)}, u32[]{:S(2)}, u32[]{:S(2)}) collective-permute-start(bf16[768,512]{1,0:T(8,128)(2,1)S(1)} %add_convert_fusion.4), channel_id=1, source_target_pairs={{8,0},{12,4},{16,8},{20,12},{24,16},{28,20},{9,1},{13,5},{17,9},{2... | collective-permute-start | bytes 2359304 | tf_op jit(solution)/shard_map/ppermute | solution.py:458
  302.2 50.9 %collective-permute-start.38 = (bf16[192,2048]{1,0:T(8,128)(2,1)S(1)}, bf16[192,2048]{1,0:T(8,128)(2,1)S(1)}, u32[]{:S(2)}, u32[]{:S(2)}) collective-permute-start(bf16[192,2048]{1,0:T(8,128)(2,1)S(1)} %copy-done.53), channel_id=1, source_target_pairs={{0,1},{1,0},{2,3},{3,2},{4,5},{5,4},{6,7},{7,6},{8,9},{9,8},{10,11... | collective-permute-start | bytes 2359304 | tf_op jit(solution)/shard_map/ppermute | solution.py:461
  303.7 50.9 %collective-permute-start.39 = (bf16[192,2048]{1,0:T(8,128)(2,1)S(1)}, bf16[192,2048]{1,0:T(8,128)(2,1)S(1)}, u32[]{:S(2)}, u32[]{:S(2)}) collective-permute-start(bf16[192,2048]{1,0:T(8,128)(2,1)S(1)} %copy-done.53), channel_id=1, source_target_pairs={{0,2},{1,3},{2,0},{3,1},{4,6},{5,7},{6,4},{7,5},{8,10},{9,11},{10,... | collective-permute-start | bytes 2359304 | tf_op jit(solution)/shard_map/ppermute | solution.py:461
  351.3 19.7 %collective-permute-start.30 = (bf16[768,512]{1,0:T(8,128)(2,1)S(1)}, bf16[768,512]{1,0:T(8,128)(2,1)S(1)}, u32[]{:S(2)}, u32[]{:S(2)}) collective-permute-start(bf16[768,512]{1,0:T(8,128)(2,1)S(1)} %get-tuple-element.170), channel_id=1, source_target_pairs={{0,4},{4,0},{8,12},{12,8},{16,20},{20,16},{24,28},{28,24},{1,5},{5... | collective-permute-start | bytes 2359304 | tf_op jit(solution)/shard_map/ppermute | solution.py:452
  351.4 54.1 %collective-permute-start.31 = (bf16[768,512]{1,0:T(8,128)(2,1)S(1)}, bf16[768,512]{1,0:T(8,128)(2,1)S(1)}, u32[]{:S(2)}, u32[]{:S(2)}) collective-permute-start(bf16[768,512]{1,0:T(8,128)(2,1)S(1)} %add_convert_fusion.3), channel_id=1, source_target_pairs={{8,0},{12,4},{16,8},{20,12},{24,16},{28,20},{9,1},{13,5},{17,9},{2... | collective-permute-start | bytes 2359304 | tf_op jit(solution)/shard_map/ppermute | solution.py:458
  421.3 22.2 %collective-permute-start.32 = (bf16[768,512]{1,0:T(8,128)(2,1)}, bf16[768,512]{1,0:T(8,128)(2,1)S(1)}, u32[]{:S(2)}, u32[]{:S(2)}) collective-permute-start(bf16[768,512]{1,0:T(8,128)(2,1)} %get-tuple-element.178), channel_id=1, source_target_pairs={{0,4},{4,0},{8,12},{12,8},{16,20},{20,16},{24,28},{28,24},{1,5},{5... | collective-permute-start | bytes 2359304 | tf_op jit(solution)/shard_map/ppermute | solution.py:452
  427.9 44.6 %collective-permute-start.33 = (bf16[768,512]{1,0:T(8,128)(2,1)}, bf16[768,512]{1,0:T(8,128)(2,1)}, u32[]{:S(2)}, u32[]{:S(2)}) collective-permute-start(bf16[768,512]{1,0:T(8,128)(2,1)} %add_convert_fusion.2), channel_id=1, source_target_pairs={{8,0},{12,4},{16,8},{20,12},{24,16},{28,20},{9,1},{13,5},{17,9},{2... | collective-permute-start | bytes 2359304 | tf_op jit(solution)/shard_map/ppermute | solution.py:458
  521.5 113.2 %reduce-scatter.9.cloned.1.call-start = ((), (), s32[]{:S(2)}) async-start(), calls=%async_computation.6 | async-start | bytes 4718592 | tf_op jit(solution)/shard_map/reduce_scatter | solution.py:618
  578.9 25.2 %collective-permute-start.25 = (bf16[96,2048]{1,0:T(8,128)(2,1)S(1)}, bf16[96,2048]{1,0:T(8,128)(2,1)S(1)}, u32[]{:S(2)}, u32[]{:S(2)}) collective-permute-start(bf16[96,2048]{1,0:T(8,128)(2,1)S(1)} %slice.169), channel_id=1, source_target_pairs={{0,2},{1,3},{2,0},{3,1},{4,6},{5,7},{6,4},{7,5},{8,10},{9,11},{10,... | collective-permute-start | bytes 1179656 | tf_op jit(solution)/shard_map/ppermute | solution.py:461
  581.7 22.4 %collective-permute-start.26 = (bf16[96,2048]{1,0:T(8,128)(2,1)S(1)}, bf16[96,2048]{1,0:T(8,128)(2,1)S(1)}, u32[]{:S(2)}, u32[]{:S(2)}) collective-permute-start(bf16[96,2048]{1,0:T(8,128)(2,1)S(1)} %slice.170), channel_id=1, source_target_pairs={{0,1},{1,0},{2,3},{3,2},{4,5},{5,4},{6,7},{7,6},{8,9},{9,8},{10,11... | collective-permute-start | bytes 1179656 | tf_op jit(solution)/shard_map/ppermute | solution.py:461
  594.6 20.3 %collective-permute-start.42 = (bf16[192,2048]{1,0:T(8,128)(2,1)S(1)}, bf16[192,2048]{1,0:T(8,128)(2,1)S(1)}, u32[]{:S(2)}, u32[]{:S(2)}) collective-permute-start(bf16[192,2048]{1,0:T(8,128)(2,1)S(1)} %get-tuple-element.239), channel_id=1, source_target_pairs={{0,1},{1,0},{2,3},{3,2},{4,5},{5,4},{6,7},{7,6},{8,9},{9,8},{10,11... | collective-permute-start | bytes 2359304 | tf_op jit(solution)/shard_map/ppermute | solution.py:461
  596.7 19.8 %collective-permute-start.43 = (bf16[192,2048]{1,0:T(8,128)(2,1)S(1)}, bf16[192,2048]{1,0:T(8,128)(2,1)S(1)}, u32[]{:S(2)}, u32[]{:S(2)}) collective-permute-start(bf16[192,2048]{1,0:T(8,128)(2,1)S(1)} %get-tuple-element.239), channel_id=1, source_target_pairs={{0,2},{1,3},{2,0},{3,1},{4,6},{5,7},{6,4},{7,5},{8,10},{9,11},{10,... | collective-permute-start | bytes 2359304 | tf_op jit(solution)/shard_map/ppermute | solution.py:461
  (125 other events, 1074.4 us)
Sparse Core Ops, SparseCore 0:
  10.5 55.3 all-gather.2
  204.7 84.0 reduce-scatter.4
  291.0 180.8 reduce-scatter.6
  521.7 33.5 reduce-scatter.10
  557.4 49.1 reduce-scatter.8

commit v3 on v2

--- a/solution.py
+++ b/solution.py
@@ -194,11 +194,15 @@
     return slice(i * KEY_CHUNK, (i + n) * KEY_CHUNK)
 
 
-def attend_kernel(
-    meta, q_ref, kva_ref, kvb_ref, bounds_ref, acc_in, sum_in, acc_ref, sum_ref, *, first
-):
+def attend_kernel(meta, q_ref, kva_ref, kvb_ref, bounds_ref, *refs, first, last):
     rows = q_ref.shape[0]
     key_rows = kva_ref.shape[0]
+    if last:
+        acc_in, sum_in, o_ref, q_out_ref, acc_ref, sum_ref = refs
+    elif first:
+        acc_ref, sum_ref = refs
+    else:
+        acc_in, sum_in, acc_ref, sum_ref = refs
     if first:
         acc_ref[...] = jnp.zeros_like(acc_ref)
         sum_ref[...] = jnp.zeros_like(sum_ref)
@@ -232,97 +236,123 @@
                 else:
                     work(kv_ref, lanes, chunk(c), slice(0, rows), False)
 
-
-def attend_stage(q, kv_a, kv_b, bounds, meta, acc, total):
+    if last:
+        total = sum_ref[...]
+        outcome = acc_ref[...] / total
+        acc_ref[...] = outcome
+        o_ref[...] = outcome.astype(bf16)
+        lanes = lane_index(rows)
+        extra = q_ref[:, HEAD_WIDTH:].astype(f32)
+        for i, part in enumerate(split_parts(jnp.log2(total))):
+            extra = jnp.where(lanes == LOG_LANE + i, -part.astype(f32), extra)
+        q_out_ref[:, :HEAD_WIDTH] = q_ref[:, :HEAD_WIDTH]
+        q_out_ref[:, HEAD_WIDTH:] = extra.astype(bf16)
+
+
+def attend_stage(q, kv_a, kv_b, bounds, meta, carried, last):
     rows = q.shape[0]
     key_rows = kv_a.shape[0]
     q_heads = q.shape[1] // (2 * HEAD_WIDTH)
     group = q.shape[1] // kv_a.shape[1]
     width = q_heads * HEAD_WIDTH
-    first = acc is None
-    if first:
-        acc = total = jnp.zeros((8, HEAD_WIDTH), f32)
+    first = not carried
     wide = 2 * HEAD_WIDTH
     per_q = pl.BlockSpec((rows, wide), lambda j, m: (0, j))
     per_kv = pl.BlockSpec((key_rows, wide), lambda j, m: (0, j // group))
     per_out = pl.BlockSpec((rows, HEAD_WIDTH), lambda j, m: (0, j))
-    carried = pl.BlockSpec((8, HEAD_WIDTH), lambda j, m: (0, 0)) if first else per_out
+    table = pl.BlockSpec((8, HEAD_WIDTH), lambda j, m: (0, 0))
+    running = jax.ShapeDtypeStruct((rows, width), f32)
+    if last:
+        out_specs = [per_out, per_q, per_out]
+        out_shape = [jax.ShapeDtypeStruct((rows, width), bf16), jax.ShapeDtypeStruct(q.shape, bf16), running]
+        scratch = [pltpu.VMEM((rows, HEAD_WIDTH), f32)]
+        aliases = {5: 2}
+    else:
+        out_specs = [per_out, per_out]
+        out_shape = [running, running]
+        scratch = []
+        aliases = {} if first else {5: 0, 6: 1}
     return pl.pallas_call(
-        functools.partial(attend_kernel, first=first),
+        functools.partial(attend_kernel, first=first, last=last),
         grid_spec=pltpu.PrefetchScalarGridSpec(
             num_scalar_prefetch=1,
             grid=(q_heads,),
-            in_specs=[
-                per_q,
-                per_kv,
-                per_kv,
-                pl.BlockSpec((8, HEAD_WIDTH), lambda j, m: (0, 0)),
-                carried,
-                carried,
-            ],
-            out_specs=[per_out, per_out],
+            in_specs=[per_q, per_kv, per_kv, table] + [per_out] * len(carried),
+            out_specs=out_specs,
+            scratch_shapes=scratch,
         ),
-        out_shape=[jax.ShapeDtypeStruct((rows, width), f32)] * 2,
-        input_output_aliases={} if first else {5: 0, 6: 1},
+        out_shape=out_shape,
+        input_output_aliases=aliases,
         compiler_params=pltpu.CompilerParams(vmem_limit_bytes=40 * MIB),
         cost_estimate=SMALL,
         name="attend_stage",
-    )(meta, q, kv_a, kv_b, bounds, acc, total)
-
-
-def finish_kernel(q_ref, acc_ref, sum_ref, o_ref, q_out_ref):
-    total = sum_ref[...]
-    o_ref[...] = (acc_ref[...] / total).astype(bf16)
-    rows = total.shape[0]
-    lanes = lane_index(rows)
-    extra = q_ref[:, HEAD_WIDTH:].astype(f32)
-    for i, part in enumerate(split_parts(jnp.log2(total))):
-        extra = jnp.where(lanes == LOG_LANE + i, -part.astype(f32), extra)
-    q_out_ref[:, :HEAD_WIDTH] = q_ref[:, :HEAD_WIDTH]
-    q_out_ref[:, HEAD_WIDTH:] = extra.astype(bf16)
-
-
-def finish(q, acc, total):
-    rows, width = acc.shape
-    narrow = pl.BlockSpec((rows, HEAD_WIDTH), lambda j: (0, j))
-    wide = pl.BlockSpec((rows, 2 * HEAD_WIDTH), lambda j: (0, j))
-    return pl.pallas_call(
-        finish_kernel,
-        grid=(width // HEAD_WIDTH,),
-        in_specs=[wide, narrow, narrow],
-        out_specs=[narrow, wide],
-        out_shape=[
-            jax.ShapeDtypeStruct((rows, width), bf16),
-            jax.ShapeDtypeStruct((rows, 2 * width), bf16),
-        ],
-        name="finish",
-    )(q, acc, total)
-
-
-def delta_kernel(do_ref, acc_ref, sum_ref, out_ref):
-    do = do_ref[...]
-    outcome = acc_ref[...] / sum_ref[...]
-    delta = jnp.sum(do.astype(f32) * outcome, axis=-1, keepdims=True)
-    rows = do.shape[0]
-    lanes = lane_index(rows)
-    extra = jnp.zeros((rows, HEAD_WIDTH), f32)
-    for i, part in enumerate(split_parts(delta)):
-        extra = jnp.where(lanes == i, -part.astype(f32), extra)
-    out_ref[:, :HEAD_WIDTH] = do
-    out_ref[:, HEAD_WIDTH:] = extra.astype(bf16)
-
-
-def with_delta(do, acc, total):
-    rows, width = acc.shape
-    narrow = pl.BlockSpec((rows, HEAD_WIDTH), lambda j: (0, j))
+    )(meta, q, kv_a, kv_b, bounds, *carried)
+
+
+def delta_kernel(owners, *refs):
+    *pieces, outcome_ref, out_ref = refs
+    for i, piece in enumerate(pieces):
+
+        @pl.when(pl.program_id(0) == i)
+        def _():
+            rows, width = piece.shape
+            lanes = lane_index(rows)
+            for j in range(width // HEAD_WIDTH):
+                head = slice(j * HEAD_WIDTH, (j + 1) * HEAD_WIDTH)
+                do = piece[:, head]
+                delta = jnp.sum(do.astype(f32) * outcome_ref[:, head], axis=-1, keepdims=True)
+                extra = jnp.zeros((rows, HEAD_WIDTH), f32)
+                for k, part in enumerate(split_parts(delta)):
+                    extra = jnp.where(lanes == k, -part.astype(f32), extra)
+                start = 2 * j * HEAD_WIDTH
+                out_ref[:, start : start + HEAD_WIDTH] = do
+                out_ref[:, start + HEAD_WIDTH : start + 2 * HEAD_WIDTH] = extra.astype(bf16)
+
+
+def with_delta(pieces, outcome):
+    owners = jnp.stack([jnp.asarray(owner, jnp.int32) for unused, owner in pieces])
+    rows, width = outcome.shape
+    share = rows // len(pieces)
+    whole = pl.BlockSpec((share, width), lambda i, m: (0, 0))
     return pl.pallas_call(
         delta_kernel,
-        grid=(width // HEAD_WIDTH,),
-        in_specs=[narrow, narrow, narrow],
-        out_specs=pl.BlockSpec((rows, 2 * HEAD_WIDTH), lambda j: (0, j)),
+        grid_spec=pltpu.PrefetchScalarGridSpec(
+            num_scalar_prefetch=1,
+            grid=(len(pieces),),
+            in_specs=[whole] * len(pieces) + [pl.BlockSpec((share, width), lambda i, m: (m[i], 0))],
+            out_specs=pl.BlockSpec((share, 2 * width), lambda i, m: (m[i], 0)),
+        ),
         out_shape=jax.ShapeDtypeStruct((rows, 2 * width), bf16),
+        cost_estimate=SMALL,
         name="with_delta",
-    )(do, acc, total)
+    )(owners, *[piece for piece, unused in pieces], outcome)
+
+
+def assemble_kernel(owners, *refs):
+    *pieces, out_ref = refs
+    for i, piece in enumerate(pieces):
+
+        @pl.when(pl.program_id(0) == i)
+        def _():
+            out_ref[...] = piece[...].astype(out_ref.dtype)
+
+
+def assemble(pieces, kind):
+    owners = jnp.stack([jnp.asarray(owner, jnp.int32) for unused, owner in pieces])
+    share, width = pieces[0][0].shape
+    return pl.pallas_call(
+        assemble_kernel,
+        grid_spec=pltpu.PrefetchScalarGridSpec(
+            num_scalar_prefetch=1,
+            grid=(len(pieces),),
+            in_specs=[pl.BlockSpec((share, width), lambda i, m: (0, 0))] * len(pieces),
+            out_specs=pl.BlockSpec((share, width), lambda i, m: (m[i], 0)),
+        ),
+        out_shape=jax.ShapeDtypeStruct((share * len(pieces), width), kind),
+        compiler_params=pltpu.CompilerParams(vmem_limit_bytes=40 * MIB),
+        cost_estimate=SMALL,
+        name="assemble",
+    )(owners, *[piece for piece, unused in pieces])
 
 
 def attend_back_kernel(
@@ -435,6 +465,88 @@
     )(meta, q, do, kv, bounds, dq)
 
 
+def project_kernel(meta, base_ref, *refs, count, final):
+    pieces, mine, other = refs[:count], refs[count : 2 * count], refs[2 * count : 3 * count]
+    if final:
+        gain_ref, out_ref, normed_ref = refs[3 * count :]
+    else:
+        (out_ref,) = refs[3 * count :]
+    first_core = meta[0] == 0
+    total = base_ref[...].astype(f32)
+    for piece, mine_ref, other_ref in zip(pieces, mine, other):
+        half = piece.shape[1] // 2
+        low, high = piece[:, :half], piece[:, half:]
+        total += dot(jnp.where(first_core, low, high), mine_ref[0])
+        total += dot(jnp.where(first_core, high, low), other_ref[0])
+    out_ref[...] = total
+    if final:
+        inverse = lax.rsqrt(jnp.mean(total * total, axis=-1, keepdims=True) + EPSILON)
+        normed_ref[...] = (total * inverse * gain_ref[...]).astype(bf16)
+
+
+def project(base, pieces, w_mine, w_other, core, gain=None):
+    meta = jnp.stack([jnp.asarray(v, jnp.int32) for v in [core] + [owner for unused, owner in pieces]])
+    rows, width = base.shape
+    count = len(pieces)
+    final = gain is not None
+    step = rows // 3 if rows % 768 == 0 else rows
+    half = w_mine.shape[1]
+    per_row = pl.BlockSpec((step, width), lambda i, m: (i, 0))
+    per_piece = pl.BlockSpec((step, 2 * half), lambda i, m: (i, 0))
+    weights = [
+        pl.BlockSpec((1, half, width), lambda i, m, k=k: (m[1 + k], 0, 0)) for k in range(count)
+    ]
+    in_specs = [per_row] + [per_piece] * count + weights + weights
+    args = [base] + [piece for piece, unused in pieces] + [w_mine] * count + [w_other] * count
+    out_shape = [jax.ShapeDtypeStruct((rows, width), f32)]
+    if final:
+        in_specs.append(pl.BlockSpec((1, width), lambda i, m: (0, 0)))
+        args.append(gain[None, :])
+        out_shape.append(jax.ShapeDtypeStruct((rows, width), bf16))
+    return pl.pallas_call(
+        functools.partial(project_kernel, count=count, final=final),
+        grid_spec=pltpu.PrefetchScalarGridSpec(
+            num_scalar_prefetch=1,
+            grid=(rows // step,),
+            in_specs=in_specs,
+            out_specs=[per_row] * len(out_shape),
+        ),
+        out_shape=out_shape,
+        compiler_params=pltpu.CompilerParams(vmem_limit_bytes=48 * MIB),
+        cost_estimate=SMALL,
+        name="project",
+    )(meta, *args)
+
+
+def project_back_kernel(meta, branch_ref, mine_ref, other_ref, out_ref):
+    half = mine_ref.shape[1]
+    mine = dot_nt(branch_ref[...], mine_ref[0])
+    other = dot_nt(branch_ref[...], other_ref[0])
+    first_core = meta[0] == 0
+    out_ref[0, :, :half] = jnp.where(first_core, mine, other).astype(bf16)
+    out_ref[0, :, half:] = jnp.where(first_core, other, mine).astype(bf16)
+
+
+def project_back(branch, w_mine, w_other, core):
+    meta = jnp.asarray(core, jnp.int32)[None]
+    rows, width = branch.shape
+    n_head, half, unused = w_mine.shape
+    weight = pl.BlockSpec((1, half, width), lambda i, m: (i, 0, 0))
+    return pl.pallas_call(
+        project_back_kernel,
+        grid_spec=pltpu.PrefetchScalarGridSpec(
+            num_scalar_prefetch=1,
+            grid=(n_head,),
+            in_specs=[pl.BlockSpec((rows, width), lambda i, m: (0, 0)), weight, weight],
+            out_specs=pl.BlockSpec((1, rows, 2 * half), lambda i, m: (i, 0, 0)),
+        ),
+        out_shape=jax.ShapeDtypeStruct((n_head, rows, 2 * half), bf16),
+        compiler_params=pltpu.CompilerParams(vmem_limit_bytes=40 * MIB),
+        cost_estimate=SMALL,
+        name="project_back",
+    )(meta, branch, w_mine, w_other)
+
+
 def after(values):
     return lax.optimization_barrier(values)
 
@@ -460,67 +572,67 @@
     def across(value, bits):
         return lax.ppermute(value, "head", [(i, i ^ bits) for i in range(n_head)])
 
-    def gather_head(value):
+    def gather_steps(value):
         me = lax.axis_index("head")
         if n_head != 4:
-            every = lax.all_gather(value, "head", axis=0)
+            every = yield lax.all_gather(value, "head", axis=0)
             return [(every[i], i) for i in range(n_head)]
         half = value.shape[0] // 2
-        by_x = across(value, 1)
-        by_y = across(value, 2)
-        low = across(by_x[:half], 2)
-        high = across(by_y[half:], 1)
+        by_x, by_y = yield across(value, 1), across(value, 2)
+        low, high = yield across(by_x[:half], 2), across(by_y[half:], 1)
         far = jnp.concatenate([low, high], axis=0)
         return [(value, me), (by_x, me ^ 1), (by_y, me ^ 2), (far, me ^ 3)]
 
-    def scatter_head(value, *beside):
+    def scatter_steps(value):
         rows, width = value.shape
         if n_head != 4:
-            total = lax.psum_scatter(value, "head", scatter_dimension=0, tiled=True).astype(f32)
-            return total, [work() for work in beside]
+            total = yield lax.psum_scatter(value, "head", scatter_dimension=0, tiled=True)
+            return total.astype(f32)
         me = lax.axis_index("head")
         x, y = me & 1, me >> 1
         part = value.reshape(2, 2, 2, rows // 8, width)
         first, second = part[:, :, 0], part[:, :, 1]
         first_x = jnp.swapaxes(first, 0, 1)
-        got_first = across(pick(first_x, 1 - x), 1)
-        got_second = across(pick(second, 1 - y), 2)
-        made = []
-        if beside:
-            got_first, got_second, made_first = after((got_first, got_second, beside[0]()))
-            made.append(made_first)
+        got_first, got_second = yield (
+            across(pick(first_x, 1 - x), 1),
+            across(pick(second, 1 - y), 2),
+        )
         sum_first = pick(first_x, x).astype(f32) + got_first.astype(f32)
         sum_second = pick(second, y).astype(f32) + got_second.astype(f32)
-        last_first = across(pick(sum_first, 1 - y).astype(bf16), 2)
-        last_second = across(pick(sum_second, 1 - x).astype(bf16), 1)
-        if beside:
-            last_first, last_second, made_second = after((last_first, last_second, beside[1]()))
-            made.append(made_second)
-        total = jnp.concatenate(
+        last_first, last_second = yield (
+            across(pick(sum_first, 1 - y).astype(bf16), 2),
+            across(pick(sum_second, 1 - x).astype(bf16), 1),
+        )
+        return jnp.concatenate(
             [
                 pick(sum_first, y) + last_first.astype(f32),
                 pick(sum_second, x) + last_second.astype(f32),
             ],
             axis=0,
         )
-        return total, made
-
-    def in_order(pieces):
-        rows = pieces[0][0].shape[0]
-        out = jnp.zeros((rows * len(pieces),) + pieces[0][0].shape[1:], pieces[0][0].dtype)
-        for piece, owner in pieces:
-            out = lax.dynamic_update_slice_in_dim(out, piece, owner * rows, 0)
-        return out
+
+    def run_steps(steps, works=()):
+        works = list(works)
+        made = []
+        arrived = next(steps)
+        while True:
+            if works:
+                arrived, done = after((arrived, works.pop(0)()))
+                made.append(done)
+            try:
+                arrived = steps.send(arrived)
+            except StopIteration as stop:
+                return stop.value, made + [work() for work in works]
 
     def exchange_head(value):
         me = lax.axis_index("head")
         if n_head != 4:
             got = lax.all_to_all(value, "head", 0, 0)
-            return got.reshape(-1, value.shape[-1])
+            return [(got[i], i) for i in range(n_head)]
         pieces = [(pick(value, me), me)]
         for bits in (3, 1, 2):
             pieces.append((across(pick(value, me ^ bits), bits), me ^ bits))
-        return in_order(pieces)
+        return pieces
 
     def body(
         tokens,
@@ -544,10 +656,6 @@
         head_index = lax.axis_index("head")
         chip, core = seq_index // 2, seq_index % 2
 
-        half_rows = w_output.shape[0] // 2
-        w_half = lax.dynamic_slice_in_dim(w_output, core * half_rows, half_rows, 0)
-        w_mine = lax.all_gather(w_half, "head", axis=0)
-
         index = seq_index * rows + jnp.arange(rows, dtype=jnp.int32)
         begin = locate(index, lengths)
         cosine, sine = rotary(index - begin)
@@ -572,40 +680,57 @@
         current = key_prep(key_raw, value_raw, key_gain, cosine, sine)
         sibling = swap_core(current)
         following = to_next(current)
+
+        half_rows = w_output.shape[0] // 2
+        w_half = lax.dynamic_slice_in_dim(w_output, core * half_rows, half_rows, 0)
+        w_half, current = after((w_half, current))
+        w_mine = lax.all_gather(w_half, "head", axis=0)
+
         query_raw = dot(first_in, w_query)
         q_wide = query_prep(metas[0], query_raw, query_gain, cosine, sine, bounds)
         d_mixed = dot_nt(cotangent, w_down)
         following, q_wide, d_mixed = after((following, q_wide, d_mixed))
 
         blocks = []
-        acc = total = None
+        carried = ()
         for stage in range(n_chip):
             blocks.append((current, sibling))
             if stage + 1 < n_chip:
                 current = following
                 sibling = swap_core(current)
                 following = to_next(current) if stage + 2 < n_chip else None
-            acc, total = attend_stage(q_wide, *blocks[stage], bounds, metas[stage], acc, total)
+            if stage == n_chip - 1:
+                w_mine, carried = after((w_mine, carried))
+                w_other = swap_core(w_mine)
+            carried = attend_stage(
+                q_wide, *blocks[stage], bounds, metas[stage], carried, stage == n_chip - 1
+            )
             if following is not None:
-                following, acc, total = after((following, acc, total))
-            if stage == 1:
-                w_mine, acc = after((w_mine, acc))
-                w_other = swap_core(w_mine)
-                w_full = jnp.where(
-                    core == 0,
-                    jnp.concatenate([w_mine, w_other], axis=1),
-                    jnp.concatenate([w_other, w_mine], axis=1),
-                )
-            if stage == n_chip - 2:
-                w_full, acc = after((w_full, acc))
-        o_low, q_back = finish(q_wide, acc, total)
-
-        hidden = xf
-        for piece, owner in gather_head(o_low):
-            hidden = hidden + dot(piece, pick(w_full, owner))
-
-        inverse2 = lax.rsqrt(jnp.mean(hidden * hidden, axis=-1, keepdims=True) + EPSILON)
-        second_in = (hidden * inverse2 * norm2_gain).astype(bf16)
+                following, carried = after((following, carried))
+        o_low, q_back, outcome = carried
+
+        steps = gather_steps(o_low)
+        arrived = next(steps)
+        if n_head == 4:
+            me = lax.axis_index("head")
+            (hidden,) = project(tokens, [(o_low, me)], w_mine, w_other, core)
+            arrived, hidden = after((arrived, hidden))
+            far = steps.send(arrived)
+            (hidden,) = project(
+                hidden, [(arrived[0], me ^ 1), (arrived[1], me ^ 2)], w_mine, w_other, core
+            )
+            far, hidden = after((far, hidden))
+            try:
+                steps.send(far)
+            except StopIteration as stop:
+                last_pieces = stop.value[3:]
+        else:
+            hidden = tokens
+            try:
+                steps.send(arrived)
+            except StopIteration as stop:
+                last_pieces = stop.value
+        hidden, second_in = project(hidden, last_pieces, w_mine, w_other, core, norm2_gain)
         gate_raw = dot(second_in, w_gate)
         up_raw = dot(second_in, w_up)
         sigmoid = jax.nn.sigmoid(gate_raw)
@@ -622,10 +747,12 @@
         grad_down = scatter_seq(down_sum, 1)
         second_part = (dot_nt(gate_low, w_gate) + dot_nt(up_low, w_up)).astype(bf16)
 
-        second_grad, (gate_sum, up_sum) = scatter_head(
-            second_part,
-            lambda: dot_tn(second_in, gate_low).astype(bf16),
-            lambda: dot_tn(second_in, up_low).astype(bf16),
+        second_grad, (gate_sum, up_sum) = run_steps(
+            scatter_steps(second_part),
+            (
+                lambda: dot_tn(second_in, gate_low).astype(bf16),
+                lambda: dot_tn(second_in, up_low).astype(bf16),
+            ),
         )
         gate_up_sum = jnp.concatenate([gate_sum, up_sum], axis=1)
         my_hidden = lax.dynamic_slice_in_dim(hidden, head_index * share, share, 0)
@@ -638,26 +765,56 @@
             scaled - my_hat * jnp.mean(scaled * my_hat, axis=-1, keepdims=True)
         )
         my_branch = hidden_grad.astype(bf16)
-        do_rows = dot_nt(my_branch, w_full.reshape(-1, w_full.shape[-1])).astype(bf16)
-        do_pieces = jnp.stack(jnp.split(do_rows, n_head, axis=1))
-        do_low = exchange_head(do_pieces)
-
-        do_wide = with_delta(do_low, acc, total)
+        do_pieces = exchange_head(project_back(my_branch, w_mine, w_other, core))
+        do_wide = with_delta(do_pieces, outcome)
         grad_down, gate_up_sum, do_wide = after((grad_down, gate_up_sum, do_wide))
         grad_gate_up = scatter_seq(gate_up_sum, 0)
 
+        def side_work(mixed_low, my_branch):
+            branch_steps = gather_steps(my_branch)
+            got = yield next(branch_steps)
+            mixed_steps = scatter_steps(dot(mixed_low, w_down).astype(bf16))
+            got_branch, got = yield branch_steps.send(got) if n_head == 4 else got, next(mixed_steps)
+            try:
+                branch_steps.send(got_branch)
+            except StopIteration as stop:
+                branch = assemble(stop.value, bf16)
+            output_sum = dot_tn(o_low, branch).astype(bf16)
+            if n_head == 4:
+                got = yield mixed_steps.send(got)
+            try:
+                mixed_steps.send(got)
+            except StopIteration as stop:
+                my_mixed = (my_hidden + stop.value).astype(bf16)
+            mixed_steps = gather_steps(my_mixed)
+            got = yield next(mixed_steps)
+            if n_head == 4:
+                got = yield mixed_steps.send(got)
+            try:
+                mixed_steps.send(got)
+            except StopIteration as stop:
+                mixed = assemble(stop.value, bf16)
+            return mixed, output_sum
+
         mixed_late, my_branch, do_wide = after((mixed_low, my_branch, do_wide))
-        mixed_sum, unused = scatter_head(dot(mixed_late, w_down).astype(bf16))
-        mixed = in_order(gather_head((my_hidden + mixed_sum).astype(bf16)))
-        branch = in_order(gather_head(my_branch))
+        side = side_work(mixed_late, my_branch)
+        waiting = next(side)
+        side_made = None
 
         dq = None
         arrived = None
+        kernels = 0
         for stage in reversed(range(n_chip)):
             kv_a, kv_b = blocks[stage]
             meta = metas[stage]
             dq, dkv_b = attend_back(q_back, do_wide, kv_b, bounds, meta, dq, 1, False, bf16)
             theirs = swap_core(dkv_b)
+            if stage != n_chip - 1 and side_made is None:
+                try:
+                    waiting, dq = after((waiting, dq))
+                    waiting = side.send(waiting)
+                except StopIteration as stop:
+                    side_made = stop.value
             dq, dkv_a = attend_back(q_back, do_wide, kv_a, bounds, meta, dq, 0, stage == 0, f32)
             dkv = dkv_a + theirs.astype(f32)
             if arrived is not None:
@@ -665,6 +822,15 @@
             if stage > 0:
                 sent, dq = after((dkv.astype(bf16), dq))
                 arrived = to_previous(sent)
+            if side_made is None:
+                try:
+                    waiting, dq = after((waiting, dq))
+                    waiting = side.send(waiting)
+                except StopIteration as stop:
+                    side_made = stop.value
+        mixed, output_sum = side_made
+        grad_gate_up, output_sum, dkv = after((grad_gate_up, output_sum, dkv))
+        grad_output = scatter_seq(output_sum, 1)
         query_grad, grad_qgain = head_back(
             query_raw, dq, query_gain, cosine, sine, SCORE_SCALE, 1
         )
@@ -684,36 +850,37 @@
             + dot_nt(key_grad, key_matrix)
             + dot_nt(value_grad, value_matrix)
         ).astype(bf16)
-        first_grad, (attn_sum, output_sum) = scatter_head(
-            first_part,
-            lambda: jnp.concatenate(
-                [
-                    dot_tn(first_in, query_grad).astype(bf16),
-                    dot_tn(first_in, key_grad).astype(bf16),
-                    dot_tn(first_in, value_grad).astype(bf16),
-                ],
-                axis=1,
+        hat1 = xf * inverse1
+        grad_norm1 = jnp.sum(first_part.astype(f32) * hat1, axis=0)
+        gains = jnp.concatenate([grad_norm1, grad_norm2, grad_qgain[0], grad_kgain[0]])
+        gains = gains.reshape(-1, HEAD_WIDTH)
+        first_grad, (attn_sum,) = run_steps(
+            scatter_steps(first_part),
+            (
+                lambda: jnp.concatenate(
+                    [
+                        dot_tn(first_in, query_grad).astype(bf16),
+                        dot_tn(first_in, key_grad).astype(bf16),
+                        dot_tn(first_in, value_grad).astype(bf16),
+                    ],
+                    axis=1,
+                ),
             ),
-            lambda: dot_tn(o_low, branch).astype(bf16),
         )
-        grad_gate_up, attn_sum, output_sum = after((grad_gate_up, attn_sum, output_sum))
         grad_attn = scatter_seq(attn_sum, 0)
-        grad_output = scatter_seq(output_sum, 1)
         widths = (query_grad.shape[1], query_grad.shape[1] + key_grad.shape[1])
         grad_query, grad_key, grad_value = jnp.split(grad_attn, widths, axis=1)
 
         my_x = lax.dynamic_slice_in_dim(tokens, head_index * share, share, 0).astype(f32)
         my_inverse1 = lax.rsqrt(jnp.mean(my_x * my_x, axis=-1, keepdims=True) + EPSILON)
         my_hat1 = my_x * my_inverse1
-        grad_norm1 = jnp.sum(first_grad * my_hat1, axis=0)
         scaled1 = first_grad * norm1_gain
         my_tokens_grad = hidden_grad + my_inverse1 * (
             scaled1 - my_hat1 * jnp.mean(scaled1 * my_hat1, axis=-1, keepdims=True)
         )
-        grad_tokens = in_order(gather_head(my_tokens_grad.astype(bf16))).astype(f32)
-
-        gains = jnp.concatenate([grad_norm1, grad_norm2, grad_qgain[0], grad_kgain[0]])
-        gains = gains.reshape(-1, HEAD_WIDTH)
+        tokens_pieces, unused = run_steps(gather_steps(my_tokens_grad.astype(bf16)))
+        grad_tokens = assemble(tokens_pieces, f32)
+
         for axis, size in (("head", n_head), ("seq", n_seq)):
             bit = 1
             while bit < size:

time: 655 us -> 601 us (0.918)
  waiting for transfers between devices: 258 us -> 197 us
  Pallas kernels: 67.9 us -> 97.9 us
  matrix products: 125 us -> 115 us
    ppermute x3, waiting for transfers between devices: 105 us -> 49.4 us  [to_previous(): return lax.ppermute(value, 'seq', [(i + 2, i) for i in range(n_seq - 2)])]
    pallas_call x6 -> x12, Pallas kernels: 24.4 us -> 56.4 us  [the longest x3 24.4 us: project(): pl.pallas_call(functools.partial(project_kernel, count=count, final=final...]
    ppermute x31, waiting for transfers between devices: 101 us -> 78.4 us  [across(): return lax.ppermute(value, 'head', [(i, i ^ bits) for i in range(n_head)])]
    reduce_scatter x4, waiting for transfers between devices: 8.26 us -> 19.6 us  [scatter_seq(): lax.psum_scatter(value, 'seq', scatter_dimension=dimension, tiled=True)]
    select_n x1 -> x0, other arithmetic: 9.68 us -> none  [body(): jnp.where(core == 0, jnp.concatenate([w_mine, w_other], axis=1), jnp.conc...]
    dot_general x10 -> x6, matrix products: 57 us -> 47.4 us  [dot(): return jnp.dot(left, right, preferred_element_type=f32)]
    dynamic_update_slice x11 -> x0, local copies, waits for them, and re-layouts: 6.97 us -> none  [in_order(): out = lax.dynamic_update_slice_in_dim(out, piece, owner * rows, 0)]
    unnamed x190 -> x186, local copies, waits for them, and re-layouts: 30.5 us -> 35.1 us
  transfers between devices with their start and end apart: 56 -> 56, of which waited for: 28 -> 26; matrix products, arithmetic and copies ran while one was open for 25% -> 20% of each run, Pallas kernels for 9% -> 15%
where the time goes in v3:
time: 601 us; the launch traced here: 591 us
  waiting for transfers between devices  197 us (33%)
  matrix products  115 us (19%)
  Pallas kernels  97.9 us (16%)
  starting transfers between devices  67.4 us (11%)
  other arithmetic  52 us (9%)
  local copies, waits for them, and re-layouts  44.8 us (7%)
  between operations  15.8 us (3%)
    ppermute x31, waiting for transfers between devices, across(): return lax.ppermute(value, 'head', [(i, i ^ bits) for i in range(n_head)])  78.4 us
    ppermute x3, waiting for transfers between devices, to_previous(): return lax.ppermute(value, 'seq', [(i + 2, i) for i in range(n_seq - 2)])  49.4 us
    dot_general x6, matrix products, dot(): return jnp.dot(left, right, preferred_element_type=f32)  47.4 us
    dot_general x6, matrix products, dot_nt(): return lax.dot_general(left, right, NT, preferred_element_type=f32)  36 us
    unnamed x186, local copies, waits for them, and re-layouts  35.1 us
    ppermute x31, starting transfers between devices, across(): return lax.ppermute(value, 'head', [(i, i ^ bits) for i in range(n_head)])  34.6 us
    dot_general x7, matrix products, dot_tn(): return lax.dot_general(left, right, TN, preferred_element_type=f32)  31.8 us
    pallas_call x8, Pallas kernels, attend_back(): pl.pallas_call(functools.partial(attend_back_kernel, first=first, group=g...  25.1 us
  transfers between devices with their start and end apart: 56, of which 26 were waited for; matrix products, arithmetic and copies ran while one was open for 20% of the time, Pallas kernels for 15%

profile of v3, /device:TPU:0, one launch (start us, length us, event | category | flops | bytes accessed | tf_op | source)
XLA Modules:
  0.0 590.6 jit_solution(12444076278225563016)
XLA Ops:
  43.5 9.7 %fusion.39 = f32[768,1536]{1,0:T(8,128)} fusion(bf16[768,2048]{1,0:T(8,128)(2,1)} %param.33, bf16[1536,2048]{1,0:T(8,128)(2,1)} %param.32), kind=kOutput, calls=%fused_computation.134 | convolution fusion | flops 4831838208 | bytes 14155776 | tf_op jit(solution)/shard_map/dot_general | solution.py:34
  60.8 12.3 %collective-permute-done.1.kva_ref.kv_ref = bf16[768,512]{1,0:T(8,128)(2,1)S(1)} collective-permute-done((bf16[768,512]{1,0:T(8,128)(2,1)}, bf16[768,512]{1,0:T(8,128)(2,1)S(1)}, u32[]{:S(2)}, u32[]{:S(2)}) %collective-permute-start.1) | collective-permute-done | bytes 786464 | tf_op jit(solution)/shard_map/ppermute | solution.py:567
  81.1 12.8 %collective-permute-done.3.kva_ref.kv_ref = bf16[768,512]{1,0:T(8,128)(2,1)S(1)} collective-permute-done((bf16[768,512]{1,0:T(8,128)(2,1)S(1)}, bf16[768,512]{1,0:T(8,128)(2,1)S(1)}, u32[]{:S(2)}, u32[]{:S(2)}) %collective-permute-start.3) | collective-permute-done | bytes 786464 | tf_op jit(solution)/shard_map/ppermute | solution.py:567
  100.5 7.4 %collective-permute-done.5.kvb_ref.kv_ref = bf16[768,512]{1,0:T(8,128)(2,1)S(1)} collective-permute-done((bf16[768,512]{1,0:T(8,128)(2,1)S(1)}, bf16[768,512]{1,0:T(8,128)(2,1)S(1)}, u32[]{:S(2)}, u32[]{:S(2)}) %collective-permute-start.5) | collective-permute-done | bytes 786464 | tf_op jit(solution)/shard_map/ppermute | solution.py:564
  129.7 8.8 %collective-permute-done.8.refs_1_ = bf16[768,512]{1,0:T(8,128)(2,1)S(1)} collective-permute-done((bf16[768,512]{1,0:T(8,128)(2,1)}, bf16[768,512]{1,0:T(8,128)(2,1)S(1)}, u32[]{:S(2)}, u32[]{:S(2)}) %collective-permute-start.8) | collective-permute-done | bytes 786464 | tf_op jit(solution)/shard_map/ppermute | solution.py:573
  146.0 9.5 %project.4.base_ref = f32[768,2048]{1,0:T(8,128)} custom-call(s32[3]{0:T(128)S(1)} %pad_add_fusion.8.meta, f32[768,2048]{1,0:T(8,128)} %project.3.base_ref, bf16[768,512]{1,0:T(8,128)(2,1)} %collective-permute-done.7.refs_0_, bf16[768,512]{1,0:T(8,128)(2,1)S(1)} %collective-permute-done.8.refs_1_, bf16[4,256,2048]{2,1,0:T(8,128)(2,1)S(1)} %bitcast.164, ...), custom_call_target="tpu_custom_call" | custom-call | flops 1 | bytes 1 | tf_op jit(solution)/shard_map/project/pallas_call | solution.py:506
  156.6 8.6 %project.5 = (f32[768,2048]{1,0:T(8,128)}, bf16[768,2048]{1,0:T(8,128)(2,1)S(1)}) custom-call(s32[2]{0:T(128)S(1)} %pad_add_fusion.1.meta, f32[768,2048]{1,0:T(8,128)} %project.4.base_ref, bf16[768,512]{1,0:T(8,128)(2,1)S(1)} %pad_maximum_fusion.3.refs_0_, bf16[4,256,2048]{2,1,0:T(8,128)(2,1)} %bitcast.163, ...), custom_call_target="tpu_custom_call" | custom-call | flops 1 | bytes 1 | tf_op jit(solution)/shard_map/project/pallas_call | solution.py:506
  165.3 8.3 %fusion.41 = f32[768,1536]{1,0:T(8,128)S(1)} fusion(bf16[768,2048]{1,0:T(8,128)(2,1)S(1)} %get-tuple-element.171, bf16[2048,1536]{1,0:T(8,128)(2,1)} %param.31), kind=kOutput, calls=%fused_computation.136 | convolution fusion | flops 4831838208 | bytes 14155776 | tf_op jit(solution)/shard_map/dot_general | solution.py:30
  173.6 19.5 %fusion.40 = f32[768,1536]{1,0:T(8,128)S(1)} fusion(bf16[768,2048]{1,0:T(8,128)(2,1)S(1)} %get-tuple-element.171, bf16[2048,1536]{1,0:T(8,128)(2,1)} %param.30), kind=kOutput, calls=%fused_computation.135 | convolution fusion | flops 4831838208 | bytes 14155776 | tf_op jit(solution)/shard_map/dot_general | solution.py:30
  207.3 8.0 %fusion.42 = f32[768,2048]{1,0:T(8,128)S(1)} fusion(bf16[768,1536]{1,0:T(8,128)(2,1)} %get-tuple-element.173, bf16[2048,1536]{1,0:T(8,128)(2,1)} %param.30), kind=kOutput, calls=%fused_computation.137 | convolution fusion | flops 4831838208 | bytes 14942208 | tf_op jit(solution)/shard_map/dot_general | solution.py:34
  215.3 8.1 %add_convert_fusion.1 = bf16[768,2048]{1,0:T(8,128)(2,1)S(1)} fusion(f32[768,2048]{1,0:T(8,128)S(1)} %fusion.42, bf16[768,1536]{1,0:T(8,128)(2,1)S(1)} %copy-done.60, bf16[2048,1536]{1,0:T(8,128)(2,1)} %param.31), kind=kOutput, calls=%fused_computation.12 | convolution fusion | flops 4834983936 | bytes 18087936 | tf_op jit(solution)/shard_map/dot_general | solution.py:34
  231.6 10.5 %collective-permute-done.12 = bf16[2,96,2048]{2,1,0:T(8,128)(2,1)S(1)} collective-permute-done((bf16[2,96,2048]{2,1,0:T(8,128)(2,1)S(1)}, bf16[2,96,2048]{2,1,0:T(8,128)(2,1)S(1)}, u32[]{:S(2)}, u32[]{:S(2)}) %collective-permute-start.12) | collective-permute-done | bytes 786464 | tf_op jit(solution)/shard_map/ppermute | solution.py:573
  266.5 8.4 %pad_maximum_fusion = bf16[2048,3072]{1,0:T(8,128)(2,1)} fusion(bf16[2048,1536]{1,0:T(8,128)(2,1)} %convolution_convert_fusion, bf16[2048,1536]{1,0:T(8,128)(2,1)S(1)} %convolution_convert_fusion.1), kind=kLoop, calls=%fused_computation | loop fusion | flops 25165824 | bytes 25165824 | tf_op jit(solution)/shard_map/concatenate | solution.py:757
  281.2 10.8 %reduce-scatter.5.cloned.1.call-done = bf16[1536,256]{1,0:T(8,128)(2,1)} async-done(((bf16[1536,2048]{1,0:T(8,128)(2,1)}), bf16[1536,256]{1,0:T(8,128)(2,1)}) %reduce-scatter.5.cloned.1.call-update) | async-done | bytes 786448 | tf_op jit(solution)/shard_map/reduce_scatter | solution.py:743
  301.0 9.2 %convolution_convert_fusion.3 = bf16[768,2048]{1,0:T(8,128)(2,1)S(1)} fusion(bf16[768,1536]{1,0:T(8,128)(2,1)S(1)} %copy-done.59, bf16[1536,2048]{1,0:T(8,128)(2,1)} %param.32), kind=kOutput, calls=%fused_computation.19 | convolution fusion | flops 4833411072 | bytes 11796480 | tf_op jit(solution)/shard_map/dot_general | solution.py:30
  319.6 11.5 %collective-permute-done.24 = bf16[2,96,2048]{2,1,0:T(8,128)(2,1)S(1)} collective-permute-done((bf16[2,96,2048]{2,1,0:T(8,128)(2,1)S(1)}, bf16[2,96,2048]{2,1,0:T(8,128)(2,1)S(1)}, u32[]{:S(2)}, u32[]{:S(2)}) %collective-permute-start.24) | collective-permute-done | bytes 786464 | tf_op jit(solution)/shard_map/ppermute | solution.py:573
  344.2 29.8 %collective-permute-done.29 = bf16[768,512]{1,0:T(8,128)(2,1)S(1)} collective-permute-done((bf16[768,512]{1,0:T(8,128)(2,1)S(1)}, bf16[768,512]{1,0:T(8,128)(2,1)S(1)}, u32[]{:S(2)}, u32[]{:S(2)}) %collective-permute-start.29) | collective-permute-done | bytes 786464 | tf_op jit(solution)/shard_map/ppermute | solution.py:570
  380.7 14.3 %collective-permute-done.31.refs_2_ = bf16[192,2048]{1,0:T(8,128)(2,1)S(1)} collective-permute-done((bf16[192,2048]{1,0:T(8,128)(2,1)S(1)}, bf16[192,2048]{1,0:T(8,128)(2,1)S(1)}, u32[]{:S(2)}, u32[]{:S(2)}) %collective-permute-start.31) | collective-permute-done | bytes 786464 | tf_op jit(solution)/shard_map/ppermute | solution.py:573
  403.2 15.5 %collective-permute-done.35 = bf16[768,512]{1,0:T(8,128)(2,1)S(1)} collective-permute-done((bf16[768,512]{1,0:T(8,128)(2,1)S(1)}, bf16[768,512]{1,0:T(8,128)(2,1)S(1)}, u32[]{:S(2)}, u32[]{:S(2)}) %collective-permute-start.35) | collective-permute-done | bytes 786464 | tf_op jit(solution)/shard_map/ppermute | solution.py:570
  439.2 8.3 %attend_back.15 = (f32[768,512]{1,0:T(8,128)S(1)}, f32[768,512]{1,0:T(8,128)S(1)}) custom-call(s32[4]{0:T(128)S(1)} %copy-done.51, bf16[768,1024]{1,0:T(8,128)(2,1)S(1)} %copy-done.9, bf16[768,1024]{1,0:T(8,128)(2,1)S(1)} %copy-done.3, bf16[768,512]{1,0:T(8,128)(2,1)S(1)} %copy-done.25, s32[8,128]{1,0:T(8,128)S(1)} %copy-done.48, ...), custom_call_target="tpu_custom_call", output_to_operand_aliasing={{0}: (5, {})} | custom-call | flops 1 | bytes 1 | tf_op jit(solution)/shard_map/attend_back/pallas_call | solution.py:437
  467.5 8.8 %reduce-scatter.7.cloned.1.call-done = bf16[256,3072]{1,0:T(8,128)(2,1)} async-done(((bf16[2048,3072]{1,0:T(8,128)(2,1)}), bf16[256,3072]{1,0:T(8,128)(2,1)}) %reduce-scatter.7.cloned.1.call-update) | async-done | bytes 1572880 | tf_op jit(solution)/shard_map/reduce_scatter | solution.py:743
  501.7 8.0 %collective-permute-done.38 = bf16[2,96,2048]{2,1,0:T(8,128)(2,1)} collective-permute-done((bf16[2,96,2048]{2,1,0:T(8,128)(2,1)S(1)}, bf16[2,96,2048]{2,1,0:T(8,128)(2,1)}, u32[]{:S(2)}, u32[]{:S(2)}) %collective-permute-start.38) | collective-permute-done | bytes 786464 | tf_op jit(solution)/shard_map/ppermute | solution.py:573
  530.2 13.3 %collective-permute-done.46 = f32[34,128]{1,0:T(8,128)S(1)} collective-permute-done((f32[34,128]{1,0:T(8,128)S(1)}, f32[34,128]{1,0:T(8,128)S(1)}, u32[]{:S(2)}, u32[]{:S(2)}) %collective-permute-start.46) | collective-permute-done | bytes 17440 | tf_op jit(solution)/shard_map/ppermute | solution.py:887
  548.6 7.7 %collective-permute-start.49 = (f32[34,128]{1,0:T(8,128)S(1)}, f32[34,128]{1,0:T(8,128)S(1)}, u32[]{:S(2)}, u32[]{:S(2)}) collective-permute-start(f32[34,128]{1,0:T(8,128)S(1)} %add.293), channel_id=1, source_target_pairs={{0,8},{4,12},{8,0},{12,4},{16,24},{20,28},{24,16},{28,20},{1,9},{5... | collective-permute-start | bytes 52232 | tf_op jit(solution)/shard_map/ppermute | solution.py:887
  (421 shorter events, 305.6 us)
Async XLA Ops:
  7.2 92.8 %all-gather.3.cloned.1.call-start = ((), (), s32[]{:S(2)}) async-start(), calls=%async_computation.8 | async-start | bytes 5242880 | tf_op jit(solution)/shard_map/all_gather | solution.py:687
  24.9 267.2 %reduce-scatter.5.cloned.1.call-start = ((), (), s32[]{:S(2)}) async-start(), calls=%async_computation.4 | async-start | bytes 7077888 | tf_op jit(solution)/shard_map/reduce_scatter | solution.py:743
  25.0 30.8 %collective-permute-start.2 = (bf16[768,512]{1,0:T(8,128)(2,1)}, bf16[768,512]{1,0:T(8,128)(2,1)S(1)}, u32[]{:S(2)}, u32[]{:S(2)}) collective-permute-start(bf16[768,512]{1,0:T(8,128)(2,1)} %key_prep.1.kva_ref.kv_ref), channel_id=1, source_target_pairs={{0,4},{4,0},{8,12},{12,8},{16,20},{20,16},{24,28},{28,24},{1,5},{5... | collective-permute-start | bytes 2359304 | tf_op jit(solution)/shard_map/ppermute | solution.py:564
  25.5 27.8 %collective-permute-start = (bf16[768,512]{1,0:T(8,128)(2,1)}, bf16[768,512]{1,0:T(8,128)(2,1)}, u32[]{:S(2)}, u32[]{:S(2)}) collective-permute-start(bf16[768,512]{1,0:T(8,128)(2,1)} %key_prep.1.kva_ref.kv_ref), channel_id=1, source_target_pairs={{0,8},{4,12},{8,16},{12,20},{16,24},{20,28},{1,9},{5,13},{9,17},{1... | collective-permute-start | bytes 2359304 | tf_op jit(solution)/shard_map/ppermute | solution.py:567
  55.7 21.8 %collective-permute-start.4 = (bf16[768,512]{1,0:T(8,128)(2,1)}, bf16[768,512]{1,0:T(8,128)(2,1)S(1)}, u32[]{:S(2)}, u32[]{:S(2)}) collective-permute-start(bf16[768,512]{1,0:T(8,128)(2,1)} %collective-permute-done.kva_ref.kv_ref), channel_id=1, source_target_pairs={{0,4},{4,0},{8,12},{12,8},{16,20},{20,16},{24,28},{28,24},{1,5},{5... | collective-permute-start | bytes 2359304 | tf_op jit(solution)/shard_map/ppermute | solution.py:564
  206.5 269.7 %reduce-scatter.7.cloned.1.call-start = ((), (), s32[]{:S(2)}) async-start(), calls=%async_computation.5 | async-start | bytes 14155776 | tf_op jit(solution)/shard_map/reduce_scatter | solution.py:743
  292.1 285.1 %reduce-scatter.11.cloned.1.call-start = ((), (), s32[]{:S(2)}) async-start(), calls=%async_computation.7 | async-start | bytes 2359296 | tf_op jit(solution)/shard_map/reduce_scatter | solution.py:743
  292.1 22.0 %collective-permute-start.20 = (bf16[192,2048]{1,0:T(8,128)(2,1)S(1)}, bf16[192,2048]{1,0:T(8,128)(2,1)S(1)}, u32[]{:S(2)}, u32[]{:S(2)}) collective-permute-start(bf16[192,2048]{1,0:T(8,128)(2,1)S(1)} %get-tuple-element.185.branch_ref.refs_0_), channel_id=1, source_target_pairs={{0,2},{1,3},{2,0},{3,1},{4,6},{5,7},{6,4},{7,5},{8,10},{9,11},{10,... | collective-permute-start | bytes 2359304 | tf_op jit(solution)/shard_map/ppermute | solution.py:573
  310.9 21.5 %collective-permute-start.25 = (bf16[2,96,2048]{2,1,0:T(8,128)(2,1)S(1)}, bf16[2,96,2048]{2,1,0:T(8,128)(2,1)S(1)}, u32[]{:S(2)}, u32[]{:S(2)}) collective-permute-start(bf16[2,96,2048]{2,1,0:T(8,128)(2,1)S(1)} %dynamic-slice_bitcast_fusion.2), channel_id=1, source_target_pairs={{0,2},{1,3},{2,0},{3,1},{4,6},{5,7},{6,4},{7,5},{8,10},{9,11},{10,... | collective-permute-start | bytes 2359304 | tf_op jit(solution)/shard_map/ppermute | solution.py:573
  314.3 24.9 %collective-permute-start.23 = (bf16[96,2048]{1,0:T(8,128)(2,1)S(1)}, bf16[96,2048]{1,0:T(8,128)(2,1)S(1)}, u32[]{:S(2)}, u32[]{:S(2)}) collective-permute-start(bf16[96,2048]{1,0:T(8,128)(2,1)S(1)} %slice.143), channel_id=1, source_target_pairs={{0,1},{1,0},{2,3},{3,2},{4,5},{5,4},{6,7},{7,6},{8,9},{9,8},{10,11... | collective-permute-start | bytes 1179656 | tf_op jit(solution)/shard_map/ppermute | solution.py:573
  315.5 23.8 %collective-permute-start.22 = (bf16[96,2048]{1,0:T(8,128)(2,1)S(1)}, bf16[96,2048]{1,0:T(8,128)(2,1)S(1)}, u32[]{:S(2)}, u32[]{:S(2)}) collective-permute-start(bf16[96,2048]{1,0:T(8,128)(2,1)S(1)} %slice.142), channel_id=1, source_target_pairs={{0,2},{1,3},{2,0},{3,1},{4,6},{5,7},{6,4},{7,5},{8,10},{9,11},{10,... | collective-permute-start | bytes 1179656 | tf_op jit(solution)/shard_map/ppermute | solution.py:573
  319.5 24.7 %collective-permute-start.28 = (bf16[768,512]{1,0:T(8,128)(2,1)S(1)}, bf16[768,512]{1,0:T(8,128)(2,1)S(1)}, u32[]{:S(2)}, u32[]{:S(2)}) collective-permute-start(bf16[768,512]{1,0:T(8,128)(2,1)S(1)} %get-tuple-element.201), channel_id=1, source_target_pairs={{0,4},{4,0},{8,12},{12,8},{16,20},{20,16},{24,28},{28,24},{1,5},{5... | collective-permute-start | bytes 2359304 | tf_op jit(solution)/shard_map/ppermute | solution.py:564
  331.1 42.9 %collective-permute-start.29 = (bf16[768,512]{1,0:T(8,128)(2,1)S(1)}, bf16[768,512]{1,0:T(8,128)(2,1)S(1)}, u32[]{:S(2)}, u32[]{:S(2)}) collective-permute-start(bf16[768,512]{1,0:T(8,128)(2,1)S(1)} %add_convert_fusion.4), channel_id=1, source_target_pairs={{8,0},{12,4},{16,8},{20,12},{24,16},{28,20},{9,1},{13,5},{17,9},{2... | collective-permute-start | bytes 2359304 | tf_op jit(solution)/shard_map/ppermute | solution.py:570
  339.9 34.5 %collective-permute-start.26 = (bf16[96,2048]{1,0:T(8,128)(2,1)S(1)}, bf16[96,2048]{1,0:T(8,128)(2,1)S(1)}, u32[]{:S(2)}, u32[]{:S(2)}) collective-permute-start(bf16[96,2048]{1,0:T(8,128)(2,1)S(1)} %fusion.17), channel_id=1, source_target_pairs={{0,2},{1,3},{2,0},{3,1},{4,6},{5,7},{6,4},{7,5},{8,10},{9,11},{10,... | collective-permute-start | bytes 1179656 | tf_op jit(solution)/shard_map/ppermute | solution.py:573
  340.2 34.1 %collective-permute-start.27 = (bf16[96,2048]{1,0:T(8,128)(2,1)S(1)}, bf16[96,2048]{1,0:T(8,128)(2,1)S(1)}, u32[]{:S(2)}, u32[]{:S(2)}) collective-permute-start(bf16[96,2048]{1,0:T(8,128)(2,1)S(1)} %fusion.18), channel_id=1, source_target_pairs={{0,1},{1,0},{2,3},{3,2},{4,5},{5,4},{6,7},{7,6},{8,9},{9,8},{10,11... | collective-permute-start | bytes 1179656 | tf_op jit(solution)/shard_map/ppermute | solution.py:573
  377.2 41.5 %collective-permute-start.35 = (bf16[768,512]{1,0:T(8,128)(2,1)S(1)}, bf16[768,512]{1,0:T(8,128)(2,1)S(1)}, u32[]{:S(2)}, u32[]{:S(2)}) collective-permute-start(bf16[768,512]{1,0:T(8,128)(2,1)S(1)} %add_convert_fusion.3), channel_id=1, source_target_pairs={{8,0},{12,4},{16,8},{20,12},{24,16},{28,20},{9,1},{13,5},{17,9},{2... | collective-permute-start | bytes 2359304 | tf_op jit(solution)/shard_map/ppermute | solution.py:570
  380.5 38.2 %collective-permute-start.34 = (bf16[768,512]{1,0:T(8,128)(2,1)S(1)}, bf16[768,512]{1,0:T(8,128)(2,1)S(1)}, u32[]{:S(2)}, u32[]{:S(2)}) collective-permute-start(bf16[768,512]{1,0:T(8,128)(2,1)S(1)} %get-tuple-element.213), channel_id=1, source_target_pairs={{0,4},{4,0},{8,12},{12,8},{16,20},{20,16},{24,28},{28,24},{1,5},{5... | collective-permute-start | bytes 2359304 | tf_op jit(solution)/shard_map/ppermute | solution.py:564
  395.4 25.8 %collective-permute-start.33 = (bf16[96,2048]{1,0:T(8,128)(2,1)S(1)}, bf16[96,2048]{1,0:T(8,128)(2,1)S(1)}, u32[]{:S(2)}, u32[]{:S(2)}) collective-permute-start(bf16[96,2048]{1,0:T(8,128)(2,1)S(1)} %slice.146), channel_id=1, source_target_pairs={{0,1},{1,0},{2,3},{3,2},{4,5},{5,4},{6,7},{7,6},{8,9},{9,8},{10,11... | collective-permute-start | bytes 1179656 | tf_op jit(solution)/shard_map/ppermute | solution.py:573
  396.0 25.2 %collective-permute-start.32 = (bf16[96,2048]{1,0:T(8,128)(2,1)S(1)}, bf16[96,2048]{1,0:T(8,128)(2,1)S(1)}, u32[]{:S(2)}, u32[]{:S(2)}) collective-permute-start(bf16[96,2048]{1,0:T(8,128)(2,1)S(1)} %slice.145), channel_id=1, source_target_pairs={{0,2},{1,3},{2,0},{3,1},{4,6},{5,7},{6,4},{7,5},{8,10},{9,11},{10,... | collective-permute-start | bytes 1179656 | tf_op jit(solution)/shard_map/ppermute | solution.py:573
  419.9 44.6 %collective-permute-start.37 = (bf16[768,512]{1,0:T(8,128)(2,1)}, bf16[768,512]{1,0:T(8,128)(2,1)}, u32[]{:S(2)}, u32[]{:S(2)}) collective-permute-start(bf16[768,512]{1,0:T(8,128)(2,1)} %add_convert_fusion.2), channel_id=1, source_target_pairs={{8,0},{12,4},{16,8},{20,12},{24,16},{28,20},{9,1},{13,5},{17,9},{2... | collective-permute-start | bytes 2359304 | tf_op jit(solution)/shard_map/ppermute | solution.py:570
  425.7 38.8 %collective-permute-start.36 = (bf16[768,512]{1,0:T(8,128)(2,1)}, bf16[768,512]{1,0:T(8,128)(2,1)}, u32[]{:S(2)}, u32[]{:S(2)}) collective-permute-start(bf16[768,512]{1,0:T(8,128)(2,1)} %get-tuple-element.227), channel_id=1, source_target_pairs={{0,4},{4,0},{8,12},{12,8},{16,20},{20,16},{24,28},{28,24},{1,5},{5... | collective-permute-start | bytes 2359304 | tf_op jit(solution)/shard_map/ppermute | solution.py:564
  476.3 102.7 %reduce-scatter.9.cloned.1.call-start = ((), (), s32[]{:S(2)}) async-start(), calls=%async_computation.6 | async-start | bytes 4718592 | tf_op jit(solution)/shard_map/reduce_scatter | solution.py:743
  527.9 33.3 %collective-permute-start.43 = (bf16[192,2048]{1,0:T(8,128)(2,1)S(1)}, bf16[192,2048]{1,0:T(8,128)(2,1)S(1)}, u32[]{:S(2)}, u32[]{:S(2)}) collective-permute-start(bf16[192,2048]{1,0:T(8,128)(2,1)S(1)} %fusion.12.refs_0_), channel_id=1, source_target_pairs={{0,2},{1,3},{2,0},{3,1},{4,6},{5,7},{6,4},{7,5},{8,10},{9,11},{10,... | collective-permute-start | bytes 2359304 | tf_op jit(solution)/shard_map/ppermute | solution.py:573
  528.0 34.3 %collective-permute-start.42 = (bf16[192,2048]{1,0:T(8,128)(2,1)S(1)}, bf16[192,2048]{1,0:T(8,128)(2,1)S(1)}, u32[]{:S(2)}, u32[]{:S(2)}) collective-permute-start(bf16[192,2048]{1,0:T(8,128)(2,1)S(1)} %fusion.12.refs_0_), channel_id=1, source_target_pairs={{0,1},{1,0},{2,3},{3,2},{4,5},{5,4},{6,7},{7,6},{8,9},{9,8},{10,11... | collective-permute-start | bytes 2359304 | tf_op jit(solution)/shard_map/ppermute | solution.py:573
  (123 other events, 1123.1 us)
Sparse Core Ops, SparseCore 0:
  25.0 55.4 all-gather.2
  206.7 85.3 reduce-scatter.4
  294.4 181.8 reduce-scatter.6
  478.4 33.9 reduce-scatter.10
  514.5 49.1 reduce-scatter.8

commit v4 on v3

--- a/solution.py
+++ b/solution.py
@@ -15,6 +15,7 @@
 SCORE_SCALE = 1.0 / math.sqrt(HEAD_WIDTH)
 SCORE_SCALE_2 = LOG2E / math.sqrt(HEAD_WIDTH)
 KEY_CHUNK = 256
+HIDDEN_STEP = 256
 FAR = 512.0
 LOG_LANE = 64
 MIB = 2**20
@@ -83,24 +84,56 @@
     return scaled * cosine + pltpu.roll(scaled, HEAD_WIDTH // 2, 1) * sine
 
 
-def key_prep_kernel(raw_ref, value_ref, gain_ref, cos_ref, sin_ref, out_ref):
-    key = normed(raw_ref[...], gain_ref[...], cos_ref[...], sin_ref[...])
-    out_ref[:, :HEAD_WIDTH] = key.astype(bf16)
-    out_ref[:, HEAD_WIDTH:] = value_ref[...].astype(bf16)
-
-
-def key_prep(raw, value, gain, cosine, sine):
-    rows, width = raw.shape
-    block = pl.BlockSpec((rows, HEAD_WIDTH), lambda j: (0, j))
-    table = pl.BlockSpec((rows, HEAD_WIDTH), lambda j: (0, 0))
-    return pl.pallas_call(
-        key_prep_kernel,
-        grid=(width // HEAD_WIDTH,),
-        in_specs=[block, block, pl.BlockSpec((1, HEAD_WIDTH), lambda j: (0, 0)), table, table],
-        out_specs=pl.BlockSpec((rows, 2 * HEAD_WIDTH), lambda j: (0, j)),
-        out_shape=jax.ShapeDtypeStruct((rows, 2 * width), bf16),
-        name="key_prep",
-    )(raw, value, gain[None, :], cosine, sine)
+def enter_kernel(
+    x_ref, gain_ref, key_w_ref, value_w_ref, key_gain_ref, cos_ref, sin_ref, in_ref, raw_ref, kv_ref
+):
+    x = x_ref[...].astype(f32)
+    inverse = lax.rsqrt(jnp.mean(x * x, axis=-1, keepdims=True) + EPSILON)
+    first_in = (x * inverse * gain_ref[...]).astype(bf16)
+    in_ref[...] = first_in
+    raw = dot(first_in, key_w_ref[...])
+    raw_ref[...] = raw
+    value = dot(first_in, value_w_ref[...]).astype(bf16)
+    for j in range(raw.shape[1] // HEAD_WIDTH):
+        head = slice(j * HEAD_WIDTH, (j + 1) * HEAD_WIDTH)
+        key = normed(raw[:, head], key_gain_ref[...], cos_ref[...], sin_ref[...])
+        start = 2 * j * HEAD_WIDTH
+        kv_ref[:, start : start + HEAD_WIDTH] = key.astype(bf16)
+        kv_ref[:, start + HEAD_WIDTH : start + 2 * HEAD_WIDTH] = value[:, head]
+
+
+def enter(tokens, gain, key_w, value_w, key_gain, cosine, sine):
+    rows, width = tokens.shape
+    kv_width = key_w.shape[1]
+    step = rows // 3 if rows % 768 == 0 else rows
+    table = pl.BlockSpec((step, HEAD_WIDTH), lambda i: (i, 0))
+    weight = pl.BlockSpec((width, kv_width), lambda i: (0, 0))
+    return pl.pallas_call(
+        enter_kernel,
+        grid=(rows // step,),
+        in_specs=[
+            pl.BlockSpec((step, width), lambda i: (i, 0)),
+            pl.BlockSpec((1, width), lambda i: (0, 0)),
+            weight,
+            weight,
+            pl.BlockSpec((1, HEAD_WIDTH), lambda i: (0, 0)),
+            table,
+            table,
+        ],
+        out_specs=[
+            pl.BlockSpec((step, width), lambda i: (i, 0)),
+            pl.BlockSpec((step, kv_width), lambda i: (i, 0)),
+            pl.BlockSpec((step, 2 * kv_width), lambda i: (i, 0)),
+        ],
+        out_shape=[
+            jax.ShapeDtypeStruct((rows, width), bf16),
+            jax.ShapeDtypeStruct((rows, kv_width), f32),
+            jax.ShapeDtypeStruct((rows, 2 * kv_width), bf16),
+        ],
+        compiler_params=pltpu.CompilerParams(vmem_limit_bytes=32 * MIB),
+        cost_estimate=SMALL,
+        name="enter",
+    )(tokens, gain[None, :], key_w, value_w, key_gain[None, :], cosine, sine)
 
 
 def query_prep_kernel(meta, raw_ref, gain_ref, cos_ref, sin_ref, bounds_ref, out_ref):
@@ -468,7 +501,7 @@
 def project_kernel(meta, base_ref, *refs, count, final):
     pieces, mine, other = refs[:count], refs[count : 2 * count], refs[2 * count : 3 * count]
     if final:
-        gain_ref, out_ref, normed_ref = refs[3 * count :]
+        gain_ref, share_ref, normed_ref = refs[3 * count :]
     else:
         (out_ref,) = refs[3 * count :]
     first_core = meta[0] == 0
@@ -478,41 +511,55 @@
         low, high = piece[:, :half], piece[:, half:]
         total += dot(jnp.where(first_core, low, high), mine_ref[0])
         total += dot(jnp.where(first_core, high, low), other_ref[0])
-    out_ref[...] = total
     if final:
         inverse = lax.rsqrt(jnp.mean(total * total, axis=-1, keepdims=True) + EPSILON)
         normed_ref[...] = (total * inverse * gain_ref[...]).astype(bf16)
 
-
-def project(base, pieces, w_mine, w_other, core, gain=None):
-    meta = jnp.stack([jnp.asarray(v, jnp.int32) for v in [core] + [owner for unused, owner in pieces]])
+        @pl.when(pl.program_id(0) == meta[1])
+        def _():
+            share_ref[...] = total
+
+    else:
+        out_ref[...] = total
+
+
+def project(base, pieces, w_mine, w_other, core, me, gain=None):
+    meta = jnp.stack(
+        [jnp.asarray(v, jnp.int32) for v in [core, me] + [owner for unused, owner in pieces]]
+    )
     rows, width = base.shape
+    n_head, half, unused = w_mine.shape
     count = len(pieces)
     final = gain is not None
-    step = rows // 3 if rows % 768 == 0 else rows
-    half = w_mine.shape[1]
+    step = rows // n_head
     per_row = pl.BlockSpec((step, width), lambda i, m: (i, 0))
     per_piece = pl.BlockSpec((step, 2 * half), lambda i, m: (i, 0))
     weights = [
-        pl.BlockSpec((1, half, width), lambda i, m, k=k: (m[1 + k], 0, 0)) for k in range(count)
+        pl.BlockSpec((1, half, width), lambda i, m, k=k: (m[2 + k], 0, 0)) for k in range(count)
     ]
     in_specs = [per_row] + [per_piece] * count + weights + weights
     args = [base] + [piece for piece, unused in pieces] + [w_mine] * count + [w_other] * count
-    out_shape = [jax.ShapeDtypeStruct((rows, width), f32)]
     if final:
         in_specs.append(pl.BlockSpec((1, width), lambda i, m: (0, 0)))
         args.append(gain[None, :])
-        out_shape.append(jax.ShapeDtypeStruct((rows, width), bf16))
+        out_specs = [pl.BlockSpec((step, width), lambda i, m: (0, 0)), per_row]
+        out_shape = [
+            jax.ShapeDtypeStruct((step, width), f32),
+            jax.ShapeDtypeStruct((rows, width), bf16),
+        ]
+    else:
+        out_specs = per_row
+        out_shape = jax.ShapeDtypeStruct((rows, width), f32)
     return pl.pallas_call(
         functools.partial(project_kernel, count=count, final=final),
         grid_spec=pltpu.PrefetchScalarGridSpec(
             num_scalar_prefetch=1,
             grid=(rows // step,),
             in_specs=in_specs,
-            out_specs=[per_row] * len(out_shape),
+            out_specs=out_specs,
         ),
         out_shape=out_shape,
-        compiler_params=pltpu.CompilerParams(vmem_limit_bytes=48 * MIB),
+        compiler_params=pltpu.CompilerParams(vmem_limit_bytes=(24 + 8 * count) * MIB),
         cost_estimate=SMALL,
         name="project",
     )(meta, *args)
@@ -545,6 +592,142 @@
         cost_estimate=SMALL,
         name="project_back",
     )(meta, branch, w_mine, w_other)
+
+
+def feed_kernel(
+    x_ref, gate_w_ref, up_w_ref, d_mixed_ref, dy_ref, mixed_ref, gate_ref, up_ref, down_ref
+):
+    x = x_ref[...]
+    gate = dot(x, gate_w_ref[...])
+    up = dot(x, up_w_ref[...])
+    d_mixed = d_mixed_ref[...]
+    sigmoid = 0.5 * jnp.tanh(0.5 * gate) + 0.5
+    silu = gate * sigmoid
+    mixed = (silu * up).astype(bf16)
+    mixed_ref[...] = mixed
+    gate_ref[...] = (d_mixed * up * (sigmoid * (1.0 + gate * (1.0 - sigmoid)))).astype(bf16)
+    up_ref[...] = (d_mixed * silu).astype(bf16)
+    shares, unused, width = down_ref.shape
+    for i in range(shares):
+        down_ref[i] = dot_tn(mixed, dy_ref[:, i * width : (i + 1) * width]).astype(bf16)
+
+
+def feed(x, w_gate, w_up, d_mixed, dy, shares):
+    rows, width = x.shape
+    hidden = w_gate.shape[1]
+    whole = pl.BlockSpec((rows, width), lambda i: (0, 0))
+    weight = pl.BlockSpec((width, HIDDEN_STEP), lambda i: (0, i))
+    act = pl.BlockSpec((rows, HIDDEN_STEP), lambda i: (0, i))
+    return pl.pallas_call(
+        feed_kernel,
+        grid=(hidden // HIDDEN_STEP,),
+        in_specs=[whole, weight, weight, act, whole],
+        out_specs=[
+            act,
+            act,
+            act,
+            pl.BlockSpec((shares, HIDDEN_STEP, width // shares), lambda i: (0, i, 0)),
+        ],
+        out_shape=[jax.ShapeDtypeStruct((rows, hidden), bf16)] * 3
+        + [jax.ShapeDtypeStruct((shares, hidden, width // shares), bf16)],
+        compiler_params=pltpu.CompilerParams(vmem_limit_bytes=40 * MIB),
+        cost_estimate=SMALL,
+        name="feed",
+    )(x, w_gate, w_up, d_mixed, dy)
+
+
+def feed_back_kernel(gate_ref, up_ref, gate_w_ref, up_w_ref, out_ref):
+    out_ref[...] = (
+        dot_nt(gate_ref[...], gate_w_ref[...]) + dot_nt(up_ref[...], up_w_ref[...])
+    ).astype(bf16)
+
+
+def feed_back(gate, up, w_gate, w_up):
+    rows, hidden = gate.shape
+    width = w_gate.shape[0]
+    step = width // 4
+    whole = pl.BlockSpec((rows, hidden), lambda i: (0, 0))
+    weight = pl.BlockSpec((step, hidden), lambda i: (i, 0))
+    return pl.pallas_call(
+        feed_back_kernel,
+        grid=(width // step,),
+        in_specs=[whole, whole, weight, weight],
+        out_specs=pl.BlockSpec((rows, step), lambda i: (0, i)),
+        out_shape=jax.ShapeDtypeStruct((rows, width), bf16),
+        compiler_params=pltpu.CompilerParams(vmem_limit_bytes=36 * MIB),
+        cost_estimate=SMALL,
+        name="feed_back",
+    )(gate, up, w_gate, w_up)
+
+
+def feed_sums_kernel(x_ref, gate_ref, up_ref, out_ref):
+    hidden = gate_ref.shape[1]
+    x = x_ref[...]
+    out_ref[:, :hidden] = dot_tn(x, gate_ref[...]).astype(bf16)
+    out_ref[:, hidden:] = dot_tn(x, up_ref[...]).astype(bf16)
+
+
+def feed_sums(x, gate, up):
+    rows, width = x.shape
+    hidden = gate.shape[1]
+    step = width // 8
+    act = pl.BlockSpec((rows, hidden), lambda i: (0, 0))
+    return pl.pallas_call(
+        feed_sums_kernel,
+        grid=(width // step,),
+        in_specs=[pl.BlockSpec((rows, step), lambda i: (0, i)), act, act],
+        out_specs=pl.BlockSpec((step, 2 * hidden), lambda i: (i, 0)),
+        out_shape=jax.ShapeDtypeStruct((width, 2 * hidden), bf16),
+        compiler_params=pltpu.CompilerParams(vmem_limit_bytes=32 * MIB),
+        cost_estimate=SMALL,
+        name="feed_sums",
+    )(x, gate, up)
+
+
+def attn_sums_kernel(x_ref, q_ref, k_ref, v_ref, o_ref, branch_ref, out_ref):
+    x = x_ref[...]
+    share = x.shape[1]
+    width = out_ref.shape[2]
+    start = 0
+    for ref in (q_ref, k_ref, v_ref):
+        out_ref[0, :share, start : start + ref.shape[1]] = dot_tn(x, ref[...]).astype(bf16)
+        start += ref.shape[1]
+    branch = branch_ref[...]
+    heads = o_ref.shape[1] // HEAD_WIDTH
+    if heads * share % width:
+        out_ref[0, share:, :] = jnp.zeros((out_ref.shape[1] - share, width), bf16)
+    for j in range(heads):
+        row, lane = output_place(j, share, width)
+        out_ref[0, row : row + HEAD_WIDTH, lane : lane + share] = dot_tn(
+            o_ref[:, j * HEAD_WIDTH : (j + 1) * HEAD_WIDTH], branch
+        ).astype(bf16)
+
+
+def output_place(head, share, width):
+    return share + HEAD_WIDTH * (head * share // width), head * share % width
+
+
+def attn_sums(x, query, key, value, o_low, branch, shares):
+    rows, width = x.shape
+    share = width // shares
+    out_width = query.shape[1] + key.shape[1] + value.shape[1]
+    heads = o_low.shape[1] // HEAD_WIDTH
+    out_rows = output_place(heads - 1, share, out_width)[0] + HEAD_WIDTH
+
+    def full(array):
+        return pl.BlockSpec(array.shape, lambda i: (0, 0))
+
+    part = pl.BlockSpec((rows, share), lambda i: (0, i))
+    return pl.pallas_call(
+        attn_sums_kernel,
+        grid=(shares,),
+        in_specs=[part, full(query), full(key), full(value), full(o_low), part],
+        out_specs=pl.BlockSpec((1, out_rows, out_width), lambda i: (i, 0, 0)),
+        out_shape=jax.ShapeDtypeStruct((shares, out_rows, out_width), bf16),
+        compiler_params=pltpu.CompilerParams(vmem_limit_bytes=24 * MIB),
+        cost_estimate=SMALL,
+        name="attn_sums",
+    )(x, query, key, value, o_low, branch)
 
 
 def after(values):
@@ -672,90 +855,72 @@
 
         metas = [stage_meta(stage) for stage in range(n_chip)]
 
-        xf = tokens.astype(f32)
-        inverse1 = lax.rsqrt(jnp.mean(xf * xf, axis=-1, keepdims=True) + EPSILON)
-        first_in = (xf * inverse1 * norm1_gain).astype(bf16)
-        key_raw = dot(first_in, key_matrix)
-        value_raw = dot(first_in, value_matrix)
-        current = key_prep(key_raw, value_raw, key_gain, cosine, sine)
+        first_in, key_raw, current = enter(
+            tokens, norm1_gain, key_matrix, value_matrix, key_gain, cosine, sine
+        )
         sibling = swap_core(current)
         following = to_next(current)
 
         half_rows = w_output.shape[0] // 2
-        w_half = lax.dynamic_slice_in_dim(w_output, core * half_rows, half_rows, 0)
-        w_half, current = after((w_half, current))
+        w_late, unused = after((w_output, current))
+        w_half = lax.dynamic_slice_in_dim(w_late, core * half_rows, half_rows, 0)
         w_mine = lax.all_gather(w_half, "head", axis=0)
 
         query_raw = dot(first_in, w_query)
         q_wide = query_prep(metas[0], query_raw, query_gain, cosine, sine, bounds)
+        following, q_wide = after((following, q_wide))
         d_mixed = dot_nt(cotangent, w_down)
-        following, q_wide, d_mixed = after((following, q_wide, d_mixed))
 
         blocks = []
         carried = ()
         for stage in range(n_chip):
             blocks.append((current, sibling))
-            if stage + 1 < n_chip:
+            if stage + 2 < n_chip:
                 current = following
                 sibling = swap_core(current)
-                following = to_next(current) if stage + 2 < n_chip else None
-            if stage == n_chip - 1:
-                w_mine, carried = after((w_mine, carried))
-                w_other = swap_core(w_mine)
+                following = to_next(current)
             carried = attend_stage(
                 q_wide, *blocks[stage], bounds, metas[stage], carried, stage == n_chip - 1
             )
-            if following is not None:
+            if stage == 0:
+                carried, d_mixed = after((carried, d_mixed))
+            if stage + 3 < n_chip:
                 following, carried = after((following, carried))
+            if stage + 2 == n_chip:
+                current, carried = after((following, carried))
+                sibling = swap_core(current)
+                w_mine, sibling, carried = after((w_mine, sibling, carried))
+                w_other = swap_core(w_mine)
         o_low, q_back, outcome = carried
 
         steps = gather_steps(o_low)
         arrived = next(steps)
+        base = tokens
         if n_head == 4:
-            me = lax.axis_index("head")
-            (hidden,) = project(tokens, [(o_low, me)], w_mine, w_other, core)
-            arrived, hidden = after((arrived, hidden))
             far = steps.send(arrived)
-            (hidden,) = project(
-                hidden, [(arrived[0], me ^ 1), (arrived[1], me ^ 2)], w_mine, w_other, core
-            )
-            far, hidden = after((far, hidden))
-            try:
-                steps.send(far)
-            except StopIteration as stop:
-                last_pieces = stop.value[3:]
-        else:
-            hidden = tokens
-            try:
-                steps.send(arrived)
-            except StopIteration as stop:
-                last_pieces = stop.value
-        hidden, second_in = project(hidden, last_pieces, w_mine, w_other, core, norm2_gain)
-        gate_raw = dot(second_in, w_gate)
-        up_raw = dot(second_in, w_up)
-        sigmoid = jax.nn.sigmoid(gate_raw)
-        silu = gate_raw * sigmoid
-        mixed_low = (silu * up_raw).astype(bf16)
-        gate_low = (d_mixed * up_raw * (sigmoid * (1.0 + gate_raw * (1.0 - sigmoid)))).astype(bf16)
-        up_low = (d_mixed * silu).astype(bf16)
-
-        def scatter_seq(value, dimension):
-            return lax.psum_scatter(value, "seq", scatter_dimension=dimension, tiled=True)
-
-        down_sum = dot_tn(mixed_low, cotangent).astype(bf16)
-        down_sum, gate_low, up_low = after((down_sum, gate_low, up_low))
-        grad_down = scatter_seq(down_sum, 1)
-        second_part = (dot_nt(gate_low, w_gate) + dot_nt(up_low, w_up)).astype(bf16)
-
-        second_grad, (gate_sum, up_sum) = run_steps(
-            scatter_steps(second_part),
-            (
-                lambda: dot_tn(second_in, gate_low).astype(bf16),
-                lambda: dot_tn(second_in, up_low).astype(bf16),
-            ),
-        )
-        gate_up_sum = jnp.concatenate([gate_sum, up_sum], axis=1)
-        my_hidden = lax.dynamic_slice_in_dim(hidden, head_index * share, share, 0)
+            pieces = [(o_low, head_index), (arrived[0], head_index ^ 1), (arrived[1], head_index ^ 2)]
+            base = project(tokens, pieces, w_mine, w_other, core, head_index)
+            arrived, base = after((far, base))
+        try:
+            steps.send(arrived)
+        except StopIteration as stop:
+            pieces = stop.value[3:] if n_head == 4 else stop.value
+        my_hidden, second_in = project(
+            base, pieces, w_mine, w_other, core, head_index, norm2_gain
+        )
+        mixed_low, gate_low, up_low, down_sum = feed(
+            second_in, w_gate, w_up, d_mixed, cotangent, n_seq
+        )
+
+        def scatter_seq(value, tiled):
+            return lax.psum_scatter(value, "seq", scatter_dimension=0, tiled=tiled)
+
+        grad_down = scatter_seq(down_sum, False)
+
+        second_grad, (gate_up_sum,) = run_steps(
+            scatter_steps(feed_back(gate_low, up_low, w_gate, w_up)),
+            (lambda: feed_sums(second_in, gate_low, up_low),),
+        )
         my_inverse = lax.rsqrt(jnp.mean(my_hidden * my_hidden, axis=-1, keepdims=True) + EPSILON)
         my_hat = my_hidden * my_inverse
         grad_norm2 = jnp.sum(second_grad * my_hat, axis=0)
@@ -768,7 +933,7 @@
         do_pieces = exchange_head(project_back(my_branch, w_mine, w_other, core))
         do_wide = with_delta(do_pieces, outcome)
         grad_down, gate_up_sum, do_wide = after((grad_down, gate_up_sum, do_wide))
-        grad_gate_up = scatter_seq(gate_up_sum, 0)
+        grad_gate_up = scatter_seq(gate_up_sum, True)
 
         def side_work(mixed_low, my_branch):
             branch_steps = gather_steps(my_branch)
@@ -779,7 +944,6 @@
                 branch_steps.send(got_branch)
             except StopIteration as stop:
                 branch = assemble(stop.value, bf16)
-            output_sum = dot_tn(o_low, branch).astype(bf16)
             if n_head == 4:
                 got = yield mixed_steps.send(got)
             try:
@@ -794,43 +958,47 @@
                 mixed_steps.send(got)
             except StopIteration as stop:
                 mixed = assemble(stop.value, bf16)
-            return mixed, output_sum
+            return mixed, branch
 
         mixed_late, my_branch, do_wide = after((mixed_low, my_branch, do_wide))
         side = side_work(mixed_late, my_branch)
         waiting = next(side)
         side_made = None
 
+        def side_step():
+            nonlocal waiting, side_made, dq
+            if side_made is None:
+                waiting, dq = after((waiting, dq))
+                try:
+                    waiting = side.send(waiting)
+                except StopIteration as stop:
+                    side_made = stop.value
+
         dq = None
         arrived = None
-        kernels = 0
+        pending = None
         for stage in reversed(range(n_chip)):
             kv_a, kv_b = blocks[stage]
             meta = metas[stage]
             dq, dkv_b = attend_back(q_back, do_wide, kv_b, bounds, meta, dq, 1, False, bf16)
             theirs = swap_core(dkv_b)
-            if stage != n_chip - 1 and side_made is None:
-                try:
-                    waiting, dq = after((waiting, dq))
-                    waiting = side.send(waiting)
-                except StopIteration as stop:
-                    side_made = stop.value
+            if stage < n_chip - 2:
+                side_step()
             dq, dkv_a = attend_back(q_back, do_wide, kv_a, bounds, meta, dq, 0, stage == 0, f32)
-            dkv = dkv_a + theirs.astype(f32)
-            if arrived is not None:
-                dkv = dkv + arrived.astype(f32)
-            if stage > 0:
-                sent, dq = after((dkv.astype(bf16), dq))
-                arrived = to_previous(sent)
-            if side_made is None:
-                try:
-                    waiting, dq = after((waiting, dq))
-                    waiting = side.send(waiting)
-                except StopIteration as stop:
-                    side_made = stop.value
-        mixed, output_sum = side_made
-        grad_gate_up, output_sum, dkv = after((grad_gate_up, output_sum, dkv))
-        grad_output = scatter_seq(output_sum, 1)
+            part = dkv_a + theirs.astype(f32)
+            if pending is not None:
+                arrived, unused = after((arrived, dq))
+                arrived = to_previous((pending + arrived.astype(f32)).astype(bf16))
+            if stage == n_chip - 1:
+                arrived = to_previous(part.astype(bf16))
+            else:
+                pending = part
+            if stage >= n_chip - 2 or stage == 0:
+                side_step()
+        while side_made is None:
+            side_step()
+        dkv = pending + arrived.astype(f32)
+        mixed, branch = side_made
         query_grad, grad_qgain = head_back(
             query_raw, dq, query_gain, cosine, sine, SCORE_SCALE, 1
         )
@@ -850,26 +1018,29 @@
             + dot_nt(key_grad, key_matrix)
             + dot_nt(value_grad, value_matrix)
         ).astype(bf16)
-        hat1 = xf * inverse1
+        xf = tokens.astype(f32)
+        hat1 = xf * lax.rsqrt(jnp.mean(xf * xf, axis=-1, keepdims=True) + EPSILON)
         grad_norm1 = jnp.sum(first_part.astype(f32) * hat1, axis=0)
         gains = jnp.concatenate([grad_norm1, grad_norm2, grad_qgain[0], grad_kgain[0]])
         gains = gains.reshape(-1, HEAD_WIDTH)
         first_grad, (attn_sum,) = run_steps(
             scatter_steps(first_part),
             (
-                lambda: jnp.concatenate(
-                    [
-                        dot_tn(first_in, query_grad).astype(bf16),
-                        dot_tn(first_in, key_grad).astype(bf16),
-                        dot_tn(first_in, value_grad).astype(bf16),
-                    ],
-                    axis=1,
+                lambda: attn_sums(
+                    first_in, query_grad, key_grad, value_grad, o_low, branch, n_seq
                 ),
             ),
         )
-        grad_attn = scatter_seq(attn_sum, 0)
+        grad_gate_up, attn_sum = after((grad_gate_up, attn_sum))
+        grad_attn = scatter_seq(attn_sum, False).astype(f32)
+        share_width = tokens.shape[1] // n_seq
         widths = (query_grad.shape[1], query_grad.shape[1] + key_grad.shape[1])
-        grad_query, grad_key, grad_value = jnp.split(grad_attn, widths, axis=1)
+        grad_query, grad_key, grad_value = jnp.split(grad_attn[:share_width], widths, axis=1)
+        output_heads = []
+        for j in range(o_low.shape[1] // HEAD_WIDTH):
+            row, lane = output_place(j, share_width, grad_attn.shape[1])
+            output_heads.append(grad_attn[row : row + HEAD_WIDTH, lane : lane + share_width])
+        grad_output = jnp.concatenate(output_heads, axis=0)
 
         my_x = lax.dynamic_slice_in_dim(tokens, head_index * share, share, 0).astype(f32)
         my_inverse1 = lax.rsqrt(jnp.mean(my_x * my_x, axis=-1, keepdims=True) + EPSILON)
@@ -895,12 +1066,12 @@
             mixed,
             grad_tokens,
             grad_norm1,
-            grad_query.astype(f32),
-            grad_key.astype(f32),
-            grad_value.astype(f32),
+            grad_query,
+            grad_key,
+            grad_value,
             grad_qgain,
             grad_kgain,
-            grad_output.astype(f32),
+            grad_output,
             grad_norm2,
             grad_gate_up[:, : w_gate.shape[1]].astype(f32),
             grad_gate_up[:, w_gate.shape[1] :].astype(f32),

time: 601 us -> 575 us (0.957)
  matrix products: 115 us -> 33 us
  Pallas kernels: 97.9 us -> 144 us
  local copies, waits for them, and re-layouts: 44.8 us -> 73.8 us
  other arithmetic: 52 us -> 33.7 us
    pallas_call x1 -> x5, Pallas kernels: 2.74 us -> 56.7 us  [the longest x1 21.9 us: feed(): pl.pallas_call(feed_kernel, grid=(hidden // HIDDEN_STEP,), in_specs=[whol...]
    dot_general x6 -> x2, matrix products: 47.4 us -> 13 us  [dot(): return jnp.dot(left, right, preferred_element_type=f32)]
    dot_general x7 -> x0, matrix products: 31.8 us -> none  [dot_tn(): return lax.dot_general(left, right, TN, preferred_element_type=f32)]
    ppermute x3, waiting for transfers between devices: 49.4 us -> 80.7 us  [to_previous(): return lax.ppermute(value, 'seq', [(i + 2, i) for i in range(n_seq - 2)])]
    unnamed x186 -> x213, local copies, waits for them, and re-layouts: 35.1 us -> 59.9 us
    dot_general x6 -> x4, matrix products: 36 us -> 20 us  [dot_nt(): return lax.dot_general(left, right, NT, preferred_element_type=f32)]
    reduce_scatter x4 -> x3, waiting for transfers between devices: 19.6 us -> 6.9 us  [scatter_seq(): return lax.psum_scatter(value, 'seq', scatter_dimension=0, tiled=tiled)]
    ppermute x3, waiting for transfers between devices: 25 us -> 14.1 us  [to_next(): return lax.ppermute(value, 'seq', [(i, i + 2) for i in range(n_seq - 2)])]
  transfers between devices with their start and end apart: 56 -> 55, of which waited for: 26 -> 32; matrix products, arithmetic and copies ran while one was open for 20% -> 12% of each run, Pallas kernels for 15% -> 20%
where the time goes in v4:
time: 575 us; the launch traced here: 566 us
  waiting for transfers between devices  202 us (35%)
  Pallas kernels  144 us (25%)
  local copies, waits for them, and re-layouts  73.8 us (13%)
  starting transfers between devices  64.9 us (11%)
  other arithmetic  33.7 us (6%)
  matrix products  33 us (6%)
  between operations  15.6 us (3%)
    ppermute x3, waiting for transfers between devices, to_previous(): return lax.ppermute(value, 'seq', [(i + 2, i) for i in range(n_seq - 2)])  80.7 us
    ppermute x31, waiting for transfers between devices, across(): return lax.ppermute(value, 'head', [(i, i ^ bits) for i in range(n_head)])  76.1 us
    unnamed x213, local copies, waits for them, and re-layouts  59.9 us
    ppermute x31, starting transfers between devices, across(): return lax.ppermute(value, 'head', [(i, i ^ bits) for i in range(n_head)])  32.9 us
    pallas_call x8, Pallas kernels, attend_back(): pl.pallas_call(functools.partial(attend_back_kernel, first=first, group=g...  25.9 us
    ppermute x5, waiting for transfers between devices, body(): lax.ppermute(gains, axis, [(i, i ^ bit) for i in range(size)])  22.3 us
    pallas_call x1, Pallas kernels, feed(): pl.pallas_call(feed_kernel, grid=(hidden // HIDDEN_STEP,), in_specs=[whol...  21.9 us
    dot_general x4, matrix products, dot_nt(): return lax.dot_general(left, right, NT, preferred_element_type=f32)  20 us
  transfers between devices with their start and end apart: 55, of which 32 were waited for; matrix products, arithmetic and copies ran while one was open for 12% of the time, Pallas kernels for 20%

profile of v4, /device:TPU:0, one launch (start us, length us, event | category | flops | bytes accessed | tf_op | source)
XLA Modules:
  0.0 566.3 jit_solution(13123521054222532686)
XLA Ops:
  23.5 5.4 collective-permute-start
  50.0 9.7 %fusion.30.d_mixed_ref = f32[768,1536]{1,0:T(8,128)} fusion(bf16[768,2048]{1,0:T(8,128)(2,1)} %dy_ref.1, bf16[1536,2048]{1,0:T(8,128)(2,1)} %param.32), kind=kOutput, calls=%fused_computation.114 | convolution fusion | flops 4831838208 | bytes 14155776 | tf_op jit(solution)/shard_map/dot_general | solution.py:35
  59.7 5.9 %attend_stage.4 = (f32[768,512]{1,0:T(8,128)S(1)}, f32[768,512]{1,0:T(8,128)S(1)}) custom-call(s32[4]{0:T(128)S(1)} %copy-done.82, bf16[768,1024]{1,0:T(8,128)(2,1)S(1)} %copy-done.13, bf16[768,512]{1,0:T(8,128)(2,1)S(1)} %copy-done.46, bf16[768,512]{1,0:T(8,128)(2,1)} %collective-permute-done.2.kvb_ref.kv_ref, s32[8,128]{1,0:T(8,128)S(1)} %copy-done.78), custom_call_target="tpu_custom_call" | custom-call | flops 1 | bytes 1 | tf_op jit(solution)/shard_map/attend_stage/pallas_call | solution.py:308
  81.4 9.0 %collective-permute-done.3.kva_ref.kv_ref = bf16[768,512]{1,0:T(8,128)(2,1)S(1)} collective-permute-done((bf16[768,512]{1,0:T(8,128)(2,1)S(1)}, bf16[768,512]{1,0:T(8,128)(2,1)S(1)}, u32[]{:S(2)}, u32[]{:S(2)}) %collective-permute-start.3) | collective-permute-done | bytes 786464 | tf_op jit(solution)/shard_map/ppermute | solution.py:750
  108.9 16.8 %collective-permute-done.9.refs_2_ = bf16[768,512]{1,0:T(8,128)(2,1)S(1)} collective-permute-done((bf16[768,512]{1,0:T(8,128)(2,1)S(1)}, bf16[768,512]{1,0:T(8,128)(2,1)S(1)}, u32[]{:S(2)}, u32[]{:S(2)}) %collective-permute-start.9) | collective-permute-done | bytes 786464 | tf_op jit(solution)/shard_map/ppermute | solution.py:756
  135.6 10.5 %project.2.base_ref = f32[768,2048]{1,0:T(8,128)} custom-call(s32[5]{0:T(128)S(1)} %stack.110.meta, bf16[768,2048]{1,0:T(8,128)(2,1)S(1)} %copy-done.8, bf16[768,512]{1,0:T(8,128)(2,1)S(1)} %get-tuple-element.161.refs_0_.o_ref, bf16[768,512]{1,0:T(8,128)(2,1)S(1)} %copy-done.73, bf16[768,512]{1,0:T(8,128)(2,1)S(1)} %copy-done.71, ...), custom_call_target="tpu_custom_call" | custom-call | flops 1 | bytes 1 | tf_op jit(solution)/shard_map/project/pallas_call | solution.py:553
  150.1 5.4 project.3
  156.6 21.9 %feed.1 = (bf16[768,1536]{1,0:T(8,128)(2,1)S(1)}, bf16[768,1536]{1,0:T(8,128)(2,1)S(1)}, bf16[768,1536]{1,0:T(8,128)(2,1)S(1)}, bf16[8,1536,256]{2,1,0:T(8,128)(2,1)}) custom-call(bf16[768,2048]{1,0:T(8,128)(2,1)S(1)} %get-tuple-element.167.x_ref, bf16[2048,1536]{1,0:T(8,128)(2,1)} %gate_w_ref.3, bf16[2048,1536]{1,0:T(8,128)(2,1)} %up_w_ref.3, ...), custom_call_target="tpu_custom_call" | custom-call | flops 1 | bytes 1 | tf_op jit(solution)/shard_map/feed/pallas_call | solution.py:621
  189.5 12.1 %feed_back.1 = bf16[768,2048]{1,0:T(8,128)(2,1)S(1)} custom-call(bf16[768,1536]{1,0:T(8,128)(2,1)S(1)} %copy-done.31, bf16[768,1536]{1,0:T(8,128)(2,1)S(1)} %copy-done.34, bf16[2048,1536]{1,0:T(8,128)(2,1)S(1)} %copy-done.17, bf16[2048,1536]{1,0:T(8,128)(2,1)} %up_w_ref.3), custom_call_target="tpu_custom_call" | custom-call | flops 1 | bytes 1 | tf_op jit(solution)/shard_map/feed_back/pallas_call | solution.py:651
  209.8 11.8 %feed_sums.1 = bf16[2048,3072]{1,0:T(8,128)(2,1)S(1)} custom-call(bf16[768,2048]{1,0:T(8,128)(2,1)S(1)} %copy-done.27, bf16[768,1536]{1,0:T(8,128)(2,1)S(1)} %copy-done.32, bf16[768,1536]{1,0:T(8,128)(2,1)S(1)} %copy-done.35), custom_call_target="tpu_custom_call" | custom-call | flops 1 | bytes 1 | tf_op jit(solution)/shard_map/feed_sums/pallas_call | solution.py:675
  233.9 5.6 collective-permute-done.14
  268.9 7.9 %convolution_convert_fusion = bf16[768,2048]{1,0:T(8,128)(2,1)S(1)} fusion(bf16[768,1536]{1,0:T(8,128)(2,1)} %copy-done.84, bf16[1536,2048]{1,0:T(8,128)(2,1)} %param.32), kind=kOutput, calls=%fused_computation.6 | convolution fusion | flops 4833411072 | bytes 11796480 | tf_op jit(solution)/shard_map/dot_general | solution.py:31
  295.1 10.2 %collective-permute-done.23 = bf16[2,96,2048]{2,1,0:T(8,128)(2,1)S(1)} collective-permute-done((bf16[2,96,2048]{2,1,0:T(8,128)(2,1)S(1)}, bf16[2,96,2048]{2,1,0:T(8,128)(2,1)S(1)}, u32[]{:S(2)}, u32[]{:S(2)}) %collective-permute-start.23) | collective-permute-done | bytes 786464 | tf_op jit(solution)/shard_map/ppermute | solution.py:756
  326.2 32.5 %collective-permute-done.35 = bf16[768,512]{1,0:T(8,128)(2,1)S(1)} collective-permute-done((bf16[768,512]{1,0:T(8,128)(2,1)S(1)}, bf16[768,512]{1,0:T(8,128)(2,1)S(1)}, u32[]{:S(2)}, u32[]{:S(2)}) %collective-permute-start.35) | collective-permute-done | bytes 786464 | tf_op jit(solution)/shard_map/ppermute | solution.py:753
  364.6 6.7 %collective-permute-start.31 = (bf16[768,512]{1,0:T(8,128)(2,1)}, bf16[768,512]{1,0:T(8,128)(2,1)}, u32[]{:S(2)}, u32[]{:S(2)}) collective-permute-start(bf16[768,512]{1,0:T(8,128)(2,1)} %get-tuple-element.208), channel_id=1, source_target_pairs={{0,4},{4,0},{8,12},{12,8},{16,20},{20,16},{24,28},{28,24},{1,5},{5... | collective-permute-start | bytes 2359304 | tf_op jit(solution)/shard_map/ppermute | solution.py:747
  371.3 8.3 %attend_back.15 = (f32[768,512]{1,0:T(8,128)S(1)}, f32[768,512]{1,0:T(8,128)S(1)}) custom-call(s32[4]{0:T(128)S(1)} %copy-done.82, bf16[768,1024]{1,0:T(8,128)(2,1)S(1)} %copy-done.5, bf16[768,1024]{1,0:T(8,128)(2,1)S(1)} %copy-done.1, bf16[768,512]{1,0:T(8,128)(2,1)S(1)} %copy-done.47, s32[8,128]{1,0:T(8,128)S(1)} %copy-done.78, ...), custom_call_target="tpu_custom_call", output_to_operand_aliasing={{0}: (5, {})} | custom-call | flops 1 | bytes 1 | tf_op jit(solution)/shard_map/attend_back/pallas_call | solution.py:470
  379.7 21.2 %collective-permute-done.36 = bf16[768,512]{1,0:T(8,128)(2,1)S(1)} collective-permute-done((bf16[768,512]{1,0:T(8,128)(2,1)S(1)}, bf16[768,512]{1,0:T(8,128)(2,1)S(1)}, u32[]{:S(2)}, u32[]{:S(2)}) %collective-permute-start.36) | collective-permute-done | bytes 786464 | tf_op jit(solution)/shard_map/ppermute | solution.py:753
  406.4 5.4 collective-permute-done.30
  417.6 5.8 %fusion.31 = f32[768,2048]{1,0:T(8,128)} fusion(bf16[768,512]{1,0:T(8,128)(2,1)} %get-tuple-element.205.q_ref, bf16[2048,512]{1,0:T(8,128)(2,1)S(1)} %copy-done), kind=kOutput, calls=%fused_computation.115 | convolution fusion | flops 1610612736 | bytes 9175040 | tf_op jit(solution)/shard_map/dot_general | solution.py:35
  423.4 27.0 %collective-permute-done.37 = bf16[768,512]{1,0:T(8,128)(2,1)} collective-permute-done((bf16[768,512]{1,0:T(8,128)(2,1)}, bf16[768,512]{1,0:T(8,128)(2,1)}, u32[]{:S(2)}, u32[]{:S(2)}) %collective-permute-start.37) | collective-permute-done | bytes 786464 | tf_op jit(solution)/shard_map/ppermute | solution.py:753
  471.7 7.5 %attn_sums.1 = bf16[8,384,1024]{2,1,0:T(8,128)(2,1)S(1)} custom-call(bf16[768,2048]{1,0:T(8,128)(2,1)S(1)} %copy-done.42, bf16[768,512]{1,0:T(8,128)(2,1)S(1)} %copy-done.40, bf16[768,256]{1,0:T(8,128)(2,1)S(1)} %copy-done.76, bf16[768,256]{1,0:T(8,128)(2,1)S(1)} %pad_maximum_fusion.8.v_ref, bf16[768,512]{1,0:T(8,128)(2,1)S(1)} %copy-done.44, ...), custom_call_target="tpu_custom_call" | custom-call | flops 1 | bytes 1 | tf_op jit(solution)/shard_map/attn_sums/pallas_call | solution.py:721
  493.7 5.6 collective-permute-done.40
  506.7 14.5 %collective-permute-done.46 = f32[34,128]{1,0:T(8,128)S(1)} collective-permute-done((f32[34,128]{1,0:T(8,128)S(1)}, f32[34,128]{1,0:T(8,128)S(1)}, u32[]{:S(2)}, u32[]{:S(2)}) %collective-permute-start.46) | collective-permute-done | bytes 17440 | tf_op jit(solution)/shard_map/ppermute | solution.py:1058
  548.6 6.9 %reduce-scatter.8.cloned.1.call-done = bf16[1,384,1024]{2,1,0:T(8,128)(2,1)} async-done(((bf16[8,384,1024]{2,1,0:T(8,128)(2,1)}), bf16[1,384,1024]{2,1,0:T(8,128)(2,1)}) %reduce-scatter.8.cloned.1.call-update) | async-done | bytes 786448 | tf_op jit(solution)/shard_map/reduce_scatter | solution.py:916
  (430 shorter events, 277.3 us)
Async XLA Ops:
  7.2 86.4 %all-gather.3.cloned.1.call-start = ((), (), s32[]{:S(2)}) async-start(), calls=%async_computation.6 | async-start | bytes 5242880 | tf_op jit(solution)/shard_map/all_gather | solution.py:867
  22.9 244.6 %reduce-scatter.4.cloned.1.call-start = ((), (), s32[]{:S(2)}) async-start(), calls=%async_computation.3 | async-start | bytes 7077888 | tf_op jit(solution)/shard_map/reduce_scatter | solution.py:916
  23.0 36.7 %collective-permute-start.2 = (bf16[768,512]{1,0:T(8,128)(2,1)S(1)}, bf16[768,512]{1,0:T(8,128)(2,1)}, u32[]{:S(2)}, u32[]{:S(2)}) collective-permute-start(bf16[768,512]{1,0:T(8,128)(2,1)S(1)} %copy-done.46), channel_id=1, source_target_pairs={{0,4},{4,0},{8,12},{12,8},{16,20},{20,16},{24,28},{28,24},{1,5},{5... | collective-permute-start | bytes 2359304 | tf_op jit(solution)/shard_map/ppermute | solution.py:747
  23.5 21.9 %collective-permute-start = (bf16[768,512]{1,0:T(8,128)(2,1)S(1)}, bf16[768,512]{1,0:T(8,128)(2,1)}, u32[]{:S(2)}, u32[]{:S(2)}) collective-permute-start(bf16[768,512]{1,0:T(8,128)(2,1)S(1)} %copy-done.46), channel_id=1, source_target_pairs={{0,8},{4,12},{8,16},{12,20},{16,24},{20,28},{1,9},{5,13},{9,17},{1... | collective-permute-start | bytes 2359304 | tf_op jit(solution)/shard_map/ppermute | solution.py:750
  45.4 21.5 %collective-permute-start.1 = (bf16[768,512]{1,0:T(8,128)(2,1)}, bf16[768,512]{1,0:T(8,128)(2,1)S(1)}, u32[]{:S(2)}, u32[]{:S(2)}) collective-permute-start(bf16[768,512]{1,0:T(8,128)(2,1)} %collective-permute-done.kva_ref.kv_ref), channel_id=1, source_target_pairs={{0,8},{4,12},{8,16},{12,20},{16,24},{20,28},{1,9},{5,13},{9,17},{1... | collective-permute-start | bytes 2359304 | tf_op jit(solution)/shard_map/ppermute | solution.py:750
  93.6 37.8 %collective-permute-start.11 = (bf16[4,256,2048]{2,1,0:T(8,128)(2,1)}, bf16[4,256,2048]{2,1,0:T(8,128)(2,1)}, u32[]{:S(2)}, u32[]{:S(2)}) collective-permute-start(bf16[4,256,2048]{2,1,0:T(8,128)(2,1)} %bitcast.147), channel_id=1, source_target_pairs={{0,4},{4,0},{8,12},{12,8},{16,20},{20,16},{24,28},{28,24},{1,5},{5... | collective-permute-start | bytes 12582920 | tf_op jit(solution)/shard_map/ppermute | solution.py:747
  107.3 20.7 %collective-permute-start.7 = (bf16[768,512]{1,0:T(8,128)(2,1)S(1)}, bf16[768,512]{1,0:T(8,128)(2,1)S(1)}, u32[]{:S(2)}, u32[]{:S(2)}) collective-permute-start(bf16[768,512]{1,0:T(8,128)(2,1)S(1)} %get-tuple-element.161.refs_0_.o_ref), channel_id=1, source_target_pairs={{0,1},{1,0},{2,3},{3,2},{4,5},{5,4},{6,7},{7,6},{8,9},{9,8},{10,11... | collective-permute-start | bytes 2359304 | tf_op jit(solution)/shard_map/ppermute | solution.py:756
  182.9 303.8 %reduce-scatter.6.cloned.1.call-start = ((), (), s32[]{:S(2)}) async-start(), calls=%async_computation.4 | async-start | bytes 14155776 | tf_op jit(solution)/shard_map/reduce_scatter | solution.py:916
  202.2 25.7 %collective-permute-start.12 = (bf16[2,96,2048]{2,1,0:T(8,128)(2,1)S(1)}, bf16[2,96,2048]{2,1,0:T(8,128)(2,1)}, u32[]{:S(2)}, u32[]{:S(2)}) collective-permute-start(bf16[2,96,2048]{2,1,0:T(8,128)(2,1)S(1)} %dynamic-slice_bitcast_fusion.5), channel_id=1, source_target_pairs={{0,1},{1,0},{2,3},{3,2},{4,5},{5,4},{6,7},{7,6},{8,9},{9,8},{10,11... | collective-permute-start | bytes 2359304 | tf_op jit(solution)/shard_map/ppermute | solution.py:756
  204.0 23.9 %collective-permute-start.13 = (bf16[2,96,2048]{2,1,0:T(8,128)(2,1)}, bf16[2,96,2048]{2,1,0:T(8,128)(2,1)}, u32[]{:S(2)}, u32[]{:S(2)}) collective-permute-start(bf16[2,96,2048]{2,1,0:T(8,128)(2,1)} %dynamic-slice_bitcast_fusion.4), channel_id=1, source_target_pairs={{0,2},{1,3},{2,0},{3,1},{4,6},{5,7},{6,4},{7,5},{8,10},{9,11},{10,... | collective-permute-start | bytes 2359304 | tf_op jit(solution)/shard_map/ppermute | solution.py:756
  267.6 287.9 %reduce-scatter.8.cloned.1.call-start = ((), (), s32[]{:S(2)}) async-start(), calls=%async_computation.5 | async-start | bytes 7077888 | tf_op jit(solution)/shard_map/reduce_scatter | solution.py:916
  277.4 27.8 %collective-permute-start.23 = (bf16[2,96,2048]{2,1,0:T(8,128)(2,1)S(1)}, bf16[2,96,2048]{2,1,0:T(8,128)(2,1)S(1)}, u32[]{:S(2)}, u32[]{:S(2)}) collective-permute-start(bf16[2,96,2048]{2,1,0:T(8,128)(2,1)S(1)} %dynamic-slice_bitcast_fusion.3), channel_id=1, source_target_pairs={{0,1},{1,0},{2,3},{3,2},{4,5},{5,4},{6,7},{7,6},{8,9},{9,8},{10,11... | collective-permute-start | bytes 2359304 | tf_op jit(solution)/shard_map/ppermute | solution.py:756
  278.8 26.4 %collective-permute-start.24 = (bf16[2,96,2048]{2,1,0:T(8,128)(2,1)S(1)}, bf16[2,96,2048]{2,1,0:T(8,128)(2,1)S(1)}, u32[]{:S(2)}, u32[]{:S(2)}) collective-permute-start(bf16[2,96,2048]{2,1,0:T(8,128)(2,1)S(1)} %dynamic-slice_bitcast_fusion.2), channel_id=1, source_target_pairs={{0,2},{1,3},{2,0},{3,1},{4,6},{5,7},{6,4},{7,5},{8,10},{9,11},{10,... | collective-permute-start | bytes 2359304 | tf_op jit(solution)/shard_map/ppermute | solution.py:756
  290.7 22.0 %collective-permute-start.34 = (bf16[768,512]{1,0:T(8,128)(2,1)S(1)}, bf16[768,512]{1,0:T(8,128)(2,1)S(1)}, u32[]{:S(2)}, u32[]{:S(2)}) collective-permute-start(bf16[768,512]{1,0:T(8,128)(2,1)S(1)} %get-tuple-element.214), channel_id=1, source_target_pairs={{0,4},{4,0},{8,12},{12,8},{16,20},{20,16},{24,28},{28,24},{1,5},{5... | collective-permute-start | bytes 2359304 | tf_op jit(solution)/shard_map/ppermute | solution.py:747
  312.7 46.0 %collective-permute-start.33 = (bf16[768,512]{1,0:T(8,128)(2,1)S(1)}, bf16[768,512]{1,0:T(8,128)(2,1)S(1)}, u32[]{:S(2)}, u32[]{:S(2)}) collective-permute-start(bf16[768,512]{1,0:T(8,128)(2,1)S(1)} %get-tuple-element.212), channel_id=1, source_target_pairs={{0,4},{4,0},{8,12},{12,8},{16,20},{20,16},{24,28},{28,24},{1,5},{5... | collective-permute-start | bytes 2359304 | tf_op jit(solution)/shard_map/ppermute | solution.py:747
  312.9 45.7 %collective-permute-start.35 = (bf16[768,512]{1,0:T(8,128)(2,1)S(1)}, bf16[768,512]{1,0:T(8,128)(2,1)S(1)}, u32[]{:S(2)}, u32[]{:S(2)}) collective-permute-start(bf16[768,512]{1,0:T(8,128)(2,1)S(1)} %add_convert_fusion.3), channel_id=1, source_target_pairs={{8,0},{12,4},{16,8},{20,12},{24,16},{28,20},{9,1},{13,5},{17,9},{2... | collective-permute-start | bytes 2359304 | tf_op jit(solution)/shard_map/ppermute | solution.py:753
  321.9 49.4 %collective-permute-start.28 = (bf16[192,2048]{1,0:T(8,128)(2,1)S(1)}, bf16[192,2048]{1,0:T(8,128)(2,1)S(1)}, u32[]{:S(2)}, u32[]{:S(2)}) collective-permute-start(bf16[192,2048]{1,0:T(8,128)(2,1)S(1)} %fusion.11.refs_0_), channel_id=1, source_target_pairs={{0,2},{1,3},{2,0},{3,1},{4,6},{5,7},{6,4},{7,5},{8,10},{9,11},{10,... | collective-permute-start | bytes 2359304 | tf_op jit(solution)/shard_map/ppermute | solution.py:756
  322.2 49.1 %collective-permute-start.27 = (bf16[192,2048]{1,0:T(8,128)(2,1)S(1)}, bf16[192,2048]{1,0:T(8,128)(2,1)S(1)}, u32[]{:S(2)}, u32[]{:S(2)}) collective-permute-start(bf16[192,2048]{1,0:T(8,128)(2,1)S(1)} %fusion.11.refs_0_), channel_id=1, source_target_pairs={{0,1},{1,0},{2,3},{3,2},{4,5},{5,4},{6,7},{7,6},{8,9},{9,8},{10,11... | collective-permute-start | bytes 2359304 | tf_op jit(solution)/shard_map/ppermute | solution.py:756
  359.0 41.9 %collective-permute-start.36 = (bf16[768,512]{1,0:T(8,128)(2,1)S(1)}, bf16[768,512]{1,0:T(8,128)(2,1)S(1)}, u32[]{:S(2)}, u32[]{:S(2)}) collective-permute-start(bf16[768,512]{1,0:T(8,128)(2,1)S(1)} %add_convert_fusion.2), channel_id=1, source_target_pairs={{8,0},{12,4},{16,8},{20,12},{24,16},{28,20},{9,1},{13,5},{17,9},{2... | collective-permute-start | bytes 2359304 | tf_op jit(solution)/shard_map/ppermute | solution.py:753
  360.3 42.6 %collective-permute-start.32 = (bf16[768,512]{1,0:T(8,128)(2,1)S(1)}, bf16[768,512]{1,0:T(8,128)(2,1)S(1)}, u32[]{:S(2)}, u32[]{:S(2)}) collective-permute-start(bf16[768,512]{1,0:T(8,128)(2,1)S(1)} %get-tuple-element.210), channel_id=1, source_target_pairs={{0,4},{4,0},{8,12},{12,8},{16,20},{20,16},{24,28},{28,24},{1,5},{5... | collective-permute-start | bytes 2359304 | tf_op jit(solution)/shard_map/ppermute | solution.py:747
  364.6 58.8 %collective-permute-start.31 = (bf16[768,512]{1,0:T(8,128)(2,1)}, bf16[768,512]{1,0:T(8,128)(2,1)}, u32[]{:S(2)}, u32[]{:S(2)}) collective-permute-start(bf16[768,512]{1,0:T(8,128)(2,1)} %get-tuple-element.208), channel_id=1, source_target_pairs={{0,4},{4,0},{8,12},{12,8},{16,20},{20,16},{24,28},{28,24},{1,5},{5... | collective-permute-start | bytes 2359304 | tf_op jit(solution)/shard_map/ppermute | solution.py:747
  404.1 46.2 %collective-permute-start.37 = (bf16[768,512]{1,0:T(8,128)(2,1)}, bf16[768,512]{1,0:T(8,128)(2,1)}, u32[]{:S(2)}, u32[]{:S(2)}) collective-permute-start(bf16[768,512]{1,0:T(8,128)(2,1)} %add_convert_fusion.1), channel_id=1, source_target_pairs={{8,0},{12,4},{16,8},{20,12},{24,16},{28,20},{9,1},{13,5},{17,9},{2... | collective-permute-start | bytes 2359304 | tf_op jit(solution)/shard_map/ppermute | solution.py:753
  503.9 26.9 %collective-permute-start.43 = (bf16[192,2048]{1,0:T(8,128)(2,1)S(1)}, bf16[192,2048]{1,0:T(8,128)(2,1)S(1)}, u32[]{:S(2)}, u32[]{:S(2)}) collective-permute-start(bf16[192,2048]{1,0:T(8,128)(2,1)S(1)} %fusion.9.refs_0_), channel_id=1, source_target_pairs={{0,2},{1,3},{2,0},{3,1},{4,6},{5,7},{6,4},{7,5},{8,10},{9,11},{10,... | collective-permute-start | bytes 2359304 | tf_op jit(solution)/shard_map/ppermute | solution.py:756
  504.6 27.3 %collective-permute-start.42 = (bf16[192,2048]{1,0:T(8,128)(2,1)S(1)}, bf16[192,2048]{1,0:T(8,128)(2,1)S(1)}, u32[]{:S(2)}, u32[]{:S(2)}) collective-permute-start(bf16[192,2048]{1,0:T(8,128)(2,1)S(1)} %fusion.9.refs_0_), channel_id=1, source_target_pairs={{0,1},{1,0},{2,3},{3,2},{4,5},{5,4},{6,7},{7,6},{8,9},{9,8},{10,11... | collective-permute-start | bytes 2359304 | tf_op jit(solution)/shard_map/ppermute | solution.py:756
  (137 other events, 955.8 us)
Sparse Core Ops, SparseCore 0:
  23.1 55.3 all-gather.2
  183.1 78.1 reduce-scatter.3
  267.7 187.4 reduce-scatter.5
  486.8 68.6 reduce-scatter.7

commit v5 on v4

v5 whole, which is shorter than its diff:
```python
import functools
import math

import jax
import jax.numpy as jnp
from jax import lax
from jax.experimental import pallas as pl
from jax.experimental.pallas import tpu as pltpu
from jax.sharding import PartitionSpec as P

HEAD_WIDTH = 128
EPSILON = 1e-06
ROPE_BASE = 1000000.0
LOG2E = math.log2(math.e)
SCORE_SCALE = 1.0 / math.sqrt(HEAD_WIDTH)
SCORE_SCALE_2 = LOG2E / math.sqrt(HEAD_WIDTH)
KEY_CHUNK = 256
HIDDEN_STEP = 256
FAR = 512.0
LOG_LANE = 64
MIB = 2**20
SMALL = pl.CostEstimate(flops=1, bytes_accessed=1, transcendentals=0)
WHOLE_VMEM = pltpu.CompilerParams(vmem_limit_bytes=60 * MIB)

f32 = jnp.float32
bf16 = jnp.bfloat16
NT = (((1,), (1,)), ((), ()))
TN = (((0,), (0,)), ((), ()))


def dot(left, right):
    return jnp.dot(left, right, preferred_element_type=f32)


def dot_nt(left, right):
    return lax.dot_general(left, right, NT, preferred_element_type=f32)


def dot_tn(left, right):
    return lax.dot_general(left, right, TN, preferred_element_type=f32)


def locate(index, lengths):
    ends = jnp.cumsum(lengths)
    starts = ends - lengths
    segment = jnp.sum((index[:, None] >= ends[None, :]).astype(jnp.int32), axis=1)
    chosen = segment[:, None] == jnp.arange(lengths.shape[0], dtype=jnp.int32)[None, :]
    return jnp.sum(jnp.where(chosen, starts[None, :], 0), axis=1)


def rotary(position):
    half = HEAD_WIDTH // 2
    freq = jnp.exp(jnp.arange(half, dtype=f32) * (-2.0 * math.log(ROPE_BASE) / HEAD_WIDTH))
    angle = position.astype(f32)[:, None] * freq[None, :]
    cosine = jnp.cos(angle)
    sine = jnp.sin(angle)
    return (
        jnp.concatenate([cosine, cosine], axis=1),
        jnp.concatenate([-sine, sine], axis=1),
    )


def lane_index(rows):
    return lax.broadcasted_iota(jnp.int32, (rows, HEAD_WIDTH), 1)


def row_index(rows):
    return lax.broadcasted_iota(jnp.int32, (rows, HEAD_WIDTH), 0)


def in_segment(index, bounds_ref):
    return (index >= bounds_ref[0:1, :]) & (index < bounds_ref[1:2, :])


def split_parts(value):
    high = value.astype(bf16)
    rest = value - high.astype(f32)
    middle = rest.astype(bf16)
    return high, middle, (rest - middle.astype(f32)).astype(bf16)


def normed(raw, gain, cosine, sine):
    inverse = lax.rsqrt(jnp.mean(raw * raw, axis=-1, keepdims=True) + EPSILON)
    scaled = raw * inverse * gain
    return scaled * cosine + pltpu.roll(scaled, HEAD_WIDTH // 2, 1) * sine


def enter_kernel(
    x_ref, gain_ref, key_w_ref, value_w_ref, key_gain_ref, cos_ref, sin_ref, in_ref, raw_ref, kv_ref
):
    x = x_ref[...].astype(f32)
    inverse = lax.rsqrt(jnp.mean(x * x, axis=-1, keepdims=True) + EPSILON)
    first_in = (x * inverse * gain_ref[...]).astype(bf16)
    in_ref[...] = first_in
    raw = dot(first_in, key_w_ref[...])
    raw_ref[...] = raw
    value = dot(first_in, value_w_ref[...]).astype(bf16)
    for j in range(raw.shape[1] // HEAD_WIDTH):
        head = slice(j * HEAD_WIDTH, (j + 1) * HEAD_WIDTH)
        key = normed(raw[:, head], key_gain_ref[...], cos_ref[...], sin_ref[...])
        start = 2 * j * HEAD_WIDTH
        kv_ref[:, start : start + HEAD_WIDTH] = key.astype(bf16)
        kv_ref[:, start + HEAD_WIDTH : start + 2 * HEAD_WIDTH] = value[:, head]


def enter(tokens, gain, key_w, value_w, key_gain, cosine, sine):
    rows, width = tokens.shape
    kv_width = key_w.shape[1]
    step = rows // 3 if rows % 768 == 0 else rows
    table = pl.BlockSpec((step, HEAD_WIDTH), lambda i: (i, 0))
    weight = pl.BlockSpec((width, kv_width), lambda i: (0, 0))
    return pl.pallas_call(
        enter_kernel,
        grid=(rows // step,),
        in_specs=[
            pl.BlockSpec((step, width), lambda i: (i, 0)),
            pl.BlockSpec((1, width), lambda i: (0, 0)),
            weight,
            weight,
            pl.BlockSpec((1, HEAD_WIDTH), lambda i: (0, 0)),
            table,
            table,
        ],
        out_specs=[
            pl.BlockSpec((step, width), lambda i: (i, 0)),
            pl.BlockSpec((step, kv_width), lambda i: (i, 0)),
            pl.BlockSpec((step, 2 * kv_width), lambda i: (i, 0)),
        ],
        out_shape=[
            jax.ShapeDtypeStruct((rows, width), bf16),
            jax.ShapeDtypeStruct((rows, kv_width), f32),
            jax.ShapeDtypeStruct((rows, 2 * kv_width), bf16),
        ],
        compiler_params=WHOLE_VMEM,
        cost_estimate=SMALL,
        name="enter",
    )(tokens, gain[None, :], key_w, value_w, key_gain[None, :], cosine, sine)


def query_prep_kernel(meta, raw_ref, gain_ref, cos_ref, sin_ref, bounds_ref, out_ref):
    rows = raw_ref.shape[0]
    query = normed(raw_ref[...], gain_ref[...], cos_ref[...], sin_ref[...])
    out_ref[:, :HEAD_WIDTH] = (query * SCORE_SCALE_2).astype(bf16)
    inside = in_segment(meta[0] + row_index(rows), bounds_ref)
    free = inside | (lane_index(rows) >= LOG_LANE)
    out_ref[:, HEAD_WIDTH:] = jnp.where(free, 0.0, -FAR).astype(bf16)


def query_prep(meta, raw, gain, cosine, sine, bounds):
    rows, width = raw.shape
    table = pl.BlockSpec((rows, HEAD_WIDTH), lambda j, m: (0, 0))
    return pl.pallas_call(
        query_prep_kernel,
        grid_spec=pltpu.PrefetchScalarGridSpec(
            num_scalar_prefetch=1,
            grid=(width // HEAD_WIDTH,),
            in_specs=[
                pl.BlockSpec((rows, HEAD_WIDTH), lambda j, m: (0, j)),
                pl.BlockSpec((1, HEAD_WIDTH), lambda j, m: (0, 0)),
                table,
                table,
                pl.BlockSpec((8, HEAD_WIDTH), lambda j, m: (0, 0)),
            ],
            out_specs=pl.BlockSpec((rows, 2 * HEAD_WIDTH), lambda j, m: (0, j)),
        ),
        out_shape=jax.ShapeDtypeStruct((rows, 2 * width), bf16),
        compiler_params=WHOLE_VMEM,
        cost_estimate=SMALL,
        name="query_prep",
    )(meta, raw, gain[None, :], cosine, sine, bounds)


def head_backward(raw, grad, gain, cosine, sine):
    inverse = lax.rsqrt(jnp.mean(raw * raw, axis=-1, keepdims=True) + EPSILON)
    hat = raw * inverse
    back = grad * cosine - pltpu.roll(grad, HEAD_WIDTH // 2, 1) * sine
    gain_grad = jnp.sum(back * hat, axis=0, keepdims=True)
    back = back * gain
    back = inverse * (back - hat * jnp.mean(back * hat, axis=-1, keepdims=True))
    return back.astype(bf16), gain_grad


def head_back_kernel(raw_ref, grad_ref, gain_ref, cos_ref, sin_ref, out_ref, gain_grad_ref, *, scale):
    @pl.when(pl.program_id(0) == 0)
    def _():
        gain_grad_ref[...] = jnp.zeros_like(gain_grad_ref)

    out_ref[...], gain_grad = head_backward(
        raw_ref[...], grad_ref[...] * scale, gain_ref[...], cos_ref[...], sin_ref[...]
    )
    gain_grad_ref[...] += gain_grad


def head_back(raw, grad, gain, cosine, sine, scale, stride):
    rows, width = raw.shape
    block = pl.BlockSpec((rows, HEAD_WIDTH), lambda j: (0, j))
    spaced = pl.BlockSpec((rows, HEAD_WIDTH), lambda j: (0, j * stride))
    table = pl.BlockSpec((rows, HEAD_WIDTH), lambda j: (0, 0))
    one = pl.BlockSpec((1, HEAD_WIDTH), lambda j: (0, 0))
    return pl.pallas_call(
        functools.partial(head_back_kernel, scale=scale),
        grid=(width // HEAD_WIDTH,),
        in_specs=[block, spaced, one, table, table],
        out_specs=[block, one],
        out_shape=[
            jax.ShapeDtypeStruct((rows, width), bf16),
            jax.ShapeDtypeStruct((1, HEAD_WIDTH), f32),
        ],
        compiler_params=WHOLE_VMEM,
        cost_estimate=SMALL,
        name="head_back",
    )(raw, grad, gain[None, :], cosine, sine)


def key_lanes(meta, key_start, rows, bounds_ref):
    inside = in_segment(key_start + row_index(rows), bounds_ref)
    lanes = lane_index(rows)
    log_lanes = (lanes >= LOG_LANE) & (lanes < LOG_LANE + 3)
    return jnp.where(inside | log_lanes, 1.0, 0.0).astype(bf16)


def block_used(meta, key_start, key_rows, rows):
    return (
        (key_start >= 0) & (key_start <= meta[0] + rows - 1) & (key_start + key_rows - 1 >= meta[1])
    )


def lower_mask(transposed):
    shape = (KEY_CHUNK, KEY_CHUNK)
    first = lax.broadcasted_iota(jnp.int32, shape, 0)
    second = lax.broadcasted_iota(jnp.int32, shape, 1)
    return first <= second if transposed else second <= first


def chunk(i, n=1):
    return slice(i * KEY_CHUNK, (i + n) * KEY_CHUNK)


def attend_kernel(meta, q_ref, kva_ref, kvb_ref, bounds_ref, *refs, first, last):
    rows = q_ref.shape[0]
    key_rows = kva_ref.shape[0]
    if last:
        acc_in, sum_in, o_ref, q_out_ref, acc_ref, sum_ref = refs
    elif first:
        acc_ref, sum_ref = refs
    else:
        acc_in, sum_in, acc_ref, sum_ref = refs
    if first:
        acc_ref[...] = jnp.zeros_like(acc_ref)
        sum_ref[...] = jnp.zeros_like(sum_ref)
    else:
        acc_ref[...] = acc_in[...]
        sum_ref[...] = sum_in[...]
    ones = jnp.ones((KEY_CHUNK, HEAD_WIDTH), bf16)

    def work(kv_ref, lanes, keys, queries, mask):
        key = jnp.concatenate([kv_ref[keys, :HEAD_WIDTH], lanes[keys, :]], axis=1)
        weight = jnp.exp2(dot_nt(q_ref[queries, :], key))
        if mask:
            weight = jnp.where(lower_mask(False), weight, 0.0)
        value = jnp.concatenate([kv_ref[keys, HEAD_WIDTH:], ones], axis=1)
        out = dot(weight.astype(bf16), value)
        acc_ref[queries, :] += out[:, :HEAD_WIDTH]
        sum_ref[queries, :] += out[:, HEAD_WIDTH:]

    for place, kv_ref in enumerate((kva_ref, kvb_ref)):
        key_start = meta[2 + place]
        diagonal = first and place == 0

        @pl.when(block_used(meta, key_start, key_rows, rows))
        def _():
            lanes = key_lanes(meta, key_start, key_rows, bounds_ref)
            for c in range(key_rows // KEY_CHUNK):
                if diagonal:
                    work(kv_ref, lanes, chunk(c), chunk(c), True)
                    if c + 1 < rows // KEY_CHUNK:
                        work(kv_ref, lanes, chunk(c), slice((c + 1) * KEY_CHUNK, rows), False)
                else:
                    work(kv_ref, lanes, chunk(c), slice(0, rows), False)

    if last:
        total = sum_ref[...]
        outcome = acc_ref[...] / total
        acc_ref[...] = outcome
        o_ref[...] = outcome.astype(bf16)
        lanes = lane_index(rows)
        extra = q_ref[:, HEAD_WIDTH:].astype(f32)
        for i, part in enumerate(split_parts(jnp.log2(total))):
            extra = jnp.where(lanes == LOG_LANE + i, -part.astype(f32), extra)
        q_out_ref[:, :HEAD_WIDTH] = q_ref[:, :HEAD_WIDTH]
        q_out_ref[:, HEAD_WIDTH:] = extra.astype(bf16)


def attend_stage(q, kv_a, kv_b, bounds, meta, carried, last):
    rows = q.shape[0]
    key_rows = kv_a.shape[0]
    q_heads = q.shape[1] // (2 * HEAD_WIDTH)
    group = q.shape[1] // kv_a.shape[1]
    width = q_heads * HEAD_WIDTH
    first = not carried
    wide = 2 * HEAD_WIDTH
    per_q = pl.BlockSpec((rows, wide), lambda j, m: (0, j))
    per_kv = pl.BlockSpec((key_rows, wide), lambda j, m: (0, j // group))
    per_out = pl.BlockSpec((rows, HEAD_WIDTH), lambda j, m: (0, j))
    table = pl.BlockSpec((8, HEAD_WIDTH), lambda j, m: (0, 0))
    running = jax.ShapeDtypeStruct((rows, width), f32)
    if last:
        out_specs = [per_out, per_q, per_out]
        out_shape = [jax.ShapeDtypeStruct((rows, width), bf16), jax.ShapeDtypeStruct(q.shape, bf16), running]
        scratch = [pltpu.VMEM((rows, HEAD_WIDTH), f32)]
        aliases = {5: 2}
    else:
        out_specs = [per_out, per_out]
        out_shape = [running, running]
        scratch = []
        aliases = {} if first else {5: 0, 6: 1}
    return pl.pallas_call(
        functools.partial(attend_kernel, first=first, last=last),
        grid_spec=pltpu.PrefetchScalarGridSpec(
            num_scalar_prefetch=1,
            grid=(q_heads,),
            in_specs=[per_q, per_kv, per_kv, table] + [per_out] * len(carried),
            out_specs=out_specs,
            scratch_shapes=scratch,
        ),
        out_shape=out_shape,
        input_output_aliases=aliases,
        compiler_params=WHOLE_VMEM,
        cost_estimate=SMALL,
        name="attend_stage",
    )(meta, q, kv_a, kv_b, bounds, *carried)


def delta_kernel(owners, *refs):
    *pieces, outcome_ref, out_ref = refs
    for i, piece in enumerate(pieces):

        @pl.when(pl.program_id(0) == i)
        def _():
            rows, width = piece.shape
            lanes = lane_index(rows)
            for j in range(width // HEAD_WIDTH):
                head = slice(j * HEAD_WIDTH, (j + 1) * HEAD_WIDTH)
                do = piece[:, head]
                delta = jnp.sum(do.astype(f32) * outcome_ref[:, head], axis=-1, keepdims=True)
                extra = jnp.zeros((rows, HEAD_WIDTH), f32)
                for k, part in enumerate(split_parts(delta)):
                    extra = jnp.where(lanes == k, -part.astype(f32), extra)
                start = 2 * j * HEAD_WIDTH
                out_ref[:, start : start + HEAD_WIDTH] = do
                out_ref[:, start + HEAD_WIDTH : start + 2 * HEAD_WIDTH] = extra.astype(bf16)


def with_delta(pieces, outcome):
    owners = jnp.stack([jnp.asarray(owner, jnp.int32) for unused, owner in pieces])
    rows, width = outcome.shape
    share = rows // len(pieces)
    whole = pl.BlockSpec((share, width), lambda i, m: (0, 0))
    return pl.pallas_call(
        delta_kernel,
        grid_spec=pltpu.PrefetchScalarGridSpec(
            num_scalar_prefetch=1,
            grid=(len(pieces),),
            in_specs=[whole] * len(pieces) + [pl.BlockSpec((share, width), lambda i, m: (m[i], 0))],
            out_specs=pl.BlockSpec((share, 2 * width), lambda i, m: (m[i], 0)),
        ),
        out_shape=jax.ShapeDtypeStruct((rows, 2 * width), bf16),
        compiler_params=WHOLE_VMEM,
        cost_estimate=SMALL,
        name="with_delta",
    )(owners, *[piece for piece, unused in pieces], outcome)


def assemble_kernel(places, *refs, count):
    blocks, out_ref = refs[:count], refs[-1]
    for i, block in enumerate(blocks):

        @pl.when(pl.program_id(0) == i)
        def _():
            out_ref[...] = block[...].astype(out_ref.dtype)


def assemble(entries, rows, kind, total=None, base=None):
    places = jnp.stack([jnp.asarray(place, jnp.int32) for unused, also, place in entries])
    width = entries[0][0].shape[1]
    count = len(entries)
    in_specs = [
        pl.BlockSpec((rows, width), lambda i, m, k=block: (k, 0)) for unused, block, also in entries
    ]
    args = [array for array, unused, also in entries]
    if base is not None:
        in_specs.append(pl.BlockSpec(memory_space=pl.ANY))
        args.append(base)
    return pl.pallas_call(
        functools.partial(assemble_kernel, count=count),
        grid_spec=pltpu.PrefetchScalarGridSpec(
            num_scalar_prefetch=1,
            grid=(count,),
            in_specs=in_specs,
            out_specs=pl.BlockSpec((rows, width), lambda i, m: (m[i], 0)),
        ),
        out_shape=jax.ShapeDtypeStruct((rows * (total or count), width), kind),
        input_output_aliases={} if base is None else {1 + count: 0},
        compiler_params=WHOLE_VMEM,
        cost_estimate=SMALL,
        name="assemble",
    )(places, *args)


def cut_kernel(in_ref, *outs, axis):
    start = 0
    for out_ref in outs:
        size = out_ref.shape[axis]
        part = in_ref[start : start + size, :] if axis == 0 else in_ref[:, start : start + size]
        out_ref[...] = part.astype(f32)
        start += size


def cut_up(array, shapes, axis):
    return pl.pallas_call(
        functools.partial(cut_kernel, axis=axis),
        out_shape=[jax.ShapeDtypeStruct(shape, f32) for shape in shapes],
        compiler_params=WHOLE_VMEM,
        cost_estimate=SMALL,
        name="cut_up",
    )(array)


def cut_columns(array, widths):
    return cut_up(array, [(array.shape[0], width) for width in widths], 1)


def cut_rows(array, heights):
    return cut_up(array, [(height, array.shape[1]) for height in heights], 0)


def attend_back_kernel(
    meta, q_ref, do_ref, kva_ref, kvb_ref, bounds_ref, *refs, first, group, diagonal
):
    if first:
        dq_ref, dkva_ref, dkvb_ref, dq_turned, sum_a, sum_b = refs
    else:
        dq_in, dq_ref, dkva_ref, dkvb_ref, dq_turned, sum_a, sum_b = refs
    rows = q_ref.shape[0]
    key_rows = kva_ref.shape[0]
    step = lax.rem(pl.program_id(0), group)
    dq_turned[...] = jnp.zeros_like(dq_turned)

    @pl.when(step == 0)
    def _():
        sum_a[...] = jnp.zeros_like(sum_a)
        sum_b[...] = jnp.zeros_like(sum_b)

    def work(kv_ref, total, lanes, ones, keys, queries, mask):
        key = kv_ref[keys, :HEAD_WIDTH]
        q = q_ref[queries, :]
        do = do_ref[queries, :]
        weight = jnp.exp2(dot_nt(jnp.concatenate([key, lanes[keys, :]], axis=1), q))
        if mask:
            weight = jnp.where(lower_mask(True), weight, 0.0)
        value = jnp.concatenate([kv_ref[keys, HEAD_WIDTH:], ones], axis=1)
        d_score = (weight * dot_nt(value, do)).astype(bf16)
        total[keys, HEAD_WIDTH:] += dot(weight.astype(bf16), do[:, :HEAD_WIDTH])
        total[keys, :HEAD_WIDTH] += dot(d_score, q[:, :HEAD_WIDTH])
        dq_turned[:, queries] += dot_tn(key, d_score)

    for place, (kv_ref, total) in enumerate(((kva_ref, sum_a), (kvb_ref, sum_b))):
        key_start = meta[2 + place]

        @pl.when(block_used(meta, key_start, key_rows, rows))
        def _():
            lanes = key_lanes(meta, key_start, key_rows, bounds_ref)
            ones = jnp.where(lane_index(KEY_CHUNK) < 3, 1.0, 0.0).astype(bf16)
            for c in range(key_rows // KEY_CHUNK):
                if diagonal and place == 0:
                    work(kv_ref, total, lanes, ones, chunk(c), chunk(c), True)
                    if c + 1 < rows // KEY_CHUNK:
                        later = slice((c + 1) * KEY_CHUNK, rows)
                        work(kv_ref, total, lanes, ones, chunk(c), later, False)
                else:
                    work(kv_ref, total, lanes, ones, chunk(c), slice(0, rows), False)

    turned = dq_turned[...].T
    dq_ref[...] = turned if first else dq_in[...] + turned

    @pl.when(step == group - 1)
    def _():
        dkva_ref[...] = sum_a[...]
        dkvb_ref[...] = sum_b[...].astype(bf16)


def attend_back(q, do, kv_a, kv_b, bounds, meta, dq, diagonal):
    rows = q.shape[0]
    key_rows = kv_a.shape[0]
    q_heads = q.shape[1] // (2 * HEAD_WIDTH)
    group = q.shape[1] // kv_a.shape[1]
    width = q_heads * HEAD_WIDTH
    first = dq is None
    wide = 2 * HEAD_WIDTH
    per_q = pl.BlockSpec((rows, wide), lambda j, m: (0, j))
    per_kv = pl.BlockSpec((key_rows, wide), lambda j, m: (0, j // group))
    per_out = pl.BlockSpec((rows, HEAD_WIDTH), lambda j, m: (0, j))
    table = pl.BlockSpec((8, HEAD_WIDTH), lambda j, m: (0, 0))
    return pl.pallas_call(
        functools.partial(attend_back_kernel, first=first, group=group, diagonal=diagonal),
        grid_spec=pltpu.PrefetchScalarGridSpec(
            num_scalar_prefetch=1,
            grid=(q_heads,),
            in_specs=[per_q, per_q, per_kv, per_kv, table] + ([] if first else [per_out]),
            out_specs=[per_out, per_kv, per_kv],
            scratch_shapes=[
                pltpu.VMEM((HEAD_WIDTH, rows), f32),
                pltpu.VMEM((key_rows, wide), f32),
                pltpu.VMEM((key_rows, wide), f32),
            ],
        ),
        out_shape=[
            jax.ShapeDtypeStruct((rows, width), f32),
            jax.ShapeDtypeStruct(kv_a.shape, f32),
            jax.ShapeDtypeStruct(kv_b.shape, bf16),
        ],
        input_output_aliases={} if first else {6: 0},
        compiler_params=WHOLE_VMEM,
        cost_estimate=SMALL,
        name="attend_back",
    )(meta, q, do, kv_a, kv_b, bounds, *(() if first else (dq,)))


def project_kernel(meta, base_ref, *refs, count, final):
    pieces, mine, other = refs[:count], refs[count : 2 * count], refs[2 * count : 3 * count]
    if final:
        gain_ref, share_ref, normed_ref = refs[3 * count :]
    else:
        (out_ref,) = refs[3 * count :]
    first_core = meta[0] == 0
    total = base_ref[...].astype(f32)
    for piece, mine_ref, other_ref in zip(pieces, mine, other):
        half = piece.shape[1] // 2
        low, high = piece[:, :half], piece[:, half:]
        total += dot(jnp.where(first_core, low, high), mine_ref[0])
        total += dot(jnp.where(first_core, high, low), other_ref[0])
    if final:
        inverse = lax.rsqrt(jnp.mean(total * total, axis=-1, keepdims=True) + EPSILON)
        normed_ref[...] = (total * inverse * gain_ref[...]).astype(bf16)

        @pl.when(pl.program_id(0) == meta[1])
        def _():
            share_ref[...] = total

    else:
        out_ref[...] = total


def project(base, pieces, w_mine, w_other, core, me, gain=None):
    meta = jnp.stack(
        [jnp.asarray(v, jnp.int32) for v in [core, me] + [owner for unused, owner in pieces]]
    )
    rows, width = base.shape
    n_head, half, unused = w_mine.shape
    count = len(pieces)
    final = gain is not None
    step = rows // n_head
    per_row = pl.BlockSpec((step, width), lambda i, m: (i, 0))
    per_piece = pl.BlockSpec((step, 2 * half), lambda i, m: (i, 0))
    weights = [
        pl.BlockSpec((1, half, width), lambda i, m, k=k: (m[2 + k], 0, 0)) for k in range(count)
    ]
    in_specs = [per_row] + [per_piece] * count + weights + weights
    args = [base] + [piece for piece, unused in pieces] + [w_mine] * count + [w_other] * count
    if final:
        in_specs.append(pl.BlockSpec((1, width), lambda i, m: (0, 0)))
        args.append(gain[None, :])
        out_specs = [pl.BlockSpec((step, width), lambda i, m: (0, 0)), per_row]
        out_shape = [
            jax.ShapeDtypeStruct((step, width), f32),
            jax.ShapeDtypeStruct((rows, width), bf16),
        ]
    else:
        out_specs = per_row
        out_shape = jax.ShapeDtypeStruct((rows, width), f32)
    return pl.pallas_call(
        functools.partial(project_kernel, count=count, final=final),
        grid_spec=pltpu.PrefetchScalarGridSpec(
            num_scalar_prefetch=1,
            grid=(rows // step,),
            in_specs=in_specs,
            out_specs=out_specs,
        ),
        out_shape=out_shape,
        compiler_params=WHOLE_VMEM,
        cost_estimate=SMALL,
        name="project",
    )(meta, *args)


def arranged_shapes(rows, width):
    return [
        jax.ShapeDtypeStruct((rows // 4, width), bf16),
        jax.ShapeDtypeStruct((rows // 4, width), bf16),
        jax.ShapeDtypeStruct((rows // 2, width), bf16),
    ]


def store_arranged(me, outs, share_y, share_x, half, value):
    along_x, along_y, stays = outs
    rows = value.shape[0]
    other_x = share_x ^ (me & 1)
    other_y = share_y ^ (me >> 1)

    def store(ref, place):
        ref[pl.ds(pl.multiple_of(place * rows, rows), rows), :] = value

    if half == 0:
        pl.when(other_x == 1)(lambda: store(along_x, other_y))
        pl.when(other_x == 0)(lambda: store(stays, other_y))
    else:
        pl.when(other_y == 1)(lambda: store(along_y, other_x))
        pl.when(other_y == 0)(lambda: store(stays, 2 + other_x))


def store_all_arranged(me, outs, value):
    rows = value.shape[0] // 8
    for i in range(8):
        block = value[i * rows : (i + 1) * rows, :]
        store_arranged(me, outs, i // 4, i // 2 % 2, i % 2, block)


def meet_kernel(stays_ref, x_ref, y_ref, mine_ref, to_y_ref, to_x_ref):
    rows = mine_ref.shape[0] // 2
    for start, got_ref, sent_ref in ((0, x_ref, to_y_ref), (2, y_ref, to_x_ref)):
        total = stays_ref[start * rows : (start + 2) * rows, :].astype(f32) + got_ref[...].astype(f32)
        mine_ref[start // 2 * rows : (start // 2 + 1) * rows, :] = total[:rows]
        sent_ref[...] = total[rows:].astype(bf16)


def meet(stays, from_x, from_y):
    rows, width = stays.shape
    return pl.pallas_call(
        meet_kernel,
        out_shape=[
            jax.ShapeDtypeStruct((rows // 2, width), f32),
            jax.ShapeDtypeStruct((rows // 4, width), bf16),
            jax.ShapeDtypeStruct((rows // 4, width), bf16),
        ],
        compiler_params=WHOLE_VMEM,
        cost_estimate=SMALL,
        name="meet",
    )(stays, from_x, from_y)


def share_sum(terms):
    first, *rest = terms
    total = first[...].astype(f32)
    if len(rest) == 2:
        return total + jnp.concatenate([part[...].astype(f32) for part in rest], axis=0)
    return total


def add_rows_kernel(base_ref, *refs):
    *terms, out_ref = refs
    out_ref[...] = (base_ref[...] + share_sum(terms)).astype(bf16)


def add_rows(base, terms):
    return pl.pallas_call(
        add_rows_kernel,
        out_shape=jax.ShapeDtypeStruct(base.shape, bf16),
        compiler_params=WHOLE_VMEM,
        cost_estimate=SMALL,
        name="add_rows",
    )(base, *terms)


def norm_backward(grad, x, gain):
    inverse = lax.rsqrt(jnp.mean(x * x, axis=-1, keepdims=True) + EPSILON)
    hat = x * inverse
    scaled = grad * gain
    back = inverse * (scaled - hat * jnp.mean(scaled * hat, axis=-1, keepdims=True))
    return back, jnp.sum(grad * hat, axis=0, keepdims=True)


def turn_kernel(meta, *refs, count):
    terms = refs[:count]
    hidden_ref, dy_ref, gain_ref, mine_ref, other_ref = refs[count : count + 5]
    out_ref, grad_ref, branch_ref, gain_grad_ref = refs[count + 5 :]

    @pl.when(pl.program_id(0) == 0)
    def _():
        back, gain_grad_ref[...] = norm_backward(
            share_sum(terms), hidden_ref[...], gain_ref[...]
        )
        total = dy_ref[...].astype(f32) + back
        grad_ref[...] = total
        branch_ref[...] = total.astype(bf16)

    half = mine_ref.shape[1]
    branch = branch_ref[...]
    mine = dot_nt(branch, mine_ref[0])
    other = dot_nt(branch, other_ref[0])
    first_core = meta[0] == 0
    out_ref[0, :, :half] = jnp.where(first_core, mine, other).astype(bf16)
    out_ref[0, :, half:] = jnp.where(first_core, other, mine).astype(bf16)


def turn(terms, hidden, dy, gain, w_mine, w_other, core, me):
    rows, width = hidden.shape
    n_head, half, unused = w_mine.shape
    meta = jnp.stack([jnp.asarray(v, jnp.int32) for v in (core, me)])

    def full(array):
        return pl.BlockSpec(array.shape, lambda i, m: (0, 0))

    weight = pl.BlockSpec((1, half, width), lambda i, m: (i ^ m[1], 0, 0))
    share = pl.BlockSpec((rows, width), lambda i, m: (0, 0))
    return pl.pallas_call(
        functools.partial(turn_kernel, count=len(terms)),
        grid_spec=pltpu.PrefetchScalarGridSpec(
            num_scalar_prefetch=1,
            grid=(n_head,),
            in_specs=[full(term) for term in terms]
            + [
                share,
                pl.BlockSpec((rows, width), lambda i, m: (m[1], 0)),
                pl.BlockSpec((1, width), lambda i, m: (0, 0)),
                weight,
                weight,
            ],
            out_specs=[
                pl.BlockSpec((1, rows, 2 * half), lambda i, m: (i, 0, 0)),
                share,
                share,
                pl.BlockSpec((1, width), lambda i, m: (0, 0)),
            ],
        ),
        out_shape=[
            jax.ShapeDtypeStruct((n_head, rows, 2 * half), bf16),
            jax.ShapeDtypeStruct((rows, width), f32),
            jax.ShapeDtypeStruct((rows, width), bf16),
            jax.ShapeDtypeStruct((1, width), f32),
        ],
        compiler_params=WHOLE_VMEM,
        cost_estimate=SMALL,
        name="turn",
    )(meta, *terms, hidden, dy, gain[None, :], w_mine, w_other)


def last_kernel(meta, *refs, count):
    terms = refs[:count]
    x_ref, grad_ref, gain_ref, rider_ref, out_ref = refs[count:]
    rows = x_ref.shape[0]
    back, unused = norm_backward(share_sum(terms), x_ref[...].astype(f32), gain_ref[...])
    out_ref[:rows, :] = (grad_ref[...] + back).astype(bf16)
    out_ref[rows:, :] = rider_ref[...]


def last(terms, tokens, hidden_grad, gain, rider, me):
    rows, width = hidden_grad.shape
    meta = jnp.asarray(me, jnp.int32)[None]

    def full(array):
        return pl.BlockSpec(array.shape, lambda i, m: (0, 0))

    out_rows = rows + rider.shape[0]
    return pl.pallas_call(
        functools.partial(last_kernel, count=len(terms)),
        grid_spec=pltpu.PrefetchScalarGridSpec(
            num_scalar_prefetch=1,
            grid=(1,),
            in_specs=[full(term) for term in terms]
            + [
                pl.BlockSpec((rows, width), lambda i, m: (m[0], 0)),
                full(hidden_grad),
                pl.BlockSpec((1, width), lambda i, m: (0, 0)),
                full(rider),
            ],
            out_specs=pl.BlockSpec((out_rows, width), lambda i, m: (0, 0)),
        ),
        out_shape=jax.ShapeDtypeStruct((out_rows, width), bf16),
        compiler_params=WHOLE_VMEM,
        cost_estimate=SMALL,
        name="last",
    )(meta, *terms, tokens, hidden_grad, gain[None, :], rider)


def feed_kernel(x_ref, gate_w_ref, up_w_ref, d_mixed_ref, mixed_ref, gate_ref, up_ref, sum_ref):
    x = x_ref[...]
    gate = dot(x, gate_w_ref[...])
    up = dot(x, up_w_ref[...])
    d_mixed = d_mixed_ref[...]
    sigmoid = 0.5 * jnp.tanh(0.5 * gate) + 0.5
    silu = gate * sigmoid
    mixed_ref[...] = (silu * up).astype(bf16)
    gate_low = (d_mixed * up * (sigmoid * (1.0 + gate * (1.0 - sigmoid)))).astype(bf16)
    up_low = (d_mixed * silu).astype(bf16)
    gate_ref[...] = gate_low
    up_ref[...] = up_low
    step = gate_low.shape[1]
    sum_ref[:, :step] = dot_tn(x, gate_low).astype(bf16)
    sum_ref[:, step:] = dot_tn(x, up_low).astype(bf16)


def feed(x, w_gate, w_up, d_mixed):
    rows, width = x.shape
    hidden = w_gate.shape[1]
    whole = pl.BlockSpec((rows, width), lambda i: (0, 0))
    weight = pl.BlockSpec((width, HIDDEN_STEP), lambda i: (0, i))
    act = pl.BlockSpec((rows, HIDDEN_STEP), lambda i: (0, i))
    return pl.pallas_call(
        feed_kernel,
        grid=(hidden // HIDDEN_STEP,),
        in_specs=[whole, weight, weight, act],
        out_specs=[act, act, act, pl.BlockSpec((width, 2 * HIDDEN_STEP), lambda i: (0, i))],
        out_shape=[jax.ShapeDtypeStruct((rows, hidden), bf16)] * 3
        + [jax.ShapeDtypeStruct((width, 2 * hidden), bf16)],
        compiler_params=WHOLE_VMEM,
        cost_estimate=SMALL,
        name="feed",
    )(x, w_gate, w_up, d_mixed)


def split_kernel(sum_ref, gate_ref, up_ref):
    step = gate_ref.shape[1]
    gate_ref[...] = sum_ref[:, :step].astype(f32)
    up_ref[...] = sum_ref[:, step:].astype(f32)


def split_gate_up(sums):
    rows, width = sums.shape
    out = pl.BlockSpec((rows, HIDDEN_STEP), lambda i: (0, i))
    return pl.pallas_call(
        split_kernel,
        grid=(width // (2 * HIDDEN_STEP),),
        in_specs=[pl.BlockSpec((rows, 2 * HIDDEN_STEP), lambda i: (0, i))],
        out_specs=[out, out],
        out_shape=[jax.ShapeDtypeStruct((rows, width // 2), f32)] * 2,
        compiler_params=WHOLE_VMEM,
        cost_estimate=SMALL,
        name="split_gate_up",
    )(sums)


def products_kernel(meta, *refs, count, turned, arranged):
    lefts, rights, outs = refs[:count], refs[count : 2 * count], refs[2 * count :]
    total = 0.0
    for left, right in zip(lefts, rights):
        total += (dot_nt if turned else dot)(left[...], right[...])
    if arranged:
        store_all_arranged(meta[0], outs, total.astype(bf16))
    else:
        outs[0][...] = total.astype(bf16)


def products(lefts, rights, turned, me, arranged):
    meta = jnp.asarray(me, jnp.int32)[None]
    rows, depth = lefts[0].shape
    width = rights[0].shape[0 if turned else 1]
    step = width // 4
    whole = pl.BlockSpec((rows, depth), lambda i, m: (0, 0))
    if turned:
        right = pl.BlockSpec((step, depth), lambda i, m: (i, 0))
    else:
        right = pl.BlockSpec((depth, step), lambda i, m: (0, i))
    shapes = arranged_shapes(rows, width) if arranged else [jax.ShapeDtypeStruct((rows, width), bf16)]
    return pl.pallas_call(
        functools.partial(products_kernel, count=len(lefts), turned=turned, arranged=arranged),
        grid_spec=pltpu.PrefetchScalarGridSpec(
            num_scalar_prefetch=1,
            grid=(width // step,),
            in_specs=[whole] * len(lefts) + [right] * len(lefts),
            out_specs=[pl.BlockSpec((v.shape[0], step), lambda i, m: (0, i)) for v in shapes],
        ),
        out_shape=shapes,
        compiler_params=WHOLE_VMEM,
        cost_estimate=SMALL,
        name="products",
    )(meta, *lefts, *rights)


def column_sums_kernel(owners, mixed_ref, o_ref, dy_ref, *refs):
    *pieces, out_ref, branch = refs
    hidden = mixed_ref.shape[1]
    for i, piece in enumerate(pieces):
        rows = piece.shape[0]
        branch[pl.ds(pl.multiple_of(owners[i] * rows, rows), rows), :] = piece[...]
    out_ref[0, :hidden, :] = dot_tn(mixed_ref[...], dy_ref[...]).astype(bf16)
    out_ref[0, hidden:, :] = dot_tn(o_ref[...], branch[...]).astype(bf16)


def column_sums(mixed, o_low, dy, pieces, shares):
    owners = jnp.stack([jnp.asarray(owner, jnp.int32) for unused, owner in pieces])
    rows, width = dy.shape
    share = width // shares
    out_rows = mixed.shape[1] + o_low.shape[1]
    return pl.pallas_call(
        column_sums_kernel,
        grid_spec=pltpu.PrefetchScalarGridSpec(
            num_scalar_prefetch=1,
            grid=(shares,),
            in_specs=[
                pl.BlockSpec(mixed.shape, lambda i, m: (0, 0)),
                pl.BlockSpec(o_low.shape, lambda i, m: (0, 0)),
                pl.BlockSpec((rows, share), lambda i, m: (0, i)),
            ]
            + [
                pl.BlockSpec((piece.shape[0], share), lambda i, m: (0, i))
                for piece, unused in pieces
            ],
            out_specs=pl.BlockSpec((1, out_rows, share), lambda i, m: (i, 0, 0)),
            scratch_shapes=[pltpu.VMEM((rows, share), bf16)],
        ),
        out_shape=jax.ShapeDtypeStruct((shares, out_rows, share), bf16),
        compiler_params=WHOLE_VMEM,
        cost_estimate=SMALL,
        name="column_sums",
    )(owners, mixed, o_low, dy, *[piece for piece, unused in pieces])


def pass_on_kernel(part_ref, theirs_ref, *refs):
    *arrived, low_ref, high_ref = refs
    half = low_ref.shape[0]
    for i, out_ref in enumerate((low_ref, high_ref)):
        rows = slice(i * half, (i + 1) * half)
        total = part_ref[rows, :] + theirs_ref[rows, :].astype(f32)
        if arrived:
            total += arrived[i][...].astype(f32)
        out_ref[...] = total.astype(bf16)


def pass_on(part, theirs, *arrived):
    rows, width = part.shape
    return pl.pallas_call(
        pass_on_kernel,
        out_shape=[jax.ShapeDtypeStruct((rows // 2, width), bf16)] * 2,
        compiler_params=WHOLE_VMEM,
        cost_estimate=SMALL,
        name="pass_on",
    )(part, theirs, *arrived)


def leave_kernel(
    meta,
    x_ref,
    q_ref,
    dkv_ref,
    theirs_ref,
    first_ref,
    second_ref,
    raw_ref,
    key_gain_ref,
    cos_ref,
    sin_ref,
    q_w_ref,
    key_w_ref,
    value_w_ref,
    key_ref,
    value_ref,
    gain_grad_ref,
    norm_grad_ref,
    *outs,
    arranged,
):
    @pl.when(pl.program_id(0) == 0)
    def _():
        gain_grad_ref[...] = jnp.zeros_like(gain_grad_ref)
        norm_grad_ref[...] = jnp.zeros_like(norm_grad_ref)

    arrived = jnp.where(pl.program_id(0) == 0, first_ref[...], second_ref[...])
    dkv = dkv_ref[...] + theirs_ref[...].astype(f32) + arrived.astype(f32)
    for j in range(key_ref.shape[1] // HEAD_WIDTH):
        head = slice(j * HEAD_WIDTH, (j + 1) * HEAD_WIDTH)
        start = 2 * j * HEAD_WIDTH
        grad, gain_grad = head_backward(
            raw_ref[:, head],
            dkv[:, start : start + HEAD_WIDTH] * (1.0 / LOG2E),
            key_gain_ref[...],
            cos_ref[...],
            sin_ref[...],
        )
        key_ref[:, head] = grad
        value_ref[:, head] = dkv[:, start + HEAD_WIDTH : start + 2 * HEAD_WIDTH].astype(bf16)
        gain_grad_ref[...] += gain_grad
    total = dot_nt(q_ref[...], q_w_ref[...])
    total += dot_nt(key_ref[...], key_w_ref[...])
    total += dot_nt(value_ref[...], value_w_ref[...])
    result = total.astype(bf16)
    if arranged:
        block = result.shape[0] // 4
        for i in range(4):
            store_arranged(
                meta[0],
                outs,
                pl.program_id(0),
                i // 2,
                i % 2,
                result[i * block : (i + 1) * block, :],
            )
    else:
        outs[0][...] = result
    x = x_ref[...].astype(f32)
    hat = x * lax.rsqrt(jnp.mean(x * x, axis=-1, keepdims=True) + EPSILON)
    norm_grad_ref[...] += jnp.sum(total * hat, axis=0, keepdims=True)


def leave(tokens, q_grad, dkv, theirs, arrived, key_raw, key_gain, cosine, sine, weights, me, arranged):
    meta = jnp.asarray(me, jnp.int32)[None]
    rows, width = tokens.shape
    kv_width = key_raw.shape[1]
    step = rows // 2

    def per_row(array):
        return pl.BlockSpec((step, array.shape[1]), lambda i, m: (i, 0))

    def full(array):
        return pl.BlockSpec(array.shape, lambda i, m: (0, 0))

    key_gain = key_gain[None, :]
    if arranged:
        shapes = arranged_shapes(rows, width)
        out_specs = [full(v) for v in shapes]
    else:
        shapes = [jax.ShapeDtypeStruct((rows, width), bf16)]
        out_specs = [per_row(shapes[0])]
    return pl.pallas_call(
        functools.partial(leave_kernel, arranged=arranged),
        grid_spec=pltpu.PrefetchScalarGridSpec(
            num_scalar_prefetch=1,
            grid=(2,),
            in_specs=[per_row(v) for v in (tokens, q_grad, dkv, theirs)]
            + [full(v) for v in arrived]
            + [per_row(key_raw), full(key_gain), per_row(cosine), per_row(sine)]
            + [full(v) for v in weights],
            out_specs=[
                per_row(key_raw),
                per_row(key_raw),
                pl.BlockSpec((1, HEAD_WIDTH), lambda i, m: (0, 0)),
                pl.BlockSpec((1, width), lambda i, m: (0, 0)),
            ]
            + out_specs,
        ),
        out_shape=[
            jax.ShapeDtypeStruct((rows, kv_width), bf16),
            jax.ShapeDtypeStruct((rows, kv_width), bf16),
            jax.ShapeDtypeStruct((1, HEAD_WIDTH), f32),
            jax.ShapeDtypeStruct((1, width), f32),
        ]
        + shapes,
        compiler_params=WHOLE_VMEM,
        cost_estimate=SMALL,
        name="leave",
    )(meta, tokens, q_grad, dkv, theirs, *arrived, key_raw, key_gain, cosine, sine, *weights)


def attn_sums_kernel(x_ref, q_ref, k_ref, v_ref, out_ref):
    x = x_ref[...]
    start = 0
    for ref in (q_ref, k_ref, v_ref):
        out_ref[:, start : start + ref.shape[1]] = dot_tn(x, ref[...]).astype(bf16)
        start += ref.shape[1]


def attn_sums(x, query, key, value):
    rows, width = x.shape
    step = width // 8
    out_width = query.shape[1] + key.shape[1] + value.shape[1]

    def full(array):
        return pl.BlockSpec(array.shape, lambda i: (0, 0))

    return pl.pallas_call(
        attn_sums_kernel,
        grid=(width // step,),
        in_specs=[pl.BlockSpec((rows, step), lambda i: (0, i)), full(query), full(key), full(value)],
        out_specs=pl.BlockSpec((step, out_width), lambda i: (i, 0)),
        out_shape=jax.ShapeDtypeStruct((width, out_width), bf16),
        compiler_params=WHOLE_VMEM,
        cost_estimate=SMALL,
        name="attn_sums",
    )(x, query, key, value)


def after(values):
    return lax.optimization_barrier(values)


def pick(array, index):
    return lax.dynamic_index_in_dim(array, index, 0, keepdims=False)


def solution(mesh):
    n_seq = mesh.shape["seq"]
    n_head = mesh.shape["head"]
    n_chip = n_seq // 2

    def swap_core(value):
        return lax.ppermute(value, "seq", [(i, i ^ 1) for i in range(n_seq)])

    def to_next(value):
        return lax.ppermute(value, "seq", [(i, i + 2) for i in range(n_seq - 2)])

    def to_previous(value):
        return lax.ppermute(value, "seq", [(i + 2, i) for i in range(n_seq - 2)])

    def across(value, bits):
        return lax.ppermute(value, "head", [(i, i ^ bits) for i in range(n_head)])

    def gather_steps(value):
        me = lax.axis_index("head")
        if n_head != 4:
            every = yield lax.all_gather(value, "head", axis=0)
            return [(every[i], i) for i in range(n_head)]
        half = value.shape[0] // 2
        by_x, by_y = yield across(value, 1), across(value, 2)
        low, high = yield across(by_x[:half], 2), across(by_y[half:], 1)
        far = jnp.concatenate([low, high], axis=0)
        return [(value, me), (by_x, me ^ 1), (by_y, me ^ 2), (far, me ^ 3)]

    def rider_entries(value, count):
        me = lax.axis_index("head")
        half = count // 2
        if n_head != 4:
            every = yield lax.all_gather(value, "head", axis=0)
            entries = [(every[i], k, 2 * i + k) for i in range(n_head) for k in range(2)]
            return entries, [every[i, count:] for i in range(n_head)]
        by_x, by_y = yield across(value, 1), across(value, 2)
        low, high = yield across(by_x[:half], 2), across(by_y[half:], 1)
        owners = ((value, me), (by_x, me ^ 1), (by_y, me ^ 2))
        entries = [(array, k, 2 * owner + k) for array, owner in owners for k in range(2)]
        entries += [(low, 0, 2 * (me ^ 3)), (high, 0, 2 * (me ^ 3) + 1)]
        return entries, [value[count:], by_x[count:], by_y[count:], high[half:]]

    def scatter_steps(value):
        if n_head != 4:
            total = yield lax.psum_scatter(value[0], "head", scatter_dimension=0, tiled=True)
            return (total,)
        along_x, along_y, stays = value
        from_x, from_y = yield across(along_x, 1), across(along_y, 2)
        mine, to_y, to_x = meet(stays, from_x, from_y)
        first, second = yield across(to_y, 2), across(to_x, 1)
        return mine, first, second

    def run_steps(steps, works=()):
        works = list(works)
        made = []
        arrived = next(steps)
        while True:
            if works:
                arrived, done = after((arrived, works.pop(0)()))
                made.append(done)
            try:
                arrived = steps.send(arrived)
            except StopIteration as stop:
                return stop.value, made + [work() for work in works]

    def end_steps(steps, arrived):
        try:
            steps.send(arrived)
        except StopIteration as stop:
            return stop.value

    def exchange_head(value):
        me = lax.axis_index("head")
        if n_head == 4:
            return [(value[0], me)] + [(across(value[i], i), me ^ i) for i in (3, 1, 2)]
        ordered = jnp.stack([pick(value, i ^ me) for i in range(n_head)])
        got = lax.all_to_all(ordered, "head", 0, 0)
        return [(got[i], i) for i in range(n_head)]

    def body(
        tokens,
        lengths,
        norm1_gain,
        w_query,
        key_matrix,
        value_matrix,
        query_gain,
        key_gain,
        w_output,
        norm2_gain,
        w_gate,
        w_up,
        w_down,
        cotangent,
    ):
        rows = tokens.shape[0]
        share = rows // n_head
        seq_index = lax.axis_index("seq")
        head_index = lax.axis_index("head")
        chip, core = seq_index // 2, seq_index % 2
        cut = n_head == 4

        index = seq_index * rows + jnp.arange(rows, dtype=jnp.int32)
        begin = locate(index, lengths)
        cosine, sine = rotary(index - begin)
        ends = jnp.cumsum(lengths)
        n_lengths = lengths.shape[0]
        bounds = jnp.zeros((8, HEAD_WIDTH), jnp.int32).at[0].set(2**30)
        bounds = bounds.at[0, :n_lengths].set(ends - lengths).at[1, :n_lengths].set(ends)

        def stage_meta(stage):
            source = 2 * (chip - stage)
            return jnp.stack(
                [seq_index * rows, begin[0], (source + core) * rows, (source + 1 - core) * rows]
            ).astype(jnp.int32)

        metas = [stage_meta(stage) for stage in range(n_chip)]

        first_in, key_raw, current = enter(
            tokens, norm1_gain, key_matrix, value_matrix, key_gain, cosine, sine
        )
        sibling = swap_core(current)
        following = to_next(current)

        half_rows = w_output.shape[0] // 2
        w_late, unused = after((w_output, current))
        w_half = lax.dynamic_slice_in_dim(w_late, core * half_rows, half_rows, 0)
        w_mine = lax.all_gather(w_half, "head", axis=0)

        query_raw = dot(first_in, w_query)
        q_wide = query_prep(metas[0], query_raw, query_gain, cosine, sine, bounds)
        following, q_wide = after((following, q_wide))

        blocks = []
        carried = ()
        for stage in range(n_chip):
            blocks.append((current, sibling))
            if stage + 2 < n_chip:
                current = following
                sibling = swap_core(current)
                following = to_next(current)
            carried = attend_stage(
                q_wide, *blocks[stage], bounds, metas[stage], carried, stage == n_chip - 1
            )
            if stage == 0:
                dy, carried = after((cotangent, carried))
                d_mixed = dot_nt(dy, w_down)
                carried, d_mixed = after((carried, d_mixed))
            if stage + 3 < n_chip:
                following, carried = after((following, carried))
            if stage + 2 == n_chip:
                current, carried = after((following, carried))
                sibling = swap_core(current)
                w_mine, sibling, carried = after((w_mine, sibling, carried))
                w_other = swap_core(w_mine)
        o_low, q_back, outcome = carried

        steps = gather_steps(o_low)
        arrived = next(steps)
        base = tokens
        if n_head == 4:
            base = project(base, [(o_low, head_index)], w_mine, w_other, core, head_index)
            arrived, base = after((arrived, base))
            far = steps.send(arrived)
            pieces = [(arrived[0], head_index ^ 1), (arrived[1], head_index ^ 2)]
            base = project(base, pieces, w_mine, w_other, core, head_index)
            arrived, base = after((far, base))
        try:
            steps.send(arrived)
        except StopIteration as stop:
            pieces = stop.value[3:] if n_head == 4 else stop.value
        my_hidden, second_in = project(
            base, pieces, w_mine, w_other, core, head_index, norm2_gain
        )
        mixed_low, gate_low, up_low, gate_up_sum = feed(second_in, w_gate, w_up, d_mixed)

        def scatter_seq(value, tiled):
            return lax.psum_scatter(value, "seq", scatter_dimension=0, tiled=tiled)

        grad_gate_up = scatter_seq(gate_up_sum, True)

        terms, (down_part,) = run_steps(
            scatter_steps(products((gate_low, up_low), (w_gate, w_up), True, head_index, cut)),
            (lambda: products((mixed_low,), (w_down,), False, head_index, cut),),
        )
        do_pieces, hidden_grad, my_branch, grad_norm2 = turn(
            terms, my_hidden, cotangent, norm2_gain, w_mine, w_other, core, head_index
        )
        do_wide = with_delta(exchange_head(do_pieces), outcome)
        down_part, my_branch, do_wide = after((down_part, my_branch, do_wide))

        dq = None
        parts = []
        moving = []
        landed = []
        hops = 0

        def hop_piece():
            if not moving:
                return None
            value = moving.pop(0)
            return lambda: to_previous(value)

        def stage_work(stage):
            return lambda: attend_back(
                q_back, do_wide, *blocks[stage], bounds, metas[stage], dq, stage == 0
            )

        def next_hop():
            nonlocal dq, hops
            if hops < n_chip - 1 and len(parts) > hops and len(landed) == (2 if hops else 0):
                sent, dq = after((pass_on(*parts[hops], *landed), dq))
                landed.clear()
                moving.extend(sent)
                hops += 1

        branch_steps = gather_steps(my_branch)
        (dq, dkv_a, dkv_b), got_branch = after(
            (stage_work(n_chip - 1)(), next(branch_steps))
        )
        theirs, dq = after((swap_core(dkv_b), dq))
        parts.append((dkv_a, theirs))
        next_hop()
        flying = hop_piece()()
        if cut:
            got_branch = branch_steps.send(got_branch)
        (dq, dkv_a, dkv_b), got_branch, flying = after(
            (stage_work(n_chip - 2)(), got_branch, flying)
        )
        branch_pieces = end_steps(branch_steps, got_branch)
        landed.append(flying)
        parts.append((dkv_a, swap_core(dkv_b)))
        flying = hop_piece()()
        column_sum = column_sums(mixed_low, o_low, cotangent, branch_pieces, n_seq)
        dkv_a, theirs = parts[1]
        column_sum, flying, theirs, dq = after((column_sum, flying, theirs, dq))
        parts[1] = (dkv_a, theirs)
        landed.append(flying)
        grad_gate_up, column_sum, dq, landed[:] = after(
            (grad_gate_up, column_sum, dq, list(landed))
        )
        grad_columns = scatter_seq(column_sum, False)
        next_hop()
        down_part, dq = after((down_part, dq))
        mixed_steps = scatter_steps(down_part)
        got_mixed = next(mixed_steps)
        for stage in reversed(range(n_chip - 2)):
            if cut and stage == n_chip - 4:
                got_mixed = mixed_steps.send(got_mixed)
            hop = hop_piece()
            flying = None if hop is None else hop()
            (dq, dkv_a, dkv_b), got_mixed, flying = after((stage_work(stage)(), got_mixed, flying))
            if hop is not None:
                landed.append(flying)
            parts.append((dkv_a, swap_core(dkv_b)))
            next_hop()
        my_mixed = add_rows(my_hidden, end_steps(mixed_steps, got_mixed))
        mixed_steps = gather_steps(my_mixed)
        got_mixed = next(mixed_steps)
        query_grad, grad_qgain = head_back(query_raw, dq, query_gain, cosine, sine, SCORE_SCALE, 1)
        grad_gate_up = split_gate_up(grad_gate_up)
        query_grad, grad_gate_up = after((query_grad, grad_gate_up))
        while hops < n_chip - 1:
            while len(landed) < 2:
                landed.append(hop_piece()())
            next_hop()
        flying = [hop_piece()() for unused in range(2 - len(landed))]
        if cut:
            flying[0], got_mixed, query_grad = after((flying[0], got_mixed, query_grad))
            got_mixed = mixed_steps.send(got_mixed)
        flying, got_mixed, query_grad = after((flying, got_mixed, query_grad))
        landed = (*landed, *flying)
        mixed_pieces = end_steps(mixed_steps, got_mixed)
        key_grad, value_grad, grad_kgain, grad_norm1, *first_part = leave(
            tokens,
            query_grad,
            *parts[-1],
            landed,
            key_raw,
            key_gain,
            cosine,
            sine,
            (w_query, key_matrix, value_matrix),
            head_index,
            cut,
        )
        gains = jnp.concatenate([grad_norm1[0], grad_norm2[0], grad_qgain[0], grad_kgain[0]])
        gains = gains.reshape(-1, HEAD_WIDTH)

        def sum_seq(total, bits):
            for bit in bits:
                total = total + lax.ppermute(total, "seq", [(i, i ^ bit) for i in range(n_seq)])
            return total

        bits = [1 << k for k in range(n_seq.bit_length() - 1)]
        steps = scatter_steps(first_part)
        got = next(steps)
        attn_sum = attn_sums(first_in, query_grad, key_grad, value_grad)
        gains = sum_seq(gains, bits[:1])
        gains, attn_sum = after((gains, attn_sum))
        got, gains, attn_sum = after((got, gains, attn_sum))
        if cut:
            got = steps.send(got)
        grad_columns, attn_sum = after((grad_columns, attn_sum))
        grad_attn = scatter_seq(attn_sum, True)
        grad_query, grad_key, grad_value = cut_columns(
            grad_attn, (query_grad.shape[1], key_grad.shape[1], value_grad.shape[1])
        )
        got, gains = after((got, sum_seq(gains, bits[1:])))
        terms = end_steps(steps, got)

        width = tokens.shape[1]
        n_gains = gains.size
        gain_rows = -(-n_gains // width)
        flat = jnp.pad(gains.reshape(-1), (0, gain_rows * width - n_gains))
        high = lax.reduce_precision(flat, 8, 7)
        middle = lax.reduce_precision(flat - high, 8, 7)
        rider = jnp.concatenate([high, middle, flat - high - middle]).astype(bf16)
        rider = rider.reshape(3 * gain_rows, width)
        rider = jnp.pad(rider, ((0, 32 - rider.shape[0]), (0, 0)))
        my_tokens_grad = last(terms, tokens, hidden_grad, norm1_gain, rider, head_index)
        steps = rider_entries(my_tokens_grad, share)
        got = next(steps)
        mixed = assemble([(piece, 0, owner) for piece, owner in mixed_pieces], share, bf16)
        grad_down, grad_output = cut_rows(grad_columns, (w_gate.shape[1], o_low.shape[1]))
        got, mixed, grad_down, grad_output = after((got, mixed, grad_down, grad_output))
        if cut:
            got = steps.send(got)
        entries, gain_pieces = end_steps(steps, got)
        near = len(entries) - 2
        grad_tokens = assemble(entries[:near], share // 2, f32, len(entries))
        grad_tokens = assemble(entries[near:], share // 2, f32, len(entries), grad_tokens)
        gains = sum(part[: 3 * gain_rows].astype(f32) for part in gain_pieces)
        gains = jnp.sum(gains.reshape(3, -1), axis=0)
        grad_norm1, grad_norm2 = gains[:width], gains[width : 2 * width]
        grad_qgain = gains[2 * width : 2 * width + HEAD_WIDTH]
        grad_kgain = gains[2 * width + HEAD_WIDTH : n_gains]
        grad_gate, grad_up = grad_gate_up
        return (
            mixed,
            grad_tokens,
            grad_norm1,
            grad_query,
            grad_key,
            grad_value,
            grad_qgain,
            grad_kgain,
            grad_output,
            grad_norm2,
            grad_gate,
            grad_up,
            grad_down,
        )

    in_specs = (
        P("seq", None),
        P(),
        P(),
        P(None, "head"),
        P(None, "head"),
        P(None, "head"),
        P(),
        P(),
        P("head", None),
        P(),
        P(None, "head"),
        P(None, "head"),
        P("head", None),
        P("seq", None),
    )
    out_specs = (
        P("seq", None),
        P("seq", None),
        P(),
        P("seq", "head"),
        P("seq", "head"),
        P("seq", "head"),
        P(),
        P(),
        P("head", "seq"),
        P(),
        P("seq", "head"),
        P("seq", "head"),
        P("head", "seq"),
    )
    return jax.shard_map(body, mesh=mesh, in_specs=in_specs, out_specs=out_specs, check_vma=False)
```

time: 575 us -> 535 us (0.930)
  Pallas kernels: 144 us -> 250 us
  waiting for transfers between devices: 202 us -> 138 us
  local copies, waits for them, and re-layouts: 73.8 us -> 18.9 us
  other arithmetic: 33.7 us -> 15.9 us
  matrix products: 33 us -> 15.6 us
  starting transfers between devices: 64.9 us -> 73.3 us
    pallas_call x7 -> x20, Pallas kernels: 43.6 us -> 120 us  [the longest x2 24.7 us: products(): pl.pallas_call(functools.partial(products_kernel, count=len(lefts), turne...]
    unnamed x213 -> x109, local copies, waits for them, and re-layouts: 59.9 us -> 12.9 us
    ppermute x5 -> x3, waiting for transfers between devices: 22.3 us -> 4.38 us  [sum_seq(): lax.ppermute(total, 'seq', [(i, i ^ bit) for i in range(n_seq)])]
    ppermute x3 -> x6, waiting for transfers between devices: 80.7 us -> 62.8 us  [to_previous(): return lax.ppermute(value, 'seq', [(i + 2, i) for i in range(n_seq - 2)])]
    ppermute x31, waiting for transfers between devices: 76.1 us -> 60.3 us  [across(): return lax.ppermute(value, 'head', [(i, i ^ bits) for i in range(n_head)])]
    pallas_call x4, Pallas kernels: 14.5 us -> 25 us  [attend_stage(): pl.pallas_call(functools.partial(attend_kernel, first=first, last=last),...]
    dot_general x4 -> x1, matrix products: 20 us -> 9.63 us  [dot_nt(): return lax.dot_general(left, right, NT, preferred_element_type=f32)]
    pallas_call x2 -> x3, Pallas kernels: 15.9 us -> 26.3 us  [project(): pl.pallas_call(functools.partial(project_kernel, count=count, final=final...]
  transfers between devices with their start and end apart: 55 -> 56, of which waited for: 32 -> 28; matrix products, arithmetic and copies ran while one was open for 12% -> 6% of each run, Pallas kernels for 20% -> 39%
where the time goes in v5:
time: 535 us; the launch traced here: 526 us
  Pallas kernels  250 us (47%)
  waiting for transfers between devices  138 us (26%)
  starting transfers between devices  73.3 us (14%)
  local copies, waits for them, and re-layouts  18.9 us (4%)
  other arithmetic  15.9 us (3%)
  matrix products  15.6 us (3%)
  between operations  14.6 us (3%)
    ppermute x6, waiting for transfers between devices, to_previous(): return lax.ppermute(value, 'seq', [(i + 2, i) for i in range(n_seq - 2)])  62.8 us
    ppermute x31, waiting for transfers between devices, across(): return lax.ppermute(value, 'head', [(i, i ^ bits) for i in range(n_head)])  60.3 us
    ppermute x31, starting transfers between devices, across(): return lax.ppermute(value, 'head', [(i, i ^ bits) for i in range(n_head)])  32.1 us
    pallas_call x4, Pallas kernels, attend_back(): pl.pallas_call(functools.partial(attend_back_kernel, first=first, group=g...  30.7 us
    pallas_call x1, Pallas kernels, feed(): pl.pallas_call(feed_kernel, grid=(hidden // HIDDEN_STEP,), in_specs=[whol...  26.4 us
    pallas_call x3, Pallas kernels, project(): pl.pallas_call(functools.partial(project_kernel, count=count, final=final...  26.3 us
    pallas_call x4, Pallas kernels, attend_stage(): pl.pallas_call(functools.partial(attend_kernel, first=first, last=last),...  25 us
    pallas_call x2, Pallas kernels, products(): pl.pallas_call(functools.partial(products_kernel, count=len(lefts), turne...  24.7 us
  transfers between devices with their start and end apart: 56, of which 28 were waited for; matrix products, arithmetic and copies ran while one was open for 6% of the time, Pallas kernels for 39%

profile of v5, /device:TPU:0, one launch (start us, length us, event | category | flops | bytes accessed | tf_op | source)
XLA Modules:
  0.0 525.7 jit_solution(5764240425410741141)
XLA Ops:
  47.3 7.1 %attend_stage.4 = (f32[768,512]{1,0:T(8,128)}, f32[768,512]{1,0:T(8,128)}) custom-call(s32[4]{0:T(128)} %get-tuple-element.427.meta, bf16[768,1024]{1,0:T(8,128)(2,1)} %query_prep.1.q_ref, bf16[768,512]{1,0:T(8,128)(2,1)} %get-tuple-element.230.kva_ref, bf16[768,512]{1,0:T(8,128)(2,1)} %copy-done.5, s32[8,128]{1,0:T(8,128)} %copy-done.28), custom_call_target="tpu_custom_call" | custom-call | flops 1 | bytes 1 | tf_op jit(solution)/shard_map/attend_stage/pallas_call | solution.py:317
  54.4 9.6 %fusion.11.d_mixed_ref = f32[768,1536]{1,0:T(8,128)} fusion(bf16[768,2048]{1,0:T(8,128)(2,1)} %dy_ref.1, bf16[1536,2048]{1,0:T(8,128)(2,1)} %refs_1_.1), kind=kOutput, calls=%fused_computation.50 | convolution fusion | flops 4831838208 | bytes 14155776 | tf_op jit(solution)/shard_map/dot_general | solution.py:36
  101.0 7.5 %project.3.base_ref = f32[768,2048]{1,0:T(8,128)} custom-call(s32[3]{0:T(128)} %pad_add_fusion.7.meta, bf16[768,2048]{1,0:T(8,128)(2,1)} %refs_3_.3, bf16[768,512]{1,0:T(8,128)(2,1)} %get-tuple-element.256.refs_0_.o_ref, bf16[4,256,2048]{2,1,0:T(8,128)(2,1)} %bitcast.55, bf16[4,256,2048]{2,1,0:T(8,128)(2,1)} %collective-permute-done.9.refs_2_.refs_4_.refs_5_.refs_7_), custom_call_target="tpu_custom_call" | custom-call | flops 1 | bytes 1 | tf_op jit(solution)/shard_map/project/pallas_call | solution.py:581
  108.6 8.7 %collective-permute-done.7.refs_0_ = bf16[768,512]{1,0:T(8,128)(2,1)S(1)} collective-permute-done((bf16[768,512]{1,0:T(8,128)(2,1)}, bf16[768,512]{1,0:T(8,128)(2,1)S(1)}, u32[]{:S(2)}, u32[]{:S(2)}) %collective-permute-start.7) | collective-permute-done | bytes 786464 | tf_op jit(solution)/shard_map/ppermute | solution.py:1104
  121.9 10.2 %project.4.base_ref = f32[768,2048]{1,0:T(8,128)} custom-call(s32[4]{0:T(128)} %add_add_fusion.meta, f32[768,2048]{1,0:T(8,128)} %project.3.base_ref, bf16[768,512]{1,0:T(8,128)(2,1)} %copy-done.14, bf16[768,512]{1,0:T(8,128)(2,1)} %copy-done.15, bf16[4,256,2048]{2,1,0:T(8,128)(2,1)} %bitcast.56, bf16[4,256,2048]{2,1,0:T(8,128)(2,1)} %bitcast.57, ...), custom_call_target="tpu_custom_call" | custom-call | flops 1 | bytes 1 | tf_op jit(solution)/shard_map/project/pallas_call | solution.py:581
  133.1 8.5 %project.5 = (f32[192,2048]{1,0:T(8,128)}, bf16[768,2048]{1,0:T(8,128)(2,1)}) custom-call(s32[3]{0:T(128)} %pad_add_fusion.5.meta, f32[768,2048]{1,0:T(8,128)} %project.4.base_ref, bf16[768,512]{1,0:T(8,128)(2,1)} %pad_maximum_fusion.refs_0_, bf16[4,256,2048]{2,1,0:T(8,128)(2,1)} %bitcast.58, ...), custom_call_target="tpu_custom_call" | custom-call | flops 1 | bytes 1 | tf_op jit(solution)/shard_map/project/pallas_call | solution.py:581
  141.6 26.4 %feed.1 = (bf16[768,1536]{1,0:T(8,128)(2,1)}, bf16[768,1536]{1,0:T(8,128)(2,1)}, bf16[768,1536]{1,0:T(8,128)(2,1)}, bf16[2048,3072]{1,0:T(8,128)(2,1)}) custom-call(bf16[768,2048]{1,0:T(8,128)(2,1)} %get-tuple-element.264.x_ref, bf16[2048,1536]{1,0:T(8,128)(2,1)} %refs_2_.1, bf16[2048,1536]{1,0:T(8,128)(2,1)} %refs_3_.2, f32[768,1536]{1,0:T(8,128)} %fusion.11.d_mixed_ref), custom_call_target="tpu_custom_call" | custom-call | flops 1 | bytes 1 | tf_op jit(solution)/shard_map/feed/pallas_call | solution.py:808
  168.4 15.4 %products.2 = (bf16[192,2048]{1,0:T(8,128)(2,1)}, bf16[192,2048]{1,0:T(8,128)(2,1)}, bf16[384,2048]{1,0:T(8,128)(2,1)}) custom-call(s32[1]{0:T(128)} %bitcast.meta, bf16[768,1536]{1,0:T(8,128)(2,1)} %get-tuple-element.266.refs_0_, bf16[768,1536]{1,0:T(8,128)(2,1)} %get-tuple-element.267.refs_1_, bf16[2048,1536]{1,0:T(8,128)(2,1)} %refs_2_.1, ...), custom_call_target="tpu_custom_call" | custom-call | flops 1 | bytes 1 | tf_op jit(solution)/shard_map/products/pallas_call | solution.py:864
  185.8 9.4 %products.3 = (bf16[192,2048]{1,0:T(8,128)(2,1)}, bf16[192,2048]{1,0:T(8,128)(2,1)}, bf16[384,2048]{1,0:T(8,128)(2,1)}) custom-call(s32[1]{0:T(128)} %bitcast.meta, bf16[768,1536]{1,0:T(8,128)(2,1)} %get-tuple-element.270.refs_0_.mixed_ref, bf16[1536,2048]{1,0:T(8,128)(2,1)} %refs_1_.1), custom_call_target="tpu_custom_call" | custom-call | flops 1 | bytes 1 | tf_op jit(solution)/shard_map/products/pallas_call | solution.py:864
  195.2 6.8 %collective-permute-done.12.x_ref = bf16[192,2048]{1,0:T(8,128)(2,1)S(1)} collective-permute-done((bf16[192,2048]{1,0:T(8,128)(2,1)}, bf16[192,2048]{1,0:T(8,128)(2,1)S(1)}, u32[]{:S(2)}, u32[]{:S(2)}) %collective-permute-start.12) | collective-permute-done | bytes 786464 | tf_op jit(solution)/shard_map/ppermute | solution.py:1104
  209.0 6.9 %collective-permute-done.14.refs_1_ = bf16[96,2048]{1,0:T(8,128)(2,1)S(1)} collective-permute-done((bf16[96,2048]{1,0:T(8,128)(2,1)}, bf16[96,2048]{1,0:T(8,128)(2,1)S(1)}, u32[]{:S(2)}, u32[]{:S(2)}) %collective-permute-start.14) | collective-permute-done | bytes 393248 | tf_op jit(solution)/shard_map/ppermute | solution.py:1104
  216.9 10.3 %turn.1 = (bf16[4,192,512]{2,1,0:T(8,128)(2,1)}, f32[192,2048]{1,0:T(8,128)}, bf16[192,2048]{1,0:T(8,128)(2,1)}, f32[1,2048]{1,0:T(1,128)}) custom-call(s32[2]{0:T(128)} %pad_add_fusion.8.meta, f32[192,2048]{1,0:T(8,128)} %get-tuple-element.280.refs_0_, bf16[96,2048]{1,0:T(8,128)(2,1)} %copy-done.41, bf16[96,2048]{1,0:T(8,128)(2,1)} %copy-done.42, ...), custom_call_target="tpu_custom_call" | custom-call | flops 1 | bytes 1 | tf_op jit(solution)/shard_map/turn/pallas_call | solution.py:715
  267.2 6.8 %attend_back.5 = (f32[768,512]{1,0:T(8,128)}, f32[768,512]{1,0:T(8,128)}, bf16[768,512]{1,0:T(8,128)(2,1)}) custom-call(s32[4]{0:T(128)} %get-tuple-element.411.meta, bf16[768,1024]{1,0:T(8,128)(2,1)} %get-tuple-element.255.q_ref, bf16[768,1024]{1,0:T(8,128)(2,1)} %with_delta.1.do_ref, ...), custom_call_target="tpu_custom_call", output_to_operand_aliasing={{0}: (6, {})} | custom-call | flops 1 | bytes 1 | tf_op jit(solution)/shard_map/attend_back/pallas_call | solution.py:504
  274.0 18.8 %collective-permute-done.24.refs_0_ = bf16[384,512]{1,0:T(8,128)(2,1)S(1)} collective-permute-done((bf16[384,512]{1,0:T(8,128)(2,1)}, bf16[384,512]{1,0:T(8,128)(2,1)S(1)}, u32[]{:S(2)}, u32[]{:S(2)}) %collective-permute-start.24) | collective-permute-done | bytes 393248 | tf_op jit(solution)/shard_map/ppermute | solution.py:1101
  295.6 13.8 %column_sums.1 = bf16[8,2048,256]{2,1,0:T(8,128)(2,1)} custom-call(s32[4]{0:T(128)} %pad_add_fusion.9.owners.places, bf16[768,1536]{1,0:T(8,128)(2,1)} %get-tuple-element.270.refs_0_.mixed_ref, bf16[768,512]{1,0:T(8,128)(2,1)} %get-tuple-element.256.refs_0_.o_ref, bf16[768,2048]{1,0:T(8,128)(2,1)} %dy_ref.1, bf16[192,2048]{1,0:T(8,128)(2,1)} %get-tuple-element.294.refs_0_, ...), custom_call_target="tpu_custom_call" | custom-call | flops 1 | bytes 1 | tf_op jit(solution)/shard_map/column_sums/pallas_call | solution.py:894
  309.4 9.2 %collective-permute-done.25.refs_1_ = bf16[384,512]{1,0:T(8,128)(2,1)S(1)} collective-permute-done((bf16[384,512]{1,0:T(8,128)(2,1)}, bf16[384,512]{1,0:T(8,128)(2,1)S(1)}, u32[]{:S(2)}, u32[]{:S(2)}) %collective-permute-start.25) | collective-permute-done | bytes 393248 | tf_op jit(solution)/shard_map/ppermute | solution.py:1101
  328.8 6.7 %attend_back.6 = (f32[768,512]{1,0:T(8,128)}, f32[768,512]{1,0:T(8,128)}, bf16[768,512]{1,0:T(8,128)(2,1)}) custom-call(s32[4]{0:T(128)} %get-tuple-element.429.meta, bf16[768,1024]{1,0:T(8,128)(2,1)} %get-tuple-element.255.q_ref, bf16[768,1024]{1,0:T(8,128)(2,1)} %with_delta.1.do_ref, bf16[768,512]{1,0:T(8,128)(2,1)} %copy-done.6, ...), custom_call_target="tpu_custom_call", output_to_operand_aliasing={{0}: (6, {})} | custom-call | flops 1 | bytes 1 | tf_op jit(solution)/shard_map/attend_back/pallas_call | solution.py:504
  335.5 13.3 %collective-permute-done.29.refs_0_ = bf16[384,512]{1,0:T(8,128)(2,1)S(1)} collective-permute-done((bf16[384,512]{1,0:T(8,128)(2,1)}, bf16[384,512]{1,0:T(8,128)(2,1)S(1)}, u32[]{:S(2)}, u32[]{:S(2)}) %collective-permute-start.29) | collective-permute-done | bytes 393248 | tf_op jit(solution)/shard_map/ppermute | solution.py:1101
  353.5 10.9 %attend_back.7 = (f32[768,512]{1,0:T(8,128)}, f32[768,512]{1,0:T(8,128)}, bf16[768,512]{1,0:T(8,128)(2,1)}) custom-call(s32[4]{0:T(128)} %get-tuple-element.427.meta, bf16[768,1024]{1,0:T(8,128)(2,1)} %get-tuple-element.255.q_ref, bf16[768,1024]{1,0:T(8,128)(2,1)} %with_delta.1.do_ref, ...), custom_call_target="tpu_custom_call", output_to_operand_aliasing={{0}: (6, {})} | custom-call | flops 1 | bytes 1 | tf_op jit(solution)/shard_map/attend_back/pallas_call | solution.py:504
  377.7 6.7 %collective-permute-start.40 = (bf16[768,512]{1,0:T(8,128)(2,1)}, bf16[768,512]{1,0:T(8,128)(2,1)S(1)}, u32[]{:S(2)}, u32[]{:S(2)}) collective-permute-start(bf16[768,512]{1,0:T(8,128)(2,1)} %get-tuple-element.368), channel_id=1, source_target_pairs={{0,4},{4,0},{8,12},{12,8},{16,20},{20,16},{24,28},{28,24},{1,5},{5... | collective-permute-start | bytes 2359304 | tf_op jit(solution)/shard_map/ppermute | solution.py:1095
  399.5 17.8 %collective-permute-done.37.second_ref = bf16[384,512]{1,0:T(8,128)(2,1)S(1)} collective-permute-done((bf16[384,512]{1,0:T(8,128)(2,1)}, bf16[384,512]{1,0:T(8,128)(2,1)S(1)}, u32[]{:S(2)}, u32[]{:S(2)}) %collective-permute-start.37) | collective-permute-done | bytes 393248 | tf_op jit(solution)/shard_map/ppermute | solution.py:1101
  419.0 12.8 %leave.1 = (bf16[768,256]{1,0:T(8,128)(2,1)}, bf16[768,256]{1,0:T(8,128)(2,1)}, f32[1,128]{1,0:T(1,128)}, f32[1,2048]{1,0:T(1,128)}, bf16[192,2048]{1,0:T(8,128)...) custom-call(s32[1]{0:T(128)} %bitcast.meta, bf16[768,2048]{1,0:T(8,128)(2,1)} %refs_3_.3, ...), custom_call_target="tpu_custom_call" | custom-call | flops 1 | bytes 1 | tf_op jit(solution)/shard_map/leave/pallas_call | solution.py:1023
  435.7 9.0 %attn_sums.1 = bf16[2048,1024]{1,0:T(8,128)(2,1)} custom-call(bf16[768,2048]{1,0:T(8,128)(2,1)} %get-tuple-element.231.x_ref, bf16[768,512]{1,0:T(8,128)(2,1)} %get-tuple-element.366.q_ref, bf16[768,256]{1,0:T(8,128)(2,1)} %get-tuple-element.379.k_ref, bf16[768,256]{1,0:T(8,128)(2,1)} %get-tuple-element.380.v_ref), custom_call_target="tpu_custom_call" | custom-call | flops 1 | bytes 1 | tf_op jit(solution)/shard_map/attn_sums/pallas_call | solution.py:1069
  484.5 11.2 %collective-permute-done.48.refs_2_.refs_3_ = bf16[224,2048]{1,0:T(8,128)(2,1)S(1)} collective-permute-done((bf16[224,2048]{1,0:T(8,128)(2,1)}, bf16[224,2048]{1,0:T(8,128)(2,1)S(1)}, u32[]{:S(2)}, u32[]{:S(2)}) %collective-permute-start.48) | collective-permute-done | bytes 917536 | tf_op jit(solution)/shard_map/ppermute | solution.py:1104
  (288 shorter events, 247.6 us)
Async XLA Ops:
  7.2 82.9 %all-gather.3.cloned.1.call-start = ((), (), s32[]{:S(2)}) async-start(), calls=%async_computation.6 | async-start | bytes 5242880 | tf_op jit(solution)/shard_map/all_gather | solution.py:1216
  19.2 299.9 %reduce-scatter.4.cloned.1.call-start = ((), (), s32[]{:S(2)}) async-start(), calls=%async_computation.3 | async-start | bytes 14155776 | tf_op jit(solution)/shard_map/reduce_scatter | solution.py:1266
  19.4 21.7 %collective-permute-start = (bf16[768,512]{1,0:T(8,128)(2,1)S(1)}, bf16[768,512]{1,0:T(8,128)(2,1)S(1)}, u32[]{:S(2)}, u32[]{:S(2)}) collective-permute-start(bf16[768,512]{1,0:T(8,128)(2,1)S(1)} %copy-done.4), channel_id=1, source_target_pairs={{0,8},{4,12},{8,16},{12,20},{16,24},{20,28},{1,9},{5,13},{9,17},{1... | collective-permute-start | bytes 2359304 | tf_op jit(solution)/shard_map/ppermute | solution.py:1098
  24.4 22.0 %collective-permute-start.2 = (bf16[768,512]{1,0:T(8,128)(2,1)S(1)}, bf16[768,512]{1,0:T(8,128)(2,1)S(1)}, u32[]{:S(2)}, u32[]{:S(2)}) collective-permute-start(bf16[768,512]{1,0:T(8,128)(2,1)S(1)} %copy-done.4), channel_id=1, source_target_pairs={{0,4},{4,0},{8,12},{12,8},{16,20},{20,16},{24,28},{28,24},{1,5},{5... | collective-permute-start | bytes 2359304 | tf_op jit(solution)/shard_map/ppermute | solution.py:1095
  41.1 23.0 %collective-permute-start.1 = (bf16[768,512]{1,0:T(8,128)(2,1)S(1)}, bf16[768,512]{1,0:T(8,128)(2,1)}, u32[]{:S(2)}, u32[]{:S(2)}) collective-permute-start(bf16[768,512]{1,0:T(8,128)(2,1)S(1)} %collective-permute-done.kva_ref), channel_id=1, source_target_pairs={{0,8},{4,12},{8,16},{12,20},{16,24},{20,28},{1,9},{5,13},{9,17},{1... | collective-permute-start | bytes 2359304 | tf_op jit(solution)/shard_map/ppermute | solution.py:1098
  46.4 24.4 %collective-permute-start.5 = (bf16[768,512]{1,0:T(8,128)(2,1)S(1)}, bf16[768,512]{1,0:T(8,128)(2,1)}, u32[]{:S(2)}, u32[]{:S(2)}) collective-permute-start(bf16[768,512]{1,0:T(8,128)(2,1)S(1)} %collective-permute-done.kva_ref), channel_id=1, source_target_pairs={{0,4},{4,0},{8,12},{12,8},{16,20},{20,16},{24,28},{28,24},{1,5},{5... | collective-permute-start | bytes 2359304 | tf_op jit(solution)/shard_map/ppermute | solution.py:1095
  67.9 19.9 %collective-permute-start.3 = (bf16[768,512]{1,0:T(8,128)(2,1)}, bf16[768,512]{1,0:T(8,128)(2,1)S(1)}, u32[]{:S(2)}, u32[]{:S(2)}) collective-permute-start(bf16[768,512]{1,0:T(8,128)(2,1)} %collective-permute-done.1.kva_ref), channel_id=1, source_target_pairs={{0,8},{4,12},{8,16},{12,20},{16,24},{20,28},{1,9},{5,13},{9,17},{1... | collective-permute-start | bytes 2359304 | tf_op jit(solution)/shard_map/ppermute | solution.py:1098
  97.4 19.8 %collective-permute-start.7 = (bf16[768,512]{1,0:T(8,128)(2,1)}, bf16[768,512]{1,0:T(8,128)(2,1)S(1)}, u32[]{:S(2)}, u32[]{:S(2)}) collective-permute-start(bf16[768,512]{1,0:T(8,128)(2,1)} %get-tuple-element.256.refs_0_.o_ref), channel_id=1, source_target_pairs={{0,1},{1,0},{2,3},{3,2},{4,5},{5,4},{6,7},{7,6},{8,9},{9,8},{10,11... | collective-permute-start | bytes 2359304 | tf_op jit(solution)/shard_map/ppermute | solution.py:1104
  168.0 282.9 %reduce-scatter.6.cloned.1.call-start = ((), (), s32[]{:S(2)}) async-start(), calls=%async_computation.4 | async-start | bytes 9437184 | tf_op jit(solution)/shard_map/reduce_scatter | solution.py:1266
  265.8 27.0 %collective-permute-start.24 = (bf16[384,512]{1,0:T(8,128)(2,1)}, bf16[384,512]{1,0:T(8,128)(2,1)S(1)}, u32[]{:S(2)}, u32[]{:S(2)}) collective-permute-start(bf16[384,512]{1,0:T(8,128)(2,1)} %get-tuple-element.308), channel_id=1, source_target_pairs={{8,0},{12,4},{16,8},{20,12},{24,16},{28,20},{9,1},{13,5},{17,9},{2... | collective-permute-start | bytes 1179656 | tf_op jit(solution)/shard_map/ppermute | solution.py:1101
  292.8 25.8 %collective-permute-start.26 = (bf16[768,512]{1,0:T(8,128)(2,1)}, bf16[768,512]{1,0:T(8,128)(2,1)S(1)}, u32[]{:S(2)}, u32[]{:S(2)}) collective-permute-start(bf16[768,512]{1,0:T(8,128)(2,1)} %get-tuple-element.313), channel_id=1, source_target_pairs={{0,4},{4,0},{8,12},{12,8},{16,20},{20,16},{24,28},{28,24},{1,5},{5... | collective-permute-start | bytes 2359304 | tf_op jit(solution)/shard_map/ppermute | solution.py:1095
  292.8 25.8 %collective-permute-start.25 = (bf16[384,512]{1,0:T(8,128)(2,1)}, bf16[384,512]{1,0:T(8,128)(2,1)S(1)}, u32[]{:S(2)}, u32[]{:S(2)}) collective-permute-start(bf16[384,512]{1,0:T(8,128)(2,1)} %get-tuple-element.312), channel_id=1, source_target_pairs={{8,0},{12,4},{16,8},{20,12},{24,16},{28,20},{9,1},{13,5},{17,9},{2... | collective-permute-start | bytes 1179656 | tf_op jit(solution)/shard_map/ppermute | solution.py:1101
  319.7 197.3 %reduce-scatter.8.cloned.1.call-start = ((), (), s32[]{:S(2)}) async-start(), calls=%async_computation.5 | async-start | bytes 4718592 | tf_op jit(solution)/shard_map/reduce_scatter | solution.py:1266
  322.6 26.2 %collective-permute-start.27 = (bf16[192,2048]{1,0:T(8,128)(2,1)S(1)}, bf16[192,2048]{1,0:T(8,128)(2,1)S(1)}, u32[]{:S(2)}, u32[]{:S(2)}) collective-permute-start(bf16[192,2048]{1,0:T(8,128)(2,1)S(1)} %copy-done.52), channel_id=1, source_target_pairs={{0,1},{1,0},{2,3},{3,2},{4,5},{5,4},{6,7},{7,6},{8,9},{9,8},{10,11... | collective-permute-start | bytes 2359304 | tf_op jit(solution)/shard_map/ppermute | solution.py:1104
  323.9 25.0 %collective-permute-start.28 = (bf16[192,2048]{1,0:T(8,128)(2,1)S(1)}, bf16[192,2048]{1,0:T(8,128)(2,1)S(1)}, u32[]{:S(2)}, u32[]{:S(2)}) collective-permute-start(bf16[192,2048]{1,0:T(8,128)(2,1)S(1)} %copy-done.51), channel_id=1, source_target_pairs={{0,2},{1,3},{2,0},{3,1},{4,6},{5,7},{6,4},{7,5},{8,10},{9,11},{10,... | collective-permute-start | bytes 2359304 | tf_op jit(solution)/shard_map/ppermute | solution.py:1104
  326.2 22.6 %collective-permute-start.29 = (bf16[384,512]{1,0:T(8,128)(2,1)}, bf16[384,512]{1,0:T(8,128)(2,1)S(1)}, u32[]{:S(2)}, u32[]{:S(2)}) collective-permute-start(bf16[384,512]{1,0:T(8,128)(2,1)} %get-tuple-element.333), channel_id=1, source_target_pairs={{8,0},{12,4},{16,8},{20,12},{24,16},{28,20},{9,1},{13,5},{17,9},{2... | collective-permute-start | bytes 1179656 | tf_op jit(solution)/shard_map/ppermute | solution.py:1101
  327.5 38.1 %collective-permute-start.33 = (bf16[384,512]{1,0:T(8,128)(2,1)}, bf16[384,512]{1,0:T(8,128)(2,1)S(1)}, u32[]{:S(2)}, u32[]{:S(2)}) collective-permute-start(bf16[384,512]{1,0:T(8,128)(2,1)} %get-tuple-element.346), channel_id=1, source_target_pairs={{8,0},{12,4},{16,8},{20,12},{24,16},{28,20},{9,1},{13,5},{17,9},{2... | collective-permute-start | bytes 1179656 | tf_op jit(solution)/shard_map/ppermute | solution.py:1101
  369.7 25.8 %collective-permute-start.35 = (bf16[192,2048]{1,0:T(8,128)(2,1)}, bf16[192,2048]{1,0:T(8,128)(2,1)S(1)}, u32[]{:S(2)}, u32[]{:S(2)}) collective-permute-start(bf16[192,2048]{1,0:T(8,128)(2,1)} %add_rows.1.refs_0_), channel_id=1, source_target_pairs={{0,1},{1,0},{2,3},{3,2},{4,5},{5,4},{6,7},{7,6},{8,9},{9,8},{10,11... | collective-permute-start | bytes 2359304 | tf_op jit(solution)/shard_map/ppermute | solution.py:1104
  370.5 25.0 %collective-permute-start.36 = (bf16[192,2048]{1,0:T(8,128)(2,1)}, bf16[192,2048]{1,0:T(8,128)(2,1)S(1)}, u32[]{:S(2)}, u32[]{:S(2)}) collective-permute-start(bf16[192,2048]{1,0:T(8,128)(2,1)} %add_rows.1.refs_0_), channel_id=1, source_target_pairs={{0,2},{1,3},{2,0},{3,1},{4,6},{5,7},{6,4},{7,5},{8,10},{9,11},{10,... | collective-permute-start | bytes 2359304 | tf_op jit(solution)/shard_map/ppermute | solution.py:1104
  376.4 21.8 %collective-permute-start.34 = (bf16[384,512]{1,0:T(8,128)(2,1)}, bf16[384,512]{1,0:T(8,128)(2,1)S(1)}, u32[]{:S(2)}, u32[]{:S(2)}) collective-permute-start(bf16[384,512]{1,0:T(8,128)(2,1)} %get-tuple-element.351), channel_id=1, source_target_pairs={{8,0},{12,4},{16,8},{20,12},{24,16},{28,20},{9,1},{13,5},{17,9},{2... | collective-permute-start | bytes 1179656 | tf_op jit(solution)/shard_map/ppermute | solution.py:1101
  377.7 39.7 %collective-permute-start.40 = (bf16[768,512]{1,0:T(8,128)(2,1)}, bf16[768,512]{1,0:T(8,128)(2,1)S(1)}, u32[]{:S(2)}, u32[]{:S(2)}) collective-permute-start(bf16[768,512]{1,0:T(8,128)(2,1)} %get-tuple-element.368), channel_id=1, source_target_pairs={{0,4},{4,0},{8,12},{12,8},{16,20},{20,16},{24,28},{28,24},{1,5},{5... | collective-permute-start | bytes 2359304 | tf_op jit(solution)/shard_map/ppermute | solution.py:1095
  394.0 23.3 %collective-permute-start.37 = (bf16[384,512]{1,0:T(8,128)(2,1)}, bf16[384,512]{1,0:T(8,128)(2,1)S(1)}, u32[]{:S(2)}, u32[]{:S(2)}) collective-permute-start(bf16[384,512]{1,0:T(8,128)(2,1)} %get-tuple-element.362), channel_id=1, source_target_pairs={{8,0},{12,4},{16,8},{20,12},{24,16},{28,20},{9,1},{13,5},{17,9},{2... | collective-permute-start | bytes 1179656 | tf_op jit(solution)/shard_map/ppermute | solution.py:1101
  473.2 22.5 %collective-permute-start.48 = (bf16[224,2048]{1,0:T(8,128)(2,1)}, bf16[224,2048]{1,0:T(8,128)(2,1)S(1)}, u32[]{:S(2)}, u32[]{:S(2)}) collective-permute-start(bf16[224,2048]{1,0:T(8,128)(2,1)} %last.1.refs_0_.refs_1_), channel_id=1, source_target_pairs={{0,1},{1,0},{2,3},{3,2},{4,5},{5,4},{6,7},{7,6},{8,9},{9,8},{10,11... | collective-permute-start | bytes 2752520 | tf_op jit(solution)/shard_map/ppermute | solution.py:1104
  474.4 22.8 %collective-permute-start.49 = (bf16[224,2048]{1,0:T(8,128)(2,1)}, bf16[224,2048]{1,0:T(8,128)(2,1)S(1)}, u32[]{:S(2)}, u32[]{:S(2)}) collective-permute-start(bf16[224,2048]{1,0:T(8,128)(2,1)} %last.1.refs_0_.refs_1_), channel_id=1, source_target_pairs={{0,2},{1,3},{2,0},{3,1},{4,6},{5,7},{6,4},{7,5},{8,10},{9,11},{10,... | collective-permute-start | bytes 2752520 | tf_op jit(solution)/shard_map/ppermute | solution.py:1104
  (86 other events, 704.1 us)
Sparse Core Ops, SparseCore 0:
  19.3 55.3 all-gather.2
  168.1 151.0 reduce-scatter.3
  321.5 122.8 reduce-scatter.5
  451.0 52.1 reduce-scatter.7

commit v6 on v5

--- a/solution.py
+++ b/solution.py
@@ -236,9 +236,9 @@
     return slice(i * KEY_CHUNK, (i + n) * KEY_CHUNK)
 
 
-def attend_kernel(meta, q_ref, kva_ref, kvb_ref, bounds_ref, *refs, first, last):
+def attend_kernel(meta, q_ref, *refs, places, first, last):
+    kv_refs, bounds_ref, refs = refs[: len(places)], refs[len(places)], refs[len(places) + 1 :]
     rows = q_ref.shape[0]
-    key_rows = kva_ref.shape[0]
     if last:
         acc_in, sum_in, o_ref, q_out_ref, acc_ref, sum_ref = refs
     elif first:
@@ -263,8 +263,9 @@
         acc_ref[queries, :] += out[:, :HEAD_WIDTH]
         sum_ref[queries, :] += out[:, HEAD_WIDTH:]
 
-    for place, kv_ref in enumerate((kva_ref, kvb_ref)):
+    for place, kv_ref in zip(places, kv_refs):
         key_start = meta[2 + place]
+        key_rows = kv_ref.shape[0]
         diagonal = first and place == 0
 
         @pl.when(block_used(meta, key_start, key_rows, rows))
@@ -291,35 +292,42 @@
         q_out_ref[:, HEAD_WIDTH:] = extra.astype(bf16)
 
 
-def attend_stage(q, kv_a, kv_b, bounds, meta, carried, last):
+def attend_stage(q, blocks, places, bounds, meta, carried, last=None):
     rows = q.shape[0]
-    key_rows = kv_a.shape[0]
+    kv = blocks[0]
     q_heads = q.shape[1] // (2 * HEAD_WIDTH)
-    group = q.shape[1] // kv_a.shape[1]
+    group = q.shape[1] // kv.shape[1]
     width = q_heads * HEAD_WIDTH
     first = not carried
     wide = 2 * HEAD_WIDTH
-    per_q = pl.BlockSpec((rows, wide), lambda j, m: (0, j))
-    per_kv = pl.BlockSpec((key_rows, wide), lambda j, m: (0, j // group))
-    per_out = pl.BlockSpec((rows, HEAD_WIDTH), lambda j, m: (0, j))
+    count = len(blocks)
+    grid = q_heads if last is None else q_heads // last[1]
+    start = 0 if last is None else last[0] * grid
+    per_q = pl.BlockSpec((rows, wide), lambda j, m: (0, j + start))
+    per_kv = pl.BlockSpec((kv.shape[0], wide), lambda j, m: (0, (j + start) // group))
+    per_out = pl.BlockSpec((rows, HEAD_WIDTH), lambda j, m: (0, j + start))
     table = pl.BlockSpec((8, HEAD_WIDTH), lambda j, m: (0, 0))
     running = jax.ShapeDtypeStruct((rows, width), f32)
-    if last:
-        out_specs = [per_out, per_q, per_out]
-        out_shape = [jax.ShapeDtypeStruct((rows, width), bf16), jax.ShapeDtypeStruct(q.shape, bf16), running]
+    if last is not None:
+        out_specs = [pl.BlockSpec((rows, HEAD_WIDTH), lambda j, m: (0, j)), per_q, per_out]
+        out_shape = [
+            jax.ShapeDtypeStruct((rows, grid * HEAD_WIDTH), bf16),
+            jax.ShapeDtypeStruct(q.shape, bf16),
+            running,
+        ]
         scratch = [pltpu.VMEM((rows, HEAD_WIDTH), f32)]
-        aliases = {5: 2}
+        aliases = {1: 1, 3 + count: 2}
     else:
         out_specs = [per_out, per_out]
         out_shape = [running, running]
         scratch = []
-        aliases = {} if first else {5: 0, 6: 1}
-    return pl.pallas_call(
-        functools.partial(attend_kernel, first=first, last=last),
+        aliases = {} if first else {3 + count: 0, 4 + count: 1}
+    return pl.pallas_call(
+        functools.partial(attend_kernel, places=places, first=first, last=last is not None),
         grid_spec=pltpu.PrefetchScalarGridSpec(
             num_scalar_prefetch=1,
-            grid=(q_heads,),
-            in_specs=[per_q, per_kv, per_kv, table] + [per_out] * len(carried),
+            grid=(grid,),
+            in_specs=[per_q] + [per_kv] * count + [table] + [per_out] * len(carried),
             out_specs=out_specs,
             scratch_shapes=scratch,
         ),
@@ -328,7 +336,7 @@
         compiler_params=WHOLE_VMEM,
         cost_estimate=SMALL,
         name="attend_stage",
-    )(meta, q, kv_a, kv_b, bounds, *carried)
+    )(meta, q, *blocks, bounds, *carried)
 
 
 def delta_kernel(owners, *refs):
@@ -434,22 +442,20 @@
     return cut_up(array, [(height, array.shape[1]) for height in heights], 0)
 
 
-def attend_back_kernel(
-    meta, q_ref, do_ref, kva_ref, kvb_ref, bounds_ref, *refs, first, group, diagonal
-):
-    if first:
-        dq_ref, dkva_ref, dkvb_ref, dq_turned, sum_a, sum_b = refs
-    else:
-        dq_in, dq_ref, dkva_ref, dkvb_ref, dq_turned, sum_a, sum_b = refs
+def attend_back_kernel(meta, q_ref, do_ref, *refs, places, first, group, diagonal):
+    count = len(places)
+    kv_refs, bounds_ref, refs = refs[:count], refs[count], refs[count + 1 :]
+    if not first:
+        dq_in, *refs = refs
+    dq_ref, dkv_refs, dq_turned, sums = refs[0], refs[1 : 1 + count], refs[1 + count], refs[2 + count :]
     rows = q_ref.shape[0]
-    key_rows = kva_ref.shape[0]
     step = lax.rem(pl.program_id(0), group)
     dq_turned[...] = jnp.zeros_like(dq_turned)
 
     @pl.when(step == 0)
     def _():
-        sum_a[...] = jnp.zeros_like(sum_a)
-        sum_b[...] = jnp.zeros_like(sum_b)
+        for total in sums:
+            total[...] = jnp.zeros_like(total)
 
     def work(kv_ref, total, lanes, ones, keys, queries, mask):
         key = kv_ref[keys, :HEAD_WIDTH]
@@ -464,8 +470,9 @@
         total[keys, :HEAD_WIDTH] += dot(d_score, q[:, :HEAD_WIDTH])
         dq_turned[:, queries] += dot_tn(key, d_score)
 
-    for place, (kv_ref, total) in enumerate(((kva_ref, sum_a), (kvb_ref, sum_b))):
+    for place, kv_ref, total in zip(places, kv_refs, sums):
         key_start = meta[2 + place]
+        key_rows = kv_ref.shape[0]
 
         @pl.when(block_used(meta, key_start, key_rows, rows))
         def _():
@@ -485,112 +492,103 @@
 
     @pl.when(step == group - 1)
     def _():
-        dkva_ref[...] = sum_a[...]
-        dkvb_ref[...] = sum_b[...].astype(bf16)
-
-
-def attend_back(q, do, kv_a, kv_b, bounds, meta, dq, diagonal):
+        for ref, total in zip(dkv_refs, sums):
+            ref[...] = total[...].astype(ref.dtype)
+
+
+def attend_back(q, do, blocks, places, bounds, meta, dq, diagonal):
     rows = q.shape[0]
-    key_rows = kv_a.shape[0]
+    kv = blocks[0]
     q_heads = q.shape[1] // (2 * HEAD_WIDTH)
-    group = q.shape[1] // kv_a.shape[1]
+    group = q.shape[1] // kv.shape[1]
     width = q_heads * HEAD_WIDTH
     first = dq is None
+    count = len(places)
     wide = 2 * HEAD_WIDTH
     per_q = pl.BlockSpec((rows, wide), lambda j, m: (0, j))
-    per_kv = pl.BlockSpec((key_rows, wide), lambda j, m: (0, j // group))
+    per_kv = pl.BlockSpec((kv.shape[0], wide), lambda j, m: (0, j // group))
     per_out = pl.BlockSpec((rows, HEAD_WIDTH), lambda j, m: (0, j))
     table = pl.BlockSpec((8, HEAD_WIDTH), lambda j, m: (0, 0))
     return pl.pallas_call(
-        functools.partial(attend_back_kernel, first=first, group=group, diagonal=diagonal),
+        functools.partial(
+            attend_back_kernel, places=places, first=first, group=group, diagonal=diagonal
+        ),
         grid_spec=pltpu.PrefetchScalarGridSpec(
             num_scalar_prefetch=1,
             grid=(q_heads,),
-            in_specs=[per_q, per_q, per_kv, per_kv, table] + ([] if first else [per_out]),
-            out_specs=[per_out, per_kv, per_kv],
-            scratch_shapes=[
-                pltpu.VMEM((HEAD_WIDTH, rows), f32),
-                pltpu.VMEM((key_rows, wide), f32),
-                pltpu.VMEM((key_rows, wide), f32),
-            ],
+            in_specs=[per_q, per_q] + [per_kv] * count + [table] + ([] if first else [per_out]),
+            out_specs=[per_out] + [per_kv] * count,
+            scratch_shapes=[pltpu.VMEM((HEAD_WIDTH, rows), f32)]
+            + [pltpu.VMEM((kv.shape[0], wide), f32)] * count,
         ),
-        out_shape=[
-            jax.ShapeDtypeStruct((rows, width), f32),
-            jax.ShapeDtypeStruct(kv_a.shape, f32),
-            jax.ShapeDtypeStruct(kv_b.shape, bf16),
-        ],
-        input_output_aliases={} if first else {6: 0},
+        out_shape=[jax.ShapeDtypeStruct((rows, width), f32)]
+        + [jax.ShapeDtypeStruct(kv.shape, bf16 if place else f32) for place in places],
+        input_output_aliases={} if first else {4 + count: 0},
         compiler_params=WHOLE_VMEM,
         cost_estimate=SMALL,
         name="attend_back",
-    )(meta, q, do, kv_a, kv_b, bounds, *(() if first else (dq,)))
-
-
-def project_kernel(meta, base_ref, *refs, count, final):
-    pieces, mine, other = refs[:count], refs[count : 2 * count], refs[2 * count : 3 * count]
-    if final:
-        gain_ref, share_ref, normed_ref = refs[3 * count :]
-    else:
-        (out_ref,) = refs[3 * count :]
+    )(meta, q, do, *blocks, bounds, *(() if first else (dq,)))
+
+
+def project_kernel(meta, base_ref, *refs, count):
+    lows, highs = refs[:count], refs[count : 2 * count]
+    mine, other = refs[2 * count : 3 * count], refs[3 * count : 4 * count]
+    gain_ref, share_ref, normed_ref = refs[4 * count :]
     first_core = meta[0] == 0
     total = base_ref[...].astype(f32)
-    for piece, mine_ref, other_ref in zip(pieces, mine, other):
-        half = piece.shape[1] // 2
-        low, high = piece[:, :half], piece[:, half:]
+    for low_ref, high_ref, mine_ref, other_ref in zip(lows, highs, mine, other):
+        low, high = low_ref[...], high_ref[...]
         total += dot(jnp.where(first_core, low, high), mine_ref[0])
         total += dot(jnp.where(first_core, high, low), other_ref[0])
-    if final:
-        inverse = lax.rsqrt(jnp.mean(total * total, axis=-1, keepdims=True) + EPSILON)
-        normed_ref[...] = (total * inverse * gain_ref[...]).astype(bf16)
-
-        @pl.when(pl.program_id(0) == meta[1])
-        def _():
-            share_ref[...] = total
-
-    else:
-        out_ref[...] = total
-
-
-def project(base, pieces, w_mine, w_other, core, me, gain=None):
+    inverse = lax.rsqrt(jnp.mean(total * total, axis=-1, keepdims=True) + EPSILON)
+    normed_ref[...] = (total * inverse * gain_ref[...]).astype(bf16)
+
+    @pl.when(pl.program_id(0) == meta[1])
+    def _():
+        share_ref[...] = total
+
+
+def project(base, pieces, w_mine, w_other, core, me, gain):
     meta = jnp.stack(
-        [jnp.asarray(v, jnp.int32) for v in [core, me] + [owner for unused, owner in pieces]]
+        [jnp.asarray(v, jnp.int32) for v in [core, me] + [piece[2] for piece in pieces]]
     )
     rows, width = base.shape
     n_head, half, unused = w_mine.shape
     count = len(pieces)
-    final = gain is not None
     step = rows // n_head
     per_row = pl.BlockSpec((step, width), lambda i, m: (i, 0))
-    per_piece = pl.BlockSpec((step, 2 * half), lambda i, m: (i, 0))
+    per_piece = pl.BlockSpec((step, half), lambda i, m: (i, 0))
     weights = [
         pl.BlockSpec((1, half, width), lambda i, m, k=k: (m[2 + k], 0, 0)) for k in range(count)
     ]
-    in_specs = [per_row] + [per_piece] * count + weights + weights
-    args = [base] + [piece for piece, unused in pieces] + [w_mine] * count + [w_other] * count
-    if final:
-        in_specs.append(pl.BlockSpec((1, width), lambda i, m: (0, 0)))
-        args.append(gain[None, :])
-        out_specs = [pl.BlockSpec((step, width), lambda i, m: (0, 0)), per_row]
-        out_shape = [
+    return pl.pallas_call(
+        functools.partial(project_kernel, count=count),
+        grid_spec=pltpu.PrefetchScalarGridSpec(
+            num_scalar_prefetch=1,
+            grid=(n_head,),
+            in_specs=[per_row]
+            + [per_piece] * (2 * count)
+            + weights
+            + weights
+            + [pl.BlockSpec((1, width), lambda i, m: (0, 0))],
+            out_specs=[pl.BlockSpec((step, width), lambda i, m: (0, 0)), per_row],
+        ),
+        out_shape=[
             jax.ShapeDtypeStruct((step, width), f32),
             jax.ShapeDtypeStruct((rows, width), bf16),
-        ]
-    else:
-        out_specs = per_row
-        out_shape = jax.ShapeDtypeStruct((rows, width), f32)
-    return pl.pallas_call(
-        functools.partial(project_kernel, count=count, final=final),
-        grid_spec=pltpu.PrefetchScalarGridSpec(
-            num_scalar_prefetch=1,
-            grid=(rows // step,),
-            in_specs=in_specs,
-            out_specs=out_specs,
-        ),
-        out_shape=out_shape,
+        ],
         compiler_params=WHOLE_VMEM,
         cost_estimate=SMALL,
         name="project",
-    )(meta, *args)
+    )(
+        meta,
+        base,
+        *[piece[0] for piece in pieces],
+        *[piece[1] for piece in pieces],
+        *[w_mine] * count,
+        *[w_other] * count,
+        gain[None, :],
+    )
 
 
 def arranged_shapes(rows, width):
@@ -682,7 +680,7 @@
 def turn_kernel(meta, *refs, count):
     terms = refs[:count]
     hidden_ref, dy_ref, gain_ref, mine_ref, other_ref = refs[count : count + 5]
-    out_ref, grad_ref, branch_ref, gain_grad_ref = refs[count + 5 :]
+    *outs, grad_ref, branch_ref, gain_grad_ref = refs[count + 5 :]
 
     @pl.when(pl.program_id(0) == 0)
     def _():
@@ -698,8 +696,14 @@
     mine = dot_nt(branch, mine_ref[0])
     other = dot_nt(branch, other_ref[0])
     first_core = meta[0] == 0
-    out_ref[0, :, :half] = jnp.where(first_core, mine, other).astype(bf16)
-    out_ref[0, :, half:] = jnp.where(first_core, other, mine).astype(bf16)
+    low = jnp.where(first_core, mine, other).astype(bf16)
+    high = jnp.where(first_core, other, mine).astype(bf16)
+    for i, out_ref in enumerate(outs):
+
+        @pl.when(pl.program_id(0) == i)
+        def _():
+            out_ref[:, :half] = low
+            out_ref[:, half:] = high
 
 
 def turn(terms, hidden, dy, gain, w_mine, w_other, core, me):
@@ -726,14 +730,14 @@
                 weight,
             ],
             out_specs=[
-                pl.BlockSpec((1, rows, 2 * half), lambda i, m: (i, 0, 0)),
+                *[pl.BlockSpec((rows, 2 * half), lambda i, m: (0, 0))] * n_head,
                 share,
                 share,
                 pl.BlockSpec((1, width), lambda i, m: (0, 0)),
             ],
         ),
         out_shape=[
-            jax.ShapeDtypeStruct((n_head, rows, 2 * half), bf16),
+            *[jax.ShapeDtypeStruct((rows, 2 * half), bf16)] * n_head,
             jax.ShapeDtypeStruct((rows, width), f32),
             jax.ShapeDtypeStruct((rows, width), bf16),
             jax.ShapeDtypeStruct((1, width), f32),
@@ -876,61 +880,92 @@
     )(meta, *lefts, *rights)
 
 
-def column_sums_kernel(owners, mixed_ref, o_ref, dy_ref, *refs):
-    *pieces, out_ref, branch = refs
-    hidden = mixed_ref.shape[1]
+def down_sums_kernel(mixed_ref, dy_ref, out_ref):
+    count, unused, share = out_ref.shape
+    for i in range(count):
+        out_ref[i] = dot_tn(mixed_ref[...], dy_ref[:, i * share : (i + 1) * share]).astype(bf16)
+
+
+def down_sums(mixed, dy, shares, more):
+    rows, width = dy.shape
+    share = width // shares
+    hidden = mixed.shape[1]
+    return pl.pallas_call(
+        down_sums_kernel,
+        grid=(shares // 2,),
+        in_specs=[
+            pl.BlockSpec(mixed.shape, lambda i: (0, 0)),
+            pl.BlockSpec((rows, 2 * share), lambda i: (0, i)),
+        ],
+        out_specs=pl.BlockSpec((2, hidden, share), lambda i: (i, 0, 0)),
+        out_shape=jax.ShapeDtypeStruct((shares, hidden + more, share), bf16),
+        compiler_params=WHOLE_VMEM,
+        cost_estimate=SMALL,
+        name="down_sums",
+    )(mixed, dy)
+
+
+def output_sums_kernel(owners, *refs, groups):
+    o_refs, pieces, (out_ref, branch) = refs[:groups], refs[groups:-3], refs[-2:]
     for i, piece in enumerate(pieces):
         rows = piece.shape[0]
         branch[pl.ds(pl.multiple_of(owners[i] * rows, rows), rows), :] = piece[...]
-    out_ref[0, :hidden, :] = dot_tn(mixed_ref[...], dy_ref[...]).astype(bf16)
-    out_ref[0, hidden:, :] = dot_tn(o_ref[...], branch[...]).astype(bf16)
-
-
-def column_sums(mixed, o_low, dy, pieces, shares):
+    count, unused, share = out_ref.shape
+    start = 0
+    for o_ref in o_refs:
+        end = start + o_ref.shape[1]
+        for i in range(count):
+            part = branch[:, i * share : (i + 1) * share]
+            out_ref[i, start:end, :] = dot_tn(o_ref[...], part).astype(bf16)
+        start = end
+
+
+def output_sums(o_groups, pieces, base):
     owners = jnp.stack([jnp.asarray(owner, jnp.int32) for unused, owner in pieces])
-    rows, width = dy.shape
-    share = width // shares
-    out_rows = mixed.shape[1] + o_low.shape[1]
-    return pl.pallas_call(
-        column_sums_kernel,
+    shares, all_rows, share = base.shape
+    size = sum(o.shape[1] for o in o_groups)
+    place = all_rows // size - 1
+    return pl.pallas_call(
+        functools.partial(output_sums_kernel, groups=len(o_groups)),
         grid_spec=pltpu.PrefetchScalarGridSpec(
             num_scalar_prefetch=1,
-            grid=(shares,),
-            in_specs=[
-                pl.BlockSpec(mixed.shape, lambda i, m: (0, 0)),
-                pl.BlockSpec(o_low.shape, lambda i, m: (0, 0)),
-                pl.BlockSpec((rows, share), lambda i, m: (0, i)),
+            grid=(shares // 2,),
+            in_specs=[pl.BlockSpec(o.shape, lambda i, m: (0, 0)) for o in o_groups]
+            + [
+                pl.BlockSpec((piece.shape[0], 2 * share), lambda i, m: (0, i))
+                for piece, unused in pieces
             ]
-            + [
-                pl.BlockSpec((piece.shape[0], share), lambda i, m: (0, i))
-                for piece, unused in pieces
-            ],
-            out_specs=pl.BlockSpec((1, out_rows, share), lambda i, m: (i, 0, 0)),
-            scratch_shapes=[pltpu.VMEM((rows, share), bf16)],
+            + [pl.BlockSpec(memory_space=pl.ANY)],
+            out_specs=pl.BlockSpec((2, size, share), lambda i, m: (i, place, 0)),
+            scratch_shapes=[pltpu.VMEM((o_groups[0].shape[0], 2 * share), bf16)],
         ),
-        out_shape=jax.ShapeDtypeStruct((shares, out_rows, share), bf16),
-        compiler_params=WHOLE_VMEM,
-        cost_estimate=SMALL,
-        name="column_sums",
-    )(owners, mixed, o_low, dy, *[piece for piece, unused in pieces])
-
-
-def pass_on_kernel(part_ref, theirs_ref, *refs):
-    *arrived, low_ref, high_ref = refs
-    half = low_ref.shape[0]
-    for i, out_ref in enumerate((low_ref, high_ref)):
-        rows = slice(i * half, (i + 1) * half)
-        total = part_ref[rows, :] + theirs_ref[rows, :].astype(f32)
-        if arrived:
-            total += arrived[i][...].astype(f32)
-        out_ref[...] = total.astype(bf16)
-
-
-def pass_on(part, theirs, *arrived):
+        out_shape=jax.ShapeDtypeStruct(base.shape, bf16),
+        input_output_aliases={1 + len(o_groups) + len(pieces): 0},
+        compiler_params=WHOLE_VMEM,
+        cost_estimate=SMALL,
+        name="output_sums",
+    )(owners, *o_groups, *[piece for piece, unused in pieces], base)
+
+
+def pass_on_kernel(part_ref, theirs_ref, *refs, count):
+    arrived, outs = refs[:-count], refs[-count:]
+    size = outs[0].shape[0]
+    for i, out_ref in enumerate(outs):
+        rows = slice(i * size, (i + 1) * size)
+        out_ref[...] = (part_ref[rows, :] + theirs_ref[rows, :].astype(f32)).astype(bf16)
+    if arrived:
+        whole = jnp.concatenate([ref[...] for ref in arrived], axis=0).astype(f32)
+        for i, out_ref in enumerate(outs):
+            rows = slice(i * size, (i + 1) * size)
+            total = part_ref[rows, :] + theirs_ref[rows, :].astype(f32) + whole[rows]
+            out_ref[...] = total.astype(bf16)
+
+
+def pass_on(part, theirs, arrived, count):
     rows, width = part.shape
     return pl.pallas_call(
-        pass_on_kernel,
-        out_shape=[jax.ShapeDtypeStruct((rows // 2, width), bf16)] * 2,
+        functools.partial(pass_on_kernel, count=count),
+        out_shape=[jax.ShapeDtypeStruct((rows // count, width), bf16)] * count,
         compiler_params=WHOLE_VMEM,
         cost_estimate=SMALL,
         name="pass_on",
@@ -956,15 +991,22 @@
     value_ref,
     gain_grad_ref,
     norm_grad_ref,
-    *outs,
+    *refs,
     arranged,
 ):
+    *outs, arrived_ref = refs
+
     @pl.when(pl.program_id(0) == 0)
     def _():
+        size = first_ref.shape[0]
+        for i, ref in enumerate((first_ref, second_ref)):
+            arrived_ref[i * size : (i + 1) * size, :] = ref[...]
         gain_grad_ref[...] = jnp.zeros_like(gain_grad_ref)
         norm_grad_ref[...] = jnp.zeros_like(norm_grad_ref)
 
-    arrived = jnp.where(pl.program_id(0) == 0, first_ref[...], second_ref[...])
+    rows = dkv_ref.shape[0]
+    here = pl.ds(pl.multiple_of(pl.program_id(0) * rows, rows), rows)
+    arrived = arrived_ref[here, :]
     dkv = dkv_ref[...] + theirs_ref[...].astype(f32) + arrived.astype(f32)
     for j in range(key_ref.shape[1] // HEAD_WIDTH):
         head = slice(j * HEAD_WIDTH, (j + 1) * HEAD_WIDTH)
@@ -1036,6 +1078,7 @@
                 pl.BlockSpec((1, width), lambda i, m: (0, 0)),
             ]
             + out_specs,
+            scratch_shapes=[pltpu.VMEM((rows, theirs.shape[1]), bf16)],
         ),
         out_shape=[
             jax.ShapeDtypeStruct((rows, kv_width), bf16),
@@ -1050,32 +1093,30 @@
     )(meta, tokens, q_grad, dkv, theirs, *arrived, key_raw, key_gain, cosine, sine, *weights)
 
 
-def attn_sums_kernel(x_ref, q_ref, k_ref, v_ref, out_ref):
+def attn_sums_kernel(x_ref, *refs):
+    *terms, out_ref = refs
     x = x_ref[...]
     start = 0
-    for ref in (q_ref, k_ref, v_ref):
+    for ref in terms:
         out_ref[:, start : start + ref.shape[1]] = dot_tn(x, ref[...]).astype(bf16)
         start += ref.shape[1]
 
 
-def attn_sums(x, query, key, value):
+def attn_sums(x, terms):
     rows, width = x.shape
     step = width // 8
-    out_width = query.shape[1] + key.shape[1] + value.shape[1]
-
-    def full(array):
-        return pl.BlockSpec(array.shape, lambda i: (0, 0))
-
+    out_width = sum(term.shape[1] for term in terms)
     return pl.pallas_call(
         attn_sums_kernel,
         grid=(width // step,),
-        in_specs=[pl.BlockSpec((rows, step), lambda i: (0, i)), full(query), full(key), full(value)],
+        in_specs=[pl.BlockSpec((rows, step), lambda i: (0, i))]
+        + [pl.BlockSpec(term.shape, lambda i: (0, 0)) for term in terms],
         out_specs=pl.BlockSpec((step, out_width), lambda i: (i, 0)),
         out_shape=jax.ShapeDtypeStruct((width, out_width), bf16),
         compiler_params=WHOLE_VMEM,
         cost_estimate=SMALL,
         name="attn_sums",
-    )(x, query, key, value)
+    )(x, *terms)
 
 
 def after(values):
@@ -1161,6 +1202,7 @@
         me = lax.axis_index("head")
         if n_head == 4:
             return [(value[0], me)] + [(across(value[i], i), me ^ i) for i in (3, 1, 2)]
+        value = jnp.stack(value)
         ordered = jnp.stack([pick(value, i ^ me) for i in range(n_head)])
         got = lax.all_to_all(ordered, "head", 0, 0)
         return [(got[i], i) for i in range(n_head)]
@@ -1227,51 +1269,66 @@
                 current = following
                 sibling = swap_core(current)
                 following = to_next(current)
-            carried = attend_stage(
-                q_wide, *blocks[stage], bounds, metas[stage], carried, stage == n_chip - 1
-            )
-            if stage == 0:
-                dy, carried = after((cotangent, carried))
-                d_mixed = dot_nt(dy, w_down)
-                carried, d_mixed = after((carried, d_mixed))
+            if stage == n_chip - 1:
+                break
+            carried = attend_stage(q_wide, blocks[stage], (0, 1), bounds, metas[stage], carried)
             if stage + 3 < n_chip:
                 following, carried = after((following, carried))
             if stage + 2 == n_chip:
                 current, carried = after((following, carried))
                 sibling = swap_core(current)
-                w_mine, sibling, carried = after((w_mine, sibling, carried))
-                w_other = swap_core(w_mine)
-        o_low, q_back, outcome = carried
-
-        steps = gather_steps(o_low)
-        arrived = next(steps)
-        base = tokens
-        if n_head == 4:
-            base = project(base, [(o_low, head_index)], w_mine, w_other, core, head_index)
-            arrived, base = after((arrived, base))
-            far = steps.send(arrived)
-            pieces = [(arrived[0], head_index ^ 1), (arrived[1], head_index ^ 2)]
-            base = project(base, pieces, w_mine, w_other, core, head_index)
-            arrived, base = after((far, base))
-        try:
-            steps.send(arrived)
-        except StopIteration as stop:
-            pieces = stop.value[3:] if n_head == 4 else stop.value
+        groups = 2 if cut else 1
+        w_mine, sibling, carried = after((w_mine, sibling, carried))
+        blocks[-1] = (current, sibling)
+        w_other = swap_core(w_mine)
+        outcome, total = carried
+        o_first, q_back, outcome = attend_stage(
+            q_wide, blocks[-1], (0, 1), bounds, metas[-1], (outcome, total), (0, groups)
+        )
+        if cut:
+            first_steps = gather_steps(o_first)
+            got_first = next(first_steps)
+            o_second, q_back, outcome = attend_stage(
+                q_back, blocks[-1], (0, 1), bounds, metas[-1], (outcome, total), (1, groups)
+            )
+            got_first, o_second = after((got_first, o_second))
+            second_steps = gather_steps(o_second)
+            got_second = next(second_steps)
+            got_first = first_steps.send(got_first)
+            o_groups = (o_first, o_second)
+            dy, unused = after((cotangent, o_second))
+            d_mixed = dot_nt(dy, w_down)
+            got_second, d_mixed = after((got_second, d_mixed))
+            got_second = second_steps.send(got_second)
+            got_first, d_mixed = after((got_first, d_mixed))
+            first_pieces = end_steps(first_steps, got_first)
+            second_pieces = end_steps(second_steps, got_second)
+            pieces = [(low[0], high[0], low[1]) for low, high in zip(first_pieces, second_pieces)]
+        else:
+            o_groups = (o_first,)
+            half = o_first.shape[1] // 2
+            every = lax.all_gather(o_first, "head", axis=0)
+            pieces = [(every[i, :, :half], every[i, :, half:], i) for i in range(n_head)]
+            d_mixed = dot_nt(cotangent, w_down)
         my_hidden, second_in = project(
-            base, pieces, w_mine, w_other, core, head_index, norm2_gain
+            tokens, pieces, w_mine, w_other, core, head_index, norm2_gain
         )
-        mixed_low, gate_low, up_low, gate_up_sum = feed(second_in, w_gate, w_up, d_mixed)
-
         def scatter_seq(value, tiled):
             return lax.psum_scatter(value, "seq", scatter_dimension=0, tiled=tiled)
 
+        mixed_low, gate_low, up_low, gate_up_sum = feed(second_in, w_gate, w_up, d_mixed)
         grad_gate_up = scatter_seq(gate_up_sum, True)
 
-        terms, (down_part,) = run_steps(
-            scatter_steps(products((gate_low, up_low), (w_gate, w_up), True, head_index, cut)),
-            (lambda: products((mixed_low,), (w_down,), False, head_index, cut),),
-        )
-        do_pieces, hidden_grad, my_branch, grad_norm2 = turn(
+        flow = scatter_steps(products((gate_low, up_low), (w_gate, w_up), True, head_index, cut))
+        got = next(flow)
+        down_part = products((mixed_low,), (w_down,), False, head_index, cut)
+        got, down_part = after((got, down_part))
+        if cut:
+            got = flow.send(got)
+        column_sum = down_sums(mixed_low, cotangent, n_seq, w_output.shape[0])
+        got, column_sum = after((got, column_sum))
+        terms = end_steps(flow, got)
+        *do_pieces, hidden_grad, my_branch, grad_norm2 = turn(
             terms, my_hidden, cotangent, norm2_gain, w_mine, w_other, core, head_index
         )
         do_wide = with_delta(exchange_head(do_pieces), outcome)
@@ -1289,22 +1346,23 @@
             value = moving.pop(0)
             return lambda: to_previous(value)
 
-        def stage_work(stage):
-            return lambda: attend_back(
-                q_back, do_wide, *blocks[stage], bounds, metas[stage], dq, stage == 0
+        def stage_work(stage, places=(0, 1)):
+            chosen = [blocks[stage][place] for place in places]
+            return attend_back(
+                q_back, do_wide, chosen, places, bounds, metas[stage], dq, stage == 0
             )
 
         def next_hop():
             nonlocal dq, hops
-            if hops < n_chip - 1 and len(parts) > hops and len(landed) == (2 if hops else 0):
-                sent, dq = after((pass_on(*parts[hops], *landed), dq))
+            if hops < n_chip - 1 and len(parts) > hops and len(landed) == (2 if hops else 0) and hops < n_chip - 1:
+                sent, dq = after((pass_on(*parts[hops], landed, 2), dq))
                 landed.clear()
                 moving.extend(sent)
                 hops += 1
 
         branch_steps = gather_steps(my_branch)
         (dq, dkv_a, dkv_b), got_branch = after(
-            (stage_work(n_chip - 1)(), next(branch_steps))
+            (stage_work(n_chip - 1), next(branch_steps))
         )
         theirs, dq = after((swap_core(dkv_b), dq))
         parts.append((dkv_a, theirs))
@@ -1313,13 +1371,13 @@
         if cut:
             got_branch = branch_steps.send(got_branch)
         (dq, dkv_a, dkv_b), got_branch, flying = after(
-            (stage_work(n_chip - 2)(), got_branch, flying)
+            (stage_work(n_chip - 2), got_branch, flying)
         )
         branch_pieces = end_steps(branch_steps, got_branch)
         landed.append(flying)
         parts.append((dkv_a, swap_core(dkv_b)))
         flying = hop_piece()()
-        column_sum = column_sums(mixed_low, o_low, cotangent, branch_pieces, n_seq)
+        column_sum = output_sums(o_groups, branch_pieces, column_sum)
         dkv_a, theirs = parts[1]
         column_sum, flying, theirs, dq = after((column_sum, flying, theirs, dq))
         parts[1] = (dkv_a, theirs)
@@ -1332,29 +1390,41 @@
         down_part, dq = after((down_part, dq))
         mixed_steps = scatter_steps(down_part)
         got_mixed = next(mixed_steps)
-        for stage in reversed(range(n_chip - 2)):
-            if cut and stage == n_chip - 4:
-                got_mixed = mixed_steps.send(got_mixed)
+        for stage in reversed(range(1, n_chip - 2)):
             hop = hop_piece()
             flying = None if hop is None else hop()
-            (dq, dkv_a, dkv_b), got_mixed, flying = after((stage_work(stage)(), got_mixed, flying))
+            (dq, dkv_a, dkv_b), got_mixed, flying = after((stage_work(stage), got_mixed, flying))
             if hop is not None:
                 landed.append(flying)
             parts.append((dkv_a, swap_core(dkv_b)))
             next_hop()
+        if cut:
+            got_mixed = mixed_steps.send(got_mixed)
+        hop = hop_piece()
+        flying = None if hop is None else hop()
+        (dq, dkv_b), got_mixed, flying = after((stage_work(0, (1,)), got_mixed, flying))
+        if hop is not None:
+            landed.append(flying)
+        theirs = swap_core(dkv_b)
+        next_hop()
         my_mixed = add_rows(my_hidden, end_steps(mixed_steps, got_mixed))
+        my_mixed, dq = after((my_mixed, dq))
         mixed_steps = gather_steps(my_mixed)
         got_mixed = next(mixed_steps)
-        query_grad, grad_qgain = head_back(query_raw, dq, query_gain, cosine, sine, SCORE_SCALE, 1)
-        grad_gate_up = split_gate_up(grad_gate_up)
-        query_grad, grad_gate_up = after((query_grad, grad_gate_up))
+        hop = hop_piece()
+        flying = None if hop is None else hop()
+        (dq, dkv_a), theirs, flying = after((stage_work(0, (0,)), theirs, flying))
+        if hop is not None:
+            landed.append(flying)
+        parts.append((dkv_a, theirs))
         while hops < n_chip - 1:
             while len(landed) < 2:
                 landed.append(hop_piece()())
             next_hop()
         flying = [hop_piece()() for unused in range(2 - len(landed))]
+        query_grad, grad_qgain = head_back(query_raw, dq, query_gain, cosine, sine, SCORE_SCALE, 1)
         if cut:
-            flying[0], got_mixed, query_grad = after((flying[0], got_mixed, query_grad))
+            got_mixed, query_grad = after((got_mixed, query_grad))
             got_mixed = mixed_steps.send(got_mixed)
         flying, got_mixed, query_grad = after((flying, got_mixed, query_grad))
         landed = (*landed, *flying)
@@ -1383,7 +1453,7 @@
         bits = [1 << k for k in range(n_seq.bit_length() - 1)]
         steps = scatter_steps(first_part)
         got = next(steps)
-        attn_sum = attn_sums(first_in, query_grad, key_grad, value_grad)
+        attn_sum = attn_sums(first_in, (query_grad, key_grad, value_grad))
         gains = sum_seq(gains, bits[:1])
         gains, attn_sum = after((gains, attn_sum))
         got, gains, attn_sum = after((got, gains, attn_sum))
@@ -1405,13 +1475,16 @@
         middle = lax.reduce_precision(flat - high, 8, 7)
         rider = jnp.concatenate([high, middle, flat - high - middle]).astype(bf16)
         rider = rider.reshape(3 * gain_rows, width)
-        rider = jnp.pad(rider, ((0, 32 - rider.shape[0]), (0, 0)))
+        rider = jnp.pad(rider, ((0, -rider.shape[0] % 16), (0, 0)))
         my_tokens_grad = last(terms, tokens, hidden_grad, norm1_gain, rider, head_index)
         steps = rider_entries(my_tokens_grad, share)
         got = next(steps)
         mixed = assemble([(piece, 0, owner) for piece, owner in mixed_pieces], share, bf16)
-        grad_down, grad_output = cut_rows(grad_columns, (w_gate.shape[1], o_low.shape[1]))
-        got, mixed, grad_down, grad_output = after((got, mixed, grad_down, grad_output))
+        grad_down, grad_output = cut_rows(grad_columns, (w_gate.shape[1], w_output.shape[0]))
+        grad_gate, grad_up = split_gate_up(grad_gate_up)
+        got, mixed, grad_down, grad_output, grad_gate, grad_up = after(
+            (got, mixed, grad_down, grad_output, grad_gate, grad_up)
+        )
         if cut:
             got = steps.send(got)
         entries, gain_pieces = end_steps(steps, got)
@@ -1423,7 +1496,6 @@
         grad_norm1, grad_norm2 = gains[:width], gains[width : 2 * width]
         grad_qgain = gains[2 * width : 2 * width + HEAD_WIDTH]
         grad_kgain = gains[2 * width + HEAD_WIDTH : n_gains]
-        grad_gate, grad_up = grad_gate_up
         return (
             mixed,
             grad_tokens,

time: 535 us -> 527 us (0.985)
  starting transfers between devices: 73.3 us -> 63.6 us
  waiting for transfers between devices: 138 us -> 145 us
    ppermute x31 -> x35, waiting for transfers between devices: 60.3 us -> 39.6 us  [across(): return lax.ppermute(value, 'head', [(i, i ^ bits) for i in range(n_head)])]
    ppermute x6, waiting for transfers between devices: 62.8 us -> 78.4 us  [to_previous(): return lax.ppermute(value, 'seq', [(i + 2, i) for i in range(n_seq - 2)])]
    ppermute x9, starting transfers between devices: 10.7 us -> 0.75 us  [swap_core(): return lax.ppermute(value, 'seq', [(i, i ^ 1) for i in range(n_seq)])]
    ppermute x3, waiting for transfers between devices: 7.21 us -> 16.2 us  [to_next(): return lax.ppermute(value, 'seq', [(i, i + 2) for i in range(n_seq - 2)])]
    ppermute x3, starting transfers between devices: 8.79 us -> 1.4 us  [sum_seq(): lax.ppermute(total, 'seq', [(i, i ^ bit) for i in range(n_seq)])]
    ppermute x31 -> x35, starting transfers between devices: 32.1 us -> 39.1 us  [across(): return lax.ppermute(value, 'head', [(i, i ^ bits) for i in range(n_head)])]
    pallas_call x15 -> x16, Pallas kernels: 104 us -> 102 us  [the longest x5 36.4 us: attend_back(): pl.pallas_call(functools.partial(attend_back_kernel, places=places, first...]
    unnamed x109 -> x113, local copies, waits for them, and re-layouts: 12.9 us -> 11.7 us
  transfers between devices with their start and end apart: 56 -> 60, of which waited for: 28 -> 28; matrix products, arithmetic and copies ran while one was open for 6% -> 6% of each run, Pallas kernels for 39% -> 38%
where the time goes in v6:
time: 527 us; the launch traced here: 519 us
  Pallas kernels  249 us (47%)
  waiting for transfers between devices  145 us (28%)
  starting transfers between devices  63.6 us (12%)
  local copies, waits for them, and re-layouts  16.3 us (3%)
  matrix products  15.5 us (3%)
  other arithmetic  14.7 us (3%)
  between operations  14.7 us (3%)
    ppermute x6, waiting for transfers between devices, to_previous(): return lax.ppermute(value, 'seq', [(i + 2, i) for i in range(n_seq - 2)])  78.4 us
    ppermute x35, waiting for transfers between devices, across(): return lax.ppermute(value, 'head', [(i, i ^ bits) for i in range(n_head)])  39.6 us
    ppermute x35, starting transfers between devices, across(): return lax.ppermute(value, 'head', [(i, i ^ bits) for i in range(n_head)])  39.1 us
    pallas_call x5, Pallas kernels, attend_back(): pl.pallas_call(functools.partial(attend_back_kernel, places=places, first...  36.4 us
    pallas_call x5, Pallas kernels, attend_stage(): pl.pallas_call(functools.partial(attend_kernel, places=places, first=firs...  26.5 us
    pallas_call x1, Pallas kernels, feed(): pl.pallas_call(feed_kernel, grid=(hidden // HIDDEN_STEP,), in_specs=[whol...  26.4 us
    pallas_call x2, Pallas kernels, products(): pl.pallas_call(functools.partial(products_kernel, count=len(lefts), turne...  25.2 us
    ppermute x3, waiting for transfers between devices, to_next(): return lax.ppermute(value, 'seq', [(i, i + 2) for i in range(n_seq - 2)])  16.2 us
  transfers between devices with their start and end apart: 60, of which 28 were waited for; matrix products, arithmetic and copies ran while one was open for 6% of the time, Pallas kernels for 38%

profile of v6, /device:TPU:0, one launch (start us, length us, event | category | flops | bytes accessed | tf_op | source)
XLA Modules:
  0.0 518.8 jit_solution(9436068529492736152)
XLA Ops:
  11.7 6.4 %enter.1 = (bf16[768,2048]{1,0:T(8,128)(2,1)}, f32[768,256]{1,0:T(8,128)}, bf16[768,512]{1,0:T(8,128)(2,1)}) custom-call(bf16[768,2048]{1,0:T(8,128)(2,1)} %refs_3_.3, f32[1,2048]{1,0:T(1,128)} %bitcast.56, bf16[2048,256]{1,0:T(8,128)(2,1)} %key_w_ref.3, bf16[2048,256]{1,0:T(8,128)(2,1)} %value_w_ref.3, f32[1,128]{1,0:T(1,128)} %bitcast.64, ...), custom_call_target="tpu_custom_call" | custom-call | flops 1 | bytes 1 | tf_op jit(solution)/shard_map/enter/pallas_call | solution.py:112
  48.0 7.1 %attend_stage.5 = (f32[768,512]{1,0:T(8,128)}, f32[768,512]{1,0:T(8,128)}) custom-call(s32[4]{0:T(128)} %get-tuple-element.443.meta, bf16[768,1024]{1,0:T(8,128)(2,1)} %query_prep.1.q_ref, bf16[768,512]{1,0:T(8,128)(2,1)} %get-tuple-element.240.refs_0_, bf16[768,512]{1,0:T(8,128)(2,1)} %copy-done.8, s32[8,128]{1,0:T(8,128)} %copy-done.31), custom_call_target="tpu_custom_call" | custom-call | flops 1 | bytes 1 | tf_op jit(solution)/shard_map/attend_stage/pallas_call | solution.py:325
  55.1 7.9 %collective-permute-done.1.refs_0_ = bf16[768,512]{1,0:T(8,128)(2,1)} collective-permute-done((bf16[768,512]{1,0:T(8,128)(2,1)S(1)}, bf16[768,512]{1,0:T(8,128)(2,1)}, u32[]{:S(2)}, u32[]{:S(2)}) %collective-permute-start.1) | collective-permute-done | bytes 786464 | tf_op jit(solution)/shard_map/ppermute | solution.py:1139
  109.1 9.5 %fusion.11.d_mixed_ref = f32[768,1536]{1,0:T(8,128)} fusion(bf16[768,2048]{1,0:T(8,128)(2,1)} %refs_4_.1, bf16[1536,2048]{1,0:T(8,128)(2,1)} %refs_1_.1), kind=kOutput, calls=%fused_computation.43 | convolution fusion | flops 4831838208 | bytes 14155776 | tf_op jit(solution)/shard_map/dot_general | solution.py:36
  126.8 14.7 %project.1 = (f32[192,2048]{1,0:T(8,128)}, bf16[768,2048]{1,0:T(8,128)(2,1)}) custom-call(s32[6]{0:T(128)} %stack.130.meta, bf16[768,2048]{1,0:T(8,128)(2,1)} %refs_3_.3, bf16[768,256]{1,0:T(8,128)(2,1)} %get-tuple-element.263.refs_0_, bf16[768,256]{1,0:T(8,128)(2,1)} %copy-done.16, bf16[768,256]{1,0:T(8,128)(2,1)} %copy-done.15, ...), custom_call_target="tpu_custom_call" | custom-call | flops 1 | bytes 1 | tf_op jit(solution)/shard_map/project/pallas_call | solution.py:564
  141.4 26.4 %feed.1 = (bf16[768,1536]{1,0:T(8,128)(2,1)}, bf16[768,1536]{1,0:T(8,128)(2,1)}, bf16[768,1536]{1,0:T(8,128)(2,1)}, bf16[2048,3072]{1,0:T(8,128)(2,1)}) custom-call(bf16[768,2048]{1,0:T(8,128)(2,1)} %get-tuple-element.275.x_ref, bf16[2048,1536]{1,0:T(8,128)(2,1)} %refs_2_.1, bf16[2048,1536]{1,0:T(8,128)(2,1)} %refs_3_.2, f32[768,1536]{1,0:T(8,128)} %fusion.11.d_mixed_ref), custom_call_target="tpu_custom_call" | custom-call | flops 1 | bytes 1 | tf_op jit(solution)/shard_map/feed/pallas_call | solution.py:812
  167.9 15.9 %products.2 = (bf16[192,2048]{1,0:T(8,128)(2,1)}, bf16[192,2048]{1,0:T(8,128)(2,1)}, bf16[384,2048]{1,0:T(8,128)(2,1)}) custom-call(s32[1]{0:T(128)} %bitcast.meta, bf16[768,1536]{1,0:T(8,128)(2,1)} %get-tuple-element.277.refs_0_, bf16[768,1536]{1,0:T(8,128)(2,1)} %get-tuple-element.278.refs_1_, bf16[2048,1536]{1,0:T(8,128)(2,1)} %refs_2_.1, ...), custom_call_target="tpu_custom_call" | custom-call | flops 1 | bytes 1 | tf_op jit(solution)/shard_map/products/pallas_call | solution.py:868
  184.8 9.4 %products.3 = (bf16[192,2048]{1,0:T(8,128)(2,1)}, bf16[192,2048]{1,0:T(8,128)(2,1)}, bf16[384,2048]{1,0:T(8,128)(2,1)}) custom-call(s32[1]{0:T(128)} %bitcast.meta, bf16[768,1536]{1,0:T(8,128)(2,1)} %get-tuple-element.281.refs_0_.mixed_ref, bf16[1536,2048]{1,0:T(8,128)(2,1)} %refs_1_.1), custom_call_target="tpu_custom_call" | custom-call | flops 1 | bytes 1 | tf_op jit(solution)/shard_map/products/pallas_call | solution.py:868
  207.6 9.2 %down_sums.1.refs_6_ = bf16[8,2048,256]{2,1,0:T(8,128)(2,1)} custom-call(bf16[768,1536]{1,0:T(8,128)(2,1)} %get-tuple-element.281.refs_0_.mixed_ref, bf16[768,2048]{1,0:T(8,128)(2,1)} %refs_4_.1), custom_call_target="tpu_custom_call" | custom-call | flops 1 | bytes 1 | tf_op jit(solution)/shard_map/down_sums/pallas_call | solution.py:893
  217.8 11.1 %turn.1 = (bf16[192,512]{1,0:T(8,128)(2,1)}, bf16[192,512]{1,0:T(8,128)(2,1)}, bf16[192,512]{1,0:T(8,128)(2,1)}, bf16[192,512]{1,0:T(8,128)(2,1)}, f32[192,2048]...) custom-call(s32[2]{0:T(128)} %pad_add_fusion.5.meta, f32[192,2048]{1,0:T(8,128)} %get-tuple-element.291.refs_0_, ...), custom_call_target="tpu_custom_call" | custom-call | flops 1 | bytes 1 | tf_op jit(solution)/shard_map/turn/pallas_call | solution.py:719
  245.8 6.6 %attend_back.5 = (f32[768,512]{1,0:T(8,128)}, f32[768,512]{1,0:T(8,128)}, bf16[768,512]{1,0:T(8,128)(2,1)}) custom-call(s32[4]{0:T(128)} %get-tuple-element.444.meta, bf16[768,1024]{1,0:T(8,128)(2,1)} %get-tuple-element.262.q_ref, bf16[768,1024]{1,0:T(8,128)(2,1)} %with_delta.1.do_ref, bf16[768,512]{1,0:T(8,128)(2,1)} %copy-done.2, ...), custom_call_target="tpu_custom_call" | custom-call | flops 1 | bytes 1 | tf_op jit(solution)/shard_map/attend_back/pallas_call | solution.py:512
  252.4 6.6 %collective-permute-done.24.refs_4_ = bf16[192,2048]{1,0:T(8,128)(2,1)S(1)} collective-permute-done((bf16[192,2048]{1,0:T(8,128)(2,1)S(1)}, bf16[192,2048]{1,0:T(8,128)(2,1)S(1)}, u32[]{:S(2)}, u32[]{:S(2)}) %collective-permute-start.24) | collective-permute-done | bytes 786464 | tf_op jit(solution)/shard_map/ppermute | solution.py:1145
  267.0 6.7 %attend_back.6 = (f32[768,512]{1,0:T(8,128)}, f32[768,512]{1,0:T(8,128)}, bf16[768,512]{1,0:T(8,128)(2,1)}) custom-call(s32[4]{0:T(128)} %get-tuple-element.431.meta, bf16[768,1024]{1,0:T(8,128)(2,1)} %get-tuple-element.262.q_ref, bf16[768,1024]{1,0:T(8,128)(2,1)} %with_delta.1.do_ref, ...), custom_call_target="tpu_custom_call", output_to_operand_aliasing={{0}: (6, {})} | custom-call | flops 1 | bytes 1 | tf_op jit(solution)/shard_map/attend_back/pallas_call | solution.py:512
  273.7 19.0 %collective-permute-done.28.refs_0_ = bf16[384,512]{1,0:T(8,128)(2,1)S(1)} collective-permute-done((bf16[384,512]{1,0:T(8,128)(2,1)}, bf16[384,512]{1,0:T(8,128)(2,1)S(1)}, u32[]{:S(2)}, u32[]{:S(2)}) %collective-permute-start.28) | collective-permute-done | bytes 393248 | tf_op jit(solution)/shard_map/ppermute | solution.py:1142
  295.5 6.5 %output_sums.1 = bf16[8,2048,256]{2,1,0:T(8,128)(2,1)} custom-call(s32[4]{0:T(128)} %pad_add_fusion.7.owners.places, bf16[768,256]{1,0:T(8,128)(2,1)} %get-tuple-element.263.refs_0_, bf16[768,256]{1,0:T(8,128)(2,1)} %get-tuple-element.267.refs_4_.refs_1_, bf16[192,2048]{1,0:T(8,128)(2,1)} %get-tuple-element.310.refs_2_, ...), custom_call_target="tpu_custom_call", output_to_operand_aliasing={{}: (7, {})} | custom-call | flops 1 | bytes 1 | tf_op jit(solution)/shard_map/output_sums/pallas_call | solution.py:928
  302.1 16.4 %collective-permute-done.29.refs_1_ = bf16[384,512]{1,0:T(8,128)(2,1)S(1)} collective-permute-done((bf16[384,512]{1,0:T(8,128)(2,1)}, bf16[384,512]{1,0:T(8,128)(2,1)S(1)}, u32[]{:S(2)}, u32[]{:S(2)}) %collective-permute-start.29) | collective-permute-done | bytes 393248 | tf_op jit(solution)/shard_map/ppermute | solution.py:1142
  326.6 6.7 %attend_back.7 = (f32[768,512]{1,0:T(8,128)}, f32[768,512]{1,0:T(8,128)}, bf16[768,512]{1,0:T(8,128)(2,1)}) custom-call(s32[4]{0:T(128)} %get-tuple-element.445.meta, bf16[768,1024]{1,0:T(8,128)(2,1)} %get-tuple-element.262.q_ref, bf16[768,1024]{1,0:T(8,128)(2,1)} %with_delta.1.do_ref, bf16[768,512]{1,0:T(8,128)(2,1)} %copy-done.9, ...), custom_call_target="tpu_custom_call", output_to_operand_aliasing={{0}: (6, {})} | custom-call | flops 1 | bytes 1 | tf_op jit(solution)/shard_map/attend_back/pallas_call | solution.py:512
  333.3 14.3 %collective-permute-done.33.refs_0_ = bf16[384,512]{1,0:T(8,128)(2,1)S(1)} collective-permute-done((bf16[384,512]{1,0:T(8,128)(2,1)}, bf16[384,512]{1,0:T(8,128)(2,1)S(1)}, u32[]{:S(2)}, u32[]{:S(2)}) %collective-permute-start.33) | collective-permute-done | bytes 393248 | tf_op jit(solution)/shard_map/ppermute | solution.py:1142
  358.6 11.8 %collective-permute-done.37.refs_1_ = bf16[384,512]{1,0:T(8,128)(2,1)S(1)} collective-permute-done((bf16[384,512]{1,0:T(8,128)(2,1)}, bf16[384,512]{1,0:T(8,128)(2,1)S(1)}, u32[]{:S(2)}, u32[]{:S(2)}) %collective-permute-start.37) | collective-permute-done | bytes 393248 | tf_op jit(solution)/shard_map/ppermute | solution.py:1142
  379.9 10.4 %attend_back.9 = (f32[768,512]{1,0:T(8,128)}, f32[768,512]{1,0:T(8,128)}) custom-call(s32[4]{0:T(128)} %get-tuple-element.443.meta, bf16[768,1024]{1,0:T(8,128)(2,1)} %get-tuple-element.262.q_ref, bf16[768,1024]{1,0:T(8,128)(2,1)} %with_delta.1.do_ref, bf16[768,512]{1,0:T(8,128)(2,1)} %get-tuple-element.240.refs_0_, ...), custom_call_target="tpu_custom_call", output_to_operand_aliasing={{0}: (5, {})} | custom-call | flops 1 | bytes 1 | tf_op jit(solution)/shard_map/attend_back/pallas_call | solution.py:512
  391.7 9.6 %collective-permute-done.42.first_ref = bf16[384,512]{1,0:T(8,128)(2,1)S(1)} collective-permute-done((bf16[384,512]{1,0:T(8,128)(2,1)}, bf16[384,512]{1,0:T(8,128)(2,1)S(1)}, u32[]{:S(2)}, u32[]{:S(2)}) %collective-permute-start.42) | collective-permute-done | bytes 393248 | tf_op jit(solution)/shard_map/ppermute | solution.py:1142
  410.6 7.2 %collective-permute-done.38.second_ref = bf16[384,512]{1,0:T(8,128)(2,1)S(1)} collective-permute-done((bf16[384,512]{1,0:T(8,128)(2,1)}, bf16[384,512]{1,0:T(8,128)(2,1)S(1)}, u32[]{:S(2)}, u32[]{:S(2)}) %collective-permute-start.38) | collective-permute-done | bytes 393248 | tf_op jit(solution)/shard_map/ppermute | solution.py:1142
  418.6 12.8 %leave.1 = (bf16[768,256]{1,0:T(8,128)(2,1)}, bf16[768,256]{1,0:T(8,128)(2,1)}, f32[1,128]{1,0:T(1,128)}, f32[1,2048]{1,0:T(1,128)}, bf16[192,2048]{1,0:T(8,128)...) custom-call(s32[1]{0:T(128)} %bitcast.meta, bf16[768,2048]{1,0:T(8,128)(2,1)} %refs_3_.3, ...), custom_call_target="tpu_custom_call" | custom-call | flops 1 | bytes 1 | tf_op jit(solution)/shard_map/leave/pallas_call | solution.py:1065
  435.9 9.0 %attn_sums.1 = bf16[2048,1024]{1,0:T(8,128)(2,1)} custom-call(bf16[768,2048]{1,0:T(8,128)(2,1)} %get-tuple-element.241.x_ref, bf16[768,512]{1,0:T(8,128)(2,1)} %get-tuple-element.383.q_ref.refs_0_, bf16[768,256]{1,0:T(8,128)(2,1)} %get-tuple-element.396.refs_1_, bf16[768,256]{1,0:T(8,128)(2,1)} %get-tuple-element.397.refs_2_), custom_call_target="tpu_custom_call" | custom-call | flops 1 | bytes 1 | tf_op jit(solution)/shard_map/attn_sums/pallas_call | solution.py:1109
  (301 shorter events, 242.9 us)
Async XLA Ops:
  7.2 80.3 %all-gather.3.cloned.1.call-start = ((), (), s32[]{:S(2)}) async-start(), calls=%async_computation.6 | async-start | bytes 5242880 | tf_op jit(solution)/shard_map/all_gather | solution.py:1258
  19.2 299.3 %reduce-scatter.4.cloned.1.call-start = ((), (), s32[]{:S(2)}) async-start(), calls=%async_computation.3 | async-start | bytes 14155776 | tf_op jit(solution)/shard_map/reduce_scatter | solution.py:1317
  19.4 27.7 %collective-permute-start.2 = (bf16[768,512]{1,0:T(8,128)(2,1)S(1)}, bf16[768,512]{1,0:T(8,128)(2,1)S(1)}, u32[]{:S(2)}, u32[]{:S(2)}) collective-permute-start(bf16[768,512]{1,0:T(8,128)(2,1)S(1)} %copy-done.7), channel_id=1, source_target_pairs={{0,4},{4,0},{8,12},{12,8},{16,20},{20,16},{24,28},{28,24},{1,5},{5... | collective-permute-start | bytes 2359304 | tf_op jit(solution)/shard_map/ppermute | solution.py:1136
  19.9 21.9 %collective-permute-start = (bf16[768,512]{1,0:T(8,128)(2,1)S(1)}, bf16[768,512]{1,0:T(8,128)(2,1)S(1)}, u32[]{:S(2)}, u32[]{:S(2)}) collective-permute-start(bf16[768,512]{1,0:T(8,128)(2,1)S(1)} %copy-done.7), channel_id=1, source_target_pairs={{0,8},{4,12},{8,16},{12,20},{16,24},{20,28},{1,9},{5,13},{9,17},{1... | collective-permute-start | bytes 2359304 | tf_op jit(solution)/shard_map/ppermute | solution.py:1139
  41.8 21.2 %collective-permute-start.1 = (bf16[768,512]{1,0:T(8,128)(2,1)S(1)}, bf16[768,512]{1,0:T(8,128)(2,1)}, u32[]{:S(2)}, u32[]{:S(2)}) collective-permute-start(bf16[768,512]{1,0:T(8,128)(2,1)S(1)} %collective-permute-done.refs_0_), channel_id=1, source_target_pairs={{0,8},{4,12},{8,16},{12,20},{16,24},{20,28},{1,9},{5,13},{9,17},{1... | collective-permute-start | bytes 2359304 | tf_op jit(solution)/shard_map/ppermute | solution.py:1139
  47.1 20.6 %collective-permute-start.5 = (bf16[768,512]{1,0:T(8,128)(2,1)S(1)}, bf16[768,512]{1,0:T(8,128)(2,1)}, u32[]{:S(2)}, u32[]{:S(2)}) collective-permute-start(bf16[768,512]{1,0:T(8,128)(2,1)S(1)} %collective-permute-done.refs_0_), channel_id=1, source_target_pairs={{0,4},{4,0},{8,12},{12,8},{16,20},{20,16},{24,28},{28,24},{1,5},{5... | collective-permute-start | bytes 2359304 | tf_op jit(solution)/shard_map/ppermute | solution.py:1136
  63.0 22.3 %collective-permute-start.3 = (bf16[768,512]{1,0:T(8,128)(2,1)}, bf16[768,512]{1,0:T(8,128)(2,1)S(1)}, u32[]{:S(2)}, u32[]{:S(2)}) collective-permute-start(bf16[768,512]{1,0:T(8,128)(2,1)} %collective-permute-done.1.refs_0_), channel_id=1, source_target_pairs={{0,8},{4,12},{8,16},{12,20},{16,24},{20,28},{1,9},{5,13},{9,17},{1... | collective-permute-start | bytes 2359304 | tf_op jit(solution)/shard_map/ppermute | solution.py:1139
  87.5 39.2 %collective-permute-start.15 = (bf16[4,256,2048]{2,1,0:T(8,128)(2,1)}, bf16[4,256,2048]{2,1,0:T(8,128)(2,1)}, u32[]{:S(2)}, u32[]{:S(2)}) collective-permute-start(bf16[4,256,2048]{2,1,0:T(8,128)(2,1)} %bitcast.46), channel_id=1, source_target_pairs={{0,4},{4,0},{8,12},{12,8},{16,20},{20,16},{24,28},{28,24},{1,5},{5... | collective-permute-start | bytes 12582920 | tf_op jit(solution)/shard_map/ppermute | solution.py:1136
  167.8 284.2 %reduce-scatter.6.cloned.1.call-start = ((), (), s32[]{:S(2)}) async-start(), calls=%async_computation.4 | async-start | bytes 9437184 | tf_op jit(solution)/shard_map/reduce_scatter | solution.py:1317
  265.7 27.0 %collective-permute-start.28 = (bf16[384,512]{1,0:T(8,128)(2,1)}, bf16[384,512]{1,0:T(8,128)(2,1)S(1)}, u32[]{:S(2)}, u32[]{:S(2)}) collective-permute-start(bf16[384,512]{1,0:T(8,128)(2,1)} %get-tuple-element.324), channel_id=1, source_target_pairs={{8,0},{12,4},{16,8},{20,12},{24,16},{28,20},{9,1},{13,5},{17,9},{2... | collective-permute-start | bytes 1179656 | tf_op jit(solution)/shard_map/ppermute | solution.py:1142
  292.7 25.7 %collective-permute-start.30 = (bf16[768,512]{1,0:T(8,128)(2,1)}, bf16[768,512]{1,0:T(8,128)(2,1)S(1)}, u32[]{:S(2)}, u32[]{:S(2)}) collective-permute-start(bf16[768,512]{1,0:T(8,128)(2,1)} %get-tuple-element.330), channel_id=1, source_target_pairs={{0,4},{4,0},{8,12},{12,8},{16,20},{20,16},{24,28},{28,24},{1,5},{5... | collective-permute-start | bytes 2359304 | tf_op jit(solution)/shard_map/ppermute | solution.py:1136
  292.7 25.7 %collective-permute-start.29 = (bf16[384,512]{1,0:T(8,128)(2,1)}, bf16[384,512]{1,0:T(8,128)(2,1)S(1)}, u32[]{:S(2)}, u32[]{:S(2)}) collective-permute-start(bf16[384,512]{1,0:T(8,128)(2,1)} %get-tuple-element.329), channel_id=1, source_target_pairs={{8,0},{12,4},{16,8},{20,12},{24,16},{28,20},{9,1},{13,5},{17,9},{2... | collective-permute-start | bytes 1179656 | tf_op jit(solution)/shard_map/ppermute | solution.py:1142
  319.5 190.5 %reduce-scatter.8.cloned.1.call-start = ((), (), s32[]{:S(2)}) async-start(), calls=%async_computation.5 | async-start | bytes 4718592 | tf_op jit(solution)/shard_map/reduce_scatter | solution.py:1317
  322.4 25.2 %collective-permute-start.31 = (bf16[192,2048]{1,0:T(8,128)(2,1)}, bf16[192,2048]{1,0:T(8,128)(2,1)S(1)}, u32[]{:S(2)}, u32[]{:S(2)}) collective-permute-start(bf16[192,2048]{1,0:T(8,128)(2,1)} %get-tuple-element.348), channel_id=1, source_target_pairs={{0,1},{1,0},{2,3},{3,2},{4,5},{5,4},{6,7},{7,6},{8,9},{9,8},{10,11... | collective-permute-start | bytes 2359304 | tf_op jit(solution)/shard_map/ppermute | solution.py:1145
  323.9 23.8 %collective-permute-start.32 = (bf16[192,2048]{1,0:T(8,128)(2,1)S(1)}, bf16[192,2048]{1,0:T(8,128)(2,1)S(1)}, u32[]{:S(2)}, u32[]{:S(2)}) collective-permute-start(bf16[192,2048]{1,0:T(8,128)(2,1)S(1)} %copy-done.55), channel_id=1, source_target_pairs={{0,2},{1,3},{2,0},{3,1},{4,6},{5,7},{6,4},{7,5},{8,10},{9,11},{10,... | collective-permute-start | bytes 2359304 | tf_op jit(solution)/shard_map/ppermute | solution.py:1145
  325.4 22.3 %collective-permute-start.33 = (bf16[384,512]{1,0:T(8,128)(2,1)}, bf16[384,512]{1,0:T(8,128)(2,1)S(1)}, u32[]{:S(2)}, u32[]{:S(2)}) collective-permute-start(bf16[384,512]{1,0:T(8,128)(2,1)} %get-tuple-element.350), channel_id=1, source_target_pairs={{8,0},{12,4},{16,8},{20,12},{24,16},{28,20},{9,1},{13,5},{17,9},{2... | collective-permute-start | bytes 1179656 | tf_op jit(solution)/shard_map/ppermute | solution.py:1142
  347.7 26.9 %collective-permute-start.34 = (bf16[768,512]{1,0:T(8,128)(2,1)}, bf16[768,512]{1,0:T(8,128)(2,1)S(1)}, u32[]{:S(2)}, u32[]{:S(2)}) collective-permute-start(bf16[768,512]{1,0:T(8,128)(2,1)} %get-tuple-element.352), channel_id=1, source_target_pairs={{0,4},{4,0},{8,12},{12,8},{16,20},{20,16},{24,28},{28,24},{1,5},{5... | collective-permute-start | bytes 2359304 | tf_op jit(solution)/shard_map/ppermute | solution.py:1136
  347.8 22.7 %collective-permute-start.37 = (bf16[384,512]{1,0:T(8,128)(2,1)}, bf16[384,512]{1,0:T(8,128)(2,1)S(1)}, u32[]{:S(2)}, u32[]{:S(2)}) collective-permute-start(bf16[384,512]{1,0:T(8,128)(2,1)} %get-tuple-element.362), channel_id=1, source_target_pairs={{8,0},{12,4},{16,8},{20,12},{24,16},{28,20},{9,1},{13,5},{17,9},{2... | collective-permute-start | bytes 1179656 | tf_op jit(solution)/shard_map/ppermute | solution.py:1142
  370.5 30.8 %collective-permute-start.41 = (bf16[768,512]{1,0:T(8,128)(2,1)}, bf16[768,512]{1,0:T(8,128)(2,1)S(1)}, u32[]{:S(2)}, u32[]{:S(2)}) collective-permute-start(bf16[768,512]{1,0:T(8,128)(2,1)} %get-tuple-element.376), channel_id=1, source_target_pairs={{0,4},{4,0},{8,12},{12,8},{16,20},{20,16},{24,28},{28,24},{1,5},{5... | collective-permute-start | bytes 2359304 | tf_op jit(solution)/shard_map/ppermute | solution.py:1136
  378.4 28.2 %collective-permute-start.40 = (bf16[192,2048]{1,0:T(8,128)(2,1)S(1)}, bf16[192,2048]{1,0:T(8,128)(2,1)S(1)}, u32[]{:S(2)}, u32[]{:S(2)}) collective-permute-start(bf16[192,2048]{1,0:T(8,128)(2,1)S(1)} %copy-done.6), channel_id=1, source_target_pairs={{0,2},{1,3},{2,0},{3,1},{4,6},{5,7},{6,4},{7,5},{8,10},{9,11},{10,... | collective-permute-start | bytes 2359304 | tf_op jit(solution)/shard_map/ppermute | solution.py:1145
  378.6 28.0 %collective-permute-start.39 = (bf16[192,2048]{1,0:T(8,128)(2,1)S(1)}, bf16[192,2048]{1,0:T(8,128)(2,1)S(1)}, u32[]{:S(2)}, u32[]{:S(2)}) collective-permute-start(bf16[192,2048]{1,0:T(8,128)(2,1)S(1)} %copy-done.6), channel_id=1, source_target_pairs={{0,1},{1,0},{2,3},{3,2},{4,5},{5,4},{6,7},{7,6},{8,9},{9,8},{10,11... | collective-permute-start | bytes 2359304 | tf_op jit(solution)/shard_map/ppermute | solution.py:1145
  378.7 22.6 %collective-permute-start.42 = (bf16[384,512]{1,0:T(8,128)(2,1)}, bf16[384,512]{1,0:T(8,128)(2,1)S(1)}, u32[]{:S(2)}, u32[]{:S(2)}) collective-permute-start(bf16[384,512]{1,0:T(8,128)(2,1)} %get-tuple-element.377), channel_id=1, source_target_pairs={{8,0},{12,4},{16,8},{20,12},{24,16},{28,20},{9,1},{13,5},{17,9},{2... | collective-permute-start | bytes 1179656 | tf_op jit(solution)/shard_map/ppermute | solution.py:1142
  390.4 27.5 %collective-permute-start.38 = (bf16[384,512]{1,0:T(8,128)(2,1)}, bf16[384,512]{1,0:T(8,128)(2,1)S(1)}, u32[]{:S(2)}, u32[]{:S(2)}) collective-permute-start(bf16[384,512]{1,0:T(8,128)(2,1)} %get-tuple-element.367), channel_id=1, source_target_pairs={{8,0},{12,4},{16,8},{20,12},{24,16},{28,20},{9,1},{13,5},{17,9},{2... | collective-permute-start | bytes 1179656 | tf_op jit(solution)/shard_map/ppermute | solution.py:1142
  431.4 19.2 %collective-permute-start.45 = (bf16[192,2048]{1,0:T(8,128)(2,1)}, bf16[192,2048]{1,0:T(8,128)(2,1)S(1)}, u32[]{:S(2)}, u32[]{:S(2)}) collective-permute-start(bf16[192,2048]{1,0:T(8,128)(2,1)} %get-tuple-element.390), channel_id=1, source_target_pairs={{0,1},{1,0},{2,3},{3,2},{4,5},{5,4},{6,7},{7,6},{8,9},{9,8},{10,11... | collective-permute-start | bytes 2359304 | tf_op jit(solution)/shard_map/ppermute | solution.py:1145
  (92 other events, 749.8 us)
Sparse Core Ops, SparseCore 0:
  19.3 55.3 all-gather.2
  167.9 148.7 reduce-scatter.3
  319.1 123.8 reduce-scatter.5
  452.2 48.0 reduce-scatter.7

commit v7 on v6

--- a/solution.py
+++ b/solution.py
@@ -20,7 +20,7 @@
 LOG_LANE = 64
 MIB = 2**20
 SMALL = pl.CostEstimate(flops=1, bytes_accessed=1, transcendentals=0)
-WHOLE_VMEM = pltpu.CompilerParams(vmem_limit_bytes=60 * MIB)
+WHOLE_VMEM = pltpu.CompilerParams(vmem_limit_bytes=52 * MIB)
 
 f32 = jnp.float32
 bf16 = jnp.bfloat16
@@ -874,7 +874,7 @@
             out_specs=[pl.BlockSpec((v.shape[0], step), lambda i, m: (0, i)) for v in shapes],
         ),
         out_shape=shapes,
-        compiler_params=WHOLE_VMEM,
+        compiler_params=pltpu.CompilerParams(vmem_limit_bytes=46 * MIB),
         cost_estimate=SMALL,
         name="products",
     )(meta, *lefts, *rights)

time: 527 us -> 518 us (0.983)
  Pallas kernels: 249 us -> 223 us
  waiting for transfers between devices: 145 us -> 170 us
    ppermute x35, waiting for transfers between devices: 39.6 us -> 49 us  [across(): return lax.ppermute(value, 'head', [(i, i ^ bits) for i in range(n_head)])]
    reduce_scatter x3, waiting for transfers between devices: 0.02 us -> 7.49 us  [scatter_seq(): return lax.psum_scatter(value, 'seq', scatter_dimension=0, tiled=tiled)]
    unnamed x113 -> x117, local copies, waits for them, and re-layouts: 11.7 us -> 11.9 us
  transfers between devices with their start and end apart: 60 -> 60, of which waited for: 28 -> 30; matrix products, arithmetic and copies ran while one was open for 6% -> 5% of each run, Pallas kernels for 38% -> 34%
where the time goes in v7:
time: 518 us; the launch traced here: 511 us
  Pallas kernels  223 us (43%)
  waiting for transfers between devices  170 us (33%)
  starting transfers between devices  58.8 us (11%)
  local copies, waits for them, and re-layouts  18.3 us (4%)
  matrix products  15.3 us (3%)
  between operations  14.8 us (3%)
  other arithmetic  10.5 us (2%)
    ppermute x6, waiting for transfers between devices, to_previous(): return lax.ppermute(value, 'seq', [(i + 2, i) for i in range(n_seq - 2)])  81.1 us
    ppermute x35, waiting for transfers between devices, across(): return lax.ppermute(value, 'head', [(i, i ^ bits) for i in range(n_head)])  49 us
    ppermute x35, starting transfers between devices, across(): return lax.ppermute(value, 'head', [(i, i ^ bits) for i in range(n_head)])  34.1 us
    pallas_call x5, Pallas kernels, attend_back(): pl.pallas_call(functools.partial(attend_back_kernel, places=places, first...  33.9 us
    pallas_call x1, Pallas kernels, feed(): pl.pallas_call(feed_kernel, grid=(hidden // HIDDEN_STEP,), in_specs=[whol...  26.3 us
    pallas_call x5, Pallas kernels, attend_stage(): pl.pallas_call(functools.partial(attend_kernel, places=places, first=firs...  24.5 us
    ppermute x3, waiting for transfers between devices, to_next(): return lax.ppermute(value, 'seq', [(i, i + 2) for i in range(n_seq - 2)])  21 us
    pallas_call x2, Pallas kernels, products(): pl.pallas_call(functools.partial(products_kernel, count=len(lefts), turne...  21 us
  transfers between devices with their start and end apart: 60, of which 30 were waited for; matrix products, arithmetic and copies ran while one was open for 5% of the time, Pallas kernels for 34%

profile of v7, /device:TPU:0, one launch (start us, length us, event | category | flops | bytes accessed | tf_op | source)
XLA Modules:
  0.0 510.7 jit_solution(13219708816076805935)
XLA Ops:
  10.9 6.8 %enter.1 = (bf16[768,2048]{1,0:T(8,128)(2,1)}, f32[768,256]{1,0:T(8,128)S(1)}, bf16[768,512]{1,0:T(8,128)(2,1)}) custom-call(bf16[768,2048]{1,0:T(8,128)(2,1)} %refs_3_.3, f32[1,2048]{1,0:T(1,128)S(1)} %bitcast.49, bf16[2048,256]{1,0:T(8,128)(2,1)} %key_w_ref.3, bf16[2048,256]{1,0:T(8,128)(2,1)} %value_w_ref.3, f32[1,128]{1,0:T(1,128)S(1)} %bitcast.57, ...), custom_call_target="tpu_custom_call" | custom-call | flops 1 | bytes 1 | tf_op jit(solution)/shard_map/enter/pallas_call | solution.py:112
  47.1 6.9 %attend_stage.5 = (f32[768,512]{1,0:T(8,128)}, f32[768,512]{1,0:T(8,128)}) custom-call(s32[4]{0:T(128)S(1)} %get-tuple-element.443.meta, bf16[768,1024]{1,0:T(8,128)(2,1)} %query_prep.1.q_ref, bf16[768,512]{1,0:T(8,128)(2,1)S(1)} %copy-done.8, bf16[768,512]{1,0:T(8,128)(2,1)} %collective-permute-done.2.refs_1_.refs_0_, ...), custom_call_target="tpu_custom_call" | custom-call | flops 1 | bytes 1 | tf_op jit(solution)/shard_map/attend_stage/pallas_call | solution.py:325
  54.0 9.9 %collective-permute-done.1.refs_0_ = bf16[768,512]{1,0:T(8,128)(2,1)S(1)} collective-permute-done((bf16[768,512]{1,0:T(8,128)(2,1)}, bf16[768,512]{1,0:T(8,128)(2,1)S(1)}, u32[]{:S(2)}, u32[]{:S(2)}) %collective-permute-start.1) | collective-permute-done | bytes 786464 | tf_op jit(solution)/shard_map/ppermute | solution.py:1139
  78.8 6.8 %collective-permute-done.3.refs_0_ = bf16[768,512]{1,0:T(8,128)(2,1)S(1)} collective-permute-done((bf16[768,512]{1,0:T(8,128)(2,1)S(1)}, bf16[768,512]{1,0:T(8,128)(2,1)S(1)}, u32[]{:S(2)}, u32[]{:S(2)}) %collective-permute-start.3) | collective-permute-done | bytes 786464 | tf_op jit(solution)/shard_map/ppermute | solution.py:1139
  108.9 9.5 %fusion.11.d_mixed_ref = f32[768,1536]{1,0:T(8,128)} fusion(bf16[768,2048]{1,0:T(8,128)(2,1)S(1)} %copy-done.42, bf16[1536,2048]{1,0:T(8,128)(2,1)} %refs_1_.1), kind=kOutput, calls=%fused_computation.43 | convolution fusion | flops 4831838208 | bytes 14155776 | tf_op jit(solution)/shard_map/dot_general | solution.py:36
  129.2 14.4 %project.1 = (f32[192,2048]{1,0:T(8,128)}, bf16[768,2048]{1,0:T(8,128)(2,1)}) custom-call(s32[6]{0:T(128)S(1)} %stack.130.meta, bf16[768,2048]{1,0:T(8,128)(2,1)} %refs_3_.3, bf16[768,256]{1,0:T(8,128)(2,1)S(1)} %get-tuple-element.263.refs_0_, bf16[768,256]{1,0:T(8,128)(2,1)S(1)} %copy-done.28, bf16[768,256]{1,0:T(8,128)(2,1)S(1)} %copy-done.26, ...), custom_call_target="tpu_custom_call" | custom-call | flops 1 | bytes 1 | tf_op jit(solution)/shard_map/project/pallas_call | solution.py:564
  143.7 26.3 %feed.1 = (bf16[768,1536]{1,0:T(8,128)(2,1)}, bf16[768,1536]{1,0:T(8,128)(2,1)}, bf16[768,1536]{1,0:T(8,128)(2,1)}, bf16[2048,3072]{1,0:T(8,128)(2,1)}) custom-call(bf16[768,2048]{1,0:T(8,128)(2,1)} %get-tuple-element.275.x_ref, bf16[2048,1536]{1,0:T(8,128)(2,1)} %refs_2_.1, bf16[2048,1536]{1,0:T(8,128)(2,1)} %refs_3_.2, f32[768,1536]{1,0:T(8,128)} %fusion.11.d_mixed_ref), custom_call_target="tpu_custom_call" | custom-call | flops 1 | bytes 1 | tf_op jit(solution)/shard_map/feed/pallas_call | solution.py:812
  173.4 13.3 %products.2 = (bf16[192,2048]{1,0:T(8,128)(2,1)S(1)}, bf16[192,2048]{1,0:T(8,128)(2,1)S(1)}, bf16[384,2048]{1,0:T(8,128)(2,1)S(1)}) custom-call(s32[1]{0:T(128)} %bitcast.meta, bf16[768,1536]{1,0:T(8,128)(2,1)S(1)} %copy-done.14, bf16[768,1536]{1,0:T(8,128)(2,1)S(1)} %copy-done.15, bf16[2048,1536]{1,0:T(8,128)(2,1)} %refs_2_.1, bf16[2048,1536]{1,0:T(8,128)(2,1)} %refs_3_.2), custom_call_target="tpu_custom_call" | custom-call | flops 1 | bytes 1 | tf_op jit(solution)/shard_map/products/pallas_call | solution.py:868
  187.8 7.7 %products.3 = (bf16[192,2048]{1,0:T(8,128)(2,1)S(1)}, bf16[192,2048]{1,0:T(8,128)(2,1)S(1)}, bf16[384,2048]{1,0:T(8,128)(2,1)S(1)}) custom-call(s32[1]{0:T(128)} %bitcast.meta, bf16[768,1536]{1,0:T(8,128)(2,1)S(1)} %copy-done.3, bf16[1536,2048]{1,0:T(8,128)(2,1)} %refs_1_.1), custom_call_target="tpu_custom_call" | custom-call | flops 1 | bytes 1 | tf_op jit(solution)/shard_map/products/pallas_call | solution.py:868
  209.6 9.2 %down_sums.1.refs_6_ = bf16[8,2048,256]{2,1,0:T(8,128)(2,1)} custom-call(bf16[768,1536]{1,0:T(8,128)(2,1)} %get-tuple-element.281.refs_0_.mixed_ref, bf16[768,2048]{1,0:T(8,128)(2,1)} %refs_4_.1), custom_call_target="tpu_custom_call" | custom-call | flops 1 | bytes 1 | tf_op jit(solution)/shard_map/down_sums/pallas_call | solution.py:893
  218.9 10.5 %turn.1 = (bf16[192,512]{1,0:T(8,128)(2,1)S(1)}, bf16[192,512]{1,0:T(8,128)(2,1)S(1)}, bf16[192,512]{1,0:T(8,128)(2,1)S(1)}, bf16[192,512]{1,0:T(8,128)(2,1)S(1)...) custom-call(s32[2]{0:T(128)S(1)} %pad_add_fusion.5.meta, ...), custom_call_target="tpu_custom_call" | custom-call | flops 1 | bytes 1 | tf_op jit(solution)/shard_map/turn/pallas_call | solution.py:719
  250.3 6.5 %collective-permute-done.24.refs_4_ = bf16[192,2048]{1,0:T(8,128)(2,1)S(1)} collective-permute-done((bf16[192,2048]{1,0:T(8,128)(2,1)S(1)}, bf16[192,2048]{1,0:T(8,128)(2,1)S(1)}, u32[]{:S(2)}, u32[]{:S(2)}) %collective-permute-start.24) | collective-permute-done | bytes 786464 | tf_op jit(solution)/shard_map/ppermute | solution.py:1145
  269.6 19.0 %collective-permute-done.28.refs_0_ = bf16[384,512]{1,0:T(8,128)(2,1)S(1)} collective-permute-done((bf16[384,512]{1,0:T(8,128)(2,1)S(1)}, bf16[384,512]{1,0:T(8,128)(2,1)S(1)}, u32[]{:S(2)}, u32[]{:S(2)}) %collective-permute-start.28) | collective-permute-done | bytes 393248 | tf_op jit(solution)/shard_map/ppermute | solution.py:1142
  296.8 17.6 %collective-permute-done.29.refs_1_ = bf16[384,512]{1,0:T(8,128)(2,1)S(1)} collective-permute-done((bf16[384,512]{1,0:T(8,128)(2,1)}, bf16[384,512]{1,0:T(8,128)(2,1)S(1)}, u32[]{:S(2)}, u32[]{:S(2)}) %collective-permute-start.29) | collective-permute-done | bytes 393248 | tf_op jit(solution)/shard_map/ppermute | solution.py:1142
  314.4 7.5 %reduce-scatter.4.cloned.1.call-done.sum_ref = bf16[256,3072]{1,0:T(8,128)(2,1)} async-done(((bf16[2048,3072]{1,0:T(8,128)(2,1)}), bf16[256,3072]{1,0:T(8,128)(2,1)}) %reduce-scatter.4.cloned.1.call-update) | async-done | bytes 1572880 | tf_op jit(solution)/shard_map/reduce_scatter | solution.py:1317
  328.3 6.4 %attend_back.7 = (f32[768,512]{1,0:T(8,128)}, f32[768,512]{1,0:T(8,128)}, bf16[768,512]{1,0:T(8,128)(2,1)S(1)}) custom-call(s32[4]{0:T(128)S(1)} %get-tuple-element.445.meta, bf16[768,1024]{1,0:T(8,128)(2,1)} %get-tuple-element.262.q_ref, bf16[768,1024]{1,0:T(8,128)(2,1)} %with_delta.1.do_ref, ...), custom_call_target="tpu_custom_call", output_to_operand_aliasing={{0}: (6, {})} | custom-call | flops 1 | bytes 1 | tf_op jit(solution)/shard_map/attend_back/pallas_call | solution.py:512
  334.7 11.0 %collective-permute-done.33.refs_0_ = bf16[384,512]{1,0:T(8,128)(2,1)S(1)} collective-permute-done((bf16[384,512]{1,0:T(8,128)(2,1)S(1)}, bf16[384,512]{1,0:T(8,128)(2,1)S(1)}, u32[]{:S(2)}, u32[]{:S(2)}) %collective-permute-start.33) | collective-permute-done | bytes 393248 | tf_op jit(solution)/shard_map/ppermute | solution.py:1142
  355.4 14.2 %collective-permute-done.37.refs_1_ = bf16[384,512]{1,0:T(8,128)(2,1)S(1)} collective-permute-done((bf16[384,512]{1,0:T(8,128)(2,1)S(1)}, bf16[384,512]{1,0:T(8,128)(2,1)S(1)}, u32[]{:S(2)}, u32[]{:S(2)}) %collective-permute-start.37) | collective-permute-done | bytes 393248 | tf_op jit(solution)/shard_map/ppermute | solution.py:1142
  377.7 10.1 %attend_back.9 = (f32[768,512]{1,0:T(8,128)}, f32[768,512]{1,0:T(8,128)}) custom-call(s32[4]{0:T(128)S(1)} %get-tuple-element.443.meta, bf16[768,1024]{1,0:T(8,128)(2,1)} %get-tuple-element.262.q_ref, bf16[768,1024]{1,0:T(8,128)(2,1)} %with_delta.1.do_ref, bf16[768,512]{1,0:T(8,128)(2,1)S(1)} %copy-done.9, ...), custom_call_target="tpu_custom_call", output_to_operand_aliasing={{0}: (5, {})} | custom-call | flops 1 | bytes 1 | tf_op jit(solution)/shard_map/attend_back/pallas_call | solution.py:512
  389.1 9.9 %collective-permute-done.42.first_ref = bf16[384,512]{1,0:T(8,128)(2,1)S(1)} collective-permute-done((bf16[384,512]{1,0:T(8,128)(2,1)S(1)}, bf16[384,512]{1,0:T(8,128)(2,1)S(1)}, u32[]{:S(2)}, u32[]{:S(2)}) %collective-permute-start.42) | collective-permute-done | bytes 393248 | tf_op jit(solution)/shard_map/ppermute | solution.py:1142
  406.5 9.3 %collective-permute-done.38.second_ref = bf16[384,512]{1,0:T(8,128)(2,1)S(1)} collective-permute-done((bf16[384,512]{1,0:T(8,128)(2,1)S(1)}, bf16[384,512]{1,0:T(8,128)(2,1)S(1)}, u32[]{:S(2)}, u32[]{:S(2)}) %collective-permute-start.38) | collective-permute-done | bytes 393248 | tf_op jit(solution)/shard_map/ppermute | solution.py:1142
  415.8 12.3 %leave.1 = (bf16[768,256]{1,0:T(8,128)(2,1)S(1)}, bf16[768,256]{1,0:T(8,128)(2,1)S(1)}, f32[1,128]{1,0:T(1,128)S(1)}, f32[1,2048]{1,0:T(1,128)S(1)}, bf16[192,20...) custom-call(s32[1]{0:T(128)} %bitcast.meta, bf16[768,2048]{1,0:T(8,128)(2,1)} %refs_3_.3, ...), custom_call_target="tpu_custom_call" | custom-call | flops 1 | bytes 1 | tf_op jit(solution)/shard_map/leave/pallas_call | solution.py:1065
  430.6 8.5 %attn_sums.1 = bf16[2048,1024]{1,0:T(8,128)(2,1)} custom-call(bf16[768,2048]{1,0:T(8,128)(2,1)} %get-tuple-element.241.x_ref, bf16[768,512]{1,0:T(8,128)(2,1)S(1)} %copy-done.7, bf16[768,256]{1,0:T(8,128)(2,1)S(1)} %get-tuple-element.396.refs_1_, bf16[768,256]{1,0:T(8,128)(2,1)S(1)} %get-tuple-element.397.refs_2_), custom_call_target="tpu_custom_call" | custom-call | flops 1 | bytes 1 | tf_op jit(solution)/shard_map/attn_sums/pallas_call | solution.py:1109
  439.1 8.5 %collective-permute-done.45.x_ref = bf16[192,2048]{1,0:T(8,128)(2,1)S(1)} collective-permute-done((bf16[192,2048]{1,0:T(8,128)(2,1)}, bf16[192,2048]{1,0:T(8,128)(2,1)S(1)}, u32[]{:S(2)}, u32[]{:S(2)}) %collective-permute-start.45) | collective-permute-done | bytes 786464 | tf_op jit(solution)/shard_map/ppermute | solution.py:1145
  (305 shorter events, 233.5 us)
Async XLA Ops:
  7.2 80.7 %all-gather.3.cloned.1.call-start = ((), (), s32[]{:S(2)}) async-start(), calls=%async_computation.6 | async-start | bytes 5242880 | tf_op jit(solution)/shard_map/all_gather | solution.py:1258
  19.7 302.2 %reduce-scatter.4.cloned.1.call-start = ((), (), s32[]{:S(2)}) async-start(), calls=%async_computation.3 | async-start | bytes 14155776 | tf_op jit(solution)/shard_map/reduce_scatter | solution.py:1317
  19.8 27.3 %collective-permute-start.2 = (bf16[768,512]{1,0:T(8,128)(2,1)}, bf16[768,512]{1,0:T(8,128)(2,1)}, u32[]{:S(2)}, u32[]{:S(2)}) collective-permute-start(bf16[768,512]{1,0:T(8,128)(2,1)} %get-tuple-element.240.refs_0_), channel_id=1, source_target_pairs={{0,4},{4,0},{8,12},{12,8},{16,20},{20,16},{24,28},{28,24},{1,5},{5... | collective-permute-start | bytes 2359304 | tf_op jit(solution)/shard_map/ppermute | solution.py:1136
  20.3 22.2 %collective-permute-start = (bf16[768,512]{1,0:T(8,128)(2,1)}, bf16[768,512]{1,0:T(8,128)(2,1)}, u32[]{:S(2)}, u32[]{:S(2)}) collective-permute-start(bf16[768,512]{1,0:T(8,128)(2,1)} %get-tuple-element.240.refs_0_), channel_id=1, source_target_pairs={{0,8},{4,12},{8,16},{12,20},{16,24},{20,28},{1,9},{5,13},{9,17},{1... | collective-permute-start | bytes 2359304 | tf_op jit(solution)/shard_map/ppermute | solution.py:1139
  42.5 21.3 %collective-permute-start.1 = (bf16[768,512]{1,0:T(8,128)(2,1)}, bf16[768,512]{1,0:T(8,128)(2,1)S(1)}, u32[]{:S(2)}, u32[]{:S(2)}) collective-permute-start(bf16[768,512]{1,0:T(8,128)(2,1)} %collective-permute-done.refs_0_), channel_id=1, source_target_pairs={{0,8},{4,12},{8,16},{12,20},{16,24},{20,28},{1,9},{5,13},{9,17},{1... | collective-permute-start | bytes 2359304 | tf_op jit(solution)/shard_map/ppermute | solution.py:1139
  47.0 21.4 %collective-permute-start.5 = (bf16[768,512]{1,0:T(8,128)(2,1)}, bf16[768,512]{1,0:T(8,128)(2,1)S(1)}, u32[]{:S(2)}, u32[]{:S(2)}) collective-permute-start(bf16[768,512]{1,0:T(8,128)(2,1)} %collective-permute-done.refs_0_), channel_id=1, source_target_pairs={{0,4},{4,0},{8,12},{12,8},{16,20},{20,16},{24,28},{28,24},{1,5},{5... | collective-permute-start | bytes 2359304 | tf_op jit(solution)/shard_map/ppermute | solution.py:1136
  63.9 21.7 %collective-permute-start.3 = (bf16[768,512]{1,0:T(8,128)(2,1)S(1)}, bf16[768,512]{1,0:T(8,128)(2,1)S(1)}, u32[]{:S(2)}, u32[]{:S(2)}) collective-permute-start(bf16[768,512]{1,0:T(8,128)(2,1)S(1)} %collective-permute-done.1.refs_0_), channel_id=1, source_target_pairs={{0,8},{4,12},{8,16},{12,20},{16,24},{20,28},{1,9},{5,13},{9,17},{1... | collective-permute-start | bytes 2359304 | tf_op jit(solution)/shard_map/ppermute | solution.py:1139
  87.9 41.3 %collective-permute-start.15 = (bf16[4,256,2048]{2,1,0:T(8,128)(2,1)}, bf16[4,256,2048]{2,1,0:T(8,128)(2,1)}, u32[]{:S(2)}, u32[]{:S(2)}) collective-permute-start(bf16[4,256,2048]{2,1,0:T(8,128)(2,1)} %bitcast.63), channel_id=1, source_target_pairs={{0,4},{4,0},{8,12},{12,8},{16,20},{20,16},{24,28},{28,24},{1,5},{5... | collective-permute-start | bytes 12582920 | tf_op jit(solution)/shard_map/ppermute | solution.py:1136
  170.0 278.4 %reduce-scatter.6.cloned.1.call-start = ((), (), s32[]{:S(2)}) async-start(), calls=%async_computation.4 | async-start | bytes 9437184 | tf_op jit(solution)/shard_map/reduce_scatter | solution.py:1317
  262.3 26.3 %collective-permute-start.28 = (bf16[384,512]{1,0:T(8,128)(2,1)S(1)}, bf16[384,512]{1,0:T(8,128)(2,1)S(1)}, u32[]{:S(2)}, u32[]{:S(2)}) collective-permute-start(bf16[384,512]{1,0:T(8,128)(2,1)S(1)} %get-tuple-element.324), channel_id=1, source_target_pairs={{8,0},{12,4},{16,8},{20,12},{24,16},{28,20},{9,1},{13,5},{17,9},{2... | collective-permute-start | bytes 1179656 | tf_op jit(solution)/shard_map/ppermute | solution.py:1142
  288.6 25.8 %collective-permute-start.30 = (bf16[768,512]{1,0:T(8,128)(2,1)S(1)}, bf16[768,512]{1,0:T(8,128)(2,1)}, u32[]{:S(2)}, u32[]{:S(2)}) collective-permute-start(bf16[768,512]{1,0:T(8,128)(2,1)S(1)} %get-tuple-element.330), channel_id=1, source_target_pairs={{0,4},{4,0},{8,12},{12,8},{16,20},{20,16},{24,28},{28,24},{1,5},{5... | collective-permute-start | bytes 2359304 | tf_op jit(solution)/shard_map/ppermute | solution.py:1136
  288.6 25.8 %collective-permute-start.29 = (bf16[384,512]{1,0:T(8,128)(2,1)}, bf16[384,512]{1,0:T(8,128)(2,1)S(1)}, u32[]{:S(2)}, u32[]{:S(2)}) collective-permute-start(bf16[384,512]{1,0:T(8,128)(2,1)} %get-tuple-element.329), channel_id=1, source_target_pairs={{8,0},{12,4},{16,8},{20,12},{24,16},{28,20},{9,1},{13,5},{17,9},{2... | collective-permute-start | bytes 1179656 | tf_op jit(solution)/shard_map/ppermute | solution.py:1142
  322.0 179.9 %reduce-scatter.8.cloned.1.call-start = ((), (), s32[]{:S(2)}) async-start(), calls=%async_computation.5 | async-start | bytes 4718592 | tf_op jit(solution)/shard_map/reduce_scatter | solution.py:1317
  324.0 21.7 %collective-permute-start.31 = (bf16[192,2048]{1,0:T(8,128)(2,1)S(1)}, bf16[192,2048]{1,0:T(8,128)(2,1)S(1)}, u32[]{:S(2)}, u32[]{:S(2)}) collective-permute-start(bf16[192,2048]{1,0:T(8,128)(2,1)S(1)} %copy-done.41), channel_id=1, source_target_pairs={{0,1},{1,0},{2,3},{3,2},{4,5},{5,4},{6,7},{7,6},{8,9},{9,8},{10,11... | collective-permute-start | bytes 2359304 | tf_op jit(solution)/shard_map/ppermute | solution.py:1145
  325.5 20.2 %collective-permute-start.32 = (bf16[192,2048]{1,0:T(8,128)(2,1)S(1)}, bf16[192,2048]{1,0:T(8,128)(2,1)S(1)}, u32[]{:S(2)}, u32[]{:S(2)}) collective-permute-start(bf16[192,2048]{1,0:T(8,128)(2,1)S(1)} %copy-done.39), channel_id=1, source_target_pairs={{0,2},{1,3},{2,0},{3,1},{4,6},{5,7},{6,4},{7,5},{8,10},{9,11},{10,... | collective-permute-start | bytes 2359304 | tf_op jit(solution)/shard_map/ppermute | solution.py:1145
  345.7 26.1 %collective-permute-start.34 = (bf16[768,512]{1,0:T(8,128)(2,1)S(1)}, bf16[768,512]{1,0:T(8,128)(2,1)S(1)}, u32[]{:S(2)}, u32[]{:S(2)}) collective-permute-start(bf16[768,512]{1,0:T(8,128)(2,1)S(1)} %get-tuple-element.352), channel_id=1, source_target_pairs={{0,4},{4,0},{8,12},{12,8},{16,20},{20,16},{24,28},{28,24},{1,5},{5... | collective-permute-start | bytes 2359304 | tf_op jit(solution)/shard_map/ppermute | solution.py:1136
  345.8 23.8 %collective-permute-start.37 = (bf16[384,512]{1,0:T(8,128)(2,1)S(1)}, bf16[384,512]{1,0:T(8,128)(2,1)S(1)}, u32[]{:S(2)}, u32[]{:S(2)}) collective-permute-start(bf16[384,512]{1,0:T(8,128)(2,1)S(1)} %get-tuple-element.362), channel_id=1, source_target_pairs={{8,0},{12,4},{16,8},{20,12},{24,16},{28,20},{9,1},{13,5},{17,9},{2... | collective-permute-start | bytes 1179656 | tf_op jit(solution)/shard_map/ppermute | solution.py:1142
  350.0 19.6 %collective-permute-start.35 = (bf16[96,2048]{1,0:T(8,128)(2,1)S(1)}, bf16[96,2048]{1,0:T(8,128)(2,1)S(1)}, u32[]{:S(2)}, u32[]{:S(2)}) collective-permute-start(bf16[96,2048]{1,0:T(8,128)(2,1)S(1)} %get-tuple-element.360), channel_id=1, source_target_pairs={{0,2},{1,3},{2,0},{3,1},{4,6},{5,7},{6,4},{7,5},{8,10},{9,11},{10,... | collective-permute-start | bytes 1179656 | tf_op jit(solution)/shard_map/ppermute | solution.py:1145
  350.0 19.6 %collective-permute-start.36 = (bf16[96,2048]{1,0:T(8,128)(2,1)S(1)}, bf16[96,2048]{1,0:T(8,128)(2,1)S(1)}, u32[]{:S(2)}, u32[]{:S(2)}) collective-permute-start(bf16[96,2048]{1,0:T(8,128)(2,1)S(1)} %get-tuple-element.361), channel_id=1, source_target_pairs={{0,1},{1,0},{2,3},{3,2},{4,5},{5,4},{6,7},{7,6},{8,9},{9,8},{10,11... | collective-permute-start | bytes 1179656 | tf_op jit(solution)/shard_map/ppermute | solution.py:1145
  369.6 29.4 %collective-permute-start.41 = (bf16[768,512]{1,0:T(8,128)(2,1)S(1)}, bf16[768,512]{1,0:T(8,128)(2,1)S(1)}, u32[]{:S(2)}, u32[]{:S(2)}) collective-permute-start(bf16[768,512]{1,0:T(8,128)(2,1)S(1)} %get-tuple-element.376), channel_id=1, source_target_pairs={{0,4},{4,0},{8,12},{12,8},{16,20},{20,16},{24,28},{28,24},{1,5},{5... | collective-permute-start | bytes 2359304 | tf_op jit(solution)/shard_map/ppermute | solution.py:1136
  374.6 29.4 %collective-permute-start.40 = (bf16[192,2048]{1,0:T(8,128)(2,1)S(1)}, bf16[192,2048]{1,0:T(8,128)(2,1)S(1)}, u32[]{:S(2)}, u32[]{:S(2)}) collective-permute-start(bf16[192,2048]{1,0:T(8,128)(2,1)S(1)} %add_rows.1.refs_0_), channel_id=1, source_target_pairs={{0,2},{1,3},{2,0},{3,1},{4,6},{5,7},{6,4},{7,5},{8,10},{9,11},{10,... | collective-permute-start | bytes 2359304 | tf_op jit(solution)/shard_map/ppermute | solution.py:1145
  375.5 28.5 %collective-permute-start.39 = (bf16[192,2048]{1,0:T(8,128)(2,1)S(1)}, bf16[192,2048]{1,0:T(8,128)(2,1)S(1)}, u32[]{:S(2)}, u32[]{:S(2)}) collective-permute-start(bf16[192,2048]{1,0:T(8,128)(2,1)S(1)} %add_rows.1.refs_0_), channel_id=1, source_target_pairs={{0,1},{1,0},{2,3},{3,2},{4,5},{5,4},{6,7},{7,6},{8,9},{9,8},{10,11... | collective-permute-start | bytes 2359304 | tf_op jit(solution)/shard_map/ppermute | solution.py:1145
  376.4 22.6 %collective-permute-start.42 = (bf16[384,512]{1,0:T(8,128)(2,1)S(1)}, bf16[384,512]{1,0:T(8,128)(2,1)S(1)}, u32[]{:S(2)}, u32[]{:S(2)}) collective-permute-start(bf16[384,512]{1,0:T(8,128)(2,1)S(1)} %get-tuple-element.377), channel_id=1, source_target_pairs={{8,0},{12,4},{16,8},{20,12},{24,16},{28,20},{9,1},{13,5},{17,9},{2... | collective-permute-start | bytes 1179656 | tf_op jit(solution)/shard_map/ppermute | solution.py:1142
  387.8 28.0 %collective-permute-start.38 = (bf16[384,512]{1,0:T(8,128)(2,1)S(1)}, bf16[384,512]{1,0:T(8,128)(2,1)S(1)}, u32[]{:S(2)}, u32[]{:S(2)}) collective-permute-start(bf16[384,512]{1,0:T(8,128)(2,1)S(1)} %get-tuple-element.367), channel_id=1, source_target_pairs={{8,0},{12,4},{16,8},{20,12},{24,16},{28,20},{9,1},{13,5},{17,9},{2... | collective-permute-start | bytes 1179656 | tf_op jit(solution)/shard_map/ppermute | solution.py:1142
  (94 other events, 1208.8 us)
Sparse Core Ops, SparseCore 0:
  19.8 55.3 all-gather.2
  170.1 151.7 reduce-scatter.3
  324.2 120.2 reduce-scatter.5
  448.5 49.1 reduce-scatter.7

commit v8 on v7

--- a/solution.py
+++ b/solution.py
@@ -1291,7 +1291,7 @@
             o_second, q_back, outcome = attend_stage(
                 q_back, blocks[-1], (0, 1), bounds, metas[-1], (outcome, total), (1, groups)
             )
-            got_first, o_second = after((got_first, o_second))
+            got_first, unused = after((got_first, o_second))
             second_steps = gather_steps(o_second)
             got_second = next(second_steps)
             got_first = first_steps.send(got_first)

time: 518 us -> 518 us (level)
  no operation moved by 1% of the time
where the time goes in v8:
time: 518 us; the launch traced here: 510 us
  Pallas kernels  223 us (43%)
  waiting for transfers between devices  167 us (32%)
  starting transfers between devices  61.1 us (12%)
  local copies, waits for them, and re-layouts  18.3 us (4%)
  matrix products  15.3 us (3%)
  between operations  14.8 us (3%)
  other arithmetic  10.5 us (2%)
    ppermute x6, waiting for transfers between devices, to_previous(): return lax.ppermute(value, 'seq', [(i + 2, i) for i in range(n_seq - 2)])  80.6 us
    ppermute x35, waiting for transfers between devices, across(): return lax.ppermute(value, 'head', [(i, i ^ bits) for i in range(n_head)])  45.8 us
    ppermute x35, starting transfers between devices, across(): return lax.ppermute(value, 'head', [(i, i ^ bits) for i in range(n_head)])  36.3 us
    pallas_call x5, Pallas kernels, attend_back(): pl.pallas_call(functools.partial(attend_back_kernel, places=places, first...  33.8 us
    pallas_call x1, Pallas kernels, feed(): pl.pallas_call(feed_kernel, grid=(hidden // HIDDEN_STEP,), in_specs=[whol...  26.3 us
    pallas_call x5, Pallas kernels, attend_stage(): pl.pallas_call(functools.partial(attend_kernel, places=places, first=firs...  24.5 us
    ppermute x3, waiting for transfers between devices, to_next(): return lax.ppermute(value, 'seq', [(i, i + 2) for i in range(n_seq - 2)])  21 us
    pallas_call x2, Pallas kernels, products(): pl.pallas_call(functools.partial(products_kernel, count=len(lefts), turne...  21 us
  transfers between devices with their start and end apart: 60, of which 30 were waited for; matrix products, arithmetic and copies ran while one was open for 5% of the time, Pallas kernels for 34%

profile of v8, /device:TPU:0, one launch (start us, length us, event | category | flops | bytes accessed | tf_op | source)
XLA Modules:
  0.0 509.8 jit_solution(16988361795032803262)
XLA Ops:
  10.9 6.8 %enter.1 = (bf16[768,2048]{1,0:T(8,128)(2,1)}, f32[768,256]{1,0:T(8,128)S(1)}, bf16[768,512]{1,0:T(8,128)(2,1)}) custom-call(bf16[768,2048]{1,0:T(8,128)(2,1)} %refs_3_.3, f32[1,2048]{1,0:T(1,128)S(1)} %bitcast.49, bf16[2048,256]{1,0:T(8,128)(2,1)} %key_w_ref.3, bf16[2048,256]{1,0:T(8,128)(2,1)} %value_w_ref.3, f32[1,128]{1,0:T(1,128)S(1)} %bitcast.57, ...), custom_call_target="tpu_custom_call" | custom-call | flops 1 | bytes 1 | tf_op jit(solution)/shard_map/enter/pallas_call | solution.py:112
  47.1 6.9 %attend_stage.5 = (f32[768,512]{1,0:T(8,128)}, f32[768,512]{1,0:T(8,128)}) custom-call(s32[4]{0:T(128)S(1)} %get-tuple-element.441.meta, bf16[768,1024]{1,0:T(8,128)(2,1)} %query_prep.1.q_ref, bf16[768,512]{1,0:T(8,128)(2,1)S(1)} %copy-done.8, bf16[768,512]{1,0:T(8,128)(2,1)} %collective-permute-done.2.refs_1_.refs_0_, ...), custom_call_target="tpu_custom_call" | custom-call | flops 1 | bytes 1 | tf_op jit(solution)/shard_map/attend_stage/pallas_call | solution.py:325
  54.0 9.9 %collective-permute-done.1.refs_0_ = bf16[768,512]{1,0:T(8,128)(2,1)S(1)} collective-permute-done((bf16[768,512]{1,0:T(8,128)(2,1)}, bf16[768,512]{1,0:T(8,128)(2,1)S(1)}, u32[]{:S(2)}, u32[]{:S(2)}) %collective-permute-start.1) | collective-permute-done | bytes 786464 | tf_op jit(solution)/shard_map/ppermute | solution.py:1139
  78.8 6.8 %collective-permute-done.3.refs_0_ = bf16[768,512]{1,0:T(8,128)(2,1)S(1)} collective-permute-done((bf16[768,512]{1,0:T(8,128)(2,1)S(1)}, bf16[768,512]{1,0:T(8,128)(2,1)S(1)}, u32[]{:S(2)}, u32[]{:S(2)}) %collective-permute-start.3) | collective-permute-done | bytes 786464 | tf_op jit(solution)/shard_map/ppermute | solution.py:1139
  107.8 9.5 %fusion.11.d_mixed_ref = f32[768,1536]{1,0:T(8,128)} fusion(bf16[768,2048]{1,0:T(8,128)(2,1)S(1)} %copy-done.42, bf16[1536,2048]{1,0:T(8,128)(2,1)} %refs_1_.1), kind=kOutput, calls=%fused_computation.43 | convolution fusion | flops 4831838208 | bytes 14155776 | tf_op jit(solution)/shard_map/dot_general | solution.py:36
  127.1 14.4 %project.1 = (f32[192,2048]{1,0:T(8,128)}, bf16[768,2048]{1,0:T(8,128)(2,1)}) custom-call(s32[6]{0:T(128)S(1)} %stack.130.meta, bf16[768,2048]{1,0:T(8,128)(2,1)} %refs_3_.3, bf16[768,256]{1,0:T(8,128)(2,1)S(1)} %get-tuple-element.262.refs_0_, bf16[768,256]{1,0:T(8,128)(2,1)S(1)} %copy-done.28, bf16[768,256]{1,0:T(8,128)(2,1)S(1)} %copy-done.26, ...), custom_call_target="tpu_custom_call" | custom-call | flops 1 | bytes 1 | tf_op jit(solution)/shard_map/project/pallas_call | solution.py:564
  141.6 26.3 %feed.1 = (bf16[768,1536]{1,0:T(8,128)(2,1)}, bf16[768,1536]{1,0:T(8,128)(2,1)}, bf16[768,1536]{1,0:T(8,128)(2,1)}, bf16[2048,3072]{1,0:T(8,128)(2,1)}) custom-call(bf16[768,2048]{1,0:T(8,128)(2,1)} %get-tuple-element.273.x_ref, bf16[2048,1536]{1,0:T(8,128)(2,1)} %refs_2_.1, bf16[2048,1536]{1,0:T(8,128)(2,1)} %refs_3_.2, f32[768,1536]{1,0:T(8,128)} %fusion.11.d_mixed_ref), custom_call_target="tpu_custom_call" | custom-call | flops 1 | bytes 1 | tf_op jit(solution)/shard_map/feed/pallas_call | solution.py:812
  171.3 13.3 %products.2 = (bf16[192,2048]{1,0:T(8,128)(2,1)S(1)}, bf16[192,2048]{1,0:T(8,128)(2,1)S(1)}, bf16[384,2048]{1,0:T(8,128)(2,1)S(1)}) custom-call(s32[1]{0:T(128)} %bitcast.meta, bf16[768,1536]{1,0:T(8,128)(2,1)S(1)} %copy-done.14, bf16[768,1536]{1,0:T(8,128)(2,1)S(1)} %copy-done.15, bf16[2048,1536]{1,0:T(8,128)(2,1)} %refs_2_.1, bf16[2048,1536]{1,0:T(8,128)(2,1)} %refs_3_.2), custom_call_target="tpu_custom_call" | custom-call | flops 1 | bytes 1 | tf_op jit(solution)/shard_map/products/pallas_call | solution.py:868
  187.7 7.7 %products.3 = (bf16[192,2048]{1,0:T(8,128)(2,1)S(1)}, bf16[192,2048]{1,0:T(8,128)(2,1)S(1)}, bf16[384,2048]{1,0:T(8,128)(2,1)S(1)}) custom-call(s32[1]{0:T(128)} %bitcast.meta, bf16[768,1536]{1,0:T(8,128)(2,1)S(1)} %copy-done.3, bf16[1536,2048]{1,0:T(8,128)(2,1)} %refs_1_.1), custom_call_target="tpu_custom_call" | custom-call | flops 1 | bytes 1 | tf_op jit(solution)/shard_map/products/pallas_call | solution.py:868
  207.8 9.2 %down_sums.1.refs_6_ = bf16[8,2048,256]{2,1,0:T(8,128)(2,1)} custom-call(bf16[768,1536]{1,0:T(8,128)(2,1)} %get-tuple-element.279.refs_0_.mixed_ref, bf16[768,2048]{1,0:T(8,128)(2,1)} %refs_4_.1), custom_call_target="tpu_custom_call" | custom-call | flops 1 | bytes 1 | tf_op jit(solution)/shard_map/down_sums/pallas_call | solution.py:893
  217.1 10.5 %turn.1 = (bf16[192,512]{1,0:T(8,128)(2,1)S(1)}, bf16[192,512]{1,0:T(8,128)(2,1)S(1)}, bf16[192,512]{1,0:T(8,128)(2,1)S(1)}, bf16[192,512]{1,0:T(8,128)(2,1)S(1)...) custom-call(s32[2]{0:T(128)S(1)} %pad_add_fusion.5.meta, ...), custom_call_target="tpu_custom_call" | custom-call | flops 1 | bytes 1 | tf_op jit(solution)/shard_map/turn/pallas_call | solution.py:719
  243.1 6.0 %attend_back.5 = (f32[768,512]{1,0:T(8,128)}, f32[768,512]{1,0:T(8,128)}, bf16[768,512]{1,0:T(8,128)(2,1)S(1)}) custom-call(s32[4]{0:T(128)S(1)} %get-tuple-element.442.meta, bf16[768,1024]{1,0:T(8,128)(2,1)} %get-tuple-element.261.q_ref, bf16[768,1024]{1,0:T(8,128)(2,1)} %with_delta.1.do_ref, bf16[768,512]{1,0:T(8,128)(2,1)S(1)} %collective-permute-done.3.refs_0_, ...), custom_call_target="tpu_custom_call" | custom-call | flops 1 | bytes 1 | tf_op jit(solution)/shard_map/attend_back/pallas_call | solution.py:512
  268.0 18.9 %collective-permute-done.28.refs_0_ = bf16[384,512]{1,0:T(8,128)(2,1)S(1)} collective-permute-done((bf16[384,512]{1,0:T(8,128)(2,1)S(1)}, bf16[384,512]{1,0:T(8,128)(2,1)S(1)}, u32[]{:S(2)}, u32[]{:S(2)}) %collective-permute-start.28) | collective-permute-done | bytes 393248 | tf_op jit(solution)/shard_map/ppermute | solution.py:1142
  295.2 17.3 %collective-permute-done.29.refs_1_ = bf16[384,512]{1,0:T(8,128)(2,1)S(1)} collective-permute-done((bf16[384,512]{1,0:T(8,128)(2,1)}, bf16[384,512]{1,0:T(8,128)(2,1)S(1)}, u32[]{:S(2)}, u32[]{:S(2)}) %collective-permute-start.29) | collective-permute-done | bytes 393248 | tf_op jit(solution)/shard_map/ppermute | solution.py:1142
  312.4 8.7 %reduce-scatter.4.cloned.1.call-done.sum_ref = bf16[256,3072]{1,0:T(8,128)(2,1)} async-done(((bf16[2048,3072]{1,0:T(8,128)(2,1)}), bf16[256,3072]{1,0:T(8,128)(2,1)}) %reduce-scatter.4.cloned.1.call-update) | async-done | bytes 1572880 | tf_op jit(solution)/shard_map/reduce_scatter | solution.py:1317
  327.5 6.4 %attend_back.7 = (f32[768,512]{1,0:T(8,128)}, f32[768,512]{1,0:T(8,128)}, bf16[768,512]{1,0:T(8,128)(2,1)S(1)}) custom-call(s32[4]{0:T(128)S(1)} %get-tuple-element.443.meta, bf16[768,1024]{1,0:T(8,128)(2,1)} %get-tuple-element.261.q_ref, bf16[768,1024]{1,0:T(8,128)(2,1)} %with_delta.1.do_ref, ...), custom_call_target="tpu_custom_call", output_to_operand_aliasing={{0}: (6, {})} | custom-call | flops 1 | bytes 1 | tf_op jit(solution)/shard_map/attend_back/pallas_call | solution.py:512
  333.9 11.0 %collective-permute-done.33.refs_0_ = bf16[384,512]{1,0:T(8,128)(2,1)S(1)} collective-permute-done((bf16[384,512]{1,0:T(8,128)(2,1)S(1)}, bf16[384,512]{1,0:T(8,128)(2,1)S(1)}, u32[]{:S(2)}, u32[]{:S(2)}) %collective-permute-start.33) | collective-permute-done | bytes 393248 | tf_op jit(solution)/shard_map/ppermute | solution.py:1142
  354.6 14.2 %collective-permute-done.37.refs_1_ = bf16[384,512]{1,0:T(8,128)(2,1)S(1)} collective-permute-done((bf16[384,512]{1,0:T(8,128)(2,1)S(1)}, bf16[384,512]{1,0:T(8,128)(2,1)S(1)}, u32[]{:S(2)}, u32[]{:S(2)}) %collective-permute-start.37) | collective-permute-done | bytes 393248 | tf_op jit(solution)/shard_map/ppermute | solution.py:1142
  376.9 10.1 %attend_back.9 = (f32[768,512]{1,0:T(8,128)}, f32[768,512]{1,0:T(8,128)}) custom-call(s32[4]{0:T(128)S(1)} %get-tuple-element.441.meta, bf16[768,1024]{1,0:T(8,128)(2,1)} %get-tuple-element.261.q_ref, bf16[768,1024]{1,0:T(8,128)(2,1)} %with_delta.1.do_ref, bf16[768,512]{1,0:T(8,128)(2,1)S(1)} %copy-done.9, ...), custom_call_target="tpu_custom_call", output_to_operand_aliasing={{0}: (5, {})} | custom-call | flops 1 | bytes 1 | tf_op jit(solution)/shard_map/attend_back/pallas_call | solution.py:512
  388.3 9.9 %collective-permute-done.42.first_ref = bf16[384,512]{1,0:T(8,128)(2,1)S(1)} collective-permute-done((bf16[384,512]{1,0:T(8,128)(2,1)S(1)}, bf16[384,512]{1,0:T(8,128)(2,1)S(1)}, u32[]{:S(2)}, u32[]{:S(2)}) %collective-permute-start.42) | collective-permute-done | bytes 393248 | tf_op jit(solution)/shard_map/ppermute | solution.py:1142
  405.7 9.3 %collective-permute-done.38.second_ref = bf16[384,512]{1,0:T(8,128)(2,1)S(1)} collective-permute-done((bf16[384,512]{1,0:T(8,128)(2,1)S(1)}, bf16[384,512]{1,0:T(8,128)(2,1)S(1)}, u32[]{:S(2)}, u32[]{:S(2)}) %collective-permute-start.38) | collective-permute-done | bytes 393248 | tf_op jit(solution)/shard_map/ppermute | solution.py:1142
  415.0 12.3 %leave.1 = (bf16[768,256]{1,0:T(8,128)(2,1)S(1)}, bf16[768,256]{1,0:T(8,128)(2,1)S(1)}, f32[1,128]{1,0:T(1,128)S(1)}, f32[1,2048]{1,0:T(1,128)S(1)}, bf16[192,20...) custom-call(s32[1]{0:T(128)} %bitcast.meta, bf16[768,2048]{1,0:T(8,128)(2,1)} %refs_3_.3, ...), custom_call_target="tpu_custom_call" | custom-call | flops 1 | bytes 1 | tf_op jit(solution)/shard_map/leave/pallas_call | solution.py:1065
  429.8 8.5 %attn_sums.1 = bf16[2048,1024]{1,0:T(8,128)(2,1)} custom-call(bf16[768,2048]{1,0:T(8,128)(2,1)} %get-tuple-element.240.x_ref, bf16[768,512]{1,0:T(8,128)(2,1)S(1)} %copy-done.7, bf16[768,256]{1,0:T(8,128)(2,1)S(1)} %get-tuple-element.394.refs_1_, bf16[768,256]{1,0:T(8,128)(2,1)S(1)} %get-tuple-element.395.refs_2_), custom_call_target="tpu_custom_call" | custom-call | flops 1 | bytes 1 | tf_op jit(solution)/shard_map/attn_sums/pallas_call | solution.py:1109
  438.3 8.5 %collective-permute-done.45.x_ref = bf16[192,2048]{1,0:T(8,128)(2,1)S(1)} collective-permute-done((bf16[192,2048]{1,0:T(8,128)(2,1)}, bf16[192,2048]{1,0:T(8,128)(2,1)S(1)}, u32[]{:S(2)}, u32[]{:S(2)}) %collective-permute-start.45) | collective-permute-done | bytes 786464 | tf_op jit(solution)/shard_map/ppermute | solution.py:1145
  (305 shorter events, 232.4 us)
Async XLA Ops:
  7.2 80.7 %all-gather.3.cloned.1.call-start = ((), (), s32[]{:S(2)}) async-start(), calls=%async_computation.6 | async-start | bytes 5242880 | tf_op jit(solution)/shard_map/all_gather | solution.py:1258
  19.7 301.4 %reduce-scatter.4.cloned.1.call-start = ((), (), s32[]{:S(2)}) async-start(), calls=%async_computation.3 | async-start | bytes 14155776 | tf_op jit(solution)/shard_map/reduce_scatter | solution.py:1317
  19.8 27.3 %collective-permute-start.2 = (bf16[768,512]{1,0:T(8,128)(2,1)}, bf16[768,512]{1,0:T(8,128)(2,1)}, u32[]{:S(2)}, u32[]{:S(2)}) collective-permute-start(bf16[768,512]{1,0:T(8,128)(2,1)} %get-tuple-element.239.refs_0_), channel_id=1, source_target_pairs={{0,4},{4,0},{8,12},{12,8},{16,20},{20,16},{24,28},{28,24},{1,5},{5... | collective-permute-start | bytes 2359304 | tf_op jit(solution)/shard_map/ppermute | solution.py:1136
  20.3 22.2 %collective-permute-start = (bf16[768,512]{1,0:T(8,128)(2,1)}, bf16[768,512]{1,0:T(8,128)(2,1)}, u32[]{:S(2)}, u32[]{:S(2)}) collective-permute-start(bf16[768,512]{1,0:T(8,128)(2,1)} %get-tuple-element.239.refs_0_), channel_id=1, source_target_pairs={{0,8},{4,12},{8,16},{12,20},{16,24},{20,28},{1,9},{5,13},{9,17},{1... | collective-permute-start | bytes 2359304 | tf_op jit(solution)/shard_map/ppermute | solution.py:1139
  42.5 21.3 %collective-permute-start.1 = (bf16[768,512]{1,0:T(8,128)(2,1)}, bf16[768,512]{1,0:T(8,128)(2,1)S(1)}, u32[]{:S(2)}, u32[]{:S(2)}) collective-permute-start(bf16[768,512]{1,0:T(8,128)(2,1)} %collective-permute-done.refs_0_), channel_id=1, source_target_pairs={{0,8},{4,12},{8,16},{12,20},{16,24},{20,28},{1,9},{5,13},{9,17},{1... | collective-permute-start | bytes 2359304 | tf_op jit(solution)/shard_map/ppermute | solution.py:1139
  47.0 21.4 %collective-permute-start.5 = (bf16[768,512]{1,0:T(8,128)(2,1)}, bf16[768,512]{1,0:T(8,128)(2,1)S(1)}, u32[]{:S(2)}, u32[]{:S(2)}) collective-permute-start(bf16[768,512]{1,0:T(8,128)(2,1)} %collective-permute-done.refs_0_), channel_id=1, source_target_pairs={{0,4},{4,0},{8,12},{12,8},{16,20},{20,16},{24,28},{28,24},{1,5},{5... | collective-permute-start | bytes 2359304 | tf_op jit(solution)/shard_map/ppermute | solution.py:1136
  63.9 21.7 %collective-permute-start.3 = (bf16[768,512]{1,0:T(8,128)(2,1)S(1)}, bf16[768,512]{1,0:T(8,128)(2,1)S(1)}, u32[]{:S(2)}, u32[]{:S(2)}) collective-permute-start(bf16[768,512]{1,0:T(8,128)(2,1)S(1)} %collective-permute-done.1.refs_0_), channel_id=1, source_target_pairs={{0,8},{4,12},{8,16},{12,20},{16,24},{20,28},{1,9},{5,13},{9,17},{1... | collective-permute-start | bytes 2359304 | tf_op jit(solution)/shard_map/ppermute | solution.py:1139
  87.9 39.2 %collective-permute-start.15 = (bf16[4,256,2048]{2,1,0:T(8,128)(2,1)}, bf16[4,256,2048]{2,1,0:T(8,128)(2,1)}, u32[]{:S(2)}, u32[]{:S(2)}) collective-permute-start(bf16[4,256,2048]{2,1,0:T(8,128)(2,1)} %bitcast.63), channel_id=1, source_target_pairs={{0,4},{4,0},{8,12},{12,8},{16,20},{20,16},{24,28},{28,24},{1,5},{5... | collective-permute-start | bytes 12582920 | tf_op jit(solution)/shard_map/ppermute | solution.py:1136
  167.9 279.6 %reduce-scatter.6.cloned.1.call-start = ((), (), s32[]{:S(2)}) async-start(), calls=%async_computation.4 | async-start | bytes 9437184 | tf_op jit(solution)/shard_map/reduce_scatter | solution.py:1317
  260.3 26.7 %collective-permute-start.28 = (bf16[384,512]{1,0:T(8,128)(2,1)S(1)}, bf16[384,512]{1,0:T(8,128)(2,1)S(1)}, u32[]{:S(2)}, u32[]{:S(2)}) collective-permute-start(bf16[384,512]{1,0:T(8,128)(2,1)S(1)} %get-tuple-element.322), channel_id=1, source_target_pairs={{8,0},{12,4},{16,8},{20,12},{24,16},{28,20},{9,1},{13,5},{17,9},{2... | collective-permute-start | bytes 1179656 | tf_op jit(solution)/shard_map/ppermute | solution.py:1142
  287.0 25.5 %collective-permute-start.30 = (bf16[768,512]{1,0:T(8,128)(2,1)S(1)}, bf16[768,512]{1,0:T(8,128)(2,1)}, u32[]{:S(2)}, u32[]{:S(2)}) collective-permute-start(bf16[768,512]{1,0:T(8,128)(2,1)S(1)} %get-tuple-element.328), channel_id=1, source_target_pairs={{0,4},{4,0},{8,12},{12,8},{16,20},{20,16},{24,28},{28,24},{1,5},{5... | collective-permute-start | bytes 2359304 | tf_op jit(solution)/shard_map/ppermute | solution.py:1136
  287.0 25.5 %collective-permute-start.29 = (bf16[384,512]{1,0:T(8,128)(2,1)}, bf16[384,512]{1,0:T(8,128)(2,1)S(1)}, u32[]{:S(2)}, u32[]{:S(2)}) collective-permute-start(bf16[384,512]{1,0:T(8,128)(2,1)} %get-tuple-element.327), channel_id=1, source_target_pairs={{8,0},{12,4},{16,8},{20,12},{24,16},{28,20},{9,1},{13,5},{17,9},{2... | collective-permute-start | bytes 1179656 | tf_op jit(solution)/shard_map/ppermute | solution.py:1142
  321.1 179.8 %reduce-scatter.8.cloned.1.call-start = ((), (), s32[]{:S(2)}) async-start(), calls=%async_computation.5 | async-start | bytes 4718592 | tf_op jit(solution)/shard_map/reduce_scatter | solution.py:1317
  323.2 21.8 %collective-permute-start.31 = (bf16[192,2048]{1,0:T(8,128)(2,1)S(1)}, bf16[192,2048]{1,0:T(8,128)(2,1)S(1)}, u32[]{:S(2)}, u32[]{:S(2)}) collective-permute-start(bf16[192,2048]{1,0:T(8,128)(2,1)S(1)} %copy-done.41), channel_id=1, source_target_pairs={{0,1},{1,0},{2,3},{3,2},{4,5},{5,4},{6,7},{7,6},{8,9},{9,8},{10,11... | collective-permute-start | bytes 2359304 | tf_op jit(solution)/shard_map/ppermute | solution.py:1145
  324.7 20.2 %collective-permute-start.32 = (bf16[192,2048]{1,0:T(8,128)(2,1)S(1)}, bf16[192,2048]{1,0:T(8,128)(2,1)S(1)}, u32[]{:S(2)}, u32[]{:S(2)}) collective-permute-start(bf16[192,2048]{1,0:T(8,128)(2,1)S(1)} %copy-done.39), channel_id=1, source_target_pairs={{0,2},{1,3},{2,0},{3,1},{4,6},{5,7},{6,4},{7,5},{8,10},{9,11},{10,... | collective-permute-start | bytes 2359304 | tf_op jit(solution)/shard_map/ppermute | solution.py:1145
  345.0 26.1 %collective-permute-start.34 = (bf16[768,512]{1,0:T(8,128)(2,1)S(1)}, bf16[768,512]{1,0:T(8,128)(2,1)S(1)}, u32[]{:S(2)}, u32[]{:S(2)}) collective-permute-start(bf16[768,512]{1,0:T(8,128)(2,1)S(1)} %get-tuple-element.350), channel_id=1, source_target_pairs={{0,4},{4,0},{8,12},{12,8},{16,20},{20,16},{24,28},{28,24},{1,5},{5... | collective-permute-start | bytes 2359304 | tf_op jit(solution)/shard_map/ppermute | solution.py:1136
  345.0 23.8 %collective-permute-start.37 = (bf16[384,512]{1,0:T(8,128)(2,1)S(1)}, bf16[384,512]{1,0:T(8,128)(2,1)S(1)}, u32[]{:S(2)}, u32[]{:S(2)}) collective-permute-start(bf16[384,512]{1,0:T(8,128)(2,1)S(1)} %get-tuple-element.360), channel_id=1, source_target_pairs={{8,0},{12,4},{16,8},{20,12},{24,16},{28,20},{9,1},{13,5},{17,9},{2... | collective-permute-start | bytes 1179656 | tf_op jit(solution)/shard_map/ppermute | solution.py:1142
  349.3 19.6 %collective-permute-start.35 = (bf16[96,2048]{1,0:T(8,128)(2,1)S(1)}, bf16[96,2048]{1,0:T(8,128)(2,1)S(1)}, u32[]{:S(2)}, u32[]{:S(2)}) collective-permute-start(bf16[96,2048]{1,0:T(8,128)(2,1)S(1)} %get-tuple-element.358), channel_id=1, source_target_pairs={{0,2},{1,3},{2,0},{3,1},{4,6},{5,7},{6,4},{7,5},{8,10},{9,11},{10,... | collective-permute-start | bytes 1179656 | tf_op jit(solution)/shard_map/ppermute | solution.py:1145
  349.3 19.6 %collective-permute-start.36 = (bf16[96,2048]{1,0:T(8,128)(2,1)S(1)}, bf16[96,2048]{1,0:T(8,128)(2,1)S(1)}, u32[]{:S(2)}, u32[]{:S(2)}) collective-permute-start(bf16[96,2048]{1,0:T(8,128)(2,1)S(1)} %get-tuple-element.359), channel_id=1, source_target_pairs={{0,1},{1,0},{2,3},{3,2},{4,5},{5,4},{6,7},{7,6},{8,9},{9,8},{10,11... | collective-permute-start | bytes 1179656 | tf_op jit(solution)/shard_map/ppermute | solution.py:1145
  368.8 29.4 %collective-permute-start.41 = (bf16[768,512]{1,0:T(8,128)(2,1)S(1)}, bf16[768,512]{1,0:T(8,128)(2,1)S(1)}, u32[]{:S(2)}, u32[]{:S(2)}) collective-permute-start(bf16[768,512]{1,0:T(8,128)(2,1)S(1)} %get-tuple-element.374), channel_id=1, source_target_pairs={{0,4},{4,0},{8,12},{12,8},{16,20},{20,16},{24,28},{28,24},{1,5},{5... | collective-permute-start | bytes 2359304 | tf_op jit(solution)/shard_map/ppermute | solution.py:1136
  373.8 29.4 %collective-permute-start.40 = (bf16[192,2048]{1,0:T(8,128)(2,1)S(1)}, bf16[192,2048]{1,0:T(8,128)(2,1)S(1)}, u32[]{:S(2)}, u32[]{:S(2)}) collective-permute-start(bf16[192,2048]{1,0:T(8,128)(2,1)S(1)} %add_rows.1.refs_0_), channel_id=1, source_target_pairs={{0,2},{1,3},{2,0},{3,1},{4,6},{5,7},{6,4},{7,5},{8,10},{9,11},{10,... | collective-permute-start | bytes 2359304 | tf_op jit(solution)/shard_map/ppermute | solution.py:1145
  374.6 28.6 %collective-permute-start.39 = (bf16[192,2048]{1,0:T(8,128)(2,1)S(1)}, bf16[192,2048]{1,0:T(8,128)(2,1)S(1)}, u32[]{:S(2)}, u32[]{:S(2)}) collective-permute-start(bf16[192,2048]{1,0:T(8,128)(2,1)S(1)} %add_rows.1.refs_0_), channel_id=1, source_target_pairs={{0,1},{1,0},{2,3},{3,2},{4,5},{5,4},{6,7},{7,6},{8,9},{9,8},{10,11... | collective-permute-start | bytes 2359304 | tf_op jit(solution)/shard_map/ppermute | solution.py:1145
  375.6 22.6 %collective-permute-start.42 = (bf16[384,512]{1,0:T(8,128)(2,1)S(1)}, bf16[384,512]{1,0:T(8,128)(2,1)S(1)}, u32[]{:S(2)}, u32[]{:S(2)}) collective-permute-start(bf16[384,512]{1,0:T(8,128)(2,1)S(1)} %get-tuple-element.375), channel_id=1, source_target_pairs={{8,0},{12,4},{16,8},{20,12},{24,16},{28,20},{9,1},{13,5},{17,9},{2... | collective-permute-start | bytes 1179656 | tf_op jit(solution)/shard_map/ppermute | solution.py:1142
  387.0 28.0 %collective-permute-start.38 = (bf16[384,512]{1,0:T(8,128)(2,1)S(1)}, bf16[384,512]{1,0:T(8,128)(2,1)S(1)}, u32[]{:S(2)}, u32[]{:S(2)}) collective-permute-start(bf16[384,512]{1,0:T(8,128)(2,1)S(1)} %get-tuple-element.365), channel_id=1, source_target_pairs={{8,0},{12,4},{16,8},{20,12},{24,16},{28,20},{9,1},{13,5},{17,9},{2... | collective-permute-start | bytes 1179656 | tf_op jit(solution)/shard_map/ppermute | solution.py:1142
  (94 other events, 1209.4 us)
Sparse Core Ops, SparseCore 0:
  19.8 55.3 all-gather.2
  168.1 153.0 reduce-scatter.3
  323.4 120.1 reduce-scatter.5
  447.7 49.0 reduce-scatter.7
